TPU v7x, 32 devices: a whole 2x2x4 slice. The times are simulated.
32 devices in a mesh: grid: 4 (over z), gx: 4 (over y, x), gy: 2 (over core).
Axes of the slice: x: 2, y: 2, z: 4, core: 2. Of those that a mesh axis runs over, the one named last changes fastest.
Arguments:
- adjoint: float32 [4, 24, 128, 512], P('grid', None, 'gx', 'gy'), may hold values from -6 to 6
- sea_mask: int32 [4, 128, 512], P('grid', 'gx', 'gy'), may hold values 0 or 1
- diffusivity: float32 [4, 128, 512], P('grid', 'gx', 'gy'), may hold values from 0.03 to 0.24
- aggregation: float32 [4, 128, 512], P('grid', 'gx', 'gy'), may hold values from 0.02 to 0.3
- breakup: float32 [4, 128, 512], P('grid', 'gx', 'gy'), may hold values from 0.02 to 0.3
- sponge: float32 [4, 128, 512], P('grid', 'gx', 'gy'), may hold values from 0.05 to 0.6
- settling: float32 [4, 3], replicated, may hold values from 0.05 to 0.5
- partner_flip: int32 [3, 4, 2], replicated, may hold values from 0 to 1
- row_offset: int32 [3, 4, 2], replicated, may hold values from 0 to 16
- col_offset: int32 [3, 4, 2], replicated, may hold values from 0 to 128
Outputs:
- adjoint_out: float32 [4, 24, 128, 512], P('grid', None, 'gx', 'gy')
Inputs may be any that keep to these rules, and one draw needn't show every extreme that they name: `partner_flip`: every child tile is paired with exactly one parent tile in its own tile column, in its own tile row or the row whose index differs in the lowest bit; a parent tile serves 0 to 6 child tiles. `row_offset`: the footprint lies inside the paired parent tile. `col_offset`: the footprint lies inside the paired parent tile.
All inputs are finite; a program needn't handle non-finite values. No bound on the sum of `sea_mask` on one device may be relied on, other than what follows from the above.
Results may differ from a plain program's by a relative error of at most 0.0001.
Values sent between devices are 32-bit elements; how exact they have to be, the bound alone decides.
No kernel may reach another device: no remote copies, remote signals or barrier semaphores. Data moves between devices by JAX's collectives and lax.ppermute only.
A program may use at most 64 MiB of HBM per device.

v0:
```python
import jax
import jax.numpy as jnp
from jax import lax
from jax.sharding import PartitionSpec as P

NCLS = 3
LEV = 8
STEPS = 2


relaxation = 0.125


def partner(value, axis, distance):
    mask = 2**distance
    pairs = [(source, source ^ mask) for source in range(lax.axis_size(axis))]
    return lax.ppermute(value, axis, pairs)


def spread(block, axis, holder):
    block = jnp.where(lax.axis_index(axis) == holder, block, jnp.zeros_like(block))
    return lax.psum(block, axis)


def padded_2(shard, sides, width):
    for axis, dim in sides:
        size, length = (lax.axis_size(axis), shard.shape[dim])
        up = [(i, (i + 1) % size) for i in range(size - 1)]
        down = [(j, i) for i, j in up]
        last = lax.slice_in_dim(shard, length - width, length, axis=dim)
        leading = lax.slice_in_dim(shard, 0, width, axis=dim)
        before = lax.ppermute(last, axis, up)
        after = lax.ppermute(leading, axis, down)
        shard = jnp.concatenate([before, shard, after], axis=dim)
    return shard


def block_sums(values):
    shape = values.shape
    return values.reshape(shape[:-2] + (shape[-2] // 2, 2, shape[-1] // 2, 2)).sum(axis=(-3, -1))


def expand_cells(values):
    return jnp.repeat(jnp.repeat(values, 2, axis=-2), 2, axis=-1)


def floc_adjoint(values, aggregation, breakup):
    shape = values.shape
    split = values.reshape((shape[0], NCLS, LEV) + shape[2:])
    agg = aggregation[:, None]
    brk = breakup[:, None]
    first = split[:, 0]
    second = split[:, 1]
    third = split[:, 2]
    new_first = (1.0 - agg) * first + agg * second
    new_second = brk * first + (1.0 - agg - brk) * second + agg * third
    new_third = brk * second + (1.0 - brk) * third
    return jnp.stack([new_first, new_second, new_third], axis=1).reshape(shape)


def settle_adjoint(values, rates):
    shape = values.shape
    split = values.reshape((shape[0], NCLS, LEV) + shape[2:])
    below = jnp.concatenate([split[:, :, 1:], jnp.zeros_like(split[:, :, :1])], axis=2)
    speed = rates[:, :, None, None, None]
    return ((1.0 - speed) * split + speed * below).reshape(shape)


def local(
    adjoint,
    sea_mask,
    diffusivity,
    aggregation,
    breakup,
    sponge,
    settling,
    partner_flip,
    row_offset,
    col_offset,
):
    n_grid = lax.axis_size("grid")
    slots = n_grid - 1
    grid_index = lax.axis_index("grid")
    row_index = lax.axis_index("gx")
    col_index = lax.axis_index("gy")
    partner_row = jnp.bitwise_xor(row_index, 1)
    is_parent = grid_index == 0
    own_slot = jnp.maximum(grid_index - 1, 0)
    flips_here = partner_flip[:, row_index, col_index]
    flips_there = partner_flip[:, partner_row, col_index]
    tops_here = row_offset[:, row_index, col_index]
    lefts_here = col_offset[:, row_index, col_index]
    tops_there = row_offset[:, partner_row, col_index]
    lefts_there = col_offset[:, partner_row, col_index]
    keep_here = (flips_here == 0).astype(jnp.float32)
    take_there = (flips_there == 1).astype(jnp.float32)
    components = adjoint.shape[1]
    cells_r = adjoint.shape[2]
    cells_c = adjoint.shape[3]
    half_r = cells_r // 2
    half_c = cells_c // 2
    anchor = jnp.zeros((), jnp.int32)
    settle_rates = settling[grid_index][None]
    weights = sponge[0]
    wet_mask = sea_mask.astype(jnp.float32)[:, None]
    row_ids = lax.broadcasted_iota(jnp.int32, (cells_r, cells_c), 0)
    col_ids = lax.broadcasted_iota(jnp.int32, (cells_r, cells_c), 1)
    covered = jnp.zeros((cells_r, cells_c), jnp.float32)
    for slot in range(slots):
        for tops, lefts, flags in (
            (tops_here, lefts_here, keep_here),
            (tops_there, lefts_there, take_there),
        ):
            inside = (
                (row_ids >= tops[slot])
                & (row_ids < tops[slot] + half_r)
                & (col_ids >= lefts[slot])
                & (col_ids < lefts[slot] + half_c)
            )
            covered = covered + flags[slot] * inside.astype(jnp.float32)
    state = adjoint
    for step_number in range(STEPS):
        current = state[0]
        child_block = block_sums(weights * current)
        down_here = jnp.stack(
            [
                keep_here[slot]
                * lax.dynamic_slice(
                    current,
                    (anchor, tops_here[slot], lefts_here[slot]),
                    (components, half_r, half_c),
                )
                for slot in range(slots)
            ]
        )
        down_there = jnp.stack(
            [
                take_there[slot]
                * lax.dynamic_slice(
                    current,
                    (anchor, tops_there[slot], lefts_there[slot]),
                    (components, half_r, half_c),
                )
                for slot in range(slots)
            ]
        )
        gathered_up = lax.all_gather(child_block[None], "grid", axis=0, tiled=True)[1:]
        up_keep = keep_here[:, None, None, None] * gathered_up
        up_send = (1.0 - keep_here)[:, None, None, None] * gathered_up
        up_cross, down_cross = partner((up_send, down_there), "gx", 0)
        down_all = spread(down_here + down_cross, "grid", 0)
        from_parent = down_all[own_slot]
        child_new = (1.0 - weights) * current + relaxation / 4.0 * expand_cells(from_parent)
        gathered = jnp.zeros_like(current)
        for slot in range(slots):
            for tops, lefts, pieces in (
                (tops_here, lefts_here, up_keep),
                (tops_there, lefts_there, up_cross),
            ):
                existing = lax.dynamic_slice(
                    gathered, (anchor, tops[slot], lefts[slot]), (components, half_r, half_c)
                )
                gathered = lax.dynamic_update_slice(
                    gathered, existing + pieces[slot], (anchor, tops[slot], lefts[slot])
                )
        parent_new = (1.0 - relaxation * covered) * current + gathered
        state = jnp.where(is_parent, parent_new, child_new)[None]
        state = floc_adjoint(state, aggregation, breakup)
        state = settle_adjoint(state, settle_rates)
        wet = wet_mask * state
        flux = diffusivity[:, None] * wet
        padded = padded_2(flux, (("gx", 2), ("gy", 3)), 1)
        state = (
            wet
            + padded[:, :, :-2, 1:-1]
            + padded[:, :, 2:, 1:-1]
            + padded[:, :, 1:-1, :-2]
            + padded[:, :, 1:-1, 2:]
            - 4.0 * flux
        )
    return state


def solution(mesh):
    in_specs = (
        P("grid", None, "gx", "gy"),
        P("grid", "gx", "gy"),
        P("grid", "gx", "gy"),
        P("grid", "gx", "gy"),
        P("grid", "gx", "gy"),
        P("grid", "gx", "gy"),
        P(),
        P(),
        P(),
        P(),
    )
    out_specs = P("grid", None, "gx", "gy")
    return jax.shard_map(local, mesh=mesh, in_specs=in_specs, out_specs=out_specs, check_vma=False)
```

profile of v0, /device:TPU:0, one launch (start us, length us, event | category | flops | bytes accessed | tf_op | source)
XLA Modules:
  0.0 315.1 jit_solution(3873924979812720771)
XLA Ops:
  6.5 1.6 fusion.35
  33.4 7.3 %dynamic-slice_multiply_fusion.11 = (f32[1,24,16,128]{3,2,1,0:T(8,128)}, f32[1,24,16,128]{3,2,1,0:T(8,128)S(1)}, f32[1,24,16,128]{3,2,1,0:T(8,128)}, f32[1,24,16...) fusion(f32[1,24,32,256]{3,2,1,0:T(8,128)} %param.10, s32[]{:T(128)S(6)} %select_n.61, ...), kind=kLoop, calls=%fused_computation.97 | loop fusion | flops 294912 | bytes 2359368 | tf_op jit(solution)/shard_map/mul | solution.py:127
  41.5 2.9 collective-permute-start.1
  44.5 2.7 copy.38
  47.2 2.1 mul.540
  49.2 7.2 %multiply_reduce_fusion.1 = f32[24,16,128]{0,2,1:T(8,128)} fusion(f32[24,16,2,128,2]{0,4,3,2,1:T(2,128)} %bitcast.116, f32[16,2,128,2]{3,2,1,0:T(8,128)S(1)} %mul.540), kind=kLoop, calls=%fused_computation.1 | loop fusion | flops 344064 | bytes 1015808 | tf_op jit(solution)/shard_map/reduce_sum | solution.py:40
  58.0 19.8 %all-gather = f32[96,16,128]{2,1,0:T(8,128)S(1)} all-gather(f32[24,16,128]{2,1,0:T(8,128)S(1)} %copy.39), channel_id=2, replica_groups=mesh['grid'=4,'gx'=4,'gy'=2] {'grid'}, dimensions={0}, use_global_device_ids=true | all-gather | bytes 983040 | tf_op jit(solution)/shard_map/all_gather | solution.py:147
  95.3 4.5 %multiply_subtract_fusion = f32[32,256]{1,0:T(8,128)} fusion(f32[]{:T(128)} %bitcast.20, f32[]{:T(128)} %bitcast.17, f32[]{:T(128)} %bitcast.14, f32[]{:T(128)} %bitcast.11, f32[]{:T(128)} %bitcast.8, f32[]{:T(128)} %bitcast.5, pred[256]{0:T(512)(128)(4,1)S(1)} %iota_compare_fusion, pred[256]{0:T(512)(128)(4,1)S(1)} %iota_compare_fusion.1, ...), kind=kLoop, calls=%fused_computation.99 | loop fusion | flops 204800 | bytes 36056 | tf_op jit(solution)/shard_map/sub | solution.py:166
  100.7 8.4 %dynamic_update_slice.36 = f32[24,32,256]{2,1,0:T(8,128)} dynamic-update-slice(f32[24,32,256]{2,1,0:T(8,128)} %broadcast.563.clone, f32[24,16,128]{2,1,0:T(8,128)} %slice_bitcast_fusion.11, s32[]{:T(128)} %constant.53.clone.1, s32[]{:T(128)S(6)} %select_n.61, s32[]{:T(128)S(6)} %select_n.62) | dynamic-update-slice | bytes 393220 | tf_op jit(solution)/shard_map/dynamic_update_slice | solution.py:163
  112.0 2.2 fusion.16
  114.2 2.0 fusion.27
  116.2 9.0 %dynamic_update_slice.37 = f32[24,32,256]{2,1,0:T(8,128)} dynamic-update-slice(f32[24,32,256]{2,1,0:T(8,128)} %dynamic_update_slice.36, f32[24,16,128]{2,1,0:T(8,128)} %fusion.27, s32[]{:T(128)} %constant.53.clone.1, s32[]{:T(128)S(6)} %select_n.63, s32[]{:T(128)S(6)} %select_n.64) | dynamic-update-slice | bytes 393220 | tf_op jit(solution)/shard_map/dynamic_update_slice | solution.py:163
  125.2 1.9 fusion.26
  127.1 9.0 %dynamic_update_slice.38 = f32[24,32,256]{2,1,0:T(8,128)} dynamic-update-slice(f32[24,32,256]{2,1,0:T(8,128)} %dynamic_update_slice.37, f32[24,16,128]{2,1,0:T(8,128)} %fusion.26, s32[]{:T(128)} %constant.53.clone.1, s32[]{:T(128)S(6)} %select_n.65, s32[]{:T(128)S(6)} %select_n.66) | dynamic-update-slice | bytes 393220 | tf_op jit(solution)/shard_map/dynamic_update_slice | solution.py:163
  136.1 2.0 fusion.25
  138.0 3.5 %dynamic_update_slice.39 = f32[24,32,256]{2,1,0:T(8,128)} dynamic-update-slice(f32[24,32,256]{2,1,0:T(8,128)} %dynamic_update_slice.38, f32[24,16,128]{2,1,0:T(8,128)} %fusion.25, s32[]{:T(128)} %constant.53.clone.1, s32[]{:T(128)S(6)} %select_n.67, s32[]{:T(128)S(6)} %select_n.68) | dynamic-update-slice | bytes 393220 | tf_op jit(solution)/shard_map/dynamic_update_slice | solution.py:163
  141.5 1.9 fusion.24
  143.4 9.0 %dynamic_update_slice.40 = f32[24,32,256]{2,1,0:T(8,128)} dynamic-update-slice(f32[24,32,256]{2,1,0:T(8,128)} %dynamic_update_slice.39, f32[24,16,128]{2,1,0:T(8,128)} %fusion.24, s32[]{:T(128)} %constant.53.clone.1, s32[]{:T(128)S(6)} %select_n.69, s32[]{:T(128)S(6)} %select_n.70) | dynamic-update-slice | bytes 393220 | tf_op jit(solution)/shard_map/dynamic_update_slice | solution.py:163
  153.7 9.0 %dynamic_update_slice.41 = f32[24,32,256]{2,1,0:T(8,128)} dynamic-update-slice(f32[24,32,256]{2,1,0:T(8,128)} %dynamic_update_slice.40, f32[24,16,128]{2,1,0:T(8,128)S(1)} %fusion.23, s32[]{:T(128)} %constant.53.clone.1, s32[]{:T(128)S(6)} %select_n.71, s32[]{:T(128)S(6)} %select_n.72) | dynamic-update-slice | bytes 393220 | tf_op jit(solution)/shard_map/dynamic_update_slice | solution.py:163
  163.7 1.6 copy.41
  165.4 3.3 %broadcast_in_dim.17 = f32[24,32,128,2]{1,0,3,2:T(8,128)} broadcast(f32[24,32,128]{1,0,2:T(8,128)} %copy.41), dimensions={0,1,2} | broadcast | bytes 1179648 | tf_op jit(solution)/shard_map/broadcast_in_dim | solution.py:44
  168.6 3.1 copy.42
  171.8 1.6 fusion.14
  174.3 3.4 %collective-permute-start.2 = (f32[1,24,1,256]{3,2,1,0:T(1,128)S(1)}, f32[1,24,1,256]{3,2,1,0:T(1,128)S(1)}, u32[]{:S(2)}, u32[]{:S(2)}) collective-permute-start(f32[1,24,1,256]{3,2,1,0:T(1,128)S(1)} %get-tuple-element.27), channel_id=1, source_target_pairs={{0,2},{2,4},{4,6},{1,3},{3,5},{5,7},{8,10},{10,12},{12,14},{9,11},... | collective-permute-start | bytes 73736 | tf_op jit(solution)/shard_map/ppermute | solution.py:32
  179.2 4.2 %collective-permute-done.3 = f32[1,24,1,256]{3,2,1,0:T(1,128)S(1)} collective-permute-done((f32[1,24,1,256]{3,2,1,0:T(1,128)S(1)}, f32[1,24,1,256]{3,2,1,0:T(1,128)S(1)}, u32[]{:S(2)}, u32[]{:S(2)}) %collective-permute-start.3) | collective-permute-done | bytes 24608 | tf_op jit(solution)/shard_map/ppermute | solution.py:33
  183.7 3.5 %collective-permute-start.4 = (f32[1,24,34,1]{3,2,1,0:T(8,128)S(1)}, f32[1,24,34,1]{3,2,1,0:T(8,128)S(1)}, u32[]{:S(2)}, u32[]{:S(2)}) collective-permute-start(f32[1,24,34,1]{3,2,1,0:T(8,128)S(1)} %get-tuple-element.11), channel_id=1, source_target_pairs={{0,1},{2,3},{4,5},{6,7},{8,9},{10,11},{12,13},{14,15},{16,17},{18,... | collective-permute-start | bytes 9800 | tf_op jit(solution)/shard_map/ppermute | solution.py:32
  188.7 2.3 collective-permute-done.5
  191.8 5.0 %dynamic-slice_multiply_fusion.5 = (f32[1,24,16,128]{3,2,1,0:T(8,128)}, f32[1,24,16,128]{3,2,1,0:T(8,128)S(1)}, f32[1,24,16,128]{3,2,1,0:T(8,128)S(1)}, f32[1,24...) fusion(f32[1,24,32,256]{3,2,1,0:T(8,128)S(1)} %fusion.6, s32[]{:T(128)S(6)} %select_n.61, ...), kind=kLoop, calls=%fused_computation.90 | loop fusion | flops 294912 | bytes 2359368 | tf_op jit(solution)/shard_map/mul | solution.py:127
  196.8 2.7 copy.43
  200.4 2.4 collective-permute-start.7
  202.8 7.2 %multiply_reduce_fusion = f32[24,16,128]{0,2,1:T(8,128)} fusion(f32[24,16,2,128,2]{0,4,3,2,1:T(2,128)} %bitcast.115, f32[16,2,128,2]{3,2,1,0:T(8,128)S(1)} %mul.540), kind=kLoop, calls=%fused_computation | loop fusion | flops 344064 | bytes 1015808 | tf_op jit(solution)/shard_map/reduce_sum | solution.py:40
  210.0 1.6 copy.44
  211.6 19.1 %all-gather.1 = f32[96,16,128]{2,1,0:T(8,128)S(1)} all-gather(f32[24,16,128]{2,1,0:T(8,128)S(1)} %copy.44), channel_id=3, replica_groups=mesh['grid'=4,'gx'=4,'gy'=2] {'grid'}, dimensions={0}, use_global_device_ids=true | all-gather | bytes 983040 | tf_op jit(solution)/shard_map/all_gather | solution.py:147
  231.8 7.7 %dynamic_update_slice.42 = f32[24,32,256]{2,1,0:T(8,128)S(1)} dynamic-update-slice(f32[24,32,256]{2,1,0:T(8,128)S(1)} %broadcast.563, f32[24,16,128]{2,1,0:T(8,128)S(1)} %slice_bitcast_fusion.5, s32[]{:T(128)} %constant.53.clone.1, s32[]{:T(128)S(6)} %select_n.61, s32[]{:T(128)S(6)} %select_n.62) | dynamic-update-slice | bytes 393220 | tf_op jit(solution)/shard_map/dynamic_update_slice | solution.py:163
  239.5 2.0 fusion.17
  241.6 2.8 collective-permute-done.6
  244.5 7.9 %dynamic_update_slice.43 = f32[24,32,256]{2,1,0:T(8,128)S(1)} dynamic-update-slice(f32[24,32,256]{2,1,0:T(8,128)S(1)} %dynamic_update_slice.42, f32[24,16,128]{2,1,0:T(8,128)S(1)} %fusion.22, s32[]{:T(128)} %constant.53.clone.1, s32[]{:T(128)S(6)} %select_n.63, s32[]{:T(128)S(6)} %select_n.64) | dynamic-update-slice | bytes 393220 | tf_op jit(solution)/shard_map/dynamic_update_slice | solution.py:163
  252.5 7.9 %dynamic_update_slice.44 = f32[24,32,256]{2,1,0:T(8,128)S(1)} dynamic-update-slice(f32[24,32,256]{2,1,0:T(8,128)S(1)} %dynamic_update_slice.43, f32[24,16,128]{2,1,0:T(8,128)S(1)} %fusion.21, s32[]{:T(128)} %constant.53.clone.1, s32[]{:T(128)S(6)} %select_n.65, s32[]{:T(128)S(6)} %select_n.66) | dynamic-update-slice | bytes 393220 | tf_op jit(solution)/shard_map/dynamic_update_slice | solution.py:163
  261.9 7.9 %dynamic_update_slice.46 = f32[24,32,256]{2,1,0:T(8,128)S(1)} dynamic-update-slice(f32[24,32,256]{2,1,0:T(8,128)S(1)} %dynamic_update_slice.45, f32[24,16,128]{2,1,0:T(8,128)S(1)} %fusion.19, s32[]{:T(128)} %constant.53.clone.1, s32[]{:T(128)S(6)} %select_n.69, s32[]{:T(128)S(6)} %select_n.70) | dynamic-update-slice | bytes 393220 | tf_op jit(solution)/shard_map/dynamic_update_slice | solution.py:163
  270.0 7.9 %dynamic_update_slice.47 = f32[24,32,256]{2,1,0:T(8,128)S(1)} dynamic-update-slice(f32[24,32,256]{2,1,0:T(8,128)S(1)} %dynamic_update_slice.46, f32[24,16,128]{2,1,0:T(8,128)S(1)} %fusion.18, s32[]{:T(128)} %constant.53.clone.1, s32[]{:T(128)S(6)} %select_n.71, s32[]{:T(128)S(6)} %select_n.72) | dynamic-update-slice | bytes 393220 | tf_op jit(solution)/shard_map/dynamic_update_slice | solution.py:163
  277.8 3.5 %all-reduce.7.cloned.1.call-done = f32[3,24,16,128]{3,2,1,0:T(8,128)} async-done(((f32[3,24,16,128]{3,2,1,0:T(8,128)}), f32[3,24,16,128]{3,2,1,0:T(8,128)}) %all-reduce.7.cloned.1.call-update) | async-done | bytes 589840 | tf_op jit(solution)/shard_map/psum | solution.py:22
  282.4 1.6 copy.46
  284.0 3.3 %broadcast_in_dim.20 = f32[24,32,128,2]{1,0,3,2:T(8,128)} broadcast(f32[24,32,128]{1,0,2:T(8,128)} %copy.46), dimensions={0,1,2} | broadcast | bytes 1179648 | tf_op jit(solution)/shard_map/broadcast_in_dim | solution.py:44
  287.3 3.1 copy.47
  292.7 2.8 collective-permute-start.8
  297.0 4.2 %collective-permute-done.9 = f32[1,24,1,256]{3,2,1,0:T(1,128)S(1)} collective-permute-done((f32[1,24,1,256]{3,2,1,0:T(1,128)S(1)}, f32[1,24,1,256]{3,2,1,0:T(1,128)S(1)}, u32[]{:S(2)}, u32[]{:S(2)}) %collective-permute-start.9) | collective-permute-done | bytes 24608 | tf_op jit(solution)/shard_map/ppermute | solution.py:33
  304.3 2.3 collective-permute-done.11
  306.6 1.7 fusion.1
  (124 shorter events, 37.9 us)
Async XLA Ops:
  6.5 37.9 %copy-start = (f32[1,24,32,256]{3,2,1,0:T(8,128)S(1)}, f32[1,24,32,256]{3,2,1,0:T(8,128)}, u32[]{:S(2)}) copy-start(f32[1,24,32,256]{3,2,1,0:T(8,128)} %param.10) | copy-start | bytes 2359300
  6.5 156.1 %all-reduce.5.cloned.1.call-start = ((), (), s32[]{:S(2)}) async-start(), calls=%async_computation | async-start | bytes 1179648 | tf_op jit(solution)/shard_map/psum | solution.py:22
  33.3 13.8 %copy-start.15 = (f32[1,32,256]{2,1,0:T(8,128)S(1)}, f32[1,32,256]{2,1,0:T(8,128)}, u32[]{:S(2)}) copy-start(f32[1,32,256]{2,1,0:T(8,128)} %param.15) | copy-start | bytes 98308
  41.5 70.4 %collective-permute-start.1 = (f32[3,24,16,128]{3,2,1,0:T(8,128)}, f32[3,24,16,128]{3,2,1,0:T(8,128)}, u32[]{:S(2)}, u32[]{:S(2)}) collective-permute-start(f32[3,24,16,128]{3,2,1,0:T(8,128)} %pad_maximum_fusion.20), channel_id=1, source_target_pairs={{0,2},{2,0},{4,6},{6,4},{1,3},{3,1},{5,7},{7,5},{8,10},{10,8},{12,... | collective-permute-start | bytes 1769480 | tf_op jit(solution)/shard_map/ppermute | solution.py:17
  78.9 35.3 %collective-permute-start = (f32[3,24,16,128]{3,2,1,0:T(8,128)}, f32[3,24,16,128]{3,2,1,0:T(8,128)}, u32[]{:S(2)}, u32[]{:S(2)}) collective-permute-start(f32[3,24,16,128]{3,2,1,0:T(8,128)} %get-tuple-element.37), channel_id=1, source_target_pairs={{0,2},{2,0},{4,6},{6,4},{1,3},{3,1},{5,7},{7,5},{8,10},{10,8},{12,... | collective-permute-start | bytes 1769480 | tf_op jit(solution)/shard_map/ppermute | solution.py:17
  114.2 167.2 %all-reduce.7.cloned.1.call-start = ((), (), s32[]{:S(2)}) async-start(), calls=%async_computation.1 | async-start | bytes 1179648 | tf_op jit(solution)/shard_map/psum | solution.py:22
  165.4 6.4 %copy-start.3 = (f32[32,256]{1,0:T(8,128)S(1)}, f32[32,256]{1,0:T(8,128)}, u32[]{:S(2)}) copy-start(f32[32,256]{1,0:T(8,128)} %multiply_subtract_fusion) | copy-start | bytes 98308
  168.6 4.8 %copy-start.5 = (f32[1,32,256]{2,1,0:T(8,128)S(1)}, f32[1,32,256]{2,1,0:T(8,128)}, u32[]{:S(2)}) copy-start(f32[1,32,256]{2,1,0:T(8,128)} %param.13) | copy-start | bytes 98308
  168.6 4.8 %copy-start.7 = (f32[1,32,256]{2,1,0:T(8,128)S(1)}, f32[1,32,256]{2,1,0:T(8,128)}, u32[]{:S(2)}) copy-start(f32[1,32,256]{2,1,0:T(8,128)} %param.14) | copy-start | bytes 98308
  168.6 4.8 %copy-start.9 = (f32[32,256]{1,0:T(8,128)S(1)}, f32[32,256]{1,0:T(8,128)}, u32[]{:S(2)}) copy-start(f32[32,256]{1,0:T(8,128)} %get-tuple-element.39) | copy-start | bytes 98308
  168.6 4.8 %copy-start.11 = (f32[32,256]{1,0:T(8,128)S(1)}, f32[32,256]{1,0:T(8,128)}, u32[]{:S(2)}) copy-start(f32[32,256]{1,0:T(8,128)} %get-tuple-element.40) | copy-start | bytes 98308
  168.6 4.8 %copy-start.13 = (f32[32,256]{1,0:T(8,128)S(1)}, f32[32,256]{1,0:T(8,128)}, u32[]{:S(2)}) copy-start(f32[32,256]{1,0:T(8,128)} %get-tuple-element.41) | copy-start | bytes 98308
  173.4 0.8 copy-start.16
  174.3 4.9 %collective-permute-start.2 = (f32[1,24,1,256]{3,2,1,0:T(1,128)S(1)}, f32[1,24,1,256]{3,2,1,0:T(1,128)S(1)}, u32[]{:S(2)}, u32[]{:S(2)}) collective-permute-start(f32[1,24,1,256]{3,2,1,0:T(1,128)S(1)} %get-tuple-element.27), channel_id=1, source_target_pairs={{0,2},{2,4},{4,6},{1,3},{3,5},{5,7},{8,10},{10,12},{12,14},{9,11},... | collective-permute-start | bytes 73736 | tf_op jit(solution)/shard_map/ppermute | solution.py:32
  177.6 5.7 %collective-permute-start.3 = (f32[1,24,1,256]{3,2,1,0:T(1,128)S(1)}, f32[1,24,1,256]{3,2,1,0:T(1,128)S(1)}, u32[]{:S(2)}, u32[]{:S(2)}) collective-permute-start(f32[1,24,1,256]{3,2,1,0:T(1,128)S(1)} %get-tuple-element.28), channel_id=1, source_target_pairs={{2,0},{4,2},{6,4},{3,1},{5,3},{7,5},{10,8},{12,10},{14,12},{11,9},... | collective-permute-start | bytes 73736 | tf_op jit(solution)/shard_map/ppermute | solution.py:33
  183.7 5.0 %collective-permute-start.4 = (f32[1,24,34,1]{3,2,1,0:T(8,128)S(1)}, f32[1,24,34,1]{3,2,1,0:T(8,128)S(1)}, u32[]{:S(2)}, u32[]{:S(2)}) collective-permute-start(f32[1,24,34,1]{3,2,1,0:T(8,128)S(1)} %get-tuple-element.11), channel_id=1, source_target_pairs={{0,1},{2,3},{4,5},{6,7},{8,9},{10,11},{12,13},{14,15},{16,17},{18,... | collective-permute-start | bytes 9800 | tf_op jit(solution)/shard_map/ppermute | solution.py:32
  187.2 3.8 %collective-permute-start.5 = (f32[1,24,34,1]{3,2,1,0:T(8,128)S(1)}, f32[1,24,34,1]{3,2,1,0:T(8,128)S(1)}, u32[]{:S(2)}, u32[]{:S(2)}) collective-permute-start(f32[1,24,34,1]{3,2,1,0:T(8,128)S(1)} %get-tuple-element.12), channel_id=1, source_target_pairs={{1,0},{3,2},{5,4},{7,6},{9,8},{11,10},{13,12},{15,14},{17,16},{19,... | collective-permute-start | bytes 9800 | tf_op jit(solution)/shard_map/ppermute | solution.py:33
  200.4 39.1 %collective-permute-start.7 = (f32[3,24,16,128]{3,2,1,0:T(8,128)}, f32[3,24,16,128]{3,2,1,0:T(8,128)}, u32[]{:S(2)}, u32[]{:S(2)}) collective-permute-start(f32[3,24,16,128]{3,2,1,0:T(8,128)} %pad_maximum_fusion.21), channel_id=1, source_target_pairs={{0,2},{2,0},{4,6},{6,4},{1,3},{3,1},{5,7},{7,5},{8,10},{10,8},{12,... | collective-permute-start | bytes 1769480 | tf_op jit(solution)/shard_map/ppermute | solution.py:17
  210.0 29.6 %copy-start.1 = (f32[1,24,16,128]{3,2,1,0:T(8,128)S(1)}, f32[1,24,16,128]{3,2,1,0:T(8,128)}, u32[]{:S(2)}) copy-start(f32[1,24,16,128]{3,2,1,0:T(8,128)} %get-tuple-element.21) | copy-start | bytes 589828
  210.0 29.6 %copy-start.2 = (f32[1,24,16,128]{3,2,1,0:T(8,128)S(1)}, f32[1,24,16,128]{3,2,1,0:T(8,128)}, u32[]{:S(2)}) copy-start(f32[1,24,16,128]{3,2,1,0:T(8,128)} %get-tuple-element.25) | copy-start | bytes 589828
  231.7 12.7 %collective-permute-start.6 = (f32[3,24,16,128]{3,2,1,0:T(8,128)}, f32[3,24,16,128]{3,2,1,0:T(8,128)S(1)}, u32[]{:S(2)}, u32[]{:S(2)}) collective-permute-start(f32[3,24,16,128]{3,2,1,0:T(8,128)} %get-tuple-element.35), channel_id=1, source_target_pairs={{0,2},{2,0},{4,6},{6,4},{1,3},{3,1},{5,7},{7,5},{8,10},{10,8},{12,... | collective-permute-start | bytes 1769480 | tf_op jit(solution)/shard_map/ppermute | solution.py:17
  284.0 6.4 %copy-start.4 = (f32[32,256]{1,0:T(8,128)S(1)}, f32[32,256]{1,0:T(8,128)}, u32[]{:S(2)}) copy-start(f32[32,256]{1,0:T(8,128)} %multiply_subtract_fusion) | copy-start | bytes 98308
  287.3 4.5 %copy-start.6 = (f32[1,32,256]{2,1,0:T(8,128)S(1)}, f32[1,32,256]{2,1,0:T(8,128)}, u32[]{:S(2)}) copy-start(f32[1,32,256]{2,1,0:T(8,128)} %param.13) | copy-start | bytes 98308
  287.3 4.5 %copy-start.8 = (f32[1,32,256]{2,1,0:T(8,128)S(1)}, f32[1,32,256]{2,1,0:T(8,128)}, u32[]{:S(2)}) copy-start(f32[1,32,256]{2,1,0:T(8,128)} %param.14) | copy-start | bytes 98308
  287.3 4.5 %copy-start.10 = (f32[32,256]{1,0:T(8,128)S(1)}, f32[32,256]{1,0:T(8,128)}, u32[]{:S(2)}) copy-start(f32[32,256]{1,0:T(8,128)} %get-tuple-element.39) | copy-start | bytes 98308
  287.3 4.5 %copy-start.12 = (f32[32,256]{1,0:T(8,128)S(1)}, f32[32,256]{1,0:T(8,128)}, u32[]{:S(2)}) copy-start(f32[32,256]{1,0:T(8,128)} %get-tuple-element.40) | copy-start | bytes 98308
  287.3 4.5 %copy-start.14 = (f32[32,256]{1,0:T(8,128)S(1)}, f32[32,256]{1,0:T(8,128)}, u32[]{:S(2)}) copy-start(f32[32,256]{1,0:T(8,128)} %get-tuple-element.41) | copy-start | bytes 98308
  291.8 0.8 copy-start.17
  292.7 4.3 %collective-permute-start.8 = (f32[1,24,1,256]{3,2,1,0:T(1,128)S(1)}, f32[1,24,1,256]{3,2,1,0:T(1,128)S(1)}, u32[]{:S(2)}, u32[]{:S(2)}) collective-permute-start(f32[1,24,1,256]{3,2,1,0:T(1,128)S(1)} %get-tuple-element.19), channel_id=1, source_target_pairs={{0,2},{2,4},{4,6},{1,3},{3,5},{5,7},{8,10},{10,12},{12,14},{9,11},... | collective-permute-start | bytes 73736 | tf_op jit(solution)/shard_map/ppermute | solution.py:32
  295.5 5.7 %collective-permute-start.9 = (f32[1,24,1,256]{3,2,1,0:T(1,128)S(1)}, f32[1,24,1,256]{3,2,1,0:T(1,128)S(1)}, u32[]{:S(2)}, u32[]{:S(2)}) collective-permute-start(f32[1,24,1,256]{3,2,1,0:T(1,128)S(1)} %get-tuple-element.20), channel_id=1, source_target_pairs={{2,0},{4,2},{6,4},{3,1},{5,3},{7,5},{10,8},{12,10},{14,12},{11,9},... | collective-permute-start | bytes 73736 | tf_op jit(solution)/shard_map/ppermute | solution.py:33
  301.5 2.8 collective-permute-start.10
  302.8 3.8 %collective-permute-start.11 = (f32[1,24,34,1]{3,2,1,0:T(8,128)S(1)}, f32[1,24,34,1]{3,2,1,0:T(8,128)S(1)}, u32[]{:S(2)}, u32[]{:S(2)}) collective-permute-start(f32[1,24,34,1]{3,2,1,0:T(8,128)S(1)} %get-tuple-element.10), channel_id=1, source_target_pairs={{1,0},{3,2},{5,4},{7,6},{9,8},{11,10},{13,12},{15,14},{17,16},{19,... | collective-permute-start | bytes 9800 | tf_op jit(solution)/shard_map/ppermute | solution.py:33
Sparse Core Ops, SparseCore 0:
  114.3 39.5 all-reduce.4
  241.7 39.6 all-reduce.6
where the time goes:
time: 320 us; the launch traced here: 315 us
  local copies, waits for them, and re-layouts  121 us (38%)
  other arithmetic  69.2 us (22%)
  between operations  44 us (14%)
  blocking collectives  38.9 us (12%)
  starting transfers between devices  22.3 us (7%)
  waiting for transfers between devices  19.9 us (6%)
    dynamic_update_slice x12, local copies, waits for them, and re-layouts, local(): lax.dynamic_update_slice(gathered, existing + pieces[slot], (anchor, tops...  88.3 us
    all_gather x2, blocking collectives, local(): lax.all_gather(child_block[None], 'grid', axis=0, tiled=True)[1:]  38.9 us
    reduce_sum x2, other arithmetic, block_sums(): values.reshape(shape[:-2] + (shape[-2] // 2, 2, shape[-1] // 2, 2))  14.3 us
    ppermute x4, waiting for transfers between devices, padded_2(): after = lax.ppermute(leading, axis, down)  13 us
    mul x2, other arithmetic, local(): keep_here[slot]  12.3 us
    ppermute x4, starting transfers between devices, padded_2(): before = lax.ppermute(last, axis, up)  11 us
    mul x6, local copies, waits for them, and re-layouts, local(): relaxation / 4.0 * expand_cells(from_parent)  9.68 us
    add x10, other arithmetic, local(): existing + pieces[slot]  9.62 us
  transfers between devices with their start and end apart: 14, of which 9 were waited for; matrix products, arithmetic and copies ran while one was open for 45% of the time, Pallas kernels for 0%

commit v1 on v0

v1 whole, which is shorter than its diff:
```python
import functools

import jax
import jax.numpy as jnp
from jax import lax
from jax.experimental import pallas as pl
from jax.experimental.pallas import tpu as pltpu
from jax.sharding import PartitionSpec as P

NCLS = 3
LEV = 8
STEPS = 2
SLOTS = 3
LANES = 128

relaxation = 0.125

VM = pl.BlockSpec(memory_space=pltpu.VMEM)
SM = pl.BlockSpec(memory_space=pltpu.SMEM)
PARAMS = pltpu.CompilerParams(vmem_limit_bytes=16 * 2**20)


def place():
    return lax.axis_index("grid"), lax.axis_index("gx"), lax.axis_index("gy")


def pieces(flip, top, left):
    _, i, j = place()
    for slot in range(SLOTS):
        for kind, row in ((0, i), (1, jnp.bitwise_xor(i, 1))):
            yield slot, kind, flip[slot, row, j] == kind, top[slot, row, j], left[slot, row, j]


def widen(half, cells):
    row = lax.broadcasted_iota(jnp.int32, (half, cells), 0)
    col = lax.broadcasted_iota(jnp.int32, (half, cells), 1)
    return (lax.shift_right_logical(col, 1) == row).astype(jnp.float32)


def narrow(cells, half):
    row = lax.broadcasted_iota(jnp.int32, (cells, half), 0)
    col = lax.broadcasted_iota(jnp.int32, (cells, half), 1)
    return (lax.shift_right_logical(row, 1) == col).astype(jnp.float32)


def payload(flip, top, left, state, sponge, straight, crossed, rows, fine):
    comps, cells_r, cells_c = state.shape
    half_r, half_c = cells_r // 2, cells_c // 2
    grid, _, _ = place()

    @pl.when(grid == 0)
    def _():
        for slot, kind, serves, first, begin in pieces(flip, top, left):
            out = (straight, crossed)[kind][slot]

            @pl.when(serves)
            def _():
                def cut(c, carry):
                    block = pltpu.roll(state[c], lax.rem(cells_r - first, cells_r), 0)[:half_r]
                    out[c] = pltpu.roll(block, lax.rem(cells_c - begin, cells_c), 1)[:, :half_c]
                    return carry

                lax.fori_loop(0, comps, cut, 0)

    @pl.when(grid > 0)
    def _():
        weight = sponge[0]

        def fold(c, carry):
            block = weight * state[c]
            for k in range(cells_c // LANES):
                part = slice(k * LANES, (k + 1) * LANES)
                fine[k] = block[:, part]
                rows[c, :, part] = fine[k, pl.ds(0, half_r, 2), :] + fine[k, pl.ds(1, half_r, 2), :]
            return carry

        lax.fori_loop(0, comps, fold, 0)
        block = jnp.dot(
            rows[...].reshape(comps * half_r, cells_c),
            narrow(cells_c, half_c),
            precision=lax.Precision.HIGHEST,
            preferred_element_type=jnp.float32,
        ).reshape(comps, half_r, half_c)
        for slot in range(SLOTS):

            @pl.when(grid == slot + 1)
            def _():
                straight[slot][...] = block
                crossed[slot][...] = block


def first_kernel(flip, top, left, state, sponge, *rest):
    outs, (rows, fine) = rest[:-2], rest[-2:]
    payload(flip, top, left, state.at[0], sponge, outs[:SLOTS], outs[SLOTS:], rows, fine)


def edge_sides(index):
    even = lax.rem(index, 2) == 0
    return even, jnp.logical_not(even)


def update_kernel(n_cols, flip, top, left, rates, state, sponge, agg, brk, mask, diff, *rest):
    got = rest[: 2 * SLOTS]
    n_side = 2 + n_cols
    bulk, sides = rest[2 * SLOTS], rest[2 * SLOTS + 1 : 2 * SLOTS + 1 + n_side]
    nested, wide, coarse, fine = rest[2 * SLOTS + 1 + n_side :]
    comps, cells_r, cells_c = bulk.shape
    half_r, half_c = cells_r // 2, cells_c // 2
    grid, i, j = place()
    row_id = lax.broadcasted_iota(jnp.int32, (cells_r, cells_c), 0)
    col_id = lax.broadcasted_iota(jnp.int32, (cells_r, cells_c), 1)

    @pl.when(grid == 0)
    def _():
        covered = jnp.zeros((cells_r, cells_c), jnp.float32)
        for _, _, serves, first, begin in pieces(flip, top, left):
            inside = (row_id >= first) & (row_id < first + half_r) & (col_id >= begin) & (col_id < begin + half_c)
            covered = covered + jnp.where(inside & serves, 1.0, 0.0)
        keep = 1.0 - relaxation * covered

        def own(c, carry):
            nested[c] = keep * state[c]
            return carry

        lax.fori_loop(0, comps, own, 0)
        for slot, kind, serves, first, begin in pieces(flip, top, left):
            piece = got[kind * SLOTS + slot]

            @pl.when(serves)
            def _():
                def put(c, carry):
                    block = piece[c]
                    block = jnp.concatenate([block, jnp.zeros_like(block)], axis=1)
                    block = pltpu.roll(block, begin, 1)
                    block = jnp.concatenate([block, jnp.zeros_like(block)], axis=0)
                    nested[c] += pltpu.roll(block, first, 0)
                    return carry

                lax.fori_loop(0, comps, put, 0)

    @pl.when(grid > 0)
    def _():
        for slot in range(SLOTS):
            for kind in range(2):

                @pl.when((grid == slot + 1) & (flip[slot, i, j] == kind))
                def _():
                    coarse[...] = got[kind * SLOTS + slot][...]

        wide[...] = jnp.dot(
            coarse[...].reshape(comps * half_r, half_c),
            widen(half_c, cells_c) * (relaxation / 4.0),
            precision=lax.Precision.HIGHEST,
            preferred_element_type=jnp.float32,
        ).reshape(comps, half_r, cells_c)
        keep = 1.0 - sponge[0]

        def own(c, carry):
            for k in range(cells_c // LANES):
                part = slice(k * LANES, (k + 1) * LANES)
                block = wide[c, :, part]
                fine[k, pl.ds(0, half_r, 2), :] = block
                fine[k, pl.ds(1, half_r, 2), :] = block
                nested[c, :, part] = keep[:, part] * state[c, :, part] + fine[k]
            return carry

        lax.fori_loop(0, comps, own, 0)

    a, b = agg[0], brk[0]
    wet = mask[0].astype(jnp.float32)
    spread = diff[0]
    row_far = edge_sides(i)
    col_far = edge_sides(j)
    lane = lax.broadcasted_iota(jnp.int32, (cells_r, LANES), 1)

    def level(step, carry):
        below, columns = carry
        l = LEV - 1 - step
        u0, u1, u2 = nested[l], nested[LEV + l], nested[2 * LEV + l]
        flocced = ((1.0 - a) * u0 + a * u1, b * u0 + (1.0 - a - b) * u1 + a * u2, b * u1 + (1.0 - b) * u2)
        columns = list(columns)
        for cls in range(NCLS):
            c = cls * LEV + l
            rate = rates[grid, cls]
            w = wet * ((1.0 - rate) * flocced[cls] + rate * below[cls])
            f = spread * w
            total = w - 4.0 * f
            total = total + jnp.where(row_id == 0, 0.0, pltpu.roll(f, 1, 0))
            total = total + jnp.where(row_id == cells_r - 1, 0.0, pltpu.roll(f, cells_r - 1, 0))
            total = total + jnp.where(col_id == 0, 0.0, pltpu.roll(f, 1, 1))
            total = total + jnp.where(col_id == cells_c - 1, 0.0, pltpu.roll(f, cells_c - 1, 1))
            bulk[c] = total
            for phase in range(2):
                sides[phase][pl.ds(c, 1), :] = jnp.where(row_far[phase], f[cells_r - 1 :], f[:1])
            for phase in range(n_cols):
                far = col_far[phase]
                slab = jnp.where(far, f[:, cells_c - LANES :], f[:, :LANES])
                turn = lax.rem(c - jnp.where(far, LANES - 1, 0) + LANES, LANES)
                columns[phase] = jnp.where(lane == c, pltpu.roll(slab, turn, 1), columns[phase])
        return flocced, tuple(columns)

    nothing = jnp.zeros((cells_r, cells_c), jnp.float32)
    empty = jnp.zeros((cells_r, LANES), jnp.float32)
    _, columns = lax.fori_loop(0, LEV, level, ((nothing,) * NCLS, (empty,) * n_cols))
    for phase in range(n_cols):
        sides[2 + phase][...] = columns[phase]


def halo_kernel(n_cols, sizes, last, flip, top, left, bulk, sponge, *rest):
    sides = rest[: 2 + n_cols]
    state = rest[2 + n_cols]
    new = state.at[0] if last else state
    comps, cells_r, cells_c = bulk.shape
    _, i, j = place()
    row_id = lax.broadcasted_iota(jnp.int32, (cells_r, cells_c), 0)
    lane = lax.broadcasted_iota(jnp.int32, (cells_r, LANES), 1)
    row_far = edge_sides(i)
    col_far = edge_sides(j)
    row_at = [jnp.where(far, cells_r - 1, 0) for far in row_far]
    row_at[1] = jnp.where((row_far[1] & (i == sizes[0] - 1)) | (row_far[0] & (i == 0)), -1, row_at[1])
    col_at = [jnp.where(far, LANES - 1, 0) for far in col_far]
    col_on = [jnp.bool_(True), jnp.logical_not((col_far[1] & (j == sizes[1] - 1)) | (col_far[0] & (j == 0)))]

    def add(c, carry):
        total = bulk[c]
        for phase in range(2):
            total = total + jnp.where(row_id == row_at[phase], sides[phase][pl.ds(c, 1), :], 0.0)
        first, final = total[:, :LANES], total[:, cells_c - LANES :]
        for phase in range(n_cols):
            far, at = col_far[phase], col_at[phase]
            slab = pltpu.roll(sides[2 + phase][...], lax.rem(at - c + LANES, LANES), 1)
            slab = jnp.where((lane == at) & col_on[phase], slab, 0.0)
            first = first + jnp.where(far, 0.0, slab)
            final = final + jnp.where(far, slab, 0.0)
        new[c] = jnp.concatenate([first, total[:, LANES : cells_c - LANES], final], axis=1) if cells_c > 2 * LANES else jnp.concatenate([first, final], axis=1)
        return carry

    lax.fori_loop(0, comps, add, 0)
    if not last:
        outs, (rows, fine) = rest[3 + n_cols : -2], rest[-2:]
        payload(flip, top, left, new, sponge, outs[:SLOTS], outs[SLOTS:], rows, fine)


def exchange(blocks):
    n_x = lax.axis_size("gx")
    got = [None] * (2 * SLOTS)
    for slot in reversed(range(SLOTS)):
        for kind in range(2):
            pairs = []
            for i in range(n_x):
                parent, child = i, (slot + 1) * n_x + (i ^ kind)
                pairs += [(parent, child), (child, parent)]
            got[kind * SLOTS + slot] = lax.ppermute(blocks[kind * SLOTS + slot], ("grid", "gx"), pairs)
    return got


def swap_pairs(size, phase):
    pairs = []
    for k in range(phase, size + phase, 2):
        first, second = k % size, (k + 1) % size
        pairs += [(first, second), (second, first)]
    return pairs


def local(adjoint, sea_mask, diffusivity, aggregation, breakup, sponge, settling, partner_flip, row_offset, col_offset):
    comps, cells_r, cells_c = adjoint.shape[1:]
    half_r, half_c = cells_r // 2, cells_c // 2
    n_x, n_y = lax.axis_size("gx"), lax.axis_size("gy")
    n_cols = 1 if n_y == 2 else 2
    f32 = jnp.float32
    tile = jax.ShapeDtypeStruct((comps, cells_r, cells_c), f32)
    block = jax.ShapeDtypeStruct((comps, half_r, half_c), f32)
    side = [jax.ShapeDtypeStruct((comps, cells_c), f32)] * 2 + [jax.ShapeDtypeStruct((cells_r, LANES), f32)] * n_cols
    fold_scratch = [pltpu.VMEM((comps, half_r, cells_c), f32), pltpu.VMEM((cells_c // LANES, cells_r, LANES), f32)]
    tables = (partner_flip, row_offset, col_offset)

    blocks = pl.pallas_call(
        first_kernel,
        out_shape=[block] * (2 * SLOTS),
        in_specs=[SM] * 3 + [VM] * 2,
        out_specs=[VM] * (2 * SLOTS),
        scratch_shapes=fold_scratch,
        compiler_params=PARAMS,
        name="first_payload",
    )(*tables, adjoint, sponge)
    state = adjoint.reshape(tile.shape)
    for step in range(STEPS):
        last = step == STEPS - 1
        got = exchange(blocks)
        bulk, *sides = pl.pallas_call(
            functools.partial(update_kernel, n_cols),
            out_shape=[tile] + side,
            in_specs=[SM] * 4 + [VM] * (6 + 2 * SLOTS),
            out_specs=[VM] * (1 + len(side)),
            scratch_shapes=[
                pltpu.VMEM(tile.shape, f32),
                pltpu.VMEM((comps, half_r, cells_c), f32),
                pltpu.VMEM(block.shape, f32),
                pltpu.VMEM((cells_c // LANES, cells_r, LANES), f32),
            ],
            compiler_params=PARAMS,
            name="update",
        )(*tables, settling, state, sponge, aggregation, breakup, sea_mask, diffusivity, *got)
        sides = [lax.ppermute(sides[k], "gx", swap_pairs(n_x, k)) for k in range(2)] + [
            lax.ppermute(sides[2 + k], "gy", swap_pairs(n_y, k)) for k in range(n_cols)
        ]
        new = jax.ShapeDtypeStruct(adjoint.shape, f32) if last else tile
        out = pl.pallas_call(
            functools.partial(halo_kernel, n_cols, (n_x, n_y), last),
            out_shape=[new] + ([] if last else [block] * (2 * SLOTS)),
            in_specs=[SM] * 3 + [VM] * (2 + len(side)),
            out_specs=[VM] * (1 if last else 1 + 2 * SLOTS),
            scratch_shapes=[] if last else fold_scratch,
            compiler_params=PARAMS,
            name="halo_last" if last else "halo",
        )(*tables, bulk, sponge, *sides)
        state, blocks = out[0], out[1:]
    return state


def solution(mesh):
    in_specs = (
        P("grid", None, "gx", "gy"),
        P("grid", "gx", "gy"),
        P("grid", "gx", "gy"),
        P("grid", "gx", "gy"),
        P("grid", "gx", "gy"),
        P("grid", "gx", "gy"),
        P(),
        P(),
        P(),
        P(),
    )
    out_specs = P("grid", None, "gx", "gy")
    return jax.shard_map(local, mesh=mesh, in_specs=in_specs, out_specs=out_specs, check_vma=False)
```

time: 320 us -> 125 us (0.39)
  local copies, waits for them, and re-layouts: 121 us -> 3.5 us
  other arithmetic: 69.2 us -> 0 us
  Pallas kernels: 0 us -> 49.4 us
  between operations: 44 us -> 0.25 us
  blocking collectives: 38.9 us -> 0 us
  waiting for transfers between devices: 19.9 us -> 44.8 us
    dynamic_update_slice x12 -> x0, local copies, waits for them, and re-layouts: 88.3 us -> none  [local(): lax.dynamic_update_slice(gathered, existing + pieces[slot], (anchor, tops...]
    pallas_call x0 -> x5, Pallas kernels: none -> 49.4 us  [the longest x2 23.3 us: local(): pl.pallas_call(functools.partial(update_kernel, n_cols), out_shape=[tile]...]
    all_gather x2 -> x0, blocking collectives: 38.9 us -> none  [local(): lax.all_gather(child_block[None], 'grid', axis=0, tiled=True)[1:]]
    ppermute x12 -> x18, waiting for transfers between devices: 16.4 us -> 44.8 us  [the longest x12 37.2 us: exchange(): lax.ppermute(blocks[kind * SLOTS + slot], ('grid', 'gx'), pairs)]
    mul x10 -> x0, other arithmetic: 17.2 us -> none  [the longest x2 12.3 us: local(): keep_here[slot]]
    reduce_sum x2 -> x0, other arithmetic: 14.3 us -> none  [block_sums(): values.reshape(shape[:-2] + (shape[-2] // 2, 2, shape[-1] // 2, 2))]
    mul x7 -> x0, local copies, waits for them, and re-layouts: 11.8 us -> none  [the longest x6 9.68 us: local(): relaxation / 4.0 * expand_cells(from_parent)]
    add x14 -> x0, other arithmetic: 10.2 us -> none  [the longest x10 9.62 us: local(): existing + pieces[slot]]
  transfers between devices with their start and end apart: 14 -> 18, of which waited for: 9 -> 11; matrix products, arithmetic and copies ran while one was open for 45% -> 0% of each run, Pallas kernels for 0% -> 0%
where the time goes in v1:
time: 125 us; the launch traced here: 123 us
  Pallas kernels  49.4 us (40%)
  waiting for transfers between devices  44.8 us (36%)
  starting transfers between devices  25.1 us (20%)
  local copies, waits for them, and re-layouts  3.5 us (3%)
    ppermute x12, waiting for transfers between devices, exchange(): lax.ppermute(blocks[kind * SLOTS + slot], ('grid', 'gx'), pairs)  37.2 us
    pallas_call x2, Pallas kernels, local(): pl.pallas_call(functools.partial(update_kernel, n_cols), out_shape=[tile]...  23.3 us
    ppermute x12, starting transfers between devices, exchange(): lax.ppermute(blocks[kind * SLOTS + slot], ('grid', 'gx'), pairs)  23 us
    pallas_call x2, Pallas kernels, local(): pl.pallas_call(functools.partial(halo_kernel, n_cols, (n_x, n_y), last),...  15.6 us
    pallas_call x1, Pallas kernels, local(): pl.pallas_call(first_kernel, out_shape=[block] * (2 * SLOTS), in_specs=[S...  10.4 us
    ppermute x4, waiting for transfers between devices, local(): lax.ppermute(sides[k], 'gx', swap_pairs(n_x, k))  5.31 us
    unnamed x23, local copies, waits for them, and re-layouts  3.5 us
  transfers between devices with their start and end apart: 18, of which 11 were waited for; matrix products, arithmetic and copies ran while one was open for 0% of the time, Pallas kernels for 0%

profile of v1, /device:TPU:0, one launch (start us, length us, event | category | flops | bytes accessed | tf_op | source)
XLA Modules:
  0.0 123.0 jit_solution(3605048058589216052)
XLA Ops:
  0.0 0.8 copy.23.flip
  0.8 0.1 copy.24.top
  0.9 0.6 copy-done.9
  1.5 0.1 copy.25.left
  1.6 1.1 copy-done
  2.7 0.8 copy-done.1
  3.5 10.4 %first_payload.1 = (f32[24,16,128]{2,1,0:T(8,128)S(1)}, f32[24,16,128]{2,1,0:T(8,128)S(1)}, f32[24,16,128]{2,1,0:T(8,128)S(1)}, f32[24,16,128]{2,1,0:T(8,128)S(1...) custom-call(s32[3,4,2]{2,1,0:T(4,128)S(1)} %copy.23.flip, s32[3,4,2]{2,1,0:T(4,128)S(1)} %copy.24.top, ...), custom_call_target="tpu_custom_call" | custom-call | tf_op jit(solution)/shard_map/first_payload/pallas_call | solution.py:277
  13.9 1.9 %collective-permute-start = (f32[24,16,128]{2,1,0:T(8,128)S(1)}, f32[24,16,128]{2,1,0:T(8,128)S(1)}, u32[]{:S(2)}, u32[]{:S(2)}) collective-permute-start(f32[24,16,128]{2,1,0:T(8,128)S(1)} %get-tuple-element.26), channel_id=1, source_target_pairs={{0,8},{8,0},{2,10},{10,2},{4,12},{12,4},{6,14},{14,6},{1,9},{9,1},... | collective-permute-start | bytes 589832 | tf_op jit(solution)/shard_map/ppermute | solution.py:253
  15.9 1.9 %collective-permute-start.1 = (f32[24,16,128]{2,1,0:T(8,128)S(1)}, f32[24,16,128]{2,1,0:T(8,128)S(1)}, u32[]{:S(2)}, u32[]{:S(2)}) collective-permute-start(f32[24,16,128]{2,1,0:T(8,128)S(1)} %get-tuple-element.27), channel_id=1, source_target_pairs={{0,16},{16,0},{2,18},{18,2},{4,20},{20,4},{6,22},{22,6},{1,17},{17... | collective-permute-start | bytes 589832 | tf_op jit(solution)/shard_map/ppermute | solution.py:253
  17.8 1.9 %collective-permute-start.2 = (f32[24,16,128]{2,1,0:T(8,128)S(1)}, f32[24,16,128]{2,1,0:T(8,128)S(1)}, u32[]{:S(2)}, u32[]{:S(2)}) collective-permute-start(f32[24,16,128]{2,1,0:T(8,128)S(1)} %get-tuple-element.28), channel_id=1, source_target_pairs={{0,24},{24,0},{2,26},{26,2},{4,28},{28,4},{6,30},{30,6},{1,25},{25... | collective-permute-start | bytes 589832 | tf_op jit(solution)/shard_map/ppermute | solution.py:253
  19.7 1.9 %collective-permute-start.3 = (f32[24,16,128]{2,1,0:T(8,128)S(1)}, f32[24,16,128]{2,1,0:T(8,128)S(1)}, u32[]{:S(2)}, u32[]{:S(2)}) collective-permute-start(f32[24,16,128]{2,1,0:T(8,128)S(1)} %get-tuple-element.29), channel_id=1, source_target_pairs={{0,10},{10,0},{2,8},{8,2},{4,14},{14,4},{6,12},{12,6},{1,11},{11,1... | collective-permute-start | bytes 589832 | tf_op jit(solution)/shard_map/ppermute | solution.py:253
  21.7 0.0 copy-start.7
  21.7 1.9 %collective-permute-start.4 = (f32[24,16,128]{2,1,0:T(8,128)S(1)}, f32[24,16,128]{2,1,0:T(8,128)S(1)}, u32[]{:S(2)}, u32[]{:S(2)}) collective-permute-start(f32[24,16,128]{2,1,0:T(8,128)S(1)} %get-tuple-element.30), channel_id=1, source_target_pairs={{0,18},{18,0},{2,16},{16,2},{4,22},{22,4},{6,20},{20,6},{1,19},{19... | collective-permute-start | bytes 589832 | tf_op jit(solution)/shard_map/ppermute | solution.py:253
  23.6 12.3 %collective-permute-done.rest_0_ = f32[24,16,128]{2,1,0:T(8,128)S(1)} collective-permute-done((f32[24,16,128]{2,1,0:T(8,128)S(1)}, f32[24,16,128]{2,1,0:T(8,128)S(1)}, u32[]{:S(2)}, u32[]{:S(2)}) %collective-permute-start) | collective-permute-done | bytes 196640 | tf_op jit(solution)/shard_map/ppermute | solution.py:253
  35.9 1.9 %collective-permute-start.5 = (f32[24,16,128]{2,1,0:T(8,128)S(1)}, f32[24,16,128]{2,1,0:T(8,128)S(1)}, u32[]{:S(2)}, u32[]{:S(2)}) collective-permute-start(f32[24,16,128]{2,1,0:T(8,128)S(1)} %get-tuple-element.31), channel_id=1, source_target_pairs={{0,26},{26,0},{2,24},{24,2},{4,30},{30,4},{6,28},{28,6},{1,27},{27... | collective-permute-start | bytes 589832 | tf_op jit(solution)/shard_map/ppermute | solution.py:253
  37.9 0.0 collective-permute-done.1.rest_1_
  37.9 0.0 collective-permute-done.2.rest_2_
  37.9 0.0 collective-permute-done.3.rest_3_
  37.9 0.0 collective-permute-done.4.rest_4_
  37.9 8.3 %collective-permute-done.5.rest_5_ = f32[24,16,128]{2,1,0:T(8,128)S(1)} collective-permute-done((f32[24,16,128]{2,1,0:T(8,128)S(1)}, f32[24,16,128]{2,1,0:T(8,128)S(1)}, u32[]{:S(2)}, u32[]{:S(2)}) %collective-permute-start.5) | collective-permute-done | bytes 196640 | tf_op jit(solution)/shard_map/ppermute | solution.py:253
  46.2 0.0 copy-start.2
  46.2 11.7 %update.2 = (f32[24,32,256]{2,1,0:T(8,128)S(1)}, f32[24,256]{1,0:T(8,128)S(1)}, f32[24,256]{1,0:T(8,128)S(1)}, f32[32,128]{1,0:T(8,128)S(1)}) custom-call(s32[3,4,2]{2,1,0:T(4,128)S(1)} %copy.23.flip, s32[3,4,2]{2,1,0:T(4,128)S(1)} %copy.24.top, s32[3,4,2]{2,1,0:T(4,128)S(1)} %copy.25.left, f32[4,3]{1,0:T(4,128)S(1)} %copy-done.7, ...), custom_call_target="tpu_custom_call" | custom-call | tf_op jit(solution)/shard_map/update/pallas_call | solution.py:290
  57.9 0.1 collective-permute-start.6
  58.0 0.1 collective-permute-start.7
  58.1 0.1 collective-permute-start.8
  58.1 1.2 collective-permute-done.8.rest_2_
  59.3 2.5 %collective-permute-done.6.rest_0_ = f32[24,256]{1,0:T(8,128)S(1)} collective-permute-done((f32[24,256]{1,0:T(8,128)S(1)}, f32[24,256]{1,0:T(8,128)S(1)}, u32[]{:S(2)}, u32[]{:S(2)}) %collective-permute-start.6) | collective-permute-done | bytes 24608 | tf_op jit(solution)/shard_map/ppermute | solution.py:304
  61.8 1.0 collective-permute-done.7.rest_1_
  62.8 12.1 %halo.1 = (f32[24,32,256]{2,1,0:T(8,128)S(1)}, f32[24,16,128]{2,1,0:T(8,128)S(1)}, f32[24,16,128]{2,1,0:T(8,128)S(1)}, f32[24,16,128]{2,1,0:T(8,128)S(1)}, f32[2...) custom-call(s32[3,4,2]{2,1,0:T(4,128)S(1)} %copy.23.flip, s32[3,4,2]{2,1,0:T(4,128)S(1)} %copy.24.top, ...), custom_call_target="tpu_custom_call" | custom-call | tf_op jit(solution)/shard_map/halo/pallas_call | solution.py:308
  74.9 1.9 %collective-permute-start.9 = (f32[24,16,128]{2,1,0:T(8,128)S(1)}, f32[24,16,128]{2,1,0:T(8,128)S(1)}, u32[]{:S(2)}, u32[]{:S(2)}) collective-permute-start(f32[24,16,128]{2,1,0:T(8,128)S(1)} %get-tuple-element.37), channel_id=1, source_target_pairs={{0,8},{8,0},{2,10},{10,2},{4,12},{12,4},{6,14},{14,6},{1,9},{9,1},... | collective-permute-start | bytes 589832 | tf_op jit(solution)/shard_map/ppermute | solution.py:253
  76.8 1.9 %collective-permute-start.10 = (f32[24,16,128]{2,1,0:T(8,128)S(1)}, f32[24,16,128]{2,1,0:T(8,128)S(1)}, u32[]{:S(2)}, u32[]{:S(2)}) collective-permute-start(f32[24,16,128]{2,1,0:T(8,128)S(1)} %get-tuple-element.38), channel_id=1, source_target_pairs={{0,16},{16,0},{2,18},{18,2},{4,20},{20,4},{6,22},{22,6},{1,17},{17... | collective-permute-start | bytes 589832 | tf_op jit(solution)/shard_map/ppermute | solution.py:253
  78.7 1.9 %collective-permute-start.11 = (f32[24,16,128]{2,1,0:T(8,128)S(1)}, f32[24,16,128]{2,1,0:T(8,128)S(1)}, u32[]{:S(2)}, u32[]{:S(2)}) collective-permute-start(f32[24,16,128]{2,1,0:T(8,128)S(1)} %get-tuple-element.39), channel_id=1, source_target_pairs={{0,24},{24,0},{2,26},{26,2},{4,28},{28,4},{6,30},{30,6},{1,25},{25... | collective-permute-start | bytes 589832 | tf_op jit(solution)/shard_map/ppermute | solution.py:253
  80.6 1.9 %collective-permute-start.12 = (f32[24,16,128]{2,1,0:T(8,128)S(1)}, f32[24,16,128]{2,1,0:T(8,128)S(1)}, u32[]{:S(2)}, u32[]{:S(2)}) collective-permute-start(f32[24,16,128]{2,1,0:T(8,128)S(1)} %get-tuple-element.40), channel_id=1, source_target_pairs={{0,10},{10,0},{2,8},{8,2},{4,14},{14,4},{6,12},{12,6},{1,11},{11,1... | collective-permute-start | bytes 589832 | tf_op jit(solution)/shard_map/ppermute | solution.py:253
  82.6 1.9 %collective-permute-start.13 = (f32[24,16,128]{2,1,0:T(8,128)S(1)}, f32[24,16,128]{2,1,0:T(8,128)S(1)}, u32[]{:S(2)}, u32[]{:S(2)}) collective-permute-start(f32[24,16,128]{2,1,0:T(8,128)S(1)} %get-tuple-element.41), channel_id=1, source_target_pairs={{0,18},{18,0},{2,16},{16,2},{4,22},{22,4},{6,20},{20,6},{1,19},{19... | collective-permute-start | bytes 589832 | tf_op jit(solution)/shard_map/ppermute | solution.py:253
  84.5 8.2 %collective-permute-done.9.rest_0_ = f32[24,16,128]{2,1,0:T(8,128)S(1)} collective-permute-done((f32[24,16,128]{2,1,0:T(8,128)S(1)}, f32[24,16,128]{2,1,0:T(8,128)S(1)}, u32[]{:S(2)}, u32[]{:S(2)}) %collective-permute-start.9) | collective-permute-done | bytes 196640 | tf_op jit(solution)/shard_map/ppermute | solution.py:253
  92.7 1.9 %collective-permute-start.14 = (f32[24,16,128]{2,1,0:T(8,128)S(1)}, f32[24,16,128]{2,1,0:T(8,128)S(1)}, u32[]{:S(2)}, u32[]{:S(2)}) collective-permute-start(f32[24,16,128]{2,1,0:T(8,128)S(1)} %get-tuple-element.42), channel_id=1, source_target_pairs={{0,26},{26,0},{2,24},{24,2},{4,30},{30,4},{6,28},{28,6},{1,27},{27... | collective-permute-start | bytes 589832 | tf_op jit(solution)/shard_map/ppermute | solution.py:253
  94.6 0.0 collective-permute-done.10.rest_1_
  94.6 0.0 collective-permute-done.11.rest_2_
  94.6 2.2 %collective-permute-done.12.rest_3_ = f32[24,16,128]{2,1,0:T(8,128)S(1)} collective-permute-done((f32[24,16,128]{2,1,0:T(8,128)S(1)}, f32[24,16,128]{2,1,0:T(8,128)S(1)}, u32[]{:S(2)}, u32[]{:S(2)}) %collective-permute-start.12) | collective-permute-done | bytes 196640 | tf_op jit(solution)/shard_map/ppermute | solution.py:253
  96.8 0.0 collective-permute-done.13.rest_4_
  96.8 6.1 %collective-permute-done.14.rest_5_ = f32[24,16,128]{2,1,0:T(8,128)S(1)} collective-permute-done((f32[24,16,128]{2,1,0:T(8,128)S(1)}, f32[24,16,128]{2,1,0:T(8,128)S(1)}, u32[]{:S(2)}, u32[]{:S(2)}) %collective-permute-start.14) | collective-permute-done | bytes 196640 | tf_op jit(solution)/shard_map/ppermute | solution.py:253
  102.9 11.6 %update.3 = (f32[24,32,256]{2,1,0:T(8,128)S(1)}, f32[24,256]{1,0:T(8,128)S(1)}, f32[24,256]{1,0:T(8,128)S(1)}, f32[32,128]{1,0:T(8,128)S(1)}) custom-call(s32[3,4,2]{2,1,0:T(4,128)S(1)} %copy.23.flip, s32[3,4,2]{2,1,0:T(4,128)S(1)} %copy.24.top, s32[3,4,2]{2,1,0:T(4,128)S(1)} %copy.25.left, f32[4,3]{1,0:T(4,128)S(1)} %copy-done.7, ...), custom_call_target="tpu_custom_call" | custom-call | tf_op jit(solution)/shard_map/update/pallas_call | solution.py:290
  114.6 0.1 collective-permute-start.15
  114.7 1.8 %collective-permute-start.16 = (f32[24,256]{1,0:T(8,128)S(1)}, f32[24,256]{1,0:T(8,128)S(1)}, u32[]{:S(2)}, u32[]{:S(2)}) collective-permute-start(f32[24,256]{1,0:T(8,128)S(1)} %get-tuple-element.45), channel_id=1, source_target_pairs={{2,4},{4,2},{6,0},{0,6},{3,5},{5,3},{7,1},{1,7},{10,12},{12,10},{1... | collective-permute-start | bytes 73736 | tf_op jit(solution)/shard_map/ppermute | solution.py:304
  116.4 1.2 collective-permute-done.17.rest_2_
  117.6 0.9 collective-permute-done.15.rest_0_
  118.5 1.0 collective-permute-done.16.rest_1_
  119.5 3.6 %halo_last.1 = f32[1,24,32,256]{3,2,1,0:T(8,128)} custom-call(s32[3,4,2]{2,1,0:T(4,128)S(1)} %copy.23.flip, s32[3,4,2]{2,1,0:T(4,128)S(1)} %copy.24.top, s32[3,4,2]{2,1,0:T(4,128)S(1)} %copy.25.left, f32[24,32,256]{2,1,0:T(8,128)S(1)} %get-tuple-element.43.bulk, f32[1,32,256]{2,1,0:T(8,128)S(1)} %copy-done.2, f32[24,256]{1,0:T(8,128)S(1)} %collective-permute-done.15.rest_0_, ...), custom_call_target="tpu_custom_call" | custom-call | tf_op jit(solution)/shard_map/halo_last/pallas_call | solution.py:308
  (16 shorter events, 0.0 us)
Async XLA Ops:
  0.0 0.8 copy-start.8
  0.8 0.7 copy-start.9
  1.6 1.1 copy-start
  2.7 0.8 copy-start.1
  3.5 42.7 %copy-start.3 = (f32[1,32,256]{2,1,0:T(8,128)S(1)}, f32[1,32,256]{2,1,0:T(8,128)}, u32[]{:S(2)}) copy-start(f32[1,32,256]{2,1,0:T(8,128)} %agg.3) | copy-start | bytes 98308
  3.5 42.7 %copy-start.4 = (f32[1,32,256]{2,1,0:T(8,128)S(1)}, f32[1,32,256]{2,1,0:T(8,128)}, u32[]{:S(2)}) copy-start(f32[1,32,256]{2,1,0:T(8,128)} %brk.3) | copy-start | bytes 98308
  3.5 42.7 %copy-start.5 = (s32[1,32,256]{2,1,0:T(8,128)S(1)}, s32[1,32,256]{2,1,0:T(8,128)}, u32[]{:S(2)}) copy-start(s32[1,32,256]{2,1,0:T(8,128)} %mask.3) | copy-start | bytes 98308
  3.5 42.7 %copy-start.6 = (f32[1,32,256]{2,1,0:T(8,128)S(1)}, f32[1,32,256]{2,1,0:T(8,128)}, u32[]{:S(2)}) copy-start(f32[1,32,256]{2,1,0:T(8,128)} %diff.3) | copy-start | bytes 98308
  13.9 22.0 %collective-permute-start = (f32[24,16,128]{2,1,0:T(8,128)S(1)}, f32[24,16,128]{2,1,0:T(8,128)S(1)}, u32[]{:S(2)}, u32[]{:S(2)}) collective-permute-start(f32[24,16,128]{2,1,0:T(8,128)S(1)} %get-tuple-element.26), channel_id=1, source_target_pairs={{0,8},{8,0},{2,10},{10,2},{4,12},{12,4},{6,14},{14,6},{1,9},{9,1},... | collective-permute-start | bytes 589832 | tf_op jit(solution)/shard_map/ppermute | solution.py:253
  15.9 22.0 %collective-permute-start.1 = (f32[24,16,128]{2,1,0:T(8,128)S(1)}, f32[24,16,128]{2,1,0:T(8,128)S(1)}, u32[]{:S(2)}, u32[]{:S(2)}) collective-permute-start(f32[24,16,128]{2,1,0:T(8,128)S(1)} %get-tuple-element.27), channel_id=1, source_target_pairs={{0,16},{16,0},{2,18},{18,2},{4,20},{20,4},{6,22},{22,6},{1,17},{17... | collective-permute-start | bytes 589832 | tf_op jit(solution)/shard_map/ppermute | solution.py:253
  17.8 20.1 %collective-permute-start.2 = (f32[24,16,128]{2,1,0:T(8,128)S(1)}, f32[24,16,128]{2,1,0:T(8,128)S(1)}, u32[]{:S(2)}, u32[]{:S(2)}) collective-permute-start(f32[24,16,128]{2,1,0:T(8,128)S(1)} %get-tuple-element.28), channel_id=1, source_target_pairs={{0,24},{24,0},{2,26},{26,2},{4,28},{28,4},{6,30},{30,6},{1,25},{25... | collective-permute-start | bytes 589832 | tf_op jit(solution)/shard_map/ppermute | solution.py:253
  19.7 18.2 %collective-permute-start.3 = (f32[24,16,128]{2,1,0:T(8,128)S(1)}, f32[24,16,128]{2,1,0:T(8,128)S(1)}, u32[]{:S(2)}, u32[]{:S(2)}) collective-permute-start(f32[24,16,128]{2,1,0:T(8,128)S(1)} %get-tuple-element.29), channel_id=1, source_target_pairs={{0,10},{10,0},{2,8},{8,2},{4,14},{14,4},{6,12},{12,6},{1,11},{11,1... | collective-permute-start | bytes 589832 | tf_op jit(solution)/shard_map/ppermute | solution.py:253
  21.7 24.6 %copy-start.7 = (f32[4,3]{1,0:T(4,128)S(1)}, f32[4,3]{1,0:T(4,128)}, u32[]{:S(2)}) copy-start(f32[4,3]{1,0:T(4,128)} %rates.3) | copy-start | bytes 148
  21.7 16.2 %collective-permute-start.4 = (f32[24,16,128]{2,1,0:T(8,128)S(1)}, f32[24,16,128]{2,1,0:T(8,128)S(1)}, u32[]{:S(2)}, u32[]{:S(2)}) collective-permute-start(f32[24,16,128]{2,1,0:T(8,128)S(1)} %get-tuple-element.30), channel_id=1, source_target_pairs={{0,18},{18,0},{2,16},{16,2},{4,22},{22,4},{6,20},{20,6},{1,19},{19... | collective-permute-start | bytes 589832 | tf_op jit(solution)/shard_map/ppermute | solution.py:253
  35.9 10.2 %collective-permute-start.5 = (f32[24,16,128]{2,1,0:T(8,128)S(1)}, f32[24,16,128]{2,1,0:T(8,128)S(1)}, u32[]{:S(2)}, u32[]{:S(2)}) collective-permute-start(f32[24,16,128]{2,1,0:T(8,128)S(1)} %get-tuple-element.31), channel_id=1, source_target_pairs={{0,26},{26,0},{2,24},{24,2},{4,30},{30,4},{6,28},{28,6},{1,27},{27... | collective-permute-start | bytes 589832 | tf_op jit(solution)/shard_map/ppermute | solution.py:253
  46.2 16.6 %copy-start.2 = (f32[1,32,256]{2,1,0:T(8,128)S(1)}, f32[1,32,256]{2,1,0:T(8,128)}, u32[]{:S(2)}) copy-start(f32[1,32,256]{2,1,0:T(8,128)} %sponge.9) | copy-start | bytes 98308
  57.9 3.9 %collective-permute-start.6 = (f32[24,256]{1,0:T(8,128)S(1)}, f32[24,256]{1,0:T(8,128)S(1)}, u32[]{:S(2)}, u32[]{:S(2)}) collective-permute-start(f32[24,256]{1,0:T(8,128)S(1)} %get-tuple-element.33), channel_id=1, source_target_pairs={{0,2},{2,0},{4,6},{6,4},{1,3},{3,1},{5,7},{7,5},{8,10},{10,8},{12,... | collective-permute-start | bytes 73736 | tf_op jit(solution)/shard_map/ppermute | solution.py:304
  58.0 4.8 %collective-permute-start.7 = (f32[24,256]{1,0:T(8,128)S(1)}, f32[24,256]{1,0:T(8,128)S(1)}, u32[]{:S(2)}, u32[]{:S(2)}) collective-permute-start(f32[24,256]{1,0:T(8,128)S(1)} %get-tuple-element.34), channel_id=1, source_target_pairs={{2,4},{4,2},{6,0},{0,6},{3,5},{5,3},{7,1},{1,7},{10,12},{12,10},{1... | collective-permute-start | bytes 73736 | tf_op jit(solution)/shard_map/ppermute | solution.py:304
  58.1 1.2 %collective-permute-start.8 = (f32[32,128]{1,0:T(8,128)S(1)}, f32[32,128]{1,0:T(8,128)S(1)}, u32[]{:S(2)}, u32[]{:S(2)}) collective-permute-start(f32[32,128]{1,0:T(8,128)S(1)} %get-tuple-element.35), channel_id=1, source_target_pairs={{0,1},{1,0},{2,3},{3,2},{4,5},{5,4},{6,7},{7,6},{8,9},{9,8},{10,11... | collective-permute-start | bytes 49160 | tf_op jit(solution)/shard_map/ppermute | solution.py:305
  74.9 17.8 %collective-permute-start.9 = (f32[24,16,128]{2,1,0:T(8,128)S(1)}, f32[24,16,128]{2,1,0:T(8,128)S(1)}, u32[]{:S(2)}, u32[]{:S(2)}) collective-permute-start(f32[24,16,128]{2,1,0:T(8,128)S(1)} %get-tuple-element.37), channel_id=1, source_target_pairs={{0,8},{8,0},{2,10},{10,2},{4,12},{12,4},{6,14},{14,6},{1,9},{9,1},... | collective-permute-start | bytes 589832 | tf_op jit(solution)/shard_map/ppermute | solution.py:253
  76.8 17.8 %collective-permute-start.10 = (f32[24,16,128]{2,1,0:T(8,128)S(1)}, f32[24,16,128]{2,1,0:T(8,128)S(1)}, u32[]{:S(2)}, u32[]{:S(2)}) collective-permute-start(f32[24,16,128]{2,1,0:T(8,128)S(1)} %get-tuple-element.38), channel_id=1, source_target_pairs={{0,16},{16,0},{2,18},{18,2},{4,20},{20,4},{6,22},{22,6},{1,17},{17... | collective-permute-start | bytes 589832 | tf_op jit(solution)/shard_map/ppermute | solution.py:253
  78.7 15.9 %collective-permute-start.11 = (f32[24,16,128]{2,1,0:T(8,128)S(1)}, f32[24,16,128]{2,1,0:T(8,128)S(1)}, u32[]{:S(2)}, u32[]{:S(2)}) collective-permute-start(f32[24,16,128]{2,1,0:T(8,128)S(1)} %get-tuple-element.39), channel_id=1, source_target_pairs={{0,24},{24,0},{2,26},{26,2},{4,28},{28,4},{6,30},{30,6},{1,25},{25... | collective-permute-start | bytes 589832 | tf_op jit(solution)/shard_map/ppermute | solution.py:253
  80.6 16.2 %collective-permute-start.12 = (f32[24,16,128]{2,1,0:T(8,128)S(1)}, f32[24,16,128]{2,1,0:T(8,128)S(1)}, u32[]{:S(2)}, u32[]{:S(2)}) collective-permute-start(f32[24,16,128]{2,1,0:T(8,128)S(1)} %get-tuple-element.40), channel_id=1, source_target_pairs={{0,10},{10,0},{2,8},{8,2},{4,14},{14,4},{6,12},{12,6},{1,11},{11,1... | collective-permute-start | bytes 589832 | tf_op jit(solution)/shard_map/ppermute | solution.py:253
  82.6 14.2 %collective-permute-start.13 = (f32[24,16,128]{2,1,0:T(8,128)S(1)}, f32[24,16,128]{2,1,0:T(8,128)S(1)}, u32[]{:S(2)}, u32[]{:S(2)}) collective-permute-start(f32[24,16,128]{2,1,0:T(8,128)S(1)} %get-tuple-element.41), channel_id=1, source_target_pairs={{0,18},{18,0},{2,16},{16,2},{4,22},{22,4},{6,20},{20,6},{1,19},{19... | collective-permute-start | bytes 589832 | tf_op jit(solution)/shard_map/ppermute | solution.py:253
  92.7 10.2 %collective-permute-start.14 = (f32[24,16,128]{2,1,0:T(8,128)S(1)}, f32[24,16,128]{2,1,0:T(8,128)S(1)}, u32[]{:S(2)}, u32[]{:S(2)}) collective-permute-start(f32[24,16,128]{2,1,0:T(8,128)S(1)} %get-tuple-element.42), channel_id=1, source_target_pairs={{0,26},{26,0},{2,24},{24,2},{4,30},{30,4},{6,28},{28,6},{1,27},{27... | collective-permute-start | bytes 589832 | tf_op jit(solution)/shard_map/ppermute | solution.py:253
  114.6 3.9 %collective-permute-start.15 = (f32[24,256]{1,0:T(8,128)S(1)}, f32[24,256]{1,0:T(8,128)S(1)}, u32[]{:S(2)}, u32[]{:S(2)}) collective-permute-start(f32[24,256]{1,0:T(8,128)S(1)} %get-tuple-element.44), channel_id=1, source_target_pairs={{0,2},{2,0},{4,6},{6,4},{1,3},{3,1},{5,7},{7,5},{8,10},{10,8},{12,... | collective-permute-start | bytes 73736 | tf_op jit(solution)/shard_map/ppermute | solution.py:304
  114.7 4.8 %collective-permute-start.16 = (f32[24,256]{1,0:T(8,128)S(1)}, f32[24,256]{1,0:T(8,128)S(1)}, u32[]{:S(2)}, u32[]{:S(2)}) collective-permute-start(f32[24,256]{1,0:T(8,128)S(1)} %get-tuple-element.45), channel_id=1, source_target_pairs={{2,4},{4,2},{6,0},{0,6},{3,5},{5,3},{7,1},{1,7},{10,12},{12,10},{1... | collective-permute-start | bytes 73736 | tf_op jit(solution)/shard_map/ppermute | solution.py:304
  116.4 1.2 collective-permute-start.17

commit v2 on v1

--- a/solution.py
+++ b/solution.py
@@ -12,6 +12,7 @@
 STEPS = 2
 SLOTS = 3
 LANES = 128
+CHUNK = 8
 
 relaxation = 0.125
 
@@ -28,7 +29,7 @@
     _, i, j = place()
     for slot in range(SLOTS):
         for kind, row in ((0, i), (1, jnp.bitwise_xor(i, 1))):
-            yield slot, kind, flip[slot, row, j] == kind, top[slot, row, j], left[slot, row, j]
+            yield slot, kind, flip[slot, j, row] == kind, top[slot, j, row], left[slot, j, row]
 
 
 def widen(half, cells):
@@ -43,6 +44,54 @@
     return (lax.shift_right_logical(row, 1) == col).astype(jnp.float32)
 
 
+def near(first, half_r):
+    base = jnp.minimum(lax.shift_right_logical(first, 3) * 8, half_r - 8)
+    return pl.multiple_of(base, 8), first - base
+
+
+def crop(source, out, first, begin):
+    comps, cells_r, cells_c = source.shape
+    half_r, half_c = out.shape[1:]
+    groups = half_r // 8
+    base, rest = near(first, half_r)
+    row = lax.broadcasted_iota(jnp.int32, (8, half_c), 0)
+    lane = lax.broadcasted_iota(jnp.int32, (8, half_c), 1)
+    turn_c = lax.rem(2 * half_c - begin, half_c)
+    turn_r = lax.rem(8 - rest, 8)
+    left_part = lane < half_c - begin
+    upper_part = row < 8 - rest
+    for c in range(0, comps, CHUNK):
+        block = source[c : c + CHUNK, pl.ds(base, half_r + 8), :].reshape(CHUNK * (groups + 1), 8, cells_c)
+        low = pltpu.roll(block[..., :half_c], turn_c, 2)
+        high = pltpu.roll(block[..., half_c:], turn_c, 2)
+        block = pltpu.roll(jnp.where(left_part, low, high), turn_r, 1).reshape(CHUNK, groups + 1, 8, half_c)
+        for k in range(groups):
+            out[c : c + CHUNK, k * 8 : k * 8 + 8, :] = jnp.where(upper_part, block[:, k], block[:, k + 1])
+
+
+def add_at(total, piece, first, begin):
+    comps, half_r, half_c = piece.shape
+    groups = half_r // 8
+    base, rest = near(first, half_r)
+    row = lax.broadcasted_iota(jnp.int32, (8, half_c), 0)
+    lane = lax.broadcasted_iota(jnp.int32, (8, half_c), 1)
+    turn_c = lax.rem(begin, half_c)
+    turn_r = lax.rem(rest, 8)
+    lower_part = row >= rest
+    right_part = lane >= begin
+    for c in range(0, comps, CHUNK):
+        block = piece[c : c + CHUNK].reshape(CHUNK * groups, 8, half_c)
+        block = pltpu.roll(block, turn_r, 1).reshape(CHUNK, groups, 8, half_c)
+        none = jnp.zeros((CHUNK, 8, half_c), jnp.float32)
+        for k in range(groups + 1):
+            here = block[:, k] if k < groups else none
+            above = block[:, k - 1] if k else none
+            turned = pltpu.roll(jnp.where(lower_part, here, above), turn_c, 2)
+            rows = pl.ds(base + k * 8, 8)
+            total[c : c + CHUNK, rows, :half_c] += jnp.where(right_part, turned, 0.0)
+            total[c : c + CHUNK, rows, half_c:] += jnp.where(right_part, 0.0, turned)
+
+
 def payload(flip, top, left, state, sponge, straight, crossed, rows, fine):
     comps, cells_r, cells_c = state.shape
     half_r, half_c = cells_r // 2, cells_c // 2
@@ -51,16 +100,10 @@
     @pl.when(grid == 0)
     def _():
         for slot, kind, serves, first, begin in pieces(flip, top, left):
-            out = (straight, crossed)[kind][slot]
 
             @pl.when(serves)
             def _():
-                def cut(c, carry):
-                    block = pltpu.roll(state[c], lax.rem(cells_r - first, cells_r), 0)[:half_r]
-                    out[c] = pltpu.roll(block, lax.rem(cells_c - begin, cells_c), 1)[:, :half_c]
-                    return carry
-
-                lax.fori_loop(0, comps, cut, 0)
+                crop(state, (straight, crossed)[kind][slot], first, begin)
 
     @pl.when(grid > 0)
     def _():
@@ -103,6 +146,7 @@
     got = rest[: 2 * SLOTS]
     n_side = 2 + n_cols
     bulk, sides = rest[2 * SLOTS], rest[2 * SLOTS + 1 : 2 * SLOTS + 1 + n_side]
+    bulk = bulk.at[0] if len(bulk.shape) == 4 else bulk
     nested, wide, coarse, fine = rest[2 * SLOTS + 1 + n_side :]
     comps, cells_r, cells_c = bulk.shape
     half_r, half_c = cells_r // 2, cells_c // 2
@@ -118,32 +162,24 @@
             covered = covered + jnp.where(inside & serves, 1.0, 0.0)
         keep = 1.0 - relaxation * covered
 
-        def own(c, carry):
-            nested[c] = keep * state[c]
+        def own(step, carry):
+            rows = pl.ds(step * CHUNK, CHUNK)
+            nested[rows] = keep * state[rows]
             return carry
 
-        lax.fori_loop(0, comps, own, 0)
+        lax.fori_loop(0, comps // CHUNK, own, 0)
         for slot, kind, serves, first, begin in pieces(flip, top, left):
-            piece = got[kind * SLOTS + slot]
 
             @pl.when(serves)
             def _():
-                def put(c, carry):
-                    block = piece[c]
-                    block = jnp.concatenate([block, jnp.zeros_like(block)], axis=1)
-                    block = pltpu.roll(block, begin, 1)
-                    block = jnp.concatenate([block, jnp.zeros_like(block)], axis=0)
-                    nested[c] += pltpu.roll(block, first, 0)
-                    return carry
-
-                lax.fori_loop(0, comps, put, 0)
+                add_at(nested, got[kind * SLOTS + slot], first, begin)
 
     @pl.when(grid > 0)
     def _():
         for slot in range(SLOTS):
             for kind in range(2):
 
-                @pl.when((grid == slot + 1) & (flip[slot, i, j] == kind))
+                @pl.when((grid == slot + 1) & (flip[slot, j, i] == kind))
                 def _():
                     coarse[...] = got[kind * SLOTS + slot][...]
 
@@ -209,33 +245,32 @@
 def halo_kernel(n_cols, sizes, last, flip, top, left, bulk, sponge, *rest):
     sides = rest[: 2 + n_cols]
     state = rest[2 + n_cols]
-    new = state.at[0] if last else state
-    comps, cells_r, cells_c = bulk.shape
+    old, new = (bulk.at[0], state.at[0]) if last else (bulk, state)
+    comps, cells_r, cells_c = new.shape
     _, i, j = place()
-    row_id = lax.broadcasted_iota(jnp.int32, (cells_r, cells_c), 0)
+    row = lax.broadcasted_iota(jnp.int32, (8, cells_c), 0)
+    even, _ = edge_sides(i)
+    first, second = sides[0][...], sides[1][...]
+    above = jnp.where(i == 0, 0.0, jnp.where(even, second, first))
+    below = jnp.where(i == sizes[0] - 1, 0.0, jnp.where(even, first, second))
+    for c in range(comps):
+        new[c, :8, :] = old[c, :8, :] + jnp.where(row == 0, above[c : c + 1], 0.0)
+        new[c, 8 : cells_r - 8, :] = old[c, 8 : cells_r - 8, :]
+        new[c, cells_r - 8 :, :] = old[c, cells_r - 8 :, :] + jnp.where(row == 7, below[c : c + 1], 0.0)
     lane = lax.broadcasted_iota(jnp.int32, (cells_r, LANES), 1)
-    row_far = edge_sides(i)
-    col_far = edge_sides(j)
-    row_at = [jnp.where(far, cells_r - 1, 0) for far in row_far]
-    row_at[1] = jnp.where((row_far[1] & (i == sizes[0] - 1)) | (row_far[0] & (i == 0)), -1, row_at[1])
-    col_at = [jnp.where(far, LANES - 1, 0) for far in col_far]
-    col_on = [jnp.bool_(True), jnp.logical_not((col_far[1] & (j == sizes[1] - 1)) | (col_far[0] & (j == 0)))]
-
-    def add(c, carry):
-        total = bulk[c]
-        for phase in range(2):
-            total = total + jnp.where(row_id == row_at[phase], sides[phase][pl.ds(c, 1), :], 0.0)
-        first, final = total[:, :LANES], total[:, cells_c - LANES :]
-        for phase in range(n_cols):
-            far, at = col_far[phase], col_at[phase]
-            slab = pltpu.roll(sides[2 + phase][...], lax.rem(at - c + LANES, LANES), 1)
-            slab = jnp.where((lane == at) & col_on[phase], slab, 0.0)
-            first = first + jnp.where(far, 0.0, slab)
-            final = final + jnp.where(far, slab, 0.0)
-        new[c] = jnp.concatenate([first, total[:, LANES : cells_c - LANES], final], axis=1) if cells_c > 2 * LANES else jnp.concatenate([first, final], axis=1)
-        return carry
-
-    lax.fori_loop(0, comps, add, 0)
+    for phase, far in zip(range(n_cols), edge_sides(j)):
+        column = sides[2 + phase][...]
+
+        @pl.when(far & (j < sizes[1] - 1))
+        def _():
+            for c in range(comps):
+                new[c, :, cells_c - LANES :] += jnp.where(lane == LANES - 1, pltpu.roll(column, LANES - 1 - c, 1), 0.0)
+
+        @pl.when(jnp.logical_not(far) & (j > 0))
+        def _():
+            for c in range(comps):
+                new[c, :, :LANES] += jnp.where(lane == 0, pltpu.roll(column, (LANES - c) % LANES, 1), 0.0)
+
     if not last:
         outs, (rows, fine) = rest[3 + n_cols : -2], rest[-2:]
         payload(flip, top, left, new, sponge, outs[:SLOTS], outs[SLOTS:], rows, fine)
@@ -272,7 +307,7 @@
     block = jax.ShapeDtypeStruct((comps, half_r, half_c), f32)
     side = [jax.ShapeDtypeStruct((comps, cells_c), f32)] * 2 + [jax.ShapeDtypeStruct((cells_r, LANES), f32)] * n_cols
     fold_scratch = [pltpu.VMEM((comps, half_r, cells_c), f32), pltpu.VMEM((cells_c // LANES, cells_r, LANES), f32)]
-    tables = (partner_flip, row_offset, col_offset)
+    tables = [table.transpose(0, 2, 1) for table in (partner_flip, row_offset, col_offset)]
 
     blocks = pl.pallas_call(
         first_kernel,
@@ -285,11 +320,12 @@
     )(*tables, adjoint, sponge)
     state = adjoint.reshape(tile.shape)
     for step in range(STEPS):
+        got = exchange(blocks)
         last = step == STEPS - 1
-        got = exchange(blocks)
+        new = jax.ShapeDtypeStruct(adjoint.shape, f32) if last else tile
         bulk, *sides = pl.pallas_call(
             functools.partial(update_kernel, n_cols),
-            out_shape=[tile] + side,
+            out_shape=[new] + side,
             in_specs=[SM] * 4 + [VM] * (6 + 2 * SLOTS),
             out_specs=[VM] * (1 + len(side)),
             scratch_shapes=[
@@ -304,7 +340,6 @@
         sides = [lax.ppermute(sides[k], "gx", swap_pairs(n_x, k)) for k in range(2)] + [
             lax.ppermute(sides[2 + k], "gy", swap_pairs(n_y, k)) for k in range(n_cols)
         ]
-        new = jax.ShapeDtypeStruct(adjoint.shape, f32) if last else tile
         out = pl.pallas_call(
             functools.partial(halo_kernel, n_cols, (n_x, n_y), last),
             out_shape=[new] + ([] if last else [block] * (2 * SLOTS)),

time: 125 us -> 97 us (0.78); the launches traced: 123 us -> 97.2 us
  Pallas kernels: 49.4 us -> 10.6 us
  starting transfers between devices: 25.1 us -> 39.9 us
  waiting for transfers between devices: 44.8 us -> 42.5 us
    pallas_call x2, Pallas kernels: 23.3 us -> 5.3 us  [local(): pl.pallas_call(functools.partial(update_kernel, n_cols), out_shape=[new]...]
    pallas_call x2, Pallas kernels: 15.6 us -> 3.64 us  [local(): pl.pallas_call(functools.partial(halo_kernel, n_cols, (n_x, n_y), last),...]
    pallas_call x1, Pallas kernels: 10.4 us -> 1.63 us  [local(): pl.pallas_call(first_kernel, out_shape=[block] * (2 * SLOTS), in_specs=[S...]
    ppermute x4, starting transfers between devices: 1.97 us -> 10.4 us  [local(): lax.ppermute(sides[k], 'gx', swap_pairs(n_x, k))]
    ppermute x12, starting transfers between devices: 23 us -> 29.5 us  [exchange(): lax.ppermute(blocks[kind * SLOTS + slot], ('grid', 'gx'), pairs)]
    ppermute x4, waiting for transfers between devices: 5.31 us -> 3.74 us  [local(): lax.ppermute(sides[k], 'gx', swap_pairs(n_x, k))]
    unnamed x23 -> x22, local copies, waits for them, and re-layouts: 3.5 us -> 3.97 us
  transfers between devices with their start and end apart: 18 -> 18, of which waited for: 11 -> 10; matrix products, arithmetic and copies ran while one was open for 0% -> 0% of each run, Pallas kernels for 0% -> 0%
where the time goes in v2:
time: 97 us; the launch traced here: 97.2 us
  waiting for transfers between devices  42.5 us (44%)
  starting transfers between devices  39.9 us (41%)
  Pallas kernels  10.6 us (11%)
  local copies, waits for them, and re-layouts  3.97 us (4%)
    ppermute x12, waiting for transfers between devices, exchange(): lax.ppermute(blocks[kind * SLOTS + slot], ('grid', 'gx'), pairs)  36.4 us
    ppermute x12, starting transfers between devices, exchange(): lax.ppermute(blocks[kind * SLOTS + slot], ('grid', 'gx'), pairs)  29.5 us
    ppermute x4, starting transfers between devices, local(): lax.ppermute(sides[k], 'gx', swap_pairs(n_x, k))  10.4 us
    pallas_call x2, Pallas kernels, local(): pl.pallas_call(functools.partial(update_kernel, n_cols), out_shape=[new]...  5.3 us
    unnamed x22, local copies, waits for them, and re-layouts  3.97 us
    ppermute x4, waiting for transfers between devices, local(): lax.ppermute(sides[k], 'gx', swap_pairs(n_x, k))  3.74 us
    pallas_call x2, Pallas kernels, local(): pl.pallas_call(functools.partial(halo_kernel, n_cols, (n_x, n_y), last),...  3.64 us
    ppermute x2, waiting for transfers between devices, local(): lax.ppermute(sides[2 + k], 'gy', swap_pairs(n_y, k))  2.36 us
  transfers between devices with their start and end apart: 18, of which 10 were waited for; matrix products, arithmetic and copies ran while one was open for 0% of the time, Pallas kernels for 0%

profile of v2, /device:TPU:0, one launch (start us, length us, event | category | flops | bytes accessed | tf_op | source)
XLA Modules:
  0.0 97.2 jit_solution(12050016146241348904)
XLA Ops:
  0.0 0.7 copy-done.7
  0.7 1.1 %copy-done = f32[1,24,32,256]{3,2,1,0:T(8,128)S(1)} copy-done((f32[1,24,32,256]{3,2,1,0:T(8,128)S(1)}, f32[1,24,32,256]{3,2,1,0:T(8,128)}, u32[]{:S(2)}) %copy-start) | copy-done | bytes 786456
  1.8 0.8 copy-done.1
  2.6 0.7 copy-done.8
  3.3 0.7 copy-done.9
  4.0 1.6 %first_payload.1 = (f32[24,16,128]{2,1,0:T(8,128)S(1)}, f32[24,16,128]{2,1,0:T(8,128)S(1)}, f32[24,16,128]{2,1,0:T(8,128)S(1)}, f32[24,16,128]{2,1,0:T(8,128)S(1...) custom-call(s32[3,2,4]{2,1,0:T(2,128)S(1)} %bitcast.5, s32[3,2,4]{2,1,0:T(2,128)S(1)} %bitcast.10, ...), custom_call_target="tpu_custom_call" | custom-call | tf_op jit(solution)/shard_map/first_payload/pallas_call | solution.py:312
  5.6 4.7 %collective-permute-start = (f32[24,16,128]{2,1,0:T(8,128)S(1)}, f32[24,16,128]{2,1,0:T(8,128)S(1)}, u32[]{:S(2)}, u32[]{:S(2)}) collective-permute-start(f32[24,16,128]{2,1,0:T(8,128)S(1)} %get-tuple-element.26), channel_id=1, source_target_pairs={{0,8},{8,0},{2,10},{10,2},{4,12},{12,4},{6,14},{14,6},{1,9},{9,1},... | collective-permute-start | bytes 589832 | tf_op jit(solution)/shard_map/ppermute | solution.py:288
  10.3 1.9 %collective-permute-start.1 = (f32[24,16,128]{2,1,0:T(8,128)S(1)}, f32[24,16,128]{2,1,0:T(8,128)S(1)}, u32[]{:S(2)}, u32[]{:S(2)}) collective-permute-start(f32[24,16,128]{2,1,0:T(8,128)S(1)} %get-tuple-element.27), channel_id=1, source_target_pairs={{0,16},{16,0},{2,18},{18,2},{4,20},{20,4},{6,22},{22,6},{1,17},{17... | collective-permute-start | bytes 589832 | tf_op jit(solution)/shard_map/ppermute | solution.py:288
  12.3 1.9 %collective-permute-start.2 = (f32[24,16,128]{2,1,0:T(8,128)S(1)}, f32[24,16,128]{2,1,0:T(8,128)S(1)}, u32[]{:S(2)}, u32[]{:S(2)}) collective-permute-start(f32[24,16,128]{2,1,0:T(8,128)S(1)} %get-tuple-element.28), channel_id=1, source_target_pairs={{0,24},{24,0},{2,26},{26,2},{4,28},{28,4},{6,30},{30,6},{1,25},{25... | collective-permute-start | bytes 589832 | tf_op jit(solution)/shard_map/ppermute | solution.py:288
  14.2 1.9 %collective-permute-start.3 = (f32[24,16,128]{2,1,0:T(8,128)S(1)}, f32[24,16,128]{2,1,0:T(8,128)S(1)}, u32[]{:S(2)}, u32[]{:S(2)}) collective-permute-start(f32[24,16,128]{2,1,0:T(8,128)S(1)} %get-tuple-element.29), channel_id=1, source_target_pairs={{0,10},{10,0},{2,8},{8,2},{4,14},{14,4},{6,12},{12,6},{1,11},{11,1... | collective-permute-start | bytes 589832 | tf_op jit(solution)/shard_map/ppermute | solution.py:288
  16.1 0.0 copy-start.10
  16.1 3.3 %collective-permute-start.4 = (f32[24,16,128]{2,1,0:T(8,128)S(1)}, f32[24,16,128]{2,1,0:T(8,128)S(1)}, u32[]{:S(2)}, u32[]{:S(2)}) collective-permute-start(f32[24,16,128]{2,1,0:T(8,128)S(1)} %get-tuple-element.30), channel_id=1, source_target_pairs={{0,18},{18,0},{2,16},{16,2},{4,22},{22,4},{6,20},{20,6},{1,19},{19... | collective-permute-start | bytes 589832 | tf_op jit(solution)/shard_map/ppermute | solution.py:288
  19.4 0.0 collective-permute-done.rest_0_
  19.4 2.8 %collective-permute-start.5 = (f32[24,16,128]{2,1,0:T(8,128)S(1)}, f32[24,16,128]{2,1,0:T(8,128)S(1)}, u32[]{:S(2)}, u32[]{:S(2)}) collective-permute-start(f32[24,16,128]{2,1,0:T(8,128)S(1)} %get-tuple-element.31), channel_id=1, source_target_pairs={{0,26},{26,0},{2,24},{24,2},{4,30},{30,4},{6,28},{28,6},{1,27},{27... | collective-permute-start | bytes 589832 | tf_op jit(solution)/shard_map/ppermute | solution.py:288
  22.2 7.0 %collective-permute-done.1.rest_1_ = f32[24,16,128]{2,1,0:T(8,128)S(1)} collective-permute-done((f32[24,16,128]{2,1,0:T(8,128)S(1)}, f32[24,16,128]{2,1,0:T(8,128)S(1)}, u32[]{:S(2)}, u32[]{:S(2)}) %collective-permute-start.1) | collective-permute-done | bytes 196640 | tf_op jit(solution)/shard_map/ppermute | solution.py:288
  29.2 0.0 collective-permute-done.2.rest_2_
  29.2 8.0 %collective-permute-done.3.rest_3_ = f32[24,16,128]{2,1,0:T(8,128)S(1)} collective-permute-done((f32[24,16,128]{2,1,0:T(8,128)S(1)}, f32[24,16,128]{2,1,0:T(8,128)S(1)}, u32[]{:S(2)}, u32[]{:S(2)}) %collective-permute-start.3) | collective-permute-done | bytes 196640 | tf_op jit(solution)/shard_map/ppermute | solution.py:288
  37.3 0.0 collective-permute-done.4.rest_4_
  37.3 0.0 collective-permute-done.5.rest_5_
  37.3 0.0 copy-start.2
  37.3 2.7 %update.2 = (f32[24,32,256]{2,1,0:T(8,128)S(1)}, f32[24,256]{1,0:T(8,128)S(1)}, f32[24,256]{1,0:T(8,128)S(1)}, f32[32,128]{1,0:T(8,128)S(1)}) custom-call(s32[3,2,4]{2,1,0:T(2,128)S(1)} %bitcast.6, s32[3,2,4]{2,1,0:T(2,128)S(1)} %bitcast.11, s32[3,2,4]{2,1,0:T(2,128)S(1)} %bitcast.16, f32[4,3]{1,0:T(4,128)S(1)} %copy-done.10, f32[24,32,256]{2,1,0:T(8,128)S(1)} %bitcast.4, ...), custom_call_target="tpu_custom_call" | custom-call | tf_op jit(solution)/shard_map/update/pallas_call | solution.py:326
  40.0 0.3 collective-permute-start.6
  40.3 8.3 %collective-permute-start.7 = (f32[24,256]{1,0:T(8,128)S(1)}, f32[24,256]{1,0:T(8,128)S(1)}, u32[]{:S(2)}, u32[]{:S(2)}) collective-permute-start(f32[24,256]{1,0:T(8,128)S(1)} %get-tuple-element.34), channel_id=1, source_target_pairs={{2,4},{4,2},{6,0},{0,6},{3,5},{5,3},{7,1},{1,7},{10,12},{12,10},{1... | collective-permute-start | bytes 73736 | tf_op jit(solution)/shard_map/ppermute | solution.py:340
  48.7 0.0 collective-permute-start.8
  48.7 1.2 %collective-permute-done.8.rest_2_ = f32[32,128]{1,0:T(8,128)S(1)} collective-permute-done((f32[32,128]{1,0:T(8,128)S(1)}, f32[32,128]{1,0:T(8,128)S(1)}, u32[]{:S(2)}, u32[]{:S(2)}) %collective-permute-start.8) | collective-permute-done | bytes 16416 | tf_op jit(solution)/shard_map/ppermute | solution.py:341
  49.8 0.0 collective-permute-done.6.rest_0_
  49.8 0.8 collective-permute-done.7.rest_1_
  50.6 1.9 %halo.1 = (f32[24,32,256]{2,1,0:T(8,128)S(1)}, f32[24,16,128]{2,1,0:T(8,128)S(1)}, f32[24,16,128]{2,1,0:T(8,128)S(1)}, f32[24,16,128]{2,1,0:T(8,128)S(1)}, f32[2...) custom-call(s32[3,2,4]{2,1,0:T(2,128)S(1)} %bitcast.7, s32[3,2,4]{2,1,0:T(2,128)S(1)} %bitcast.12, ...), custom_call_target="tpu_custom_call" | custom-call | tf_op jit(solution)/shard_map/halo/pallas_call | solution.py:343
  52.5 1.9 %collective-permute-start.9 = (f32[24,16,128]{2,1,0:T(8,128)S(1)}, f32[24,16,128]{2,1,0:T(8,128)S(1)}, u32[]{:S(2)}, u32[]{:S(2)}) collective-permute-start(f32[24,16,128]{2,1,0:T(8,128)S(1)} %get-tuple-element.37), channel_id=1, source_target_pairs={{0,8},{8,0},{2,10},{10,2},{4,12},{12,4},{6,14},{14,6},{1,9},{9,1},... | collective-permute-start | bytes 589832 | tf_op jit(solution)/shard_map/ppermute | solution.py:288
  54.4 1.9 %collective-permute-start.10 = (f32[24,16,128]{2,1,0:T(8,128)S(1)}, f32[24,16,128]{2,1,0:T(8,128)S(1)}, u32[]{:S(2)}, u32[]{:S(2)}) collective-permute-start(f32[24,16,128]{2,1,0:T(8,128)S(1)} %get-tuple-element.38), channel_id=1, source_target_pairs={{0,16},{16,0},{2,18},{18,2},{4,20},{20,4},{6,22},{22,6},{1,17},{17... | collective-permute-start | bytes 589832 | tf_op jit(solution)/shard_map/ppermute | solution.py:288
  56.4 1.9 %collective-permute-start.11 = (f32[24,16,128]{2,1,0:T(8,128)S(1)}, f32[24,16,128]{2,1,0:T(8,128)S(1)}, u32[]{:S(2)}, u32[]{:S(2)}) collective-permute-start(f32[24,16,128]{2,1,0:T(8,128)S(1)} %get-tuple-element.39), channel_id=1, source_target_pairs={{0,24},{24,0},{2,26},{26,2},{4,28},{28,4},{6,30},{30,6},{1,25},{25... | collective-permute-start | bytes 589832 | tf_op jit(solution)/shard_map/ppermute | solution.py:288
  58.3 2.4 %collective-permute-start.12 = (f32[24,16,128]{2,1,0:T(8,128)S(1)}, f32[24,16,128]{2,1,0:T(8,128)S(1)}, u32[]{:S(2)}, u32[]{:S(2)}) collective-permute-start(f32[24,16,128]{2,1,0:T(8,128)S(1)} %get-tuple-element.40), channel_id=1, source_target_pairs={{0,10},{10,0},{2,8},{8,2},{4,14},{14,4},{6,12},{12,6},{1,11},{11,1... | collective-permute-start | bytes 589832 | tf_op jit(solution)/shard_map/ppermute | solution.py:288
  60.7 2.8 %collective-permute-start.13 = (f32[24,16,128]{2,1,0:T(8,128)S(1)}, f32[24,16,128]{2,1,0:T(8,128)S(1)}, u32[]{:S(2)}, u32[]{:S(2)}) collective-permute-start(f32[24,16,128]{2,1,0:T(8,128)S(1)} %get-tuple-element.41), channel_id=1, source_target_pairs={{0,18},{18,0},{2,16},{16,2},{4,22},{22,4},{6,20},{20,6},{1,19},{19... | collective-permute-start | bytes 589832 | tf_op jit(solution)/shard_map/ppermute | solution.py:288
  63.6 13.0 %collective-permute-done.9.rest_0_ = f32[24,16,128]{2,1,0:T(8,128)S(1)} collective-permute-done((f32[24,16,128]{2,1,0:T(8,128)S(1)}, f32[24,16,128]{2,1,0:T(8,128)S(1)}, u32[]{:S(2)}, u32[]{:S(2)}) %collective-permute-start.9) | collective-permute-done | bytes 196640 | tf_op jit(solution)/shard_map/ppermute | solution.py:288
  76.5 1.9 %collective-permute-start.14 = (f32[24,16,128]{2,1,0:T(8,128)S(1)}, f32[24,16,128]{2,1,0:T(8,128)S(1)}, u32[]{:S(2)}, u32[]{:S(2)}) collective-permute-start(f32[24,16,128]{2,1,0:T(8,128)S(1)} %get-tuple-element.42), channel_id=1, source_target_pairs={{0,26},{26,0},{2,24},{24,2},{4,30},{30,4},{6,28},{28,6},{1,27},{27... | collective-permute-start | bytes 589832 | tf_op jit(solution)/shard_map/ppermute | solution.py:288
  78.5 0.0 collective-permute-done.10.rest_1_
  78.5 0.0 collective-permute-done.11.rest_2_
  78.5 2.0 %collective-permute-done.12.rest_3_ = f32[24,16,128]{2,1,0:T(8,128)S(1)} collective-permute-done((f32[24,16,128]{2,1,0:T(8,128)S(1)}, f32[24,16,128]{2,1,0:T(8,128)S(1)}, u32[]{:S(2)}, u32[]{:S(2)}) %collective-permute-start.12) | collective-permute-done | bytes 196640 | tf_op jit(solution)/shard_map/ppermute | solution.py:288
  80.5 0.0 collective-permute-done.13.rest_4_
  80.5 6.4 %collective-permute-done.14.rest_5_ = f32[24,16,128]{2,1,0:T(8,128)S(1)} collective-permute-done((f32[24,16,128]{2,1,0:T(8,128)S(1)}, f32[24,16,128]{2,1,0:T(8,128)S(1)}, u32[]{:S(2)}, u32[]{:S(2)}) %collective-permute-start.14) | collective-permute-done | bytes 196640 | tf_op jit(solution)/shard_map/ppermute | solution.py:288
  86.9 2.6 %update.3 = (f32[1,24,32,256]{3,2,1,0:T(8,128)S(1)}, f32[24,256]{1,0:T(8,128)S(1)}, f32[24,256]{1,0:T(8,128)S(1)}, f32[32,128]{1,0:T(8,128)S(1)}) custom-call(s32[3,2,4]{2,1,0:T(2,128)S(1)} %bitcast.8, s32[3,2,4]{2,1,0:T(2,128)S(1)} %bitcast.13, s32[3,2,4]{2,1,0:T(2,128)S(1)} %bitcast.18, f32[4,3]{1,0:T(4,128)S(1)} %copy-done.10, ...), custom_call_target="tpu_custom_call" | custom-call | tf_op jit(solution)/shard_map/update/pallas_call | solution.py:326
  89.5 1.2 %collective-permute-start.15 = (f32[24,256]{1,0:T(8,128)S(1)}, f32[24,256]{1,0:T(8,128)S(1)}, u32[]{:S(2)}, u32[]{:S(2)}) collective-permute-start(f32[24,256]{1,0:T(8,128)S(1)} %get-tuple-element.44), channel_id=1, source_target_pairs={{0,2},{2,0},{4,6},{6,4},{1,3},{3,1},{5,7},{7,5},{8,10},{10,8},{12,... | collective-permute-start | bytes 73736 | tf_op jit(solution)/shard_map/ppermute | solution.py:340
  90.7 0.6 collective-permute-start.16
  91.3 0.0 collective-permute-start.17
  91.3 1.2 %collective-permute-done.17.rest_2_ = f32[32,128]{1,0:T(8,128)S(1)} collective-permute-done((f32[32,128]{1,0:T(8,128)S(1)}, f32[32,128]{1,0:T(8,128)S(1)}, u32[]{:S(2)}, u32[]{:S(2)}) %collective-permute-start.17) | collective-permute-done | bytes 16416 | tf_op jit(solution)/shard_map/ppermute | solution.py:341
  92.5 0.9 collective-permute-done.15.rest_0_
  93.4 2.0 %collective-permute-done.16.rest_1_ = f32[24,256]{1,0:T(8,128)S(1)} collective-permute-done((f32[24,256]{1,0:T(8,128)S(1)}, f32[24,256]{1,0:T(8,128)S(1)}, u32[]{:S(2)}, u32[]{:S(2)}) %collective-permute-start.16) | collective-permute-done | bytes 24608 | tf_op jit(solution)/shard_map/ppermute | solution.py:340
  95.4 1.8 %halo_last.1 = f32[1,24,32,256]{3,2,1,0:T(8,128)} custom-call(s32[3,2,4]{2,1,0:T(2,128)S(1)} %bitcast.9, s32[3,2,4]{2,1,0:T(2,128)S(1)} %bitcast.14, s32[3,2,4]{2,1,0:T(2,128)S(1)} %bitcast.19, f32[1,24,32,256]{3,2,1,0:T(8,128)S(1)} %get-tuple-element.43.bulk, f32[1,32,256]{2,1,0:T(8,128)S(1)} %copy-done.2, f32[24,256]{1,0:T(8,128)S(1)} %collective-permute-done.15.rest_0_, ...), custom_call_target="tpu_custom_call" | custom-call | tf_op jit(solution)/shard_map/halo_last/pallas_call | solution.py:343
  (15 shorter events, 0.0 us)
Async XLA Ops:
  0.0 0.7 copy-start.7
  0.7 1.1 %copy-start = (f32[1,24,32,256]{3,2,1,0:T(8,128)S(1)}, f32[1,24,32,256]{3,2,1,0:T(8,128)}, u32[]{:S(2)}) copy-start(f32[1,24,32,256]{3,2,1,0:T(8,128)} %state.1) | copy-start | bytes 2359300
  1.8 0.8 copy-start.1
  2.6 0.7 copy-start.8
  3.3 0.7 copy-start.9
  3.9 33.3 %copy-start.3 = (f32[1,32,256]{2,1,0:T(8,128)S(1)}, f32[1,32,256]{2,1,0:T(8,128)}, u32[]{:S(2)}) copy-start(f32[1,32,256]{2,1,0:T(8,128)} %agg.3) | copy-start | bytes 98308
  3.9 33.3 %copy-start.4 = (f32[1,32,256]{2,1,0:T(8,128)S(1)}, f32[1,32,256]{2,1,0:T(8,128)}, u32[]{:S(2)}) copy-start(f32[1,32,256]{2,1,0:T(8,128)} %brk.3) | copy-start | bytes 98308
  4.0 33.4 %copy-start.5 = (s32[1,32,256]{2,1,0:T(8,128)S(1)}, s32[1,32,256]{2,1,0:T(8,128)}, u32[]{:S(2)}) copy-start(s32[1,32,256]{2,1,0:T(8,128)} %mask.3) | copy-start | bytes 98308
  4.0 33.4 %copy-start.6 = (f32[1,32,256]{2,1,0:T(8,128)S(1)}, f32[1,32,256]{2,1,0:T(8,128)}, u32[]{:S(2)}) copy-start(f32[1,32,256]{2,1,0:T(8,128)} %diff.3) | copy-start | bytes 98308
  5.6 13.8 %collective-permute-start = (f32[24,16,128]{2,1,0:T(8,128)S(1)}, f32[24,16,128]{2,1,0:T(8,128)S(1)}, u32[]{:S(2)}, u32[]{:S(2)}) collective-permute-start(f32[24,16,128]{2,1,0:T(8,128)S(1)} %get-tuple-element.26), channel_id=1, source_target_pairs={{0,8},{8,0},{2,10},{10,2},{4,12},{12,4},{6,14},{14,6},{1,9},{9,1},... | collective-permute-start | bytes 589832 | tf_op jit(solution)/shard_map/ppermute | solution.py:288
  10.3 18.9 %collective-permute-start.1 = (f32[24,16,128]{2,1,0:T(8,128)S(1)}, f32[24,16,128]{2,1,0:T(8,128)S(1)}, u32[]{:S(2)}, u32[]{:S(2)}) collective-permute-start(f32[24,16,128]{2,1,0:T(8,128)S(1)} %get-tuple-element.27), channel_id=1, source_target_pairs={{0,16},{16,0},{2,18},{18,2},{4,20},{20,4},{6,22},{22,6},{1,17},{17... | collective-permute-start | bytes 589832 | tf_op jit(solution)/shard_map/ppermute | solution.py:288
  12.3 17.0 %collective-permute-start.2 = (f32[24,16,128]{2,1,0:T(8,128)S(1)}, f32[24,16,128]{2,1,0:T(8,128)S(1)}, u32[]{:S(2)}, u32[]{:S(2)}) collective-permute-start(f32[24,16,128]{2,1,0:T(8,128)S(1)} %get-tuple-element.28), channel_id=1, source_target_pairs={{0,24},{24,0},{2,26},{26,2},{4,28},{28,4},{6,30},{30,6},{1,25},{25... | collective-permute-start | bytes 589832 | tf_op jit(solution)/shard_map/ppermute | solution.py:288
  14.2 23.1 %collective-permute-start.3 = (f32[24,16,128]{2,1,0:T(8,128)S(1)}, f32[24,16,128]{2,1,0:T(8,128)S(1)}, u32[]{:S(2)}, u32[]{:S(2)}) collective-permute-start(f32[24,16,128]{2,1,0:T(8,128)S(1)} %get-tuple-element.29), channel_id=1, source_target_pairs={{0,10},{10,0},{2,8},{8,2},{4,14},{14,4},{6,12},{12,6},{1,11},{11,1... | collective-permute-start | bytes 589832 | tf_op jit(solution)/shard_map/ppermute | solution.py:288
  16.1 21.2 %copy-start.10 = (f32[4,3]{1,0:T(4,128)S(1)}, f32[4,3]{1,0:T(4,128)}, u32[]{:S(2)}) copy-start(f32[4,3]{1,0:T(4,128)} %rates.3) | copy-start | bytes 148
  16.1 21.1 %collective-permute-start.4 = (f32[24,16,128]{2,1,0:T(8,128)S(1)}, f32[24,16,128]{2,1,0:T(8,128)S(1)}, u32[]{:S(2)}, u32[]{:S(2)}) collective-permute-start(f32[24,16,128]{2,1,0:T(8,128)S(1)} %get-tuple-element.30), channel_id=1, source_target_pairs={{0,18},{18,0},{2,16},{16,2},{4,22},{22,4},{6,20},{20,6},{1,19},{19... | collective-permute-start | bytes 589832 | tf_op jit(solution)/shard_map/ppermute | solution.py:288
  19.4 17.9 %collective-permute-start.5 = (f32[24,16,128]{2,1,0:T(8,128)S(1)}, f32[24,16,128]{2,1,0:T(8,128)S(1)}, u32[]{:S(2)}, u32[]{:S(2)}) collective-permute-start(f32[24,16,128]{2,1,0:T(8,128)S(1)} %get-tuple-element.31), channel_id=1, source_target_pairs={{0,26},{26,0},{2,24},{24,2},{4,30},{30,4},{6,28},{28,6},{1,27},{27... | collective-permute-start | bytes 589832 | tf_op jit(solution)/shard_map/ppermute | solution.py:288
  37.3 13.3 %copy-start.2 = (f32[1,32,256]{2,1,0:T(8,128)S(1)}, f32[1,32,256]{2,1,0:T(8,128)}, u32[]{:S(2)}) copy-start(f32[1,32,256]{2,1,0:T(8,128)} %sponge.9) | copy-start | bytes 98308
  40.0 9.8 %collective-permute-start.6 = (f32[24,256]{1,0:T(8,128)S(1)}, f32[24,256]{1,0:T(8,128)S(1)}, u32[]{:S(2)}, u32[]{:S(2)}) collective-permute-start(f32[24,256]{1,0:T(8,128)S(1)} %get-tuple-element.33), channel_id=1, source_target_pairs={{0,2},{2,0},{4,6},{6,4},{1,3},{3,1},{5,7},{7,5},{8,10},{10,8},{12,... | collective-permute-start | bytes 73736 | tf_op jit(solution)/shard_map/ppermute | solution.py:340
  40.3 10.3 %collective-permute-start.7 = (f32[24,256]{1,0:T(8,128)S(1)}, f32[24,256]{1,0:T(8,128)S(1)}, u32[]{:S(2)}, u32[]{:S(2)}) collective-permute-start(f32[24,256]{1,0:T(8,128)S(1)} %get-tuple-element.34), channel_id=1, source_target_pairs={{2,4},{4,2},{6,0},{0,6},{3,5},{5,3},{7,1},{1,7},{10,12},{12,10},{1... | collective-permute-start | bytes 73736 | tf_op jit(solution)/shard_map/ppermute | solution.py:340
  48.7 1.2 %collective-permute-start.8 = (f32[32,128]{1,0:T(8,128)S(1)}, f32[32,128]{1,0:T(8,128)S(1)}, u32[]{:S(2)}, u32[]{:S(2)}) collective-permute-start(f32[32,128]{1,0:T(8,128)S(1)} %get-tuple-element.35), channel_id=1, source_target_pairs={{0,1},{1,0},{2,3},{3,2},{4,5},{5,4},{6,7},{7,6},{8,9},{9,8},{10,11... | collective-permute-start | bytes 49160 | tf_op jit(solution)/shard_map/ppermute | solution.py:341
  52.5 24.0 %collective-permute-start.9 = (f32[24,16,128]{2,1,0:T(8,128)S(1)}, f32[24,16,128]{2,1,0:T(8,128)S(1)}, u32[]{:S(2)}, u32[]{:S(2)}) collective-permute-start(f32[24,16,128]{2,1,0:T(8,128)S(1)} %get-tuple-element.37), channel_id=1, source_target_pairs={{0,8},{8,0},{2,10},{10,2},{4,12},{12,4},{6,14},{14,6},{1,9},{9,1},... | collective-permute-start | bytes 589832 | tf_op jit(solution)/shard_map/ppermute | solution.py:288
  54.4 24.0 %collective-permute-start.10 = (f32[24,16,128]{2,1,0:T(8,128)S(1)}, f32[24,16,128]{2,1,0:T(8,128)S(1)}, u32[]{:S(2)}, u32[]{:S(2)}) collective-permute-start(f32[24,16,128]{2,1,0:T(8,128)S(1)} %get-tuple-element.38), channel_id=1, source_target_pairs={{0,16},{16,0},{2,18},{18,2},{4,20},{20,4},{6,22},{22,6},{1,17},{17... | collective-permute-start | bytes 589832 | tf_op jit(solution)/shard_map/ppermute | solution.py:288
  56.4 22.1 %collective-permute-start.11 = (f32[24,16,128]{2,1,0:T(8,128)S(1)}, f32[24,16,128]{2,1,0:T(8,128)S(1)}, u32[]{:S(2)}, u32[]{:S(2)}) collective-permute-start(f32[24,16,128]{2,1,0:T(8,128)S(1)} %get-tuple-element.39), channel_id=1, source_target_pairs={{0,24},{24,0},{2,26},{26,2},{4,28},{28,4},{6,30},{30,6},{1,25},{25... | collective-permute-start | bytes 589832 | tf_op jit(solution)/shard_map/ppermute | solution.py:288
  58.3 22.2 %collective-permute-start.12 = (f32[24,16,128]{2,1,0:T(8,128)S(1)}, f32[24,16,128]{2,1,0:T(8,128)S(1)}, u32[]{:S(2)}, u32[]{:S(2)}) collective-permute-start(f32[24,16,128]{2,1,0:T(8,128)S(1)} %get-tuple-element.40), channel_id=1, source_target_pairs={{0,10},{10,0},{2,8},{8,2},{4,14},{14,4},{6,12},{12,6},{1,11},{11,1... | collective-permute-start | bytes 589832 | tf_op jit(solution)/shard_map/ppermute | solution.py:288
  60.7 19.7 %collective-permute-start.13 = (f32[24,16,128]{2,1,0:T(8,128)S(1)}, f32[24,16,128]{2,1,0:T(8,128)S(1)}, u32[]{:S(2)}, u32[]{:S(2)}) collective-permute-start(f32[24,16,128]{2,1,0:T(8,128)S(1)} %get-tuple-element.41), channel_id=1, source_target_pairs={{0,18},{18,0},{2,16},{16,2},{4,22},{22,4},{6,20},{20,6},{1,19},{19... | collective-permute-start | bytes 589832 | tf_op jit(solution)/shard_map/ppermute | solution.py:288
  76.5 10.4 %collective-permute-start.14 = (f32[24,16,128]{2,1,0:T(8,128)S(1)}, f32[24,16,128]{2,1,0:T(8,128)S(1)}, u32[]{:S(2)}, u32[]{:S(2)}) collective-permute-start(f32[24,16,128]{2,1,0:T(8,128)S(1)} %get-tuple-element.42), channel_id=1, source_target_pairs={{0,26},{26,0},{2,24},{24,2},{4,30},{30,4},{6,28},{28,6},{1,27},{27... | collective-permute-start | bytes 589832 | tf_op jit(solution)/shard_map/ppermute | solution.py:288
  89.5 3.9 %collective-permute-start.15 = (f32[24,256]{1,0:T(8,128)S(1)}, f32[24,256]{1,0:T(8,128)S(1)}, u32[]{:S(2)}, u32[]{:S(2)}) collective-permute-start(f32[24,256]{1,0:T(8,128)S(1)} %get-tuple-element.44), channel_id=1, source_target_pairs={{0,2},{2,0},{4,6},{6,4},{1,3},{3,1},{5,7},{7,5},{8,10},{10,8},{12,... | collective-permute-start | bytes 73736 | tf_op jit(solution)/shard_map/ppermute | solution.py:340
  90.7 4.7 %collective-permute-start.16 = (f32[24,256]{1,0:T(8,128)S(1)}, f32[24,256]{1,0:T(8,128)S(1)}, u32[]{:S(2)}, u32[]{:S(2)}) collective-permute-start(f32[24,256]{1,0:T(8,128)S(1)} %get-tuple-element.45), channel_id=1, source_target_pairs={{2,4},{4,2},{6,0},{0,6},{3,5},{5,3},{7,1},{1,7},{10,12},{12,10},{1... | collective-permute-start | bytes 73736 | tf_op jit(solution)/shard_map/ppermute | solution.py:340
  91.3 1.2 %collective-permute-start.17 = (f32[32,128]{1,0:T(8,128)S(1)}, f32[32,128]{1,0:T(8,128)S(1)}, u32[]{:S(2)}, u32[]{:S(2)}) collective-permute-start(f32[32,128]{1,0:T(8,128)S(1)} %get-tuple-element.46), channel_id=1, source_target_pairs={{0,1},{1,0},{2,3},{3,2},{4,5},{5,4},{6,7},{7,6},{8,9},{9,8},{10,11... | collective-permute-start | bytes 49160 | tf_op jit(solution)/shard_map/ppermute | solution.py:341

commit v3 on v2

--- a/solution.py
+++ b/solution.py
@@ -23,6 +23,13 @@
 
 def place():
     return lax.axis_index("grid"), lax.axis_index("gx"), lax.axis_index("gy")
+
+
+ORDER = ((0, 0), (0, 1), (1, 0), (1, 1), (2, 0), (2, 1))
+
+
+def sorted_out(blocks):
+    return [blocks[ORDER.index((slot, kind))] for kind in range(2) for slot in range(SLOTS)]
 
 
 def pieces(flip, top, left):
@@ -134,6 +141,7 @@
 
 def first_kernel(flip, top, left, state, sponge, *rest):
     outs, (rows, fine) = rest[:-2], rest[-2:]
+    outs = sorted_out(outs)
     payload(flip, top, left, state.at[0], sponge, outs[:SLOTS], outs[SLOTS:], rows, fine)
 
 
@@ -143,7 +151,7 @@
 
 
 def update_kernel(n_cols, flip, top, left, rates, state, sponge, agg, brk, mask, diff, *rest):
-    got = rest[: 2 * SLOTS]
+    got = sorted_out(rest[: 2 * SLOTS])
     n_side = 2 + n_cols
     bulk, sides = rest[2 * SLOTS], rest[2 * SLOTS + 1 : 2 * SLOTS + 1 + n_side]
     bulk = bulk.at[0] if len(bulk.shape) == 4 else bulk
@@ -273,19 +281,19 @@
 
     if not last:
         outs, (rows, fine) = rest[3 + n_cols : -2], rest[-2:]
+        outs = sorted_out(outs)
         payload(flip, top, left, new, sponge, outs[:SLOTS], outs[SLOTS:], rows, fine)
 
 
 def exchange(blocks):
     n_x = lax.axis_size("gx")
-    got = [None] * (2 * SLOTS)
-    for slot in reversed(range(SLOTS)):
-        for kind in range(2):
-            pairs = []
-            for i in range(n_x):
-                parent, child = i, (slot + 1) * n_x + (i ^ kind)
-                pairs += [(parent, child), (child, parent)]
-            got[kind * SLOTS + slot] = lax.ppermute(blocks[kind * SLOTS + slot], ("grid", "gx"), pairs)
+    got = []
+    for (slot, kind), block in zip(ORDER, blocks):
+        pairs = []
+        for i in range(n_x):
+            parent, child = i, (slot + 1) * n_x + (i ^ kind)
+            pairs += [(parent, child), (child, parent)]
+        got.append(lax.ppermute(block, ("grid", "gx"), pairs))
     return got
 
 

time: 97 us -> 87.2 us (0.90); the launches traced: 97.2 us -> 86.4 us
  waiting for transfers between devices: 42.5 us -> 21.3 us
  starting transfers between devices: 39.9 us -> 49.6 us
    ppermute x12, waiting for transfers between devices: 36.4 us -> 16.5 us  [exchange(): got.append(lax.ppermute(block, ('grid', 'gx'), pairs))]
    ppermute x12, starting transfers between devices: 29.5 us -> 44.3 us  [exchange(): got.append(lax.ppermute(block, ('grid', 'gx'), pairs))]
    ppermute x4, starting transfers between devices: 10.4 us -> 5.3 us  [local(): lax.ppermute(sides[k], 'gx', swap_pairs(n_x, k))]
    ppermute x4, waiting for transfers between devices: 3.74 us -> 2.39 us  [local(): lax.ppermute(sides[k], 'gx', swap_pairs(n_x, k))]
  transfers between devices with their start and end apart: 18 -> 18, of which waited for: 10 -> 7; matrix products, arithmetic and copies ran while one was open for 0% -> 0% of each run, Pallas kernels for 0% -> 0%
where the time goes in v3:
time: 87.2 us; the launch traced here: 86.4 us
  starting transfers between devices  49.6 us (57%)
  waiting for transfers between devices  21.3 us (24%)
  Pallas kernels  11.3 us (13%)
  local copies, waits for them, and re-layouts  3.97 us (5%)
    ppermute x12, starting transfers between devices, exchange(): got.append(lax.ppermute(block, ('grid', 'gx'), pairs))  44.3 us
    ppermute x12, waiting for transfers between devices, exchange(): got.append(lax.ppermute(block, ('grid', 'gx'), pairs))  16.5 us
    pallas_call x2, Pallas kernels, local(): pl.pallas_call(functools.partial(update_kernel, n_cols), out_shape=[new]...  5.61 us
    ppermute x4, starting transfers between devices, local(): lax.ppermute(sides[k], 'gx', swap_pairs(n_x, k))  5.3 us
    unnamed x22, local copies, waits for them, and re-layouts  3.97 us
    pallas_call x2, Pallas kernels, local(): pl.pallas_call(functools.partial(halo_kernel, n_cols, (n_x, n_y), last),...  3.86 us
    ppermute x4, waiting for transfers between devices, local(): lax.ppermute(sides[k], 'gx', swap_pairs(n_x, k))  2.39 us
    ppermute x2, waiting for transfers between devices, local(): lax.ppermute(sides[2 + k], 'gy', swap_pairs(n_y, k))  2.36 us
  transfers between devices with their start and end apart: 18, of which 7 were waited for; matrix products, arithmetic and copies ran while one was open for 0% of the time, Pallas kernels for 0%

profile of v3, /device:TPU:0, one launch (start us, length us, event | category | flops | bytes accessed | tf_op | source)
XLA Modules:
  0.0 86.4 jit_solution(304760925897142964)
XLA Ops:
  0.0 0.7 copy-done.7
  0.7 1.1 %copy-done = f32[1,24,32,256]{3,2,1,0:T(8,128)S(1)} copy-done((f32[1,24,32,256]{3,2,1,0:T(8,128)S(1)}, f32[1,24,32,256]{3,2,1,0:T(8,128)}, u32[]{:S(2)}) %copy-start) | copy-done | bytes 786456
  1.8 0.8 copy-done.1
  2.6 0.7 copy-done.8
  3.3 0.7 copy-done.9
  4.0 1.9 %first_payload.1 = (f32[24,16,128]{2,1,0:T(8,128)S(1)}, f32[24,16,128]{2,1,0:T(8,128)S(1)}, f32[24,16,128]{2,1,0:T(8,128)S(1)}, f32[24,16,128]{2,1,0:T(8,128)S(1...) custom-call(s32[3,2,4]{2,1,0:T(2,128)S(1)} %bitcast.5, s32[3,2,4]{2,1,0:T(2,128)S(1)} %bitcast.10, ...), custom_call_target="tpu_custom_call" | custom-call | tf_op jit(solution)/shard_map/first_payload/pallas_call | solution.py:320
  5.8 4.5 %collective-permute-start = (f32[24,16,128]{2,1,0:T(8,128)S(1)}, f32[24,16,128]{2,1,0:T(8,128)S(1)}, u32[]{:S(2)}, u32[]{:S(2)}) collective-permute-start(f32[24,16,128]{2,1,0:T(8,128)S(1)} %get-tuple-element.26), channel_id=1, source_target_pairs={{0,8},{8,0},{2,10},{10,2},{4,12},{12,4},{6,14},{14,6},{1,9},{9,1},... | collective-permute-start | bytes 589832 | tf_op jit(solution)/shard_map/ppermute | solution.py:296
  10.3 2.8 %collective-permute-start.1 = (f32[24,16,128]{2,1,0:T(8,128)S(1)}, f32[24,16,128]{2,1,0:T(8,128)S(1)}, u32[]{:S(2)}, u32[]{:S(2)}) collective-permute-start(f32[24,16,128]{2,1,0:T(8,128)S(1)} %get-tuple-element.27), channel_id=1, source_target_pairs={{0,10},{10,0},{2,8},{8,2},{4,14},{14,4},{6,12},{12,6},{1,11},{11,1... | collective-permute-start | bytes 589832 | tf_op jit(solution)/shard_map/ppermute | solution.py:296
  13.2 1.9 %collective-permute-start.2 = (f32[24,16,128]{2,1,0:T(8,128)S(1)}, f32[24,16,128]{2,1,0:T(8,128)S(1)}, u32[]{:S(2)}, u32[]{:S(2)}) collective-permute-start(f32[24,16,128]{2,1,0:T(8,128)S(1)} %get-tuple-element.28), channel_id=1, source_target_pairs={{0,16},{16,0},{2,18},{18,2},{4,20},{20,4},{6,22},{22,6},{1,17},{17... | collective-permute-start | bytes 589832 | tf_op jit(solution)/shard_map/ppermute | solution.py:296
  15.1 4.8 %collective-permute-start.3 = (f32[24,16,128]{2,1,0:T(8,128)S(1)}, f32[24,16,128]{2,1,0:T(8,128)S(1)}, u32[]{:S(2)}, u32[]{:S(2)}) collective-permute-start(f32[24,16,128]{2,1,0:T(8,128)S(1)} %get-tuple-element.29), channel_id=1, source_target_pairs={{0,18},{18,0},{2,16},{16,2},{4,22},{22,4},{6,20},{20,6},{1,19},{19... | collective-permute-start | bytes 589832 | tf_op jit(solution)/shard_map/ppermute | solution.py:296
  20.0 0.0 copy-start.10
  20.0 1.9 %collective-permute-start.4 = (f32[24,16,128]{2,1,0:T(8,128)S(1)}, f32[24,16,128]{2,1,0:T(8,128)S(1)}, u32[]{:S(2)}, u32[]{:S(2)}) collective-permute-start(f32[24,16,128]{2,1,0:T(8,128)S(1)} %get-tuple-element.30), channel_id=1, source_target_pairs={{0,24},{24,0},{2,26},{26,2},{4,28},{28,4},{6,30},{30,6},{1,25},{25... | collective-permute-start | bytes 589832 | tf_op jit(solution)/shard_map/ppermute | solution.py:296
  21.9 0.0 collective-permute-done.rest_0_
  21.9 6.6 %collective-permute-start.5 = (f32[24,16,128]{2,1,0:T(8,128)S(1)}, f32[24,16,128]{2,1,0:T(8,128)S(1)}, u32[]{:S(2)}, u32[]{:S(2)}) collective-permute-start(f32[24,16,128]{2,1,0:T(8,128)S(1)} %get-tuple-element.31), channel_id=1, source_target_pairs={{0,26},{26,0},{2,24},{24,2},{4,30},{30,4},{6,28},{28,6},{1,27},{27... | collective-permute-start | bytes 589832 | tf_op jit(solution)/shard_map/ppermute | solution.py:296
  28.5 9.0 %collective-permute-done.1.rest_1_ = f32[24,16,128]{2,1,0:T(8,128)S(1)} collective-permute-done((f32[24,16,128]{2,1,0:T(8,128)S(1)}, f32[24,16,128]{2,1,0:T(8,128)S(1)}, u32[]{:S(2)}, u32[]{:S(2)}) %collective-permute-start.1) | collective-permute-done | bytes 196640 | tf_op jit(solution)/shard_map/ppermute | solution.py:296
  37.6 0.0 collective-permute-done.2.rest_2_
  37.6 0.0 collective-permute-done.3.rest_3_
  37.6 0.0 collective-permute-done.4.rest_4_
  37.6 0.0 collective-permute-done.5.rest_5_
  37.6 0.0 copy-start.2
  37.7 2.8 %update.2 = (f32[24,32,256]{2,1,0:T(8,128)S(1)}, f32[24,256]{1,0:T(8,128)S(1)}, f32[24,256]{1,0:T(8,128)S(1)}, f32[32,128]{1,0:T(8,128)S(1)}) custom-call(s32[3,2,4]{2,1,0:T(2,128)S(1)} %bitcast.6, s32[3,2,4]{2,1,0:T(2,128)S(1)} %bitcast.11, s32[3,2,4]{2,1,0:T(2,128)S(1)} %bitcast.16, f32[4,3]{1,0:T(4,128)S(1)} %copy-done.10, f32[24,32,256]{2,1,0:T(8,128)S(1)} %bitcast.4, ...), custom_call_target="tpu_custom_call" | custom-call | tf_op jit(solution)/shard_map/update/pallas_call | solution.py:334
  40.5 0.1 collective-permute-start.6
  40.6 2.8 %collective-permute-start.7 = (f32[24,256]{1,0:T(8,128)S(1)}, f32[24,256]{1,0:T(8,128)S(1)}, u32[]{:S(2)}, u32[]{:S(2)}) collective-permute-start(f32[24,256]{1,0:T(8,128)S(1)} %get-tuple-element.34), channel_id=1, source_target_pairs={{2,4},{4,2},{6,0},{0,6},{3,5},{5,3},{7,1},{1,7},{10,12},{12,10},{1... | collective-permute-start | bytes 73736 | tf_op jit(solution)/shard_map/ppermute | solution.py:348
  43.3 0.0 collective-permute-start.8
  43.3 1.2 %collective-permute-done.8.rest_2_ = f32[32,128]{1,0:T(8,128)S(1)} collective-permute-done((f32[32,128]{1,0:T(8,128)S(1)}, f32[32,128]{1,0:T(8,128)S(1)}, u32[]{:S(2)}, u32[]{:S(2)}) %collective-permute-start.8) | collective-permute-done | bytes 16416 | tf_op jit(solution)/shard_map/ppermute | solution.py:349
  44.5 0.0 collective-permute-done.6.rest_0_
  44.5 0.9 %collective-permute-done.7.rest_1_ = f32[24,256]{1,0:T(8,128)S(1)} collective-permute-done((f32[24,256]{1,0:T(8,128)S(1)}, f32[24,256]{1,0:T(8,128)S(1)}, u32[]{:S(2)}, u32[]{:S(2)}) %collective-permute-start.7) | collective-permute-done | bytes 24608 | tf_op jit(solution)/shard_map/ppermute | solution.py:348
  45.4 2.1 %halo.1 = (f32[24,32,256]{2,1,0:T(8,128)S(1)}, f32[24,16,128]{2,1,0:T(8,128)S(1)}, f32[24,16,128]{2,1,0:T(8,128)S(1)}, f32[24,16,128]{2,1,0:T(8,128)S(1)}, f32[2...) custom-call(s32[3,2,4]{2,1,0:T(2,128)S(1)} %bitcast.7, s32[3,2,4]{2,1,0:T(2,128)S(1)} %bitcast.12, ...), custom_call_target="tpu_custom_call" | custom-call | tf_op jit(solution)/shard_map/halo/pallas_call | solution.py:351
  47.4 1.9 %collective-permute-start.9 = (f32[24,16,128]{2,1,0:T(8,128)S(1)}, f32[24,16,128]{2,1,0:T(8,128)S(1)}, u32[]{:S(2)}, u32[]{:S(2)}) collective-permute-start(f32[24,16,128]{2,1,0:T(8,128)S(1)} %get-tuple-element.37), channel_id=1, source_target_pairs={{0,8},{8,0},{2,10},{10,2},{4,12},{12,4},{6,14},{14,6},{1,9},{9,1},... | collective-permute-start | bytes 589832 | tf_op jit(solution)/shard_map/ppermute | solution.py:296
  49.4 4.4 %collective-permute-start.10 = (f32[24,16,128]{2,1,0:T(8,128)S(1)}, f32[24,16,128]{2,1,0:T(8,128)S(1)}, u32[]{:S(2)}, u32[]{:S(2)}) collective-permute-start(f32[24,16,128]{2,1,0:T(8,128)S(1)} %get-tuple-element.38), channel_id=1, source_target_pairs={{0,10},{10,0},{2,8},{8,2},{4,14},{14,4},{6,12},{12,6},{1,11},{11,1... | collective-permute-start | bytes 589832 | tf_op jit(solution)/shard_map/ppermute | solution.py:296
  53.8 1.9 %collective-permute-start.11 = (f32[24,16,128]{2,1,0:T(8,128)S(1)}, f32[24,16,128]{2,1,0:T(8,128)S(1)}, u32[]{:S(2)}, u32[]{:S(2)}) collective-permute-start(f32[24,16,128]{2,1,0:T(8,128)S(1)} %get-tuple-element.39), channel_id=1, source_target_pairs={{0,16},{16,0},{2,18},{18,2},{4,20},{20,4},{6,22},{22,6},{1,17},{17... | collective-permute-start | bytes 589832 | tf_op jit(solution)/shard_map/ppermute | solution.py:296
  55.7 5.2 %collective-permute-start.12 = (f32[24,16,128]{2,1,0:T(8,128)S(1)}, f32[24,16,128]{2,1,0:T(8,128)S(1)}, u32[]{:S(2)}, u32[]{:S(2)}) collective-permute-start(f32[24,16,128]{2,1,0:T(8,128)S(1)} %get-tuple-element.40), channel_id=1, source_target_pairs={{0,18},{18,0},{2,16},{16,2},{4,22},{22,4},{6,20},{20,6},{1,19},{19... | collective-permute-start | bytes 589832 | tf_op jit(solution)/shard_map/ppermute | solution.py:296
  61.0 1.9 %collective-permute-start.13 = (f32[24,16,128]{2,1,0:T(8,128)S(1)}, f32[24,16,128]{2,1,0:T(8,128)S(1)}, u32[]{:S(2)}, u32[]{:S(2)}) collective-permute-start(f32[24,16,128]{2,1,0:T(8,128)S(1)} %get-tuple-element.41), channel_id=1, source_target_pairs={{0,24},{24,0},{2,26},{26,2},{4,28},{28,4},{6,30},{30,6},{1,25},{25... | collective-permute-start | bytes 589832 | tf_op jit(solution)/shard_map/ppermute | solution.py:296
  62.9 0.0 collective-permute-done.9.rest_0_
  62.9 6.2 %collective-permute-start.14 = (f32[24,16,128]{2,1,0:T(8,128)S(1)}, f32[24,16,128]{2,1,0:T(8,128)S(1)}, u32[]{:S(2)}, u32[]{:S(2)}) collective-permute-start(f32[24,16,128]{2,1,0:T(8,128)S(1)} %get-tuple-element.42), channel_id=1, source_target_pairs={{0,26},{26,0},{2,24},{24,2},{4,30},{30,4},{6,28},{28,6},{1,27},{27... | collective-permute-start | bytes 589832 | tf_op jit(solution)/shard_map/ppermute | solution.py:296
  69.1 7.4 %collective-permute-done.10.rest_1_ = f32[24,16,128]{2,1,0:T(8,128)S(1)} collective-permute-done((f32[24,16,128]{2,1,0:T(8,128)S(1)}, f32[24,16,128]{2,1,0:T(8,128)S(1)}, u32[]{:S(2)}, u32[]{:S(2)}) %collective-permute-start.10) | collective-permute-done | bytes 196640 | tf_op jit(solution)/shard_map/ppermute | solution.py:296
  76.6 0.0 collective-permute-done.11.rest_2_
  76.6 0.0 collective-permute-done.12.rest_3_
  76.6 0.0 collective-permute-done.13.rest_4_
  76.6 0.0 collective-permute-done.14.rest_5_
  76.6 2.8 %update.3 = (f32[1,24,32,256]{3,2,1,0:T(8,128)S(1)}, f32[24,256]{1,0:T(8,128)S(1)}, f32[24,256]{1,0:T(8,128)S(1)}, f32[32,128]{1,0:T(8,128)S(1)}) custom-call(s32[3,2,4]{2,1,0:T(2,128)S(1)} %bitcast.8, s32[3,2,4]{2,1,0:T(2,128)S(1)} %bitcast.13, s32[3,2,4]{2,1,0:T(2,128)S(1)} %bitcast.18, f32[4,3]{1,0:T(4,128)S(1)} %copy-done.10, ...), custom_call_target="tpu_custom_call" | custom-call | tf_op jit(solution)/shard_map/update/pallas_call | solution.py:334
  79.4 0.5 collective-permute-start.15
  79.9 2.0 %collective-permute-start.16 = (f32[24,256]{1,0:T(8,128)S(1)}, f32[24,256]{1,0:T(8,128)S(1)}, u32[]{:S(2)}, u32[]{:S(2)}) collective-permute-start(f32[24,256]{1,0:T(8,128)S(1)} %get-tuple-element.45), channel_id=1, source_target_pairs={{2,4},{4,2},{6,0},{0,6},{3,5},{5,3},{7,1},{1,7},{10,12},{12,10},{1... | collective-permute-start | bytes 73736 | tf_op jit(solution)/shard_map/ppermute | solution.py:348
  81.9 0.0 collective-permute-start.17
  81.9 1.2 %collective-permute-done.17.rest_2_ = f32[32,128]{1,0:T(8,128)S(1)} collective-permute-done((f32[32,128]{1,0:T(8,128)S(1)}, f32[32,128]{1,0:T(8,128)S(1)}, u32[]{:S(2)}, u32[]{:S(2)}) %collective-permute-start.17) | collective-permute-done | bytes 16416 | tf_op jit(solution)/shard_map/ppermute | solution.py:349
  83.1 0.2 collective-permute-done.15.rest_0_
  83.3 1.3 %collective-permute-done.16.rest_1_ = f32[24,256]{1,0:T(8,128)S(1)} collective-permute-done((f32[24,256]{1,0:T(8,128)S(1)}, f32[24,256]{1,0:T(8,128)S(1)}, u32[]{:S(2)}, u32[]{:S(2)}) %collective-permute-start.16) | collective-permute-done | bytes 24608 | tf_op jit(solution)/shard_map/ppermute | solution.py:348
  84.6 1.8 %halo_last.1 = f32[1,24,32,256]{3,2,1,0:T(8,128)} custom-call(s32[3,2,4]{2,1,0:T(2,128)S(1)} %bitcast.9, s32[3,2,4]{2,1,0:T(2,128)S(1)} %bitcast.14, s32[3,2,4]{2,1,0:T(2,128)S(1)} %bitcast.19, f32[1,24,32,256]{3,2,1,0:T(8,128)S(1)} %get-tuple-element.43.bulk, f32[1,32,256]{2,1,0:T(8,128)S(1)} %copy-done.2, f32[24,256]{1,0:T(8,128)S(1)} %collective-permute-done.15.rest_0_, ...), custom_call_target="tpu_custom_call" | custom-call | tf_op jit(solution)/shard_map/halo_last/pallas_call | solution.py:351
  (15 shorter events, 0.0 us)
Async XLA Ops:
  0.0 0.7 copy-start.7
  0.7 1.1 %copy-start = (f32[1,24,32,256]{3,2,1,0:T(8,128)S(1)}, f32[1,24,32,256]{3,2,1,0:T(8,128)}, u32[]{:S(2)}) copy-start(f32[1,24,32,256]{3,2,1,0:T(8,128)} %state.1) | copy-start | bytes 2359300
  1.8 0.8 copy-start.1
  2.6 0.7 copy-start.8
  3.3 0.7 copy-start.9
  3.9 33.7 %copy-start.3 = (f32[1,32,256]{2,1,0:T(8,128)S(1)}, f32[1,32,256]{2,1,0:T(8,128)}, u32[]{:S(2)}) copy-start(f32[1,32,256]{2,1,0:T(8,128)} %agg.3) | copy-start | bytes 98308
  3.9 33.7 %copy-start.4 = (f32[1,32,256]{2,1,0:T(8,128)S(1)}, f32[1,32,256]{2,1,0:T(8,128)}, u32[]{:S(2)}) copy-start(f32[1,32,256]{2,1,0:T(8,128)} %brk.3) | copy-start | bytes 98308
  4.0 33.7 %copy-start.5 = (s32[1,32,256]{2,1,0:T(8,128)S(1)}, s32[1,32,256]{2,1,0:T(8,128)}, u32[]{:S(2)}) copy-start(s32[1,32,256]{2,1,0:T(8,128)} %mask.3) | copy-start | bytes 98308
  4.0 33.7 %copy-start.6 = (f32[1,32,256]{2,1,0:T(8,128)S(1)}, f32[1,32,256]{2,1,0:T(8,128)}, u32[]{:S(2)}) copy-start(f32[1,32,256]{2,1,0:T(8,128)} %diff.3) | copy-start | bytes 98308
  5.8 16.1 %collective-permute-start = (f32[24,16,128]{2,1,0:T(8,128)S(1)}, f32[24,16,128]{2,1,0:T(8,128)S(1)}, u32[]{:S(2)}, u32[]{:S(2)}) collective-permute-start(f32[24,16,128]{2,1,0:T(8,128)S(1)} %get-tuple-element.26), channel_id=1, source_target_pairs={{0,8},{8,0},{2,10},{10,2},{4,12},{12,4},{6,14},{14,6},{1,9},{9,1},... | collective-permute-start | bytes 589832 | tf_op jit(solution)/shard_map/ppermute | solution.py:296
  10.3 27.2 %collective-permute-start.1 = (f32[24,16,128]{2,1,0:T(8,128)S(1)}, f32[24,16,128]{2,1,0:T(8,128)S(1)}, u32[]{:S(2)}, u32[]{:S(2)}) collective-permute-start(f32[24,16,128]{2,1,0:T(8,128)S(1)} %get-tuple-element.27), channel_id=1, source_target_pairs={{0,10},{10,0},{2,8},{8,2},{4,14},{14,4},{6,12},{12,6},{1,11},{11,1... | collective-permute-start | bytes 589832 | tf_op jit(solution)/shard_map/ppermute | solution.py:296
  13.2 24.4 %collective-permute-start.2 = (f32[24,16,128]{2,1,0:T(8,128)S(1)}, f32[24,16,128]{2,1,0:T(8,128)S(1)}, u32[]{:S(2)}, u32[]{:S(2)}) collective-permute-start(f32[24,16,128]{2,1,0:T(8,128)S(1)} %get-tuple-element.28), channel_id=1, source_target_pairs={{0,16},{16,0},{2,18},{18,2},{4,20},{20,4},{6,22},{22,6},{1,17},{17... | collective-permute-start | bytes 589832 | tf_op jit(solution)/shard_map/ppermute | solution.py:296
  15.1 22.4 %collective-permute-start.3 = (f32[24,16,128]{2,1,0:T(8,128)S(1)}, f32[24,16,128]{2,1,0:T(8,128)S(1)}, u32[]{:S(2)}, u32[]{:S(2)}) collective-permute-start(f32[24,16,128]{2,1,0:T(8,128)S(1)} %get-tuple-element.29), channel_id=1, source_target_pairs={{0,18},{18,0},{2,16},{16,2},{4,22},{22,4},{6,20},{20,6},{1,19},{19... | collective-permute-start | bytes 589832 | tf_op jit(solution)/shard_map/ppermute | solution.py:296
  20.0 17.7 %copy-start.10 = (f32[4,3]{1,0:T(4,128)S(1)}, f32[4,3]{1,0:T(4,128)}, u32[]{:S(2)}) copy-start(f32[4,3]{1,0:T(4,128)} %rates.3) | copy-start | bytes 148
  20.0 17.6 %collective-permute-start.4 = (f32[24,16,128]{2,1,0:T(8,128)S(1)}, f32[24,16,128]{2,1,0:T(8,128)S(1)}, u32[]{:S(2)}, u32[]{:S(2)}) collective-permute-start(f32[24,16,128]{2,1,0:T(8,128)S(1)} %get-tuple-element.30), channel_id=1, source_target_pairs={{0,24},{24,0},{2,26},{26,2},{4,28},{28,4},{6,30},{30,6},{1,25},{25... | collective-permute-start | bytes 589832 | tf_op jit(solution)/shard_map/ppermute | solution.py:296
  21.9 15.7 %collective-permute-start.5 = (f32[24,16,128]{2,1,0:T(8,128)S(1)}, f32[24,16,128]{2,1,0:T(8,128)S(1)}, u32[]{:S(2)}, u32[]{:S(2)}) collective-permute-start(f32[24,16,128]{2,1,0:T(8,128)S(1)} %get-tuple-element.31), channel_id=1, source_target_pairs={{0,26},{26,0},{2,24},{24,2},{4,30},{30,4},{6,28},{28,6},{1,27},{27... | collective-permute-start | bytes 589832 | tf_op jit(solution)/shard_map/ppermute | solution.py:296
  37.6 7.7 %copy-start.2 = (f32[1,32,256]{2,1,0:T(8,128)S(1)}, f32[1,32,256]{2,1,0:T(8,128)}, u32[]{:S(2)}) copy-start(f32[1,32,256]{2,1,0:T(8,128)} %sponge.9) | copy-start | bytes 98308
  40.5 4.0 %collective-permute-start.6 = (f32[24,256]{1,0:T(8,128)S(1)}, f32[24,256]{1,0:T(8,128)S(1)}, u32[]{:S(2)}, u32[]{:S(2)}) collective-permute-start(f32[24,256]{1,0:T(8,128)S(1)} %get-tuple-element.33), channel_id=1, source_target_pairs={{0,2},{2,0},{4,6},{6,4},{1,3},{3,1},{5,7},{7,5},{8,10},{10,8},{12,... | collective-permute-start | bytes 73736 | tf_op jit(solution)/shard_map/ppermute | solution.py:348
  40.6 4.8 %collective-permute-start.7 = (f32[24,256]{1,0:T(8,128)S(1)}, f32[24,256]{1,0:T(8,128)S(1)}, u32[]{:S(2)}, u32[]{:S(2)}) collective-permute-start(f32[24,256]{1,0:T(8,128)S(1)} %get-tuple-element.34), channel_id=1, source_target_pairs={{2,4},{4,2},{6,0},{0,6},{3,5},{5,3},{7,1},{1,7},{10,12},{12,10},{1... | collective-permute-start | bytes 73736 | tf_op jit(solution)/shard_map/ppermute | solution.py:348
  43.3 1.2 %collective-permute-start.8 = (f32[32,128]{1,0:T(8,128)S(1)}, f32[32,128]{1,0:T(8,128)S(1)}, u32[]{:S(2)}, u32[]{:S(2)}) collective-permute-start(f32[32,128]{1,0:T(8,128)S(1)} %get-tuple-element.35), channel_id=1, source_target_pairs={{0,1},{1,0},{2,3},{3,2},{4,5},{5,4},{6,7},{7,6},{8,9},{9,8},{10,11... | collective-permute-start | bytes 49160 | tf_op jit(solution)/shard_map/ppermute | solution.py:349
  47.4 15.4 %collective-permute-start.9 = (f32[24,16,128]{2,1,0:T(8,128)S(1)}, f32[24,16,128]{2,1,0:T(8,128)S(1)}, u32[]{:S(2)}, u32[]{:S(2)}) collective-permute-start(f32[24,16,128]{2,1,0:T(8,128)S(1)} %get-tuple-element.37), channel_id=1, source_target_pairs={{0,8},{8,0},{2,10},{10,2},{4,12},{12,4},{6,14},{14,6},{1,9},{9,1},... | collective-permute-start | bytes 589832 | tf_op jit(solution)/shard_map/ppermute | solution.py:296
  49.4 27.2 %collective-permute-start.10 = (f32[24,16,128]{2,1,0:T(8,128)S(1)}, f32[24,16,128]{2,1,0:T(8,128)S(1)}, u32[]{:S(2)}, u32[]{:S(2)}) collective-permute-start(f32[24,16,128]{2,1,0:T(8,128)S(1)} %get-tuple-element.38), channel_id=1, source_target_pairs={{0,10},{10,0},{2,8},{8,2},{4,14},{14,4},{6,12},{12,6},{1,11},{11,1... | collective-permute-start | bytes 589832 | tf_op jit(solution)/shard_map/ppermute | solution.py:296
  53.8 22.8 %collective-permute-start.11 = (f32[24,16,128]{2,1,0:T(8,128)S(1)}, f32[24,16,128]{2,1,0:T(8,128)S(1)}, u32[]{:S(2)}, u32[]{:S(2)}) collective-permute-start(f32[24,16,128]{2,1,0:T(8,128)S(1)} %get-tuple-element.39), channel_id=1, source_target_pairs={{0,16},{16,0},{2,18},{18,2},{4,20},{20,4},{6,22},{22,6},{1,17},{17... | collective-permute-start | bytes 589832 | tf_op jit(solution)/shard_map/ppermute | solution.py:296
  55.7 20.8 %collective-permute-start.12 = (f32[24,16,128]{2,1,0:T(8,128)S(1)}, f32[24,16,128]{2,1,0:T(8,128)S(1)}, u32[]{:S(2)}, u32[]{:S(2)}) collective-permute-start(f32[24,16,128]{2,1,0:T(8,128)S(1)} %get-tuple-element.40), channel_id=1, source_target_pairs={{0,18},{18,0},{2,16},{16,2},{4,22},{22,4},{6,20},{20,6},{1,19},{19... | collective-permute-start | bytes 589832 | tf_op jit(solution)/shard_map/ppermute | solution.py:296
  61.0 15.6 %collective-permute-start.13 = (f32[24,16,128]{2,1,0:T(8,128)S(1)}, f32[24,16,128]{2,1,0:T(8,128)S(1)}, u32[]{:S(2)}, u32[]{:S(2)}) collective-permute-start(f32[24,16,128]{2,1,0:T(8,128)S(1)} %get-tuple-element.41), channel_id=1, source_target_pairs={{0,24},{24,0},{2,26},{26,2},{4,28},{28,4},{6,30},{30,6},{1,25},{25... | collective-permute-start | bytes 589832 | tf_op jit(solution)/shard_map/ppermute | solution.py:296
  62.9 13.7 %collective-permute-start.14 = (f32[24,16,128]{2,1,0:T(8,128)S(1)}, f32[24,16,128]{2,1,0:T(8,128)S(1)}, u32[]{:S(2)}, u32[]{:S(2)}) collective-permute-start(f32[24,16,128]{2,1,0:T(8,128)S(1)} %get-tuple-element.42), channel_id=1, source_target_pairs={{0,26},{26,0},{2,24},{24,2},{4,30},{30,4},{6,28},{28,6},{1,27},{27... | collective-permute-start | bytes 589832 | tf_op jit(solution)/shard_map/ppermute | solution.py:296
  79.4 3.9 %collective-permute-start.15 = (f32[24,256]{1,0:T(8,128)S(1)}, f32[24,256]{1,0:T(8,128)S(1)}, u32[]{:S(2)}, u32[]{:S(2)}) collective-permute-start(f32[24,256]{1,0:T(8,128)S(1)} %get-tuple-element.44), channel_id=1, source_target_pairs={{0,2},{2,0},{4,6},{6,4},{1,3},{3,1},{5,7},{7,5},{8,10},{10,8},{12,... | collective-permute-start | bytes 73736 | tf_op jit(solution)/shard_map/ppermute | solution.py:348
  79.9 4.7 %collective-permute-start.16 = (f32[24,256]{1,0:T(8,128)S(1)}, f32[24,256]{1,0:T(8,128)S(1)}, u32[]{:S(2)}, u32[]{:S(2)}) collective-permute-start(f32[24,256]{1,0:T(8,128)S(1)} %get-tuple-element.45), channel_id=1, source_target_pairs={{2,4},{4,2},{6,0},{0,6},{3,5},{5,3},{7,1},{1,7},{10,12},{12,10},{1... | collective-permute-start | bytes 73736 | tf_op jit(solution)/shard_map/ppermute | solution.py:348
  81.9 1.2 %collective-permute-start.17 = (f32[32,128]{1,0:T(8,128)S(1)}, f32[32,128]{1,0:T(8,128)S(1)}, u32[]{:S(2)}, u32[]{:S(2)}) collective-permute-start(f32[32,128]{1,0:T(8,128)S(1)} %get-tuple-element.46), channel_id=1, source_target_pairs={{0,1},{1,0},{2,3},{3,2},{4,5},{5,4},{6,7},{7,6},{8,9},{9,8},{10,11... | collective-permute-start | bytes 49160 | tf_op jit(solution)/shard_map/ppermute | solution.py:349

commit v4 on v3

--- a/solution.py
+++ b/solution.py
@@ -139,10 +139,26 @@
                 crossed[slot][...] = block
 
 
-def first_kernel(flip, top, left, state, sponge, *rest):
-    outs, (rows, fine) = rest[:-2], rest[-2:]
-    outs = sorted_out(outs)
+def first_kernel(*refs):
+    given, outs, token = refs[:5], sorted_out(refs[5 : 5 + 2 * SLOTS]), refs[5 + 2 * SLOTS]
+    rows, fine, *held, done = refs[6 + 2 * SLOTS :]
+    token[...] = jnp.zeros_like(token)
+    copies = [pltpu.make_async_copy(source, to, done.at[k]) for k, (source, to) in enumerate(zip(given, held))]
+    for copy in copies:
+        copy.start()
+    for copy in copies:
+        copy.wait()
+    flip, top, left, state, sponge = held
     payload(flip, top, left, state.at[0], sponge, outs[:SLOTS], outs[SLOTS:], rows, fine)
+
+
+def stage_kernel(token, *refs):
+    given, held, done = refs[:10], refs[10:20], refs[20]
+    copies = [pltpu.make_async_copy(source, to, done.at[k]) for k, (source, to) in enumerate(zip(given, held))]
+    for copy in copies:
+        copy.start()
+    for copy in copies:
+        copy.wait()
 
 
 def edge_sides(index):
@@ -317,16 +333,29 @@
     fold_scratch = [pltpu.VMEM((comps, half_r, cells_c), f32), pltpu.VMEM((cells_c // LANES, cells_r, LANES), f32)]
     tables = [table.transpose(0, 2, 1) for table in (partner_flip, row_offset, col_offset)]
 
-    blocks = pl.pallas_call(
+    *blocks, token = pl.pallas_call(
         first_kernel,
-        out_shape=[block] * (2 * SLOTS),
-        in_specs=[SM] * 3 + [VM] * 2,
-        out_specs=[VM] * (2 * SLOTS),
-        scratch_shapes=fold_scratch,
-        compiler_params=PARAMS,
+        out_shape=[block] * (2 * SLOTS) + [jax.ShapeDtypeStruct((8, LANES), f32)],
+        in_specs=[pl.BlockSpec(memory_space=pltpu.HBM)] * 5,
+        out_specs=[VM] * (2 * SLOTS + 1),
+        scratch_shapes=fold_scratch
+        + [pltpu.SMEM(table.shape, table.dtype) for table in tables]
+        + [pltpu.VMEM(adjoint.shape, f32), pltpu.VMEM(sponge.shape, f32), pltpu.SemaphoreType.DMA((5,))],
+        compiler_params=pltpu.CompilerParams(vmem_limit_bytes=60 * 2**20),
         name="first_payload",
     )(*tables, adjoint, sponge)
-    state = adjoint.reshape(tile.shape)
+    fields = (adjoint, sponge, settling, aggregation, breakup, sea_mask, diffusivity, *tables)
+    state, sponge, rates, *fields = pl.pallas_call(
+        stage_kernel,
+        out_shape=[jax.ShapeDtypeStruct(field.shape, field.dtype) for field in fields],
+        in_specs=[VM] + [pl.BlockSpec(memory_space=pltpu.HBM)] * 10,
+        out_specs=[VM] * 10,
+        scratch_shapes=[pltpu.SemaphoreType.DMA((10,))],
+        compiler_params=PARAMS,
+        name="stage_fields",
+    )(token, *fields)
+    state = state.reshape(tile.shape)
+    fields, tables = fields[:4], fields[4:]
     for step in range(STEPS):
         got = exchange(blocks)
         last = step == STEPS - 1
@@ -344,7 +373,7 @@
             ],
             compiler_params=PARAMS,
             name="update",
-        )(*tables, settling, state, sponge, aggregation, breakup, sea_mask, diffusivity, *got)
+        )(*tables, rates, state, sponge, *fields, *got)
         sides = [lax.ppermute(sides[k], "gx", swap_pairs(n_x, k)) for k in range(2)] + [
             lax.ppermute(sides[2 + k], "gy", swap_pairs(n_y, k)) for k in range(n_cols)
         ]

time: 87.2 us -> 85.5 us (0.981)
  waiting for transfers between devices: 21.3 us -> 17.1 us
  starting transfers between devices: 49.6 us -> 52.9 us
  local copies, waits for them, and re-layouts: 3.97 us -> 3.06 us
    ppermute x12, waiting for transfers between devices: 16.5 us -> 12.5 us  [exchange(): got.append(lax.ppermute(block, ('grid', 'gx'), pairs))]
    ppermute x12, starting transfers between devices: 44.3 us -> 46.3 us  [exchange(): got.append(lax.ppermute(block, ('grid', 'gx'), pairs))]
    ppermute x4, starting transfers between devices: 5.3 us -> 6.66 us  [local(): lax.ppermute(sides[k], 'gx', swap_pairs(n_x, k))]
    pallas_call x1 -> x2, Pallas kernels: 1.85 us -> 3.12 us  [the longest x1 2.73 us: local(): pl.pallas_call(first_kernel, out_shape=[block] * (2 * SLOTS) + [jax.Shape...]
    unnamed x22, local copies, waits for them, and re-layouts: 3.97 us -> 3.06 us
    pallas_call x2, Pallas kernels: 5.61 us -> 4.73 us  [local(): pl.pallas_call(functools.partial(update_kernel, n_cols), out_shape=[new]...]
  transfers between devices with their start and end apart: 18 -> 18, of which waited for: 7 -> 6; matrix products, arithmetic and copies ran while one was open for 0% -> 0% of each run, Pallas kernels for 0% -> 0%
where the time goes in v4:
time: 85.5 us; the launch traced here: 84.5 us
  starting transfers between devices  52.9 us (62%)
  waiting for transfers between devices  17.1 us (20%)
  Pallas kernels  11.1 us (13%)
  local copies, waits for them, and re-layouts  3.06 us (4%)
    ppermute x12, starting transfers between devices, exchange(): got.append(lax.ppermute(block, ('grid', 'gx'), pairs))  46.3 us
    ppermute x12, waiting for transfers between devices, exchange(): got.append(lax.ppermute(block, ('grid', 'gx'), pairs))  12.5 us
    ppermute x4, starting transfers between devices, local(): lax.ppermute(sides[k], 'gx', swap_pairs(n_x, k))  6.66 us
    pallas_call x2, Pallas kernels, local(): pl.pallas_call(functools.partial(update_kernel, n_cols), out_shape=[new]...  4.73 us
    pallas_call x2, Pallas kernels, local(): pl.pallas_call(functools.partial(halo_kernel, n_cols, (n_x, n_y), last),...  3.21 us
    unnamed x22, local copies, waits for them, and re-layouts  3.06 us
    pallas_call x1, Pallas kernels, local(): pl.pallas_call(first_kernel, out_shape=[block] * (2 * SLOTS) + [jax.Shape...  2.73 us
    ppermute x2, waiting for transfers between devices, local(): lax.ppermute(sides[2 + k], 'gy', swap_pairs(n_y, k))  2.36 us
  transfers between devices with their start and end apart: 18, of which 6 were waited for; matrix products, arithmetic and copies ran while one was open for 0% of the time, Pallas kernels for 0%

profile of v4, /device:TPU:0, one launch (start us, length us, event | category | flops | bytes accessed | tf_op | source)
XLA Modules:
  0.0 84.5 jit_solution(4178586058141995763)
XLA Ops:
  0.0 2.7 %first_payload.1 = (f32[24,16,128]{2,1,0:T(8,128)}, f32[24,16,128]{2,1,0:T(8,128)}, f32[24,16,128]{2,1,0:T(8,128)}, f32[24,16,128]{2,1,0:T(8,128)}, f32[24,16,12...) custom-call(s32[3,2,4]{2,1,0:T(2,128)} %bitcast.5, s32[3,2,4]{2,1,0:T(2,128)} %bitcast.7, ...), custom_call_target="tpu_custom_call" | custom-call | tf_op jit(solution)/shard_map/first_payload/pallas_call | solution.py:336
  2.8 5.2 %collective-permute-start = (f32[24,16,128]{2,1,0:T(8,128)}, f32[24,16,128]{2,1,0:T(8,128)S(1)}, u32[]{:S(2)}, u32[]{:S(2)}) collective-permute-start(f32[24,16,128]{2,1,0:T(8,128)} %get-tuple-element.48), channel_id=1, source_target_pairs={{0,8},{8,0},{2,10},{10,2},{4,12},{12,4},{6,14},{14,6},{1,9},{9,1},... | collective-permute-start | bytes 589832 | tf_op jit(solution)/shard_map/ppermute | solution.py:312
  8.0 3.5 %collective-permute-start.1 = (f32[24,16,128]{2,1,0:T(8,128)}, f32[24,16,128]{2,1,0:T(8,128)S(1)}, u32[]{:S(2)}, u32[]{:S(2)}) collective-permute-start(f32[24,16,128]{2,1,0:T(8,128)} %get-tuple-element.49), channel_id=1, source_target_pairs={{0,10},{10,0},{2,8},{8,2},{4,14},{14,4},{6,12},{12,6},{1,11},{11,1... | collective-permute-start | bytes 589832 | tf_op jit(solution)/shard_map/ppermute | solution.py:312
  11.4 0.0 copy-start.8
  11.4 1.9 %collective-permute-start.2 = (f32[24,16,128]{2,1,0:T(8,128)}, f32[24,16,128]{2,1,0:T(8,128)S(1)}, u32[]{:S(2)}, u32[]{:S(2)}) collective-permute-start(f32[24,16,128]{2,1,0:T(8,128)} %get-tuple-element.50), channel_id=1, source_target_pairs={{0,16},{16,0},{2,18},{18,2},{4,20},{20,4},{6,22},{22,6},{1,17},{17... | collective-permute-start | bytes 589832 | tf_op jit(solution)/shard_map/ppermute | solution.py:312
  13.4 0.0 copy-start.7
  13.4 0.0 copy-start.6
  13.4 4.2 %collective-permute-start.3 = (f32[24,16,128]{2,1,0:T(8,128)}, f32[24,16,128]{2,1,0:T(8,128)S(1)}, u32[]{:S(2)}, u32[]{:S(2)}) collective-permute-start(f32[24,16,128]{2,1,0:T(8,128)} %get-tuple-element.51), channel_id=1, source_target_pairs={{0,18},{18,0},{2,16},{16,2},{4,22},{22,4},{6,20},{20,6},{1,19},{19... | collective-permute-start | bytes 589832 | tf_op jit(solution)/shard_map/ppermute | solution.py:312
  17.6 1.9 %collective-permute-start.4 = (f32[24,16,128]{2,1,0:T(8,128)}, f32[24,16,128]{2,1,0:T(8,128)S(1)}, u32[]{:S(2)}, u32[]{:S(2)}) collective-permute-start(f32[24,16,128]{2,1,0:T(8,128)} %get-tuple-element.52), channel_id=1, source_target_pairs={{0,24},{24,0},{2,26},{26,2},{4,28},{28,4},{6,30},{30,6},{1,25},{25... | collective-permute-start | bytes 589832 | tf_op jit(solution)/shard_map/ppermute | solution.py:312
  19.5 0.0 collective-permute-done.rest_0_
  19.6 7.2 %collective-permute-start.5 = (f32[24,16,128]{2,1,0:T(8,128)}, f32[24,16,128]{2,1,0:T(8,128)S(1)}, u32[]{:S(2)}, u32[]{:S(2)}) collective-permute-start(f32[24,16,128]{2,1,0:T(8,128)} %get-tuple-element.53), channel_id=1, source_target_pairs={{0,26},{26,0},{2,24},{24,2},{4,30},{30,4},{6,28},{28,6},{1,27},{27... | collective-permute-start | bytes 589832 | tf_op jit(solution)/shard_map/ppermute | solution.py:312
  26.9 0.0 copy-start.2
  26.9 0.7 copy-done.2
  27.6 0.8 copy-done.3
  28.4 0.8 copy-done.4
  29.1 0.8 copy-done.5
  29.9 0.4 stage_fields.1
  30.3 5.3 %collective-permute-done.1.rest_1_ = f32[24,16,128]{2,1,0:T(8,128)S(1)} collective-permute-done((f32[24,16,128]{2,1,0:T(8,128)}, f32[24,16,128]{2,1,0:T(8,128)S(1)}, u32[]{:S(2)}, u32[]{:S(2)}) %collective-permute-start.1) | collective-permute-done | bytes 196640 | tf_op jit(solution)/shard_map/ppermute | solution.py:312
  35.6 0.0 collective-permute-done.2.rest_2_
  35.6 0.0 collective-permute-done.3.rest_3_
  35.6 0.0 collective-permute-done.5.rest_5_
  35.6 2.4 %update.2 = (f32[24,32,256]{2,1,0:T(8,128)S(1)}, f32[24,256]{1,0:T(8,128)S(1)}, f32[24,256]{1,0:T(8,128)S(1)}, f32[32,128]{1,0:T(8,128)S(1)}) custom-call(s32[3,2,4]{2,1,0:T(2,128)S(1)} %get-tuple-element.38.flip, s32[3,2,4]{2,1,0:T(2,128)S(1)} %get-tuple-element.39.top, s32[3,2,4]{2,1,0:T(2,128)S(1)} %get-tuple-element.40.left, ...), custom_call_target="tpu_custom_call" | custom-call | tf_op jit(solution)/shard_map/update/pallas_call | solution.py:363
  38.0 0.4 collective-permute-start.6
  38.4 3.0 %collective-permute-start.7 = (f32[24,256]{1,0:T(8,128)S(1)}, f32[24,256]{1,0:T(8,128)S(1)}, u32[]{:S(2)}, u32[]{:S(2)}) collective-permute-start(f32[24,256]{1,0:T(8,128)S(1)} %get-tuple-element.56), channel_id=1, source_target_pairs={{2,4},{4,2},{6,0},{0,6},{3,5},{5,3},{7,1},{1,7},{10,12},{12,10},{1... | collective-permute-start | bytes 73736 | tf_op jit(solution)/shard_map/ppermute | solution.py:377
  41.4 1.2 %collective-permute-done.8.rest_2_ = f32[32,128]{1,0:T(8,128)S(1)} collective-permute-done((f32[32,128]{1,0:T(8,128)S(1)}, f32[32,128]{1,0:T(8,128)S(1)}, u32[]{:S(2)}, u32[]{:S(2)}) %collective-permute-start.8) | collective-permute-done | bytes 16416 | tf_op jit(solution)/shard_map/ppermute | solution.py:378
  42.6 0.0 collective-permute-done.6.rest_0_
  42.6 0.9 %collective-permute-done.7.rest_1_ = f32[24,256]{1,0:T(8,128)S(1)} collective-permute-done((f32[24,256]{1,0:T(8,128)S(1)}, f32[24,256]{1,0:T(8,128)S(1)}, u32[]{:S(2)}, u32[]{:S(2)}) %collective-permute-start.7) | collective-permute-done | bytes 24608 | tf_op jit(solution)/shard_map/ppermute | solution.py:377
  43.5 1.4 %halo.1 = (f32[24,32,256]{2,1,0:T(8,128)S(1)}, f32[24,16,128]{2,1,0:T(8,128)S(1)}, f32[24,16,128]{2,1,0:T(8,128)S(1)}, f32[24,16,128]{2,1,0:T(8,128)S(1)}, f32[2...) custom-call(s32[3,2,4]{2,1,0:T(2,128)S(1)} %get-tuple-element.38.flip, ...), custom_call_target="tpu_custom_call" | custom-call | tf_op jit(solution)/shard_map/halo/pallas_call | solution.py:380
  44.9 2.0 %collective-permute-start.9 = (f32[24,16,128]{2,1,0:T(8,128)S(1)}, f32[24,16,128]{2,1,0:T(8,128)S(1)}, u32[]{:S(2)}, u32[]{:S(2)}) collective-permute-start(f32[24,16,128]{2,1,0:T(8,128)S(1)} %get-tuple-element.59), channel_id=1, source_target_pairs={{0,8},{8,0},{2,10},{10,2},{4,12},{12,4},{6,14},{14,6},{1,9},{9,1},... | collective-permute-start | bytes 589832 | tf_op jit(solution)/shard_map/ppermute | solution.py:312
  46.9 5.0 %collective-permute-start.10 = (f32[24,16,128]{2,1,0:T(8,128)S(1)}, f32[24,16,128]{2,1,0:T(8,128)S(1)}, u32[]{:S(2)}, u32[]{:S(2)}) collective-permute-start(f32[24,16,128]{2,1,0:T(8,128)S(1)} %get-tuple-element.60), channel_id=1, source_target_pairs={{0,10},{10,0},{2,8},{8,2},{4,14},{14,4},{6,12},{12,6},{1,11},{11,1... | collective-permute-start | bytes 589832 | tf_op jit(solution)/shard_map/ppermute | solution.py:312
  52.0 1.9 %collective-permute-start.11 = (f32[24,16,128]{2,1,0:T(8,128)S(1)}, f32[24,16,128]{2,1,0:T(8,128)S(1)}, u32[]{:S(2)}, u32[]{:S(2)}) collective-permute-start(f32[24,16,128]{2,1,0:T(8,128)S(1)} %get-tuple-element.61), channel_id=1, source_target_pairs={{0,16},{16,0},{2,18},{18,2},{4,20},{20,4},{6,22},{22,6},{1,17},{17... | collective-permute-start | bytes 589832 | tf_op jit(solution)/shard_map/ppermute | solution.py:312
  53.9 4.5 %collective-permute-start.12 = (f32[24,16,128]{2,1,0:T(8,128)S(1)}, f32[24,16,128]{2,1,0:T(8,128)S(1)}, u32[]{:S(2)}, u32[]{:S(2)}) collective-permute-start(f32[24,16,128]{2,1,0:T(8,128)S(1)} %get-tuple-element.62), channel_id=1, source_target_pairs={{0,18},{18,0},{2,16},{16,2},{4,22},{22,4},{6,20},{20,6},{1,19},{19... | collective-permute-start | bytes 589832 | tf_op jit(solution)/shard_map/ppermute | solution.py:312
  58.4 1.9 %collective-permute-start.13 = (f32[24,16,128]{2,1,0:T(8,128)S(1)}, f32[24,16,128]{2,1,0:T(8,128)S(1)}, u32[]{:S(2)}, u32[]{:S(2)}) collective-permute-start(f32[24,16,128]{2,1,0:T(8,128)S(1)} %get-tuple-element.63), channel_id=1, source_target_pairs={{0,24},{24,0},{2,26},{26,2},{4,28},{28,4},{6,30},{30,6},{1,25},{25... | collective-permute-start | bytes 589832 | tf_op jit(solution)/shard_map/ppermute | solution.py:312
  60.4 0.0 collective-permute-done.9.rest_0_
  60.4 6.9 %collective-permute-start.14 = (f32[24,16,128]{2,1,0:T(8,128)S(1)}, f32[24,16,128]{2,1,0:T(8,128)S(1)}, u32[]{:S(2)}, u32[]{:S(2)}) collective-permute-start(f32[24,16,128]{2,1,0:T(8,128)S(1)} %get-tuple-element.64), channel_id=1, source_target_pairs={{0,26},{26,0},{2,24},{24,2},{4,30},{30,4},{6,28},{28,6},{1,27},{27... | collective-permute-start | bytes 589832 | tf_op jit(solution)/shard_map/ppermute | solution.py:312
  67.3 7.2 %collective-permute-done.10.rest_1_ = f32[24,16,128]{2,1,0:T(8,128)S(1)} collective-permute-done((f32[24,16,128]{2,1,0:T(8,128)S(1)}, f32[24,16,128]{2,1,0:T(8,128)S(1)}, u32[]{:S(2)}, u32[]{:S(2)}) %collective-permute-start.10) | collective-permute-done | bytes 196640 | tf_op jit(solution)/shard_map/ppermute | solution.py:312
  74.5 0.0 collective-permute-done.11.rest_2_
  74.5 0.0 collective-permute-done.12.rest_3_
  74.5 0.0 collective-permute-done.13.rest_4_
  74.5 0.0 collective-permute-done.14.rest_5_
  74.5 2.4 %update.3 = (f32[1,24,32,256]{3,2,1,0:T(8,128)S(1)}, f32[24,256]{1,0:T(8,128)S(1)}, f32[24,256]{1,0:T(8,128)S(1)}, f32[32,128]{1,0:T(8,128)S(1)}) custom-call(s32[3,2,4]{2,1,0:T(2,128)S(1)} %get-tuple-element.38.flip, s32[3,2,4]{2,1,0:T(2,128)S(1)} %get-tuple-element.39.top, s32[3,2,4]{2,1,0:T(2,128)S(1)} %get-tuple-element.40.left, ...), custom_call_target="tpu_custom_call" | custom-call | tf_op jit(solution)/shard_map/update/pallas_call | solution.py:363
  76.9 1.1 %collective-permute-start.15 = (f32[24,256]{1,0:T(8,128)S(1)}, f32[24,256]{1,0:T(8,128)S(1)}, u32[]{:S(2)}, u32[]{:S(2)}) collective-permute-start(f32[24,256]{1,0:T(8,128)S(1)} %get-tuple-element.66), channel_id=1, source_target_pairs={{0,2},{2,0},{4,6},{6,4},{1,3},{3,1},{5,7},{7,5},{8,10},{10,8},{12,... | collective-permute-start | bytes 73736 | tf_op jit(solution)/shard_map/ppermute | solution.py:377
  78.0 2.2 %collective-permute-start.16 = (f32[24,256]{1,0:T(8,128)S(1)}, f32[24,256]{1,0:T(8,128)S(1)}, u32[]{:S(2)}, u32[]{:S(2)}) collective-permute-start(f32[24,256]{1,0:T(8,128)S(1)} %get-tuple-element.67), channel_id=1, source_target_pairs={{2,4},{4,2},{6,0},{0,6},{3,5},{5,3},{7,1},{1,7},{10,12},{12,10},{1... | collective-permute-start | bytes 73736 | tf_op jit(solution)/shard_map/ppermute | solution.py:377
  80.1 0.0 collective-permute-start.17
  80.1 1.2 %collective-permute-done.17.rest_2_ = f32[32,128]{1,0:T(8,128)S(1)} collective-permute-done((f32[32,128]{1,0:T(8,128)S(1)}, f32[32,128]{1,0:T(8,128)S(1)}, u32[]{:S(2)}, u32[]{:S(2)}) %collective-permute-start.17) | collective-permute-done | bytes 16416 | tf_op jit(solution)/shard_map/ppermute | solution.py:378
  81.3 0.0 collective-permute-done.15.rest_0_
  81.3 1.4 %collective-permute-done.16.rest_1_ = f32[24,256]{1,0:T(8,128)S(1)} collective-permute-done((f32[24,256]{1,0:T(8,128)S(1)}, f32[24,256]{1,0:T(8,128)S(1)}, u32[]{:S(2)}, u32[]{:S(2)}) %collective-permute-start.16) | collective-permute-done | bytes 24608 | tf_op jit(solution)/shard_map/ppermute | solution.py:377
  82.7 1.8 %halo_last.1 = f32[1,24,32,256]{3,2,1,0:T(8,128)} custom-call(s32[3,2,4]{2,1,0:T(2,128)S(1)} %get-tuple-element.38.flip, s32[3,2,4]{2,1,0:T(2,128)S(1)} %get-tuple-element.39.top, s32[3,2,4]{2,1,0:T(2,128)S(1)} %get-tuple-element.40.left, f32[1,24,32,256]{3,2,1,0:T(8,128)S(1)} %get-tuple-element.65.bulk, f32[1,32,256]{2,1,0:T(8,128)S(1)} %get-tuple-element.43.sponge, ...), custom_call_target="tpu_custom_call" | custom-call | tf_op jit(solution)/shard_map/halo_last/pallas_call | solution.py:380
  (16 shorter events, 0.0 us)
Async XLA Ops:
  0.0 26.8 %copy-start = (f32[1,24,32,256]{3,2,1,0:T(8,128)S(1)}, f32[1,24,32,256]{3,2,1,0:T(8,128)}, u32[]{:S(2)}) copy-start(f32[1,24,32,256]{3,2,1,0:T(8,128)} %refs_0_.1) | copy-start | bytes 2359300
  0.0 26.8 %copy-start.1 = (f32[1,32,256]{2,1,0:T(8,128)S(1)}, f32[1,32,256]{2,1,0:T(8,128)}, u32[]{:S(2)}) copy-start(f32[1,32,256]{2,1,0:T(8,128)} %refs_1_.1) | copy-start | bytes 98308
  0.0 26.8 %copy-start.10 = (f32[4,3]{1,0:T(4,128)S(1)}, f32[4,3]{1,0:T(4,128)}, u32[]{:S(2)}) copy-start(f32[4,3]{1,0:T(4,128)} %refs_2_.1) | copy-start | bytes 148
  2.7 24.1 %copy-start.9 = (f32[8,128]{1,0:T(8,128)S(1)}, f32[8,128]{1,0:T(8,128)}, u32[]{:S(2)}) copy-start(f32[8,128]{1,0:T(8,128)} %get-tuple-element.37.token) | copy-start | bytes 12292
  2.8 16.8 %collective-permute-start = (f32[24,16,128]{2,1,0:T(8,128)}, f32[24,16,128]{2,1,0:T(8,128)S(1)}, u32[]{:S(2)}, u32[]{:S(2)}) collective-permute-start(f32[24,16,128]{2,1,0:T(8,128)} %get-tuple-element.48), channel_id=1, source_target_pairs={{0,8},{8,0},{2,10},{10,2},{4,12},{12,4},{6,14},{14,6},{1,9},{9,1},... | collective-permute-start | bytes 589832 | tf_op jit(solution)/shard_map/ppermute | solution.py:312
  8.0 27.6 %collective-permute-start.1 = (f32[24,16,128]{2,1,0:T(8,128)}, f32[24,16,128]{2,1,0:T(8,128)S(1)}, u32[]{:S(2)}, u32[]{:S(2)}) collective-permute-start(f32[24,16,128]{2,1,0:T(8,128)} %get-tuple-element.49), channel_id=1, source_target_pairs={{0,10},{10,0},{2,8},{8,2},{4,14},{14,4},{6,12},{12,6},{1,11},{11,1... | collective-permute-start | bytes 589832 | tf_op jit(solution)/shard_map/ppermute | solution.py:312
  11.4 15.4 %copy-start.8 = (s32[3,4,2]{1,2,0:T(2,128)S(1)}, s32[3,4,2]{1,2,0:T(2,128)}, u32[]{:S(2)}) copy-start(s32[3,4,2]{1,2,0:T(2,128)} %param.19) | copy-start | bytes 292
  11.4 24.2 %collective-permute-start.2 = (f32[24,16,128]{2,1,0:T(8,128)}, f32[24,16,128]{2,1,0:T(8,128)S(1)}, u32[]{:S(2)}, u32[]{:S(2)}) collective-permute-start(f32[24,16,128]{2,1,0:T(8,128)} %get-tuple-element.50), channel_id=1, source_target_pairs={{0,16},{16,0},{2,18},{18,2},{4,20},{20,4},{6,22},{22,6},{1,17},{17... | collective-permute-start | bytes 589832 | tf_op jit(solution)/shard_map/ppermute | solution.py:312
  13.4 13.5 %copy-start.7 = (s32[3,4,2]{1,2,0:T(2,128)S(1)}, s32[3,4,2]{1,2,0:T(2,128)}, u32[]{:S(2)}) copy-start(s32[3,4,2]{1,2,0:T(2,128)} %param.18) | copy-start | bytes 292
  13.4 13.5 %copy-start.6 = (s32[3,4,2]{1,2,0:T(2,128)S(1)}, s32[3,4,2]{1,2,0:T(2,128)}, u32[]{:S(2)}) copy-start(s32[3,4,2]{1,2,0:T(2,128)} %param.17) | copy-start | bytes 292
  13.4 22.2 %collective-permute-start.3 = (f32[24,16,128]{2,1,0:T(8,128)}, f32[24,16,128]{2,1,0:T(8,128)S(1)}, u32[]{:S(2)}, u32[]{:S(2)}) collective-permute-start(f32[24,16,128]{2,1,0:T(8,128)} %get-tuple-element.51), channel_id=1, source_target_pairs={{0,18},{18,0},{2,16},{16,2},{4,22},{22,4},{6,20},{20,6},{1,19},{19... | collective-permute-start | bytes 589832 | tf_op jit(solution)/shard_map/ppermute | solution.py:312
  17.6 18.0 %collective-permute-start.4 = (f32[24,16,128]{2,1,0:T(8,128)}, f32[24,16,128]{2,1,0:T(8,128)S(1)}, u32[]{:S(2)}, u32[]{:S(2)}) collective-permute-start(f32[24,16,128]{2,1,0:T(8,128)} %get-tuple-element.52), channel_id=1, source_target_pairs={{0,24},{24,0},{2,26},{26,2},{4,28},{28,4},{6,30},{30,6},{1,25},{25... | collective-permute-start | bytes 589832 | tf_op jit(solution)/shard_map/ppermute | solution.py:312
  19.6 16.1 %collective-permute-start.5 = (f32[24,16,128]{2,1,0:T(8,128)}, f32[24,16,128]{2,1,0:T(8,128)S(1)}, u32[]{:S(2)}, u32[]{:S(2)}) collective-permute-start(f32[24,16,128]{2,1,0:T(8,128)} %get-tuple-element.53), channel_id=1, source_target_pairs={{0,26},{26,0},{2,24},{24,2},{4,30},{30,4},{6,28},{28,6},{1,27},{27... | collective-permute-start | bytes 589832 | tf_op jit(solution)/shard_map/ppermute | solution.py:312
  26.9 0.8 copy-start.2
  27.6 0.8 copy-start.3
  28.4 0.8 copy-start.4
  29.1 0.8 copy-start.5
  38.0 4.6 %collective-permute-start.6 = (f32[24,256]{1,0:T(8,128)S(1)}, f32[24,256]{1,0:T(8,128)S(1)}, u32[]{:S(2)}, u32[]{:S(2)}) collective-permute-start(f32[24,256]{1,0:T(8,128)S(1)} %get-tuple-element.55), channel_id=1, source_target_pairs={{0,2},{2,0},{4,6},{6,4},{1,3},{3,1},{5,7},{7,5},{8,10},{10,8},{12,... | collective-permute-start | bytes 73736 | tf_op jit(solution)/shard_map/ppermute | solution.py:377
  38.4 5.1 %collective-permute-start.7 = (f32[24,256]{1,0:T(8,128)S(1)}, f32[24,256]{1,0:T(8,128)S(1)}, u32[]{:S(2)}, u32[]{:S(2)}) collective-permute-start(f32[24,256]{1,0:T(8,128)S(1)} %get-tuple-element.56), channel_id=1, source_target_pairs={{2,4},{4,2},{6,0},{0,6},{3,5},{5,3},{7,1},{1,7},{10,12},{12,10},{1... | collective-permute-start | bytes 73736 | tf_op jit(solution)/shard_map/ppermute | solution.py:377
  41.4 1.2 %collective-permute-start.8 = (f32[32,128]{1,0:T(8,128)S(1)}, f32[32,128]{1,0:T(8,128)S(1)}, u32[]{:S(2)}, u32[]{:S(2)}) collective-permute-start(f32[32,128]{1,0:T(8,128)S(1)} %get-tuple-element.57), channel_id=1, source_target_pairs={{0,1},{1,0},{2,3},{3,2},{4,5},{5,4},{6,7},{7,6},{8,9},{9,8},{10,11... | collective-permute-start | bytes 49160 | tf_op jit(solution)/shard_map/ppermute | solution.py:378
  44.9 15.4 %collective-permute-start.9 = (f32[24,16,128]{2,1,0:T(8,128)S(1)}, f32[24,16,128]{2,1,0:T(8,128)S(1)}, u32[]{:S(2)}, u32[]{:S(2)}) collective-permute-start(f32[24,16,128]{2,1,0:T(8,128)S(1)} %get-tuple-element.59), channel_id=1, source_target_pairs={{0,8},{8,0},{2,10},{10,2},{4,12},{12,4},{6,14},{14,6},{1,9},{9,1},... | collective-permute-start | bytes 589832 | tf_op jit(solution)/shard_map/ppermute | solution.py:312
  46.9 27.5 %collective-permute-start.10 = (f32[24,16,128]{2,1,0:T(8,128)S(1)}, f32[24,16,128]{2,1,0:T(8,128)S(1)}, u32[]{:S(2)}, u32[]{:S(2)}) collective-permute-start(f32[24,16,128]{2,1,0:T(8,128)S(1)} %get-tuple-element.60), channel_id=1, source_target_pairs={{0,10},{10,0},{2,8},{8,2},{4,14},{14,4},{6,12},{12,6},{1,11},{11,1... | collective-permute-start | bytes 589832 | tf_op jit(solution)/shard_map/ppermute | solution.py:312
  52.0 22.5 %collective-permute-start.11 = (f32[24,16,128]{2,1,0:T(8,128)S(1)}, f32[24,16,128]{2,1,0:T(8,128)S(1)}, u32[]{:S(2)}, u32[]{:S(2)}) collective-permute-start(f32[24,16,128]{2,1,0:T(8,128)S(1)} %get-tuple-element.61), channel_id=1, source_target_pairs={{0,16},{16,0},{2,18},{18,2},{4,20},{20,4},{6,22},{22,6},{1,17},{17... | collective-permute-start | bytes 589832 | tf_op jit(solution)/shard_map/ppermute | solution.py:312
  53.9 20.6 %collective-permute-start.12 = (f32[24,16,128]{2,1,0:T(8,128)S(1)}, f32[24,16,128]{2,1,0:T(8,128)S(1)}, u32[]{:S(2)}, u32[]{:S(2)}) collective-permute-start(f32[24,16,128]{2,1,0:T(8,128)S(1)} %get-tuple-element.62), channel_id=1, source_target_pairs={{0,18},{18,0},{2,16},{16,2},{4,22},{22,4},{6,20},{20,6},{1,19},{19... | collective-permute-start | bytes 589832 | tf_op jit(solution)/shard_map/ppermute | solution.py:312
  58.4 16.1 %collective-permute-start.13 = (f32[24,16,128]{2,1,0:T(8,128)S(1)}, f32[24,16,128]{2,1,0:T(8,128)S(1)}, u32[]{:S(2)}, u32[]{:S(2)}) collective-permute-start(f32[24,16,128]{2,1,0:T(8,128)S(1)} %get-tuple-element.63), channel_id=1, source_target_pairs={{0,24},{24,0},{2,26},{26,2},{4,28},{28,4},{6,30},{30,6},{1,25},{25... | collective-permute-start | bytes 589832 | tf_op jit(solution)/shard_map/ppermute | solution.py:312
  60.4 14.1 %collective-permute-start.14 = (f32[24,16,128]{2,1,0:T(8,128)S(1)}, f32[24,16,128]{2,1,0:T(8,128)S(1)}, u32[]{:S(2)}, u32[]{:S(2)}) collective-permute-start(f32[24,16,128]{2,1,0:T(8,128)S(1)} %get-tuple-element.64), channel_id=1, source_target_pairs={{0,26},{26,0},{2,24},{24,2},{4,30},{30,4},{6,28},{28,6},{1,27},{27... | collective-permute-start | bytes 589832 | tf_op jit(solution)/shard_map/ppermute | solution.py:312
  76.9 4.4 %collective-permute-start.15 = (f32[24,256]{1,0:T(8,128)S(1)}, f32[24,256]{1,0:T(8,128)S(1)}, u32[]{:S(2)}, u32[]{:S(2)}) collective-permute-start(f32[24,256]{1,0:T(8,128)S(1)} %get-tuple-element.66), channel_id=1, source_target_pairs={{0,2},{2,0},{4,6},{6,4},{1,3},{3,1},{5,7},{7,5},{8,10},{10,8},{12,... | collective-permute-start | bytes 73736 | tf_op jit(solution)/shard_map/ppermute | solution.py:377
  78.0 4.7 %collective-permute-start.16 = (f32[24,256]{1,0:T(8,128)S(1)}, f32[24,256]{1,0:T(8,128)S(1)}, u32[]{:S(2)}, u32[]{:S(2)}) collective-permute-start(f32[24,256]{1,0:T(8,128)S(1)} %get-tuple-element.67), channel_id=1, source_target_pairs={{2,4},{4,2},{6,0},{0,6},{3,5},{5,3},{7,1},{1,7},{10,12},{12,10},{1... | collective-permute-start | bytes 73736 | tf_op jit(solution)/shard_map/ppermute | solution.py:377
  80.1 1.2 %collective-permute-start.17 = (f32[32,128]{1,0:T(8,128)S(1)}, f32[32,128]{1,0:T(8,128)S(1)}, u32[]{:S(2)}, u32[]{:S(2)}) collective-permute-start(f32[32,128]{1,0:T(8,128)S(1)} %get-tuple-element.68), channel_id=1, source_target_pairs={{0,1},{1,0},{2,3},{3,2},{4,5},{5,4},{6,7},{7,6},{8,9},{9,8},{10,11... | collective-permute-start | bytes 49160 | tf_op jit(solution)/shard_map/ppermute | solution.py:378

commit v5 on v4

--- a/solution.py
+++ b/solution.py
@@ -32,11 +32,16 @@
     return [blocks[ORDER.index((slot, kind))] for kind in range(2) for slot in range(SLOTS)]
 
 
-def pieces(flip, top, left):
+def pieces_of(flip, top, left):
     _, i, j = place()
     for slot in range(SLOTS):
         for kind, row in ((0, i), (1, jnp.bitwise_xor(i, 1))):
             yield slot, kind, flip[slot, j, row] == kind, top[slot, j, row], left[slot, j, row]
+
+
+def pieces(plan):
+    for k in range(2 * SLOTS):
+        yield k // 2, k % 2, plan[3 * k] == 1, plan[3 * k + 1], plan[3 * k + 2]
 
 
 def widen(half, cells):
@@ -99,44 +104,57 @@
             total[c : c + CHUNK, rows, half_c:] += jnp.where(right_part, 0.0, turned)
 
 
-def payload(flip, top, left, state, sponge, straight, crossed, rows, fine):
+def fold(state, sponge, rows, fine):
     comps, cells_r, cells_c = state.shape
     half_r, half_c = cells_r // 2, cells_c // 2
-    grid, _, _ = place()
-
-    @pl.when(grid == 0)
-    def _():
-        for slot, kind, serves, first, begin in pieces(flip, top, left):
-
-            @pl.when(serves)
-            def _():
-                crop(state, (straight, crossed)[kind][slot], first, begin)
-
-    @pl.when(grid > 0)
-    def _():
-        weight = sponge[0]
-
-        def fold(c, carry):
-            block = weight * state[c]
-            for k in range(cells_c // LANES):
-                part = slice(k * LANES, (k + 1) * LANES)
-                fine[k] = block[:, part]
-                rows[c, :, part] = fine[k, pl.ds(0, half_r, 2), :] + fine[k, pl.ds(1, half_r, 2), :]
-            return carry
-
-        lax.fori_loop(0, comps, fold, 0)
-        block = jnp.dot(
-            rows[...].reshape(comps * half_r, cells_c),
-            narrow(cells_c, half_c),
-            precision=lax.Precision.HIGHEST,
-            preferred_element_type=jnp.float32,
-        ).reshape(comps, half_r, half_c)
-        for slot in range(SLOTS):
-
-            @pl.when(grid == slot + 1)
-            def _():
-                straight[slot][...] = block
-                crossed[slot][...] = block
+    weight = sponge[0]
+
+    def one(c, carry):
+        block = weight * state[c]
+        for k in range(cells_c // LANES):
+            part = slice(k * LANES, (k + 1) * LANES)
+            fine[k] = block[:, part]
+            rows[c, :, part] = fine[k, pl.ds(0, half_r, 2), :] + fine[k, pl.ds(1, half_r, 2), :]
+        return carry
+
+    lax.fori_loop(0, comps, one, 0, unroll=4)
+    return jnp.dot(
+        rows[...].reshape(comps * half_r, cells_c),
+        narrow(cells_c, half_c),
+        precision=lax.Precision.HIGHEST,
+        preferred_element_type=jnp.float32,
+    ).reshape(comps, half_r, half_c)
+
+
+def pack_fold(out, comps, above, below, low, high, sponge, fine):
+    weight = sponge[0]
+    cells_r, cells_c = weight.shape
+    half_r, half_c = cells_r // 2, cells_c // 2
+    lines = jnp.concatenate([weight[:1] * above, weight[cells_r - 1 :] * below], axis=0)
+    out[: 2 * comps, :] = jnp.dot(
+        lines, narrow(cells_c, half_c), precision=lax.Precision.HIGHEST, preferred_element_type=jnp.float32
+    )
+    for k, line in enumerate((weight[:, :1] * low, weight[:, cells_c - 1 :] * high)):
+        fine[k] = line
+        out[2 * comps + k * half_r : 2 * comps + (k + 1) * half_r, :] = (
+            fine[k, pl.ds(0, half_r, 2), :] + fine[k, pl.ds(1, half_r, 2), :]
+        )
+
+
+def patch(block, extra, outs):
+    comps, half_r, half_c = block.shape
+    row = lax.broadcasted_iota(jnp.int32, (half_r, half_c), 0)
+    lane = lax.broadcasted_iota(jnp.int32, (half_r, half_c), 1)
+    low = extra[2 * comps : 2 * comps + half_r, :]
+    high = extra[2 * comps + half_r : 2 * comps + 2 * half_r, :]
+    for c in range(comps):
+        total = block[c]
+        total = total + jnp.where(row == 0, extra[c : c + 1, :], 0.0)
+        total = total + jnp.where(row == half_r - 1, extra[comps + c : comps + c + 1, :], 0.0)
+        total = total + jnp.where(lane == 0, pltpu.roll(low, (half_c - c) % half_c, 1), 0.0)
+        total = total + jnp.where(lane == half_c - 1, pltpu.roll(high, half_c - 1 - c, 1), 0.0)
+        for out in outs:
+            out[c] = total
 
 
 def first_kernel(*refs):
@@ -149,16 +167,47 @@
     for copy in copies:
         copy.wait()
     flip, top, left, state, sponge = held
-    payload(flip, top, left, state.at[0], sponge, outs[:SLOTS], outs[SLOTS:], rows, fine)
+    state = state.at[0]
+    grid, _, _ = place()
+
+    @pl.when(grid == 0)
+    def _():
+        for slot, kind, serves, first, begin in pieces_of(flip, top, left):
+
+            @pl.when(serves)
+            def _():
+                crop(state, outs[kind * SLOTS + slot], first, begin)
+
+    @pl.when(grid > 0)
+    def _():
+        block = fold(state, sponge, rows, fine)
+        for slot in range(SLOTS):
+
+            @pl.when(grid == slot + 1)
+            def _():
+                outs[slot][...] = block
+                outs[SLOTS + slot][...] = block
 
 
 def stage_kernel(token, *refs):
-    given, held, done = refs[:10], refs[10:20], refs[20]
-    copies = [pltpu.make_async_copy(source, to, done.at[k]) for k, (source, to) in enumerate(zip(given, held))]
+    given, held, (rates, plan), scratch = refs[:10], list(refs[10:16]), refs[16:18], refs[18:]
+    speeds, *tables, done = scratch
+    copies = [
+        pltpu.make_async_copy(source, to, done.at[k])
+        for k, (source, to) in enumerate(zip(given, held + [speeds] + tables))
+    ]
     for copy in copies:
         copy.start()
     for copy in copies:
         copy.wait()
+    grid, i, j = place()
+    for cls in range(NCLS):
+        rates[cls] = jnp.full(rates.shape[1:], speeds[grid, cls], jnp.float32)
+    for k, (_, _, serves, first, begin) in enumerate(pieces_of(*tables)):
+        plan[3 * k] = serves.astype(jnp.int32)
+        plan[3 * k + 1] = first
+        plan[3 * k + 2] = begin
+    plan[6 * SLOTS] = tables[0][jnp.maximum(grid - 1, 0), j, i]
 
 
 def edge_sides(index):
@@ -166,13 +215,11 @@
     return even, jnp.logical_not(even)
 
 
-def update_kernel(n_cols, flip, top, left, rates, state, sponge, agg, brk, mask, diff, *rest):
-    got = sorted_out(rest[: 2 * SLOTS])
-    n_side = 2 + n_cols
-    bulk, sides = rest[2 * SLOTS], rest[2 * SLOTS + 1 : 2 * SLOTS + 1 + n_side]
-    bulk = bulk.at[0] if len(bulk.shape) == 4 else bulk
-    nested, wide, coarse, fine = rest[2 * SLOTS + 1 + n_side :]
-    comps, cells_r, cells_c = bulk.shape
+def update_kernel(n_cols, plan, rates, state, sponge, agg, brk, mask, diff, *rest):
+    got, rest = sorted_out(rest[: 2 * SLOTS]), rest[2 * SLOTS :]
+    wets, flux, sides = rest[0], rest[1], rest[2 : 4 + n_cols]
+    nested, wide, coarse, fine = rest[4 + n_cols :]
+    comps, cells_r, cells_c = wets.shape
     half_r, half_c = cells_r // 2, cells_c // 2
     grid, i, j = place()
     row_id = lax.broadcasted_iota(jnp.int32, (cells_r, cells_c), 0)
@@ -181,7 +228,7 @@
     @pl.when(grid == 0)
     def _():
         covered = jnp.zeros((cells_r, cells_c), jnp.float32)
-        for _, _, serves, first, begin in pieces(flip, top, left):
+        for _, _, serves, first, begin in pieces(plan):
             inside = (row_id >= first) & (row_id < first + half_r) & (col_id >= begin) & (col_id < begin + half_c)
             covered = covered + jnp.where(inside & serves, 1.0, 0.0)
         keep = 1.0 - relaxation * covered
@@ -192,7 +239,7 @@
             return carry
 
         lax.fori_loop(0, comps // CHUNK, own, 0)
-        for slot, kind, serves, first, begin in pieces(flip, top, left):
+        for slot, kind, serves, first, begin in pieces(plan):
 
             @pl.when(serves)
             def _():
@@ -203,7 +250,7 @@
         for slot in range(SLOTS):
             for kind in range(2):
 
-                @pl.when((grid == slot + 1) & (flip[slot, j, i] == kind))
+                @pl.when((grid == slot + 1) & (plan[6 * SLOTS] == kind))
                 def _():
                     coarse[...] = got[kind * SLOTS + slot][...]
 
@@ -224,12 +271,12 @@
                 nested[c, :, part] = keep[:, part] * state[c, :, part] + fine[k]
             return carry
 
-        lax.fori_loop(0, comps, own, 0)
+        lax.fori_loop(0, comps, own, 0, unroll=4)
 
     a, b = agg[0], brk[0]
     wet = mask[0].astype(jnp.float32)
     spread = diff[0]
-    row_far = edge_sides(i)
+    row_far = edge_sides(i)[::-1]
     col_far = edge_sides(j)
     lane = lax.broadcasted_iota(jnp.int32, (cells_r, LANES), 1)
 
@@ -241,15 +288,11 @@
         columns = list(columns)
         for cls in range(NCLS):
             c = cls * LEV + l
-            rate = rates[grid, cls]
+            rate = rates[cls]
             w = wet * ((1.0 - rate) * flocced[cls] + rate * below[cls])
             f = spread * w
-            total = w - 4.0 * f
-            total = total + jnp.where(row_id == 0, 0.0, pltpu.roll(f, 1, 0))
-            total = total + jnp.where(row_id == cells_r - 1, 0.0, pltpu.roll(f, cells_r - 1, 0))
-            total = total + jnp.where(col_id == 0, 0.0, pltpu.roll(f, 1, 1))
-            total = total + jnp.where(col_id == cells_c - 1, 0.0, pltpu.roll(f, cells_c - 1, 1))
-            bulk[c] = total
+            wets[c] = w
+            flux[c] = f
             for phase in range(2):
                 sides[phase][pl.ds(c, 1), :] = jnp.where(row_far[phase], f[cells_r - 1 :], f[:1])
             for phase in range(n_cols):
@@ -261,44 +304,93 @@
 
     nothing = jnp.zeros((cells_r, cells_c), jnp.float32)
     empty = jnp.zeros((cells_r, LANES), jnp.float32)
-    _, columns = lax.fori_loop(0, LEV, level, ((nothing,) * NCLS, (empty,) * n_cols))
+    _, columns = lax.fori_loop(0, LEV, level, ((nothing,) * NCLS, (empty,) * n_cols), unroll=True)
     for phase in range(n_cols):
         sides[2 + phase][...] = columns[phase]
 
 
-def halo_kernel(n_cols, sizes, last, flip, top, left, bulk, sponge, *rest):
-    sides = rest[: 2 + n_cols]
-    state = rest[2 + n_cols]
+def spread_kernel(last, wets, flux, *rest):
+    bulk = rest[0].at[0] if last else rest[1]
+    comps, cells_r, cells_c = bulk.shape
+    grid, _, _ = place()
+    row_id = lax.broadcasted_iota(jnp.int32, (cells_r, cells_c), 0)
+    col_id = lax.broadcasted_iota(jnp.int32, (cells_r, cells_c), 1)
+
+    def one(c, carry):
+        f = flux[c]
+        total = wets[c] - 4.0 * f
+        total = total + jnp.where(row_id == 0, 0.0, pltpu.roll(f, 1, 0))
+        total = total + jnp.where(row_id == cells_r - 1, 0.0, pltpu.roll(f, cells_r - 1, 0))
+        total = total + jnp.where(col_id == 0, 0.0, pltpu.roll(f, 1, 1))
+        total = total + jnp.where(col_id == cells_c - 1, 0.0, pltpu.roll(f, cells_c - 1, 1))
+        bulk[c] = total
+        return carry
+
+    lax.fori_loop(0, comps, one, 0, unroll=2)
+    if not last:
+        sponge, _, folded, rows, fine = rest
+
+        @pl.when(grid > 0)
+        def _():
+            folded[...] = fold(bulk, sponge, rows, fine)
+
+
+def halo_kernel(n_cols, sizes, last, *rest):
+    plan, rest = (None, rest) if last else (rest[0], rest[1:])
+    bulk, rest = rest[0], rest[1:]
+    given, rest = ((), rest) if last else (rest[:2], rest[2:])
+    sides, state, rest = rest[: 2 + n_cols], rest[2 + n_cols], rest[3 + n_cols :]
     old, new = (bulk.at[0], state.at[0]) if last else (bulk, state)
     comps, cells_r, cells_c = new.shape
-    _, i, j = place()
+    grid, i, j = place()
     row = lax.broadcasted_iota(jnp.int32, (8, cells_c), 0)
     even, _ = edge_sides(i)
-    first, second = sides[0][...], sides[1][...]
+    second, first = sides[0][...], sides[1][...]
     above = jnp.where(i == 0, 0.0, jnp.where(even, second, first))
     below = jnp.where(i == sizes[0] - 1, 0.0, jnp.where(even, first, second))
+    low = high = jnp.zeros((cells_r, LANES), jnp.float32)
+    for phase, far in zip(range(n_cols), edge_sides(j)):
+        column = sides[2 + phase][...]
+        low = low + jnp.where(jnp.logical_not(far) & (j > 0), column, 0.0)
+        high = high + jnp.where(far & (j < sizes[1] - 1), column, 0.0)
     for c in range(comps):
         new[c, :8, :] = old[c, :8, :] + jnp.where(row == 0, above[c : c + 1], 0.0)
         new[c, 8 : cells_r - 8, :] = old[c, 8 : cells_r - 8, :]
         new[c, cells_r - 8 :, :] = old[c, cells_r - 8 :, :] + jnp.where(row == 7, below[c : c + 1], 0.0)
     lane = lax.broadcasted_iota(jnp.int32, (cells_r, LANES), 1)
-    for phase, far in zip(range(n_cols), edge_sides(j)):
-        column = sides[2 + phase][...]
-
-        @pl.when(far & (j < sizes[1] - 1))
+
+    @pl.when(j < sizes[1] - 1)
+    def _():
+        for c in range(comps):
+            new[c, :, cells_c - LANES :] += jnp.where(lane == LANES - 1, pltpu.roll(high, LANES - 1 - c, 1), 0.0)
+
+    @pl.when(j > 0)
+    def _():
+        for c in range(comps):
+            new[c, :, :LANES] += jnp.where(lane == 0, pltpu.roll(low, (LANES - c) % LANES, 1), 0.0)
+
+    if last:
+        return
+    sponge, folded = given
+    outs, (packed, fine) = rest[: 2 * SLOTS], rest[2 * SLOTS :]
+
+    @pl.when(grid == 0)
+    def _():
+        for slot, kind, serves, start, begin in pieces(plan):
+
+            @pl.when(serves)
+            def _():
+                crop(new, outs[ORDER.index((slot, kind))], start, begin)
+
+    @pl.when(grid > 0)
+    def _():
+        pack_fold(packed, comps, above, below, low, high, sponge, fine)
+
+    for slot in range(SLOTS):
+
+        @pl.when(grid == slot + 1)
         def _():
-            for c in range(comps):
-                new[c, :, cells_c - LANES :] += jnp.where(lane == LANES - 1, pltpu.roll(column, LANES - 1 - c, 1), 0.0)
-
-        @pl.when(jnp.logical_not(far) & (j > 0))
-        def _():
-            for c in range(comps):
-                new[c, :, :LANES] += jnp.where(lane == 0, pltpu.roll(column, (LANES - c) % LANES, 1), 0.0)
-
-    if not last:
-        outs, (rows, fine) = rest[3 + n_cols : -2], rest[-2:]
-        outs = sorted_out(outs)
-        payload(flip, top, left, new, sponge, outs[:SLOTS], outs[SLOTS:], rows, fine)
+            patch(folded, packed, [outs[ORDER.index((slot, kind))] for kind in range(2)])
 
 
 def exchange(blocks):
@@ -344,27 +436,30 @@
         compiler_params=pltpu.CompilerParams(vmem_limit_bytes=60 * 2**20),
         name="first_payload",
     )(*tables, adjoint, sponge)
-    fields = (adjoint, sponge, settling, aggregation, breakup, sea_mask, diffusivity, *tables)
-    state, sponge, rates, *fields = pl.pallas_call(
+    fields = (adjoint, sponge, aggregation, breakup, sea_mask, diffusivity)
+    state, sponge, *fields, rates, plan = pl.pallas_call(
         stage_kernel,
-        out_shape=[jax.ShapeDtypeStruct(field.shape, field.dtype) for field in fields],
+        out_shape=[jax.ShapeDtypeStruct(field.shape, field.dtype) for field in fields]
+        + [jax.ShapeDtypeStruct((NCLS, 1, cells_c), f32), jax.ShapeDtypeStruct((6 * SLOTS + 1,), jnp.int32)],
         in_specs=[VM] + [pl.BlockSpec(memory_space=pltpu.HBM)] * 10,
-        out_specs=[VM] * 10,
-        scratch_shapes=[pltpu.SemaphoreType.DMA((10,))],
+        out_specs=[VM] * 7 + [SM],
+        scratch_shapes=[pltpu.SMEM(settling.shape, f32)]
+        + [pltpu.SMEM(table.shape, table.dtype) for table in tables]
+        + [pltpu.SemaphoreType.DMA((10,))],
         compiler_params=PARAMS,
         name="stage_fields",
-    )(token, *fields)
+    )(token, *fields, settling, *tables)
     state = state.reshape(tile.shape)
-    fields, tables = fields[:4], fields[4:]
+    fold_scratch = [pltpu.VMEM((comps, half_r, cells_c), f32), pltpu.VMEM((cells_c // LANES, cells_r, LANES), f32)]
     for step in range(STEPS):
-        got = exchange(blocks)
         last = step == STEPS - 1
         new = jax.ShapeDtypeStruct(adjoint.shape, f32) if last else tile
-        bulk, *sides = pl.pallas_call(
+        got = exchange(blocks)
+        wets, flux, *sides = pl.pallas_call(
             functools.partial(update_kernel, n_cols),
-            out_shape=[new] + side,
-            in_specs=[SM] * 4 + [VM] * (6 + 2 * SLOTS),
-            out_specs=[VM] * (1 + len(side)),
+            out_shape=[tile] * 2 + side,
+            in_specs=[SM] + [VM] * (7 + 2 * SLOTS),
+            out_specs=[VM] * (2 + len(side)),
             scratch_shapes=[
                 pltpu.VMEM(tile.shape, f32),
                 pltpu.VMEM((comps, half_r, cells_c), f32),
@@ -373,20 +468,28 @@
             ],
             compiler_params=PARAMS,
             name="update",
-        )(*tables, rates, state, sponge, *fields, *got)
-        sides = [lax.ppermute(sides[k], "gx", swap_pairs(n_x, k)) for k in range(2)] + [
+        )(plan, rates, state, sponge, *fields, *got)
+        sides = [lax.ppermute(sides[k], "gx", swap_pairs(n_x, 1 - k)) for k in range(2)] + [
             lax.ppermute(sides[2 + k], "gy", swap_pairs(n_y, k)) for k in range(n_cols)
         ]
-        out = pl.pallas_call(
+        bulk, *folded = pl.pallas_call(
+            functools.partial(spread_kernel, last),
+            out_shape=[new] + ([] if last else [block]),
+            in_specs=[VM] * (2 if last else 3),
+            out_specs=[VM] * (1 if last else 2),
+            scratch_shapes=[] if last else fold_scratch,
+            compiler_params=PARAMS,
+            name="spread_last" if last else "spread",
+        )(wets, flux, *([] if last else [sponge]))
+        state, *blocks = pl.pallas_call(
             functools.partial(halo_kernel, n_cols, (n_x, n_y), last),
             out_shape=[new] + ([] if last else [block] * (2 * SLOTS)),
-            in_specs=[SM] * 3 + [VM] * (2 + len(side)),
+            in_specs=[SM] * (0 if last else 1) + [VM] * (1 + len(side) + (0 if last else 2)),
             out_specs=[VM] * (1 if last else 1 + 2 * SLOTS),
-            scratch_shapes=[] if last else fold_scratch,
+            scratch_shapes=[] if last else [pltpu.VMEM((2 * comps + 2 * half_r, half_c), f32), fold_scratch[1]],
             compiler_params=PARAMS,
             name="halo_last" if last else "halo",
-        )(*tables, bulk, sponge, *sides)
-        state, blocks = out[0], out[1:]
+        )(*([] if last else [plan]), bulk, *([] if last else [sponge, *folded]), *sides)
     return state
 
 

time: 85.5 us -> 81.8 us (0.957)
  waiting for transfers between devices: 17.1 us -> 13.7 us
  starting transfers between devices: 52.9 us -> 51.8 us
  Pallas kernels: 11.1 us -> 12.1 us
    ppermute x2, waiting for transfers between devices: 2.36 us -> 0.01 us  [local(): lax.ppermute(sides[2 + k], 'gy', swap_pairs(n_y, k))]
    ppermute x4, starting transfers between devices: 6.66 us -> 5.08 us  [local(): lax.ppermute(sides[k], 'gx', swap_pairs(n_x, 1 - k))]
    ppermute x12, waiting for transfers between devices: 12.5 us -> 11 us  [exchange(): got.append(lax.ppermute(block, ('grid', 'gx'), pairs))]
    pallas_call x1, Pallas kernels: 0.39 us -> 1.7 us  [local(): pl.pallas_call(stage_kernel, out_shape=[jax.ShapeDtypeStruct(field.shape,...]
    pallas_call x2 -> x4, Pallas kernels: 4.73 us -> 5.31 us  [the longest x2 2.82 us: local(): pl.pallas_call(functools.partial(update_kernel, n_cols), out_shape=[tile]...]
  transfers between devices with their start and end apart: 18 -> 18, of which waited for: 6 -> 5; matrix products, arithmetic and copies ran while one was open for 0% -> 0% of each run, Pallas kernels for 0% -> 5%
where the time goes in v5:
time: 81.8 us; the launch traced here: 81 us
  starting transfers between devices  51.8 us (63%)
  waiting for transfers between devices  13.7 us (17%)
  Pallas kernels  12.1 us (15%)
  local copies, waits for them, and re-layouts  3.06 us (4%)
    ppermute x12, starting transfers between devices, exchange(): got.append(lax.ppermute(block, ('grid', 'gx'), pairs))  46.7 us
    ppermute x12, waiting for transfers between devices, exchange(): got.append(lax.ppermute(block, ('grid', 'gx'), pairs))  11 us
    ppermute x4, starting transfers between devices, local(): lax.ppermute(sides[k], 'gx', swap_pairs(n_x, 1 - k))  5.08 us
    unnamed x22, local copies, waits for them, and re-layouts  3.06 us
    pallas_call x2, Pallas kernels, local(): pl.pallas_call(functools.partial(update_kernel, n_cols), out_shape=[tile]...  2.82 us
    pallas_call x1, Pallas kernels, local(): pl.pallas_call(first_kernel, out_shape=[block] * (2 * SLOTS) + [jax.Shape...  2.73 us
    ppermute x4, waiting for transfers between devices, local(): lax.ppermute(sides[k], 'gx', swap_pairs(n_x, 1 - k))  2.65 us
    pallas_call x2, Pallas kernels, local(): pl.pallas_call(functools.partial(spread_kernel, last), out_shape=[new] +...  2.49 us
  transfers between devices with their start and end apart: 18, of which 5 were waited for; matrix products, arithmetic and copies ran while one was open for 0% of the time, Pallas kernels for 5%

profile of v5, /device:TPU:0, one launch (start us, length us, event | category | flops | bytes accessed | tf_op | source)
XLA Modules:
  0.0 81.0 jit_solution(14558742528860082708)
XLA Ops:
  0.0 2.7 %first_payload.1 = (f32[24,16,128]{2,1,0:T(8,128)}, f32[24,16,128]{2,1,0:T(8,128)}, f32[24,16,128]{2,1,0:T(8,128)}, f32[24,16,128]{2,1,0:T(8,128)}, f32[24,16,12...) custom-call(s32[3,2,4]{2,1,0:T(2,128)} %bitcast.5, s32[3,2,4]{2,1,0:T(2,128)} %bitcast.7, ...), custom_call_target="tpu_custom_call" | custom-call | tf_op jit(solution)/shard_map/first_payload/pallas_call | solution.py:428
  2.8 5.1 %collective-permute-start = (f32[24,16,128]{2,1,0:T(8,128)}, f32[24,16,128]{2,1,0:T(8,128)S(1)}, u32[]{:S(2)}, u32[]{:S(2)}) collective-permute-start(f32[24,16,128]{2,1,0:T(8,128)} %get-tuple-element.48), channel_id=1, source_target_pairs={{0,8},{8,0},{2,10},{10,2},{4,12},{12,4},{6,14},{14,6},{1,9},{9,1},... | collective-permute-start | bytes 589832 | tf_op jit(solution)/shard_map/ppermute | solution.py:404
  7.9 3.5 %collective-permute-start.1 = (f32[24,16,128]{2,1,0:T(8,128)}, f32[24,16,128]{2,1,0:T(8,128)S(1)}, u32[]{:S(2)}, u32[]{:S(2)}) collective-permute-start(f32[24,16,128]{2,1,0:T(8,128)} %get-tuple-element.49), channel_id=1, source_target_pairs={{0,10},{10,0},{2,8},{8,2},{4,14},{14,4},{6,12},{12,6},{1,11},{11,1... | collective-permute-start | bytes 589832 | tf_op jit(solution)/shard_map/ppermute | solution.py:404
  11.4 0.0 copy-start.8
  11.4 1.9 %collective-permute-start.2 = (f32[24,16,128]{2,1,0:T(8,128)}, f32[24,16,128]{2,1,0:T(8,128)S(1)}, u32[]{:S(2)}, u32[]{:S(2)}) collective-permute-start(f32[24,16,128]{2,1,0:T(8,128)} %get-tuple-element.50), channel_id=1, source_target_pairs={{0,16},{16,0},{2,18},{18,2},{4,20},{20,4},{6,22},{22,6},{1,17},{17... | collective-permute-start | bytes 589832 | tf_op jit(solution)/shard_map/ppermute | solution.py:404
  13.4 0.0 copy-start.7
  13.4 0.0 copy-start.6
  13.4 4.1 %collective-permute-start.3 = (f32[24,16,128]{2,1,0:T(8,128)}, f32[24,16,128]{2,1,0:T(8,128)S(1)}, u32[]{:S(2)}, u32[]{:S(2)}) collective-permute-start(f32[24,16,128]{2,1,0:T(8,128)} %get-tuple-element.51), channel_id=1, source_target_pairs={{0,18},{18,0},{2,16},{16,2},{4,22},{22,4},{6,20},{20,6},{1,19},{19... | collective-permute-start | bytes 589832 | tf_op jit(solution)/shard_map/ppermute | solution.py:404
  17.5 1.9 %collective-permute-start.4 = (f32[24,16,128]{2,1,0:T(8,128)}, f32[24,16,128]{2,1,0:T(8,128)S(1)}, u32[]{:S(2)}, u32[]{:S(2)}) collective-permute-start(f32[24,16,128]{2,1,0:T(8,128)} %get-tuple-element.52), channel_id=1, source_target_pairs={{0,24},{24,0},{2,26},{26,2},{4,28},{28,4},{6,30},{30,6},{1,25},{25... | collective-permute-start | bytes 589832 | tf_op jit(solution)/shard_map/ppermute | solution.py:404
  19.5 0.0 collective-permute-done.rest_0_
  19.5 7.3 %collective-permute-start.5 = (f32[24,16,128]{2,1,0:T(8,128)}, f32[24,16,128]{2,1,0:T(8,128)S(1)}, u32[]{:S(2)}, u32[]{:S(2)}) collective-permute-start(f32[24,16,128]{2,1,0:T(8,128)} %get-tuple-element.53), channel_id=1, source_target_pairs={{0,26},{26,0},{2,24},{24,2},{4,30},{30,4},{6,28},{28,6},{1,27},{27... | collective-permute-start | bytes 589832 | tf_op jit(solution)/shard_map/ppermute | solution.py:404
  26.9 0.0 copy-start.2
  26.9 0.7 copy-done.2
  27.6 0.8 copy-done.3
  28.4 0.8 copy-done.4
  29.1 0.8 copy-done.5
  29.9 1.7 %stage_fields.1 = (f32[1,24,32,256]{3,2,1,0:T(8,128)S(1)}, f32[1,32,256]{2,1,0:T(8,128)S(1)}, f32[1,32,256]{2,1,0:T(8,128)S(1)}, f32[1,32,256]{2,1,0:T(8,128)S(1...) custom-call(f32[8,128]{1,0:T(8,128)S(1)} %copy-done.9, ...), custom_call_target="tpu_custom_call" | custom-call | tf_op jit(solution)/shard_map/stage_fields/pallas_call | solution.py:440
  31.6 3.6 %collective-permute-done.1.rest_1_ = f32[24,16,128]{2,1,0:T(8,128)S(1)} collective-permute-done((f32[24,16,128]{2,1,0:T(8,128)}, f32[24,16,128]{2,1,0:T(8,128)S(1)}, u32[]{:S(2)}, u32[]{:S(2)}) %collective-permute-start.1) | collective-permute-done | bytes 196640 | tf_op jit(solution)/shard_map/ppermute | solution.py:404
  35.2 0.0 collective-permute-done.2.rest_2_
  35.2 0.0 collective-permute-done.3.rest_3_
  35.2 0.0 collective-permute-done.4.rest_4_
  35.2 0.0 collective-permute-done.5.rest_5_
  35.2 1.4 %update.2 = (f32[24,32,256]{2,1,0:T(8,128)S(1)}, f32[24,32,256]{2,1,0:T(8,128)S(1)}, f32[24,256]{1,0:T(8,128)S(1)}, f32[24,256]{1,0:T(8,128)S(1)}, f32[32,128]{1,0:T(8,128)S(1)}) custom-call(s32[19]{0:T(128)S(1)} %get-tuple-element.40.plan.rest_0_, f32[3,1,256]{2,1,0:T(1,128)S(1)} %get-tuple-element.41.rates, f32[24,32,256]{2,1,0:T(8,128)S(1)} %bitcast.4, ...), custom_call_target="tpu_custom_call" | custom-call | tf_op jit(solution)/shard_map/update/pallas_call | solution.py:458
  36.6 1.6 %collective-permute-start.6 = (f32[24,256]{1,0:T(8,128)S(1)}, f32[24,256]{1,0:T(8,128)S(1)}, u32[]{:S(2)}, u32[]{:S(2)}) collective-permute-start(f32[24,256]{1,0:T(8,128)S(1)} %get-tuple-element.58), channel_id=1, source_target_pairs={{2,4},{4,2},{6,0},{0,6},{3,5},{5,3},{7,1},{1,7},{10,12},{12,10},{1... | collective-permute-start | bytes 73736 | tf_op jit(solution)/shard_map/ppermute | solution.py:472
  38.2 1.8 %collective-permute-start.7 = (f32[24,256]{1,0:T(8,128)S(1)}, f32[24,256]{1,0:T(8,128)S(1)}, u32[]{:S(2)}, u32[]{:S(2)}) collective-permute-start(f32[24,256]{1,0:T(8,128)S(1)} %get-tuple-element.59), channel_id=1, source_target_pairs={{0,2},{2,0},{4,6},{6,4},{1,3},{3,1},{5,7},{7,5},{8,10},{10,8},{12,... | collective-permute-start | bytes 73736 | tf_op jit(solution)/shard_map/ppermute | solution.py:472
  40.0 0.0 collective-permute-start.8
  40.0 1.2 %spread.1 = (f32[24,32,256]{2,1,0:T(8,128)S(1)}, f32[24,16,128]{2,1,0:T(8,128)S(1)}) custom-call(f32[24,32,256]{2,1,0:T(8,128)S(1)} %get-tuple-element.54.wets, f32[24,32,256]{2,1,0:T(8,128)S(1)} %get-tuple-element.55.flux, f32[1,32,256]{2,1,0:T(8,128)S(1)} %get-tuple-element.43.sponge.rest_0_.rest_2_), custom_call_target="tpu_custom_call" | custom-call | tf_op jit(solution)/shard_map/spread/pallas_call | solution.py:475
  41.3 0.0 collective-permute-done.8.rest_6_
  41.3 0.1 collective-permute-done.6.rest_4_
  41.4 0.7 collective-permute-done.7.rest_5_
  42.1 1.3 %halo.1 = (f32[24,32,256]{2,1,0:T(8,128)S(1)}, f32[24,16,128]{2,1,0:T(8,128)S(1)}, f32[24,16,128]{2,1,0:T(8,128)S(1)}, f32[24,16,128]{2,1,0:T(8,128)S(1)}, f32[2...) custom-call(s32[19]{0:T(128)S(1)} %get-tuple-element.40.plan.rest_0_, ...), custom_call_target="tpu_custom_call" | custom-call | tf_op jit(solution)/shard_map/halo/pallas_call | solution.py:484
  43.3 1.9 %collective-permute-start.9 = (f32[24,16,128]{2,1,0:T(8,128)S(1)}, f32[24,16,128]{2,1,0:T(8,128)S(1)}, u32[]{:S(2)}, u32[]{:S(2)}) collective-permute-start(f32[24,16,128]{2,1,0:T(8,128)S(1)} %get-tuple-element.62), channel_id=1, source_target_pairs={{0,8},{8,0},{2,10},{10,2},{4,12},{12,4},{6,14},{14,6},{1,9},{9,1},... | collective-permute-start | bytes 589832 | tf_op jit(solution)/shard_map/ppermute | solution.py:404
  45.3 5.6 %collective-permute-start.10 = (f32[24,16,128]{2,1,0:T(8,128)S(1)}, f32[24,16,128]{2,1,0:T(8,128)S(1)}, u32[]{:S(2)}, u32[]{:S(2)}) collective-permute-start(f32[24,16,128]{2,1,0:T(8,128)S(1)} %get-tuple-element.63), channel_id=1, source_target_pairs={{0,10},{10,0},{2,8},{8,2},{4,14},{14,4},{6,12},{12,6},{1,11},{11,1... | collective-permute-start | bytes 589832 | tf_op jit(solution)/shard_map/ppermute | solution.py:404
  50.8 1.9 %collective-permute-start.11 = (f32[24,16,128]{2,1,0:T(8,128)S(1)}, f32[24,16,128]{2,1,0:T(8,128)S(1)}, u32[]{:S(2)}, u32[]{:S(2)}) collective-permute-start(f32[24,16,128]{2,1,0:T(8,128)S(1)} %get-tuple-element.64), channel_id=1, source_target_pairs={{0,16},{16,0},{2,18},{18,2},{4,20},{20,4},{6,22},{22,6},{1,17},{17... | collective-permute-start | bytes 589832 | tf_op jit(solution)/shard_map/ppermute | solution.py:404
  52.8 4.1 %collective-permute-start.12 = (f32[24,16,128]{2,1,0:T(8,128)S(1)}, f32[24,16,128]{2,1,0:T(8,128)S(1)}, u32[]{:S(2)}, u32[]{:S(2)}) collective-permute-start(f32[24,16,128]{2,1,0:T(8,128)S(1)} %get-tuple-element.65), channel_id=1, source_target_pairs={{0,18},{18,0},{2,16},{16,2},{4,22},{22,4},{6,20},{20,6},{1,19},{19... | collective-permute-start | bytes 589832 | tf_op jit(solution)/shard_map/ppermute | solution.py:404
  56.9 1.9 %collective-permute-start.13 = (f32[24,16,128]{2,1,0:T(8,128)S(1)}, f32[24,16,128]{2,1,0:T(8,128)S(1)}, u32[]{:S(2)}, u32[]{:S(2)}) collective-permute-start(f32[24,16,128]{2,1,0:T(8,128)S(1)} %get-tuple-element.66), channel_id=1, source_target_pairs={{0,24},{24,0},{2,26},{26,2},{4,28},{28,4},{6,30},{30,6},{1,25},{25... | collective-permute-start | bytes 589832 | tf_op jit(solution)/shard_map/ppermute | solution.py:404
  58.8 0.0 collective-permute-done.9.rest_0_
  58.8 7.4 %collective-permute-start.14 = (f32[24,16,128]{2,1,0:T(8,128)S(1)}, f32[24,16,128]{2,1,0:T(8,128)S(1)}, u32[]{:S(2)}, u32[]{:S(2)}) collective-permute-start(f32[24,16,128]{2,1,0:T(8,128)S(1)} %get-tuple-element.67), channel_id=1, source_target_pairs={{0,26},{26,0},{2,24},{24,2},{4,30},{30,4},{6,28},{28,6},{1,27},{27... | collective-permute-start | bytes 589832 | tf_op jit(solution)/shard_map/ppermute | solution.py:404
  66.2 7.4 %collective-permute-done.10.rest_1_ = f32[24,16,128]{2,1,0:T(8,128)S(1)} collective-permute-done((f32[24,16,128]{2,1,0:T(8,128)S(1)}, f32[24,16,128]{2,1,0:T(8,128)S(1)}, u32[]{:S(2)}, u32[]{:S(2)}) %collective-permute-start.10) | collective-permute-done | bytes 196640 | tf_op jit(solution)/shard_map/ppermute | solution.py:404
  73.6 0.0 collective-permute-done.11.rest_2_
  73.6 0.0 collective-permute-done.14.rest_5_
  73.6 1.4 %update.3 = (f32[24,32,256]{2,1,0:T(8,128)S(1)}, f32[24,32,256]{2,1,0:T(8,128)S(1)}, f32[24,256]{1,0:T(8,128)S(1)}, f32[24,256]{1,0:T(8,128)S(1)}, f32[32,128]{1,0:T(8,128)S(1)}) custom-call(s32[19]{0:T(128)S(1)} %get-tuple-element.40.plan.rest_0_, f32[3,1,256]{2,1,0:T(1,128)S(1)} %get-tuple-element.41.rates, f32[24,32,256]{2,1,0:T(8,128)S(1)} %get-tuple-element.61.state, ...), custom_call_target="tpu_custom_call" | custom-call | tf_op jit(solution)/shard_map/update/pallas_call | solution.py:458
  75.0 0.9 %collective-permute-start.15 = (f32[24,256]{1,0:T(8,128)S(1)}, f32[24,256]{1,0:T(8,128)S(1)}, u32[]{:S(2)}, u32[]{:S(2)}) collective-permute-start(f32[24,256]{1,0:T(8,128)S(1)} %get-tuple-element.70), channel_id=1, source_target_pairs={{2,4},{4,2},{6,0},{0,6},{3,5},{5,3},{7,1},{1,7},{10,12},{12,10},{1... | collective-permute-start | bytes 73736 | tf_op jit(solution)/shard_map/ppermute | solution.py:472
  75.9 0.8 collective-permute-start.16
  76.7 1.2 %spread_last.1.rest_0_ = f32[1,24,32,256]{3,2,1,0:T(8,128)S(1)} custom-call(f32[24,32,256]{2,1,0:T(8,128)S(1)} %get-tuple-element.68.wets, f32[24,32,256]{2,1,0:T(8,128)S(1)} %get-tuple-element.69.flux), custom_call_target="tpu_custom_call" | custom-call | tf_op jit(solution)/shard_map/spread_last/pallas_call | solution.py:475
  78.0 1.9 %collective-permute-done.15.rest_1_ = f32[24,256]{1,0:T(8,128)S(1)} collective-permute-done((f32[24,256]{1,0:T(8,128)S(1)}, f32[24,256]{1,0:T(8,128)S(1)}, u32[]{:S(2)}, u32[]{:S(2)}) %collective-permute-start.15) | collective-permute-done | bytes 24608 | tf_op jit(solution)/shard_map/ppermute | solution.py:472
  79.8 0.0 collective-permute-done.16.rest_2_
  79.8 1.1 %halo_last.1 = f32[1,24,32,256]{3,2,1,0:T(8,128)} custom-call(f32[1,24,32,256]{3,2,1,0:T(8,128)S(1)} %spread_last.1.rest_0_, f32[24,256]{1,0:T(8,128)S(1)} %collective-permute-done.15.rest_1_, f32[24,256]{1,0:T(8,128)S(1)} %collective-permute-done.16.rest_2_, f32[32,128]{1,0:T(8,128)S(1)} %collective-permute-done.17.rest_3_), custom_call_target="tpu_custom_call" | custom-call | tf_op jit(solution)/shard_map/halo_last/pallas_call | solution.py:484
  (18 shorter events, 0.0 us)
Async XLA Ops:
  0.0 26.8 %copy-start = (f32[1,24,32,256]{3,2,1,0:T(8,128)S(1)}, f32[1,24,32,256]{3,2,1,0:T(8,128)}, u32[]{:S(2)}) copy-start(f32[1,24,32,256]{3,2,1,0:T(8,128)} %refs_0_.1) | copy-start | bytes 2359300
  0.0 26.8 %copy-start.1 = (f32[1,32,256]{2,1,0:T(8,128)S(1)}, f32[1,32,256]{2,1,0:T(8,128)}, u32[]{:S(2)}) copy-start(f32[1,32,256]{2,1,0:T(8,128)} %refs_1_.1) | copy-start | bytes 98308
  0.0 26.8 %copy-start.10 = (f32[4,3]{1,0:T(4,128)S(1)}, f32[4,3]{1,0:T(4,128)}, u32[]{:S(2)}) copy-start(f32[4,3]{1,0:T(4,128)} %refs_6_.1) | copy-start | bytes 148
  2.7 24.1 %copy-start.9 = (f32[8,128]{1,0:T(8,128)S(1)}, f32[8,128]{1,0:T(8,128)}, u32[]{:S(2)}) copy-start(f32[8,128]{1,0:T(8,128)} %get-tuple-element.39.token) | copy-start | bytes 12292
  2.8 16.7 %collective-permute-start = (f32[24,16,128]{2,1,0:T(8,128)}, f32[24,16,128]{2,1,0:T(8,128)S(1)}, u32[]{:S(2)}, u32[]{:S(2)}) collective-permute-start(f32[24,16,128]{2,1,0:T(8,128)} %get-tuple-element.48), channel_id=1, source_target_pairs={{0,8},{8,0},{2,10},{10,2},{4,12},{12,4},{6,14},{14,6},{1,9},{9,1},... | collective-permute-start | bytes 589832 | tf_op jit(solution)/shard_map/ppermute | solution.py:404
  7.9 27.3 %collective-permute-start.1 = (f32[24,16,128]{2,1,0:T(8,128)}, f32[24,16,128]{2,1,0:T(8,128)S(1)}, u32[]{:S(2)}, u32[]{:S(2)}) collective-permute-start(f32[24,16,128]{2,1,0:T(8,128)} %get-tuple-element.49), channel_id=1, source_target_pairs={{0,10},{10,0},{2,8},{8,2},{4,14},{14,4},{6,12},{12,6},{1,11},{11,1... | collective-permute-start | bytes 589832 | tf_op jit(solution)/shard_map/ppermute | solution.py:404
  11.4 15.4 %copy-start.8 = (s32[3,4,2]{1,2,0:T(2,128)S(1)}, s32[3,4,2]{1,2,0:T(2,128)}, u32[]{:S(2)}) copy-start(s32[3,4,2]{1,2,0:T(2,128)} %param.19) | copy-start | bytes 292
  11.4 23.7 %collective-permute-start.2 = (f32[24,16,128]{2,1,0:T(8,128)}, f32[24,16,128]{2,1,0:T(8,128)S(1)}, u32[]{:S(2)}, u32[]{:S(2)}) collective-permute-start(f32[24,16,128]{2,1,0:T(8,128)} %get-tuple-element.50), channel_id=1, source_target_pairs={{0,16},{16,0},{2,18},{18,2},{4,20},{20,4},{6,22},{22,6},{1,17},{17... | collective-permute-start | bytes 589832 | tf_op jit(solution)/shard_map/ppermute | solution.py:404
  13.4 13.5 %copy-start.7 = (s32[3,4,2]{1,2,0:T(2,128)S(1)}, s32[3,4,2]{1,2,0:T(2,128)}, u32[]{:S(2)}) copy-start(s32[3,4,2]{1,2,0:T(2,128)} %param.18) | copy-start | bytes 292
  13.4 13.5 %copy-start.6 = (s32[3,4,2]{1,2,0:T(2,128)S(1)}, s32[3,4,2]{1,2,0:T(2,128)}, u32[]{:S(2)}) copy-start(s32[3,4,2]{1,2,0:T(2,128)} %param.17) | copy-start | bytes 292
  13.4 21.8 %collective-permute-start.3 = (f32[24,16,128]{2,1,0:T(8,128)}, f32[24,16,128]{2,1,0:T(8,128)S(1)}, u32[]{:S(2)}, u32[]{:S(2)}) collective-permute-start(f32[24,16,128]{2,1,0:T(8,128)} %get-tuple-element.51), channel_id=1, source_target_pairs={{0,18},{18,0},{2,16},{16,2},{4,22},{22,4},{6,20},{20,6},{1,19},{19... | collective-permute-start | bytes 589832 | tf_op jit(solution)/shard_map/ppermute | solution.py:404
  17.5 17.6 %collective-permute-start.4 = (f32[24,16,128]{2,1,0:T(8,128)}, f32[24,16,128]{2,1,0:T(8,128)S(1)}, u32[]{:S(2)}, u32[]{:S(2)}) collective-permute-start(f32[24,16,128]{2,1,0:T(8,128)} %get-tuple-element.52), channel_id=1, source_target_pairs={{0,24},{24,0},{2,26},{26,2},{4,28},{28,4},{6,30},{30,6},{1,25},{25... | collective-permute-start | bytes 589832 | tf_op jit(solution)/shard_map/ppermute | solution.py:404
  19.5 15.7 %collective-permute-start.5 = (f32[24,16,128]{2,1,0:T(8,128)}, f32[24,16,128]{2,1,0:T(8,128)S(1)}, u32[]{:S(2)}, u32[]{:S(2)}) collective-permute-start(f32[24,16,128]{2,1,0:T(8,128)} %get-tuple-element.53), channel_id=1, source_target_pairs={{0,26},{26,0},{2,24},{24,2},{4,30},{30,4},{6,28},{28,6},{1,27},{27... | collective-permute-start | bytes 589832 | tf_op jit(solution)/shard_map/ppermute | solution.py:404
  26.9 0.8 copy-start.2
  27.6 0.8 copy-start.3
  28.4 0.8 copy-start.4
  29.1 0.8 copy-start.5
  36.6 4.8 %collective-permute-start.6 = (f32[24,256]{1,0:T(8,128)S(1)}, f32[24,256]{1,0:T(8,128)S(1)}, u32[]{:S(2)}, u32[]{:S(2)}) collective-permute-start(f32[24,256]{1,0:T(8,128)S(1)} %get-tuple-element.58), channel_id=1, source_target_pairs={{2,4},{4,2},{6,0},{0,6},{3,5},{5,3},{7,1},{1,7},{10,12},{12,10},{1... | collective-permute-start | bytes 73736 | tf_op jit(solution)/shard_map/ppermute | solution.py:472
  38.2 3.9 %collective-permute-start.7 = (f32[24,256]{1,0:T(8,128)S(1)}, f32[24,256]{1,0:T(8,128)S(1)}, u32[]{:S(2)}, u32[]{:S(2)}) collective-permute-start(f32[24,256]{1,0:T(8,128)S(1)} %get-tuple-element.59), channel_id=1, source_target_pairs={{0,2},{2,0},{4,6},{6,4},{1,3},{3,1},{5,7},{7,5},{8,10},{10,8},{12,... | collective-permute-start | bytes 73736 | tf_op jit(solution)/shard_map/ppermute | solution.py:472
  40.0 1.3 %collective-permute-start.8 = (f32[32,128]{1,0:T(8,128)S(1)}, f32[32,128]{1,0:T(8,128)S(1)}, u32[]{:S(2)}, u32[]{:S(2)}) collective-permute-start(f32[32,128]{1,0:T(8,128)S(1)} %get-tuple-element.60), channel_id=1, source_target_pairs={{0,1},{1,0},{2,3},{3,2},{4,5},{5,4},{6,7},{7,6},{8,9},{9,8},{10,11... | collective-permute-start | bytes 49160 | tf_op jit(solution)/shard_map/ppermute | solution.py:473
  43.3 15.4 %collective-permute-start.9 = (f32[24,16,128]{2,1,0:T(8,128)S(1)}, f32[24,16,128]{2,1,0:T(8,128)S(1)}, u32[]{:S(2)}, u32[]{:S(2)}) collective-permute-start(f32[24,16,128]{2,1,0:T(8,128)S(1)} %get-tuple-element.62), channel_id=1, source_target_pairs={{0,8},{8,0},{2,10},{10,2},{4,12},{12,4},{6,14},{14,6},{1,9},{9,1},... | collective-permute-start | bytes 589832 | tf_op jit(solution)/shard_map/ppermute | solution.py:404
  45.3 28.3 %collective-permute-start.10 = (f32[24,16,128]{2,1,0:T(8,128)S(1)}, f32[24,16,128]{2,1,0:T(8,128)S(1)}, u32[]{:S(2)}, u32[]{:S(2)}) collective-permute-start(f32[24,16,128]{2,1,0:T(8,128)S(1)} %get-tuple-element.63), channel_id=1, source_target_pairs={{0,10},{10,0},{2,8},{8,2},{4,14},{14,4},{6,12},{12,6},{1,11},{11,1... | collective-permute-start | bytes 589832 | tf_op jit(solution)/shard_map/ppermute | solution.py:404
  50.8 22.8 %collective-permute-start.11 = (f32[24,16,128]{2,1,0:T(8,128)S(1)}, f32[24,16,128]{2,1,0:T(8,128)S(1)}, u32[]{:S(2)}, u32[]{:S(2)}) collective-permute-start(f32[24,16,128]{2,1,0:T(8,128)S(1)} %get-tuple-element.64), channel_id=1, source_target_pairs={{0,16},{16,0},{2,18},{18,2},{4,20},{20,4},{6,22},{22,6},{1,17},{17... | collective-permute-start | bytes 589832 | tf_op jit(solution)/shard_map/ppermute | solution.py:404
  52.8 20.8 %collective-permute-start.12 = (f32[24,16,128]{2,1,0:T(8,128)S(1)}, f32[24,16,128]{2,1,0:T(8,128)S(1)}, u32[]{:S(2)}, u32[]{:S(2)}) collective-permute-start(f32[24,16,128]{2,1,0:T(8,128)S(1)} %get-tuple-element.65), channel_id=1, source_target_pairs={{0,18},{18,0},{2,16},{16,2},{4,22},{22,4},{6,20},{20,6},{1,19},{19... | collective-permute-start | bytes 589832 | tf_op jit(solution)/shard_map/ppermute | solution.py:404
  56.9 16.8 %collective-permute-start.13 = (f32[24,16,128]{2,1,0:T(8,128)S(1)}, f32[24,16,128]{2,1,0:T(8,128)S(1)}, u32[]{:S(2)}, u32[]{:S(2)}) collective-permute-start(f32[24,16,128]{2,1,0:T(8,128)S(1)} %get-tuple-element.66), channel_id=1, source_target_pairs={{0,24},{24,0},{2,26},{26,2},{4,28},{28,4},{6,30},{30,6},{1,25},{25... | collective-permute-start | bytes 589832 | tf_op jit(solution)/shard_map/ppermute | solution.py:404
  58.8 14.8 %collective-permute-start.14 = (f32[24,16,128]{2,1,0:T(8,128)S(1)}, f32[24,16,128]{2,1,0:T(8,128)S(1)}, u32[]{:S(2)}, u32[]{:S(2)}) collective-permute-start(f32[24,16,128]{2,1,0:T(8,128)S(1)} %get-tuple-element.67), channel_id=1, source_target_pairs={{0,26},{26,0},{2,24},{24,2},{4,30},{30,4},{6,28},{28,6},{1,27},{27... | collective-permute-start | bytes 589832 | tf_op jit(solution)/shard_map/ppermute | solution.py:404
  75.0 4.8 %collective-permute-start.15 = (f32[24,256]{1,0:T(8,128)S(1)}, f32[24,256]{1,0:T(8,128)S(1)}, u32[]{:S(2)}, u32[]{:S(2)}) collective-permute-start(f32[24,256]{1,0:T(8,128)S(1)} %get-tuple-element.70), channel_id=1, source_target_pairs={{2,4},{4,2},{6,0},{0,6},{3,5},{5,3},{7,1},{1,7},{10,12},{12,10},{1... | collective-permute-start | bytes 73736 | tf_op jit(solution)/shard_map/ppermute | solution.py:472
  75.9 3.9 %collective-permute-start.16 = (f32[24,256]{1,0:T(8,128)S(1)}, f32[24,256]{1,0:T(8,128)S(1)}, u32[]{:S(2)}, u32[]{:S(2)}) collective-permute-start(f32[24,256]{1,0:T(8,128)S(1)} %get-tuple-element.71), channel_id=1, source_target_pairs={{0,2},{2,0},{4,6},{6,4},{1,3},{3,1},{5,7},{7,5},{8,10},{10,8},{12,... | collective-permute-start | bytes 73736 | tf_op jit(solution)/shard_map/ppermute | solution.py:472
  76.7 1.3 %collective-permute-start.17 = (f32[32,128]{1,0:T(8,128)S(1)}, f32[32,128]{1,0:T(8,128)S(1)}, u32[]{:S(2)}, u32[]{:S(2)}) collective-permute-start(f32[32,128]{1,0:T(8,128)S(1)} %get-tuple-element.72), channel_id=1, source_target_pairs={{0,1},{1,0},{2,3},{3,2},{4,5},{5,4},{6,7},{7,6},{8,9},{9,8},{10,11... | collective-permute-start | bytes 49160 | tf_op jit(solution)/shard_map/ppermute | solution.py:473

commit v6 on v5

--- a/solution.py
+++ b/solution.py
@@ -25,11 +25,11 @@
     return lax.axis_index("grid"), lax.axis_index("gx"), lax.axis_index("gy")
 
 
-ORDER = ((0, 0), (0, 1), (1, 0), (1, 1), (2, 0), (2, 1))
-
-
-def sorted_out(blocks):
-    return [blocks[ORDER.index((slot, kind))] for kind in range(2) for slot in range(SLOTS)]
+TURNED = 2
+FORWARDED = 0
+EARLY = ((FORWARDED, 0), (TURNED, 1))
+LATE = ((0, 1), (2, 1), (1, 0), (1, 1), (2, 0))
+GOT = (EARLY[0],) + LATE
 
 
 def pieces_of(flip, top, left):
@@ -158,35 +158,34 @@
 
 
 def first_kernel(*refs):
-    given, outs, token = refs[:5], sorted_out(refs[5 : 5 + 2 * SLOTS]), refs[5 + 2 * SLOTS]
-    rows, fine, *held, done = refs[6 + 2 * SLOTS :]
-    token[...] = jnp.zeros_like(token)
+    given, early, mask, late, refs = refs[:5], refs[5:7], refs[7], refs[8:13], refs[13:]
+    rows, fine, *held, done = refs
     copies = [pltpu.make_async_copy(source, to, done.at[k]) for k, (source, to) in enumerate(zip(given, held))]
     for copy in copies:
         copy.start()
     for copy in copies:
         copy.wait()
-    flip, top, left, state, sponge = held
+    *tables, state, sponge = held
     state = state.at[0]
     grid, _, _ = place()
 
     @pl.when(grid == 0)
     def _():
-        for slot, kind, serves, first, begin in pieces_of(flip, top, left):
-
-            @pl.when(serves)
-            def _():
-                crop(state, outs[kind * SLOTS + slot], first, begin)
+        table = list(pieces_of(*tables))
+        crop_all(state, table, EARLY, early)
+        crop_all(state, table, LATE, late)
+        mark_turned(mask, table)
 
     @pl.when(grid > 0)
     def _():
+        mask[...] = jnp.zeros_like(mask)
         block = fold(state, sponge, rows, fine)
         for slot in range(SLOTS):
 
             @pl.when(grid == slot + 1)
             def _():
-                outs[slot][...] = block
-                outs[SLOTS + slot][...] = block
+                for out in child_outs(slot, early, late):
+                    out[...] = block
 
 
 def stage_kernel(token, *refs):
@@ -216,7 +215,7 @@
 
 
 def update_kernel(n_cols, plan, rates, state, sponge, agg, brk, mask, diff, *rest):
-    got, rest = sorted_out(rest[: 2 * SLOTS]), rest[2 * SLOTS :]
+    got, rest = rest[: 2 * SLOTS + 1], rest[2 * SLOTS + 1 :]
     wets, flux, sides = rest[0], rest[1], rest[2 : 4 + n_cols]
     nested, wide, coarse, fine = rest[4 + n_cols :]
     comps, cells_r, cells_c = wets.shape
@@ -243,16 +242,16 @@
 
             @pl.when(serves)
             def _():
-                add_at(nested, got[kind * SLOTS + slot], first, begin)
+                add_at(nested, got[-1 if (slot, kind) == (FORWARDED, 1) else GOT.index((slot, kind))], first, begin)
 
     @pl.when(grid > 0)
     def _():
         for slot in range(SLOTS):
-            for kind in range(2):
-
-                @pl.when((grid == slot + 1) & (plan[6 * SLOTS] == kind))
+            for kind in range(1 if slot == TURNED else 2):
+
+                @pl.when((grid == slot + 1) & ((plan[6 * SLOTS] == kind) | (slot == TURNED)))
                 def _():
-                    coarse[...] = got[kind * SLOTS + slot][...]
+                    coarse[...] = got[GOT.index((slot, kind))][...]
 
         wide[...] = jnp.dot(
             coarse[...].reshape(comps * half_r, half_c),
@@ -372,37 +371,96 @@
     if last:
         return
     sponge, folded = given
-    outs, (packed, fine) = rest[: 2 * SLOTS], rest[2 * SLOTS :]
+    early, mask, packed, fine = rest[:2], *rest[2:]
 
     @pl.when(grid == 0)
     def _():
-        for slot, kind, serves, start, begin in pieces(plan):
+        table = list(pieces(plan))
+        crop_all(new, table, EARLY, early)
+        mark_turned(mask, table)
+
+    @pl.when(grid > 0)
+    def _():
+        mask[...] = jnp.zeros_like(mask)
+        pack_fold(packed, comps, above, below, low, high, sponge, fine)
+
+    @pl.when(grid == FORWARDED + 1)
+    def _():
+        patch(folded, packed, child_outs(FORWARDED, early, ()))
+
+
+def crop_all(state, table, order, outs):
+    for slot, kind, serves, first, begin in table:
+        if (slot, kind) in order and ((slot, kind) != (TURNED, 1) or order is EARLY):
 
             @pl.when(serves)
             def _():
-                crop(new, outs[ORDER.index((slot, kind))], start, begin)
-
-    @pl.when(grid > 0)
-    def _():
-        pack_fold(packed, comps, above, below, low, high, sponge, fine)
+                crop(state, outs[order.index((slot, kind))], first, begin)
+
+
+def mark_turned(mask, table):
+    for slot, kind, serves, _, _ in table:
+        if (slot, kind) == (TURNED, 0):
+            mask[...] = jnp.full(mask.shape, jnp.where(serves, 0.0, 1.0), jnp.float32)
+
+
+def child_outs(slot, early, late):
+    if slot == FORWARDED:
+        return [early[0]]
+    return [late[LATE.index((slot, kind))] for kind in range(2)]
+
+
+def late_kernel(plan, state, folded, packed, *outs):
+    grid, _, _ = place()
+
+    @pl.when(grid == 0)
+    def _():
+        crop_all(state, list(pieces(plan)), LATE, outs)
 
     for slot in range(SLOTS):
-
-        @pl.when(grid == slot + 1)
-        def _():
-            patch(folded, packed, [outs[ORDER.index((slot, kind))] for kind in range(2)])
-
-
-def exchange(blocks):
+        if slot != FORWARDED:
+
+            @pl.when(grid == slot + 1)
+            def _():
+                patch(folded, packed, child_outs(slot, (), outs))
+
+
+def merge_kernel(mask, own, other, out):
+    out[...] = jnp.where(mask[:1, :] > 0.5, other[...], own[...])
+
+
+def between_parents(block):
+    return lax.ppermute(block, ("grid", "gx"), [(i, i ^ 1) for i in range(lax.axis_size("gx"))])
+
+
+def with_children(block, slot, kind, down=True, up=True):
     n_x = lax.axis_size("gx")
-    got = []
-    for (slot, kind), block in zip(ORDER, blocks):
-        pairs = []
-        for i in range(n_x):
-            parent, child = i, (slot + 1) * n_x + (i ^ kind)
-            pairs += [(parent, child), (child, parent)]
-        got.append(lax.ppermute(block, ("grid", "gx"), pairs))
-    return got
+    pairs = []
+    for i in range(n_x):
+        parent, child = i, (slot + 1) * n_x + (i ^ kind)
+        pairs += [(parent, child)] * down + [(child, parent)] * up
+    return lax.ppermute(block, ("grid", "gx"), pairs)
+
+
+def exchange(early, mask, late):
+    blocks = dict(zip(LATE, late))
+    blocks[EARLY[0]] = early[0]
+    other = between_parents(early[1])
+    own = blocks[TURNED, 0]
+    blocks[TURNED, 0] = pl.pallas_call(
+        merge_kernel,
+        out_shape=jax.ShapeDtypeStruct(own.shape, own.dtype),
+        in_specs=[VM] * 3,
+        out_specs=VM,
+        compiler_params=PARAMS,
+        name="merge",
+    )(mask, own, other)
+    got = [
+        with_children(blocks[slot, kind], slot, kind, up=(slot, kind) != (FORWARDED, 1), down=(slot, kind) != (TURNED, 1))
+        for slot, kind in GOT
+    ]
+    forward, got[3] = lax.optimization_barrier((got[0], got[3]))
+    return got + [between_parents(forward)]
 
 
 def swap_pairs(size, phase):
@@ -425,17 +483,19 @@
     fold_scratch = [pltpu.VMEM((comps, half_r, cells_c), f32), pltpu.VMEM((cells_c // LANES, cells_r, LANES), f32)]
     tables = [table.transpose(0, 2, 1) for table in (partner_flip, row_offset, col_offset)]
 
-    *blocks, token = pl.pallas_call(
+    flag = jax.ShapeDtypeStruct((8, half_c), f32)
+    blocks = pl.pallas_call(
         first_kernel,
-        out_shape=[block] * (2 * SLOTS) + [jax.ShapeDtypeStruct((8, LANES), f32)],
+        out_shape=[block] * 2 + [flag] + [block] * 5,
         in_specs=[pl.BlockSpec(memory_space=pltpu.HBM)] * 5,
-        out_specs=[VM] * (2 * SLOTS + 1),
+        out_specs=[VM] * 8,
         scratch_shapes=fold_scratch
         + [pltpu.SMEM(table.shape, table.dtype) for table in tables]
         + [pltpu.VMEM(adjoint.shape, f32), pltpu.VMEM(sponge.shape, f32), pltpu.SemaphoreType.DMA((5,))],
         compiler_params=pltpu.CompilerParams(vmem_limit_bytes=60 * 2**20),
         name="first_payload",
     )(*tables, adjoint, sponge)
+    early, mask, late = blocks[:2], blocks[2], blocks[3:]
     fields = (adjoint, sponge, aggregation, breakup, sea_mask, diffusivity)
     state, sponge, *fields, rates, plan = pl.pallas_call(
         stage_kernel,
@@ -448,17 +508,17 @@
         + [pltpu.SemaphoreType.DMA((10,))],
         compiler_params=PARAMS,
         name="stage_fields",
-    )(token, *fields, settling, *tables)
+    )(mask, *fields, settling, *tables)
     state = state.reshape(tile.shape)
     fold_scratch = [pltpu.VMEM((comps, half_r, cells_c), f32), pltpu.VMEM((cells_c // LANES, cells_r, LANES), f32)]
     for step in range(STEPS):
         last = step == STEPS - 1
         new = jax.ShapeDtypeStruct(adjoint.shape, f32) if last else tile
-        got = exchange(blocks)
+        got = exchange(early, mask, late)
         wets, flux, *sides = pl.pallas_call(
             functools.partial(update_kernel, n_cols),
             out_shape=[tile] * 2 + side,
-            in_specs=[SM] + [VM] * (7 + 2 * SLOTS),
+            in_specs=[SM] + [VM] * (8 + 2 * SLOTS),
             out_specs=[VM] * (2 + len(side)),
             scratch_shapes=[
                 pltpu.VMEM(tile.shape, f32),
@@ -481,15 +541,27 @@
             compiler_params=PARAMS,
             name="spread_last" if last else "spread",
         )(wets, flux, *([] if last else [sponge]))
-        state, *blocks = pl.pallas_call(
+        extra = jax.ShapeDtypeStruct((2 * comps + 2 * half_r, half_c), f32)
+        extra = jax.ShapeDtypeStruct((2 * comps + 2 * half_r, half_c), f32)
+        state, *out = pl.pallas_call(
             functools.partial(halo_kernel, n_cols, (n_x, n_y), last),
-            out_shape=[new] + ([] if last else [block] * (2 * SLOTS)),
+            out_shape=[new] + ([] if last else [block] * 2 + [flag, extra]),
             in_specs=[SM] * (0 if last else 1) + [VM] * (1 + len(side) + (0 if last else 2)),
-            out_specs=[VM] * (1 if last else 1 + 2 * SLOTS),
-            scratch_shapes=[] if last else [pltpu.VMEM((2 * comps + 2 * half_r, half_c), f32), fold_scratch[1]],
+            out_specs=[VM] * (1 if last else 5),
+            scratch_shapes=[] if last else fold_scratch[1:],
             compiler_params=PARAMS,
             name="halo_last" if last else "halo",
         )(*([] if last else [plan]), bulk, *([] if last else [sponge, *folded]), *sides)
+        if not last:
+            early, mask, packed = out[:2], out[2], out[3]
+            late = pl.pallas_call(
+                late_kernel,
+                out_shape=[block] * 5,
+                in_specs=[SM] + [VM] * 3,
+                out_specs=[VM] * 5,
+                compiler_params=PARAMS,
+                name="late_payload",
+            )(plan, state, *folded, packed)
     return state
 
 

time: 81.8 us -> 78.3 us (0.957)
  starting transfers between devices: 51.8 us -> 43.3 us
  waiting for transfers between devices: 13.7 us -> 18.6 us
  Pallas kernels: 12.1 us -> 14.2 us
  local copies, waits for them, and re-layouts: 3.06 us -> 0.97 us
    ppermute x12 -> x16, starting transfers between devices: 46.7 us -> 37.5 us  [the longest x12 23.4 us: with_children(): return lax.ppermute(block, ('grid', 'gx'), pairs)]
    ppermute x12 -> x16, waiting for transfers between devices: 11 us -> 16.6 us  [the longest x12 16.6 us: with_children(): return lax.ppermute(block, ('grid', 'gx'), pairs)]
    unnamed x22 -> x24, local copies, waits for them, and re-layouts: 3.06 us -> 0.97 us
    pallas_call x1 -> x4, Pallas kernels: 2.73 us -> 4.54 us  [the longest x1 3.25 us: local(): pl.pallas_call(first_kernel, out_shape=[block] * 2 + [flag] + [block] * 5...]
  transfers between devices with their start and end apart: 18 -> 22, of which waited for: 5 -> 7; matrix products, arithmetic and copies ran while one was open for 0% -> 0% of each run, Pallas kernels for 5% -> 7%
where the time goes in v6:
time: 78.3 us; the launch traced here: 77.6 us
  starting transfers between devices  43.3 us (55%)
  waiting for transfers between devices  18.6 us (24%)
  Pallas kernels  14.2 us (18%)
  local copies, waits for them, and re-layouts  0.97 us (1%)
    ppermute x12, starting transfers between devices, with_children(): return lax.ppermute(block, ('grid', 'gx'), pairs)  23.4 us
    ppermute x12, waiting for transfers between devices, with_children(): return lax.ppermute(block, ('grid', 'gx'), pairs)  16.6 us
    ppermute x4, starting transfers between devices, between_parents(): lax.ppermute(block, ('grid', 'gx'), [(i, i ^ 1) for i in range(lax.axis_s...  14.1 us
    ppermute x4, starting transfers between devices, local(): lax.ppermute(sides[k], 'gx', swap_pairs(n_x, 1 - k))  5.76 us
    pallas_call x2, Pallas kernels, local(): pl.pallas_call(functools.partial(update_kernel, n_cols), out_shape=[tile]...  3.38 us
    pallas_call x1, Pallas kernels, local(): pl.pallas_call(first_kernel, out_shape=[block] * 2 + [flag] + [block] * 5...  3.25 us
    pallas_call x2, Pallas kernels, local(): pl.pallas_call(functools.partial(spread_kernel, last), out_shape=[new] +...  2.49 us
    pallas_call x2, Pallas kernels, local(): pl.pallas_call(functools.partial(halo_kernel, n_cols, (n_x, n_y), last),...  2.11 us
  transfers between devices with their start and end apart: 22, of which 7 were waited for; matrix products, arithmetic and copies ran while one was open for 0% of the time, Pallas kernels for 7%

profile of v6, /device:TPU:0, one launch (start us, length us, event | category | flops | bytes accessed | tf_op | source)
XLA Modules:
  0.0 77.6 jit_solution(5591540340682766305)
XLA Ops:
  0.0 3.2 %first_payload.1 = (f32[24,16,128]{2,1,0:T(8,128)}, f32[24,16,128]{2,1,0:T(8,128)}, f32[8,128]{1,0:T(8,128)}, f32[24,16,128]{2,1,0:T(8,128)}, f32[24,16,128]{2,1...) custom-call(s32[3,2,4]{2,1,0:T(2,128)} %bitcast.5, s32[3,2,4]{2,1,0:T(2,128)} %bitcast.7, ...), custom_call_target="tpu_custom_call" | custom-call | tf_op jit(solution)/shard_map/first_payload/pallas_call | solution.py:487
  3.3 4.7 %collective-permute-start = (f32[24,16,128]{2,1,0:T(8,128)}, f32[24,16,128]{2,1,0:T(8,128)S(1)}, u32[]{:S(2)}, u32[]{:S(2)}) collective-permute-start(f32[24,16,128]{2,1,0:T(8,128)} %get-tuple-element.56), channel_id=1, source_target_pairs={{0,8},{8,0},{2,10},{10,2},{4,12},{12,4},{6,14},{14,6},{1,9},{9,1},... | collective-permute-start | bytes 589832 | tf_op jit(solution)/shard_map/ppermute | solution.py:442
  7.9 1.9 %collective-permute-start.3 = (f32[24,16,128]{2,1,0:T(8,128)}, f32[24,16,128]{2,1,0:T(8,128)S(1)}, u32[]{:S(2)}, u32[]{:S(2)}) collective-permute-start(f32[24,16,128]{2,1,0:T(8,128)} %get-tuple-element.59), channel_id=1, source_target_pairs={{0,16},{16,0},{2,18},{18,2},{4,20},{20,4},{6,22},{22,6},{1,17},{17... | collective-permute-start | bytes 589832 | tf_op jit(solution)/shard_map/ppermute | solution.py:442
  9.9 3.4 %collective-permute-start.5 = (f32[24,16,128]{2,1,0:T(8,128)}, f32[24,16,128]{2,1,0:T(8,128)S(1)}, u32[]{:S(2)}, u32[]{:S(2)}) collective-permute-start(f32[24,16,128]{2,1,0:T(8,128)} %get-tuple-element.63), channel_id=1, source_target_pairs={{0,2},{2,0},{4,6},{6,4},{1,3},{3,1},{5,7},{7,5}} | collective-permute-start | bytes 589832 | tf_op jit(solution)/shard_map/ppermute | solution.py:433
  13.3 1.3 %collective-permute-start.1 = (f32[24,16,128]{2,1,0:T(8,128)}, f32[24,16,128]{2,1,0:T(8,128)S(1)}, u32[]{:S(2)}, u32[]{:S(2)}) collective-permute-start(f32[24,16,128]{2,1,0:T(8,128)} %get-tuple-element.57), channel_id=1, source_target_pairs={{0,10},{2,8},{4,14},{6,12},{1,11},{3,9},{5,15},{7,13}} | collective-permute-start | bytes 589832 | tf_op jit(solution)/shard_map/ppermute | solution.py:442
  14.6 1.3 %collective-permute-start.2 = (f32[24,16,128]{2,1,0:T(8,128)}, f32[24,16,128]{2,1,0:T(8,128)S(1)}, u32[]{:S(2)}, u32[]{:S(2)}) collective-permute-start(f32[24,16,128]{2,1,0:T(8,128)} %get-tuple-element.58), channel_id=1, source_target_pairs={{26,0},{24,2},{30,4},{28,6},{27,1},{25,3},{31,5},{29,7}} | collective-permute-start | bytes 589832 | tf_op jit(solution)/shard_map/ppermute | solution.py:442
  15.9 0.0 collective-permute-done.rest_0_
  15.9 1.9 %collective-permute-start.4 = (f32[24,16,128]{2,1,0:T(8,128)}, f32[24,16,128]{2,1,0:T(8,128)S(1)}, u32[]{:S(2)}, u32[]{:S(2)}) collective-permute-start(f32[24,16,128]{2,1,0:T(8,128)} %get-tuple-element.61), channel_id=1, source_target_pairs={{0,18},{18,0},{2,16},{16,2},{4,22},{22,4},{6,20},{20,6},{1,19},{19... | collective-permute-start | bytes 589832 | tf_op jit(solution)/shard_map/ppermute | solution.py:442
  17.8 4.9 %collective-permute-start.7 = (f32[24,16,128]{2,1,0:T(8,128)S(1)}, f32[24,16,128]{2,1,0:T(8,128)S(1)}, u32[]{:S(2)}, u32[]{:S(2)}) collective-permute-start(f32[24,16,128]{2,1,0:T(8,128)S(1)} %collective-permute-done.rest_0_), channel_id=1, source_target_pairs={{0,2},{2,0},{4,6},{6,4},{1,3},{3,1},{5,7},{7,5}} | collective-permute-start | bytes 589832 | tf_op jit(solution)/shard_map/ppermute | solution.py:433
  22.8 0.0 collective-permute-done.5.other
  22.8 0.9 %copy-done.1 = f32[24,16,128]{2,1,0:T(8,128)S(1)} copy-done((f32[24,16,128]{2,1,0:T(8,128)S(1)}, f32[24,16,128]{2,1,0:T(8,128)}, u32[]{:S(2)}) %copy-start.1) | copy-done | bytes 196632
  23.7 0.0 copy-start.6
  23.8 0.0 copy-start.8
  23.8 0.0 copy-start.9
  23.8 0.0 copy-start.10
  23.8 0.0 copy-start.11
  23.8 2.1 %collective-permute-start.6 = (f32[24,16,128]{2,1,0:T(8,128)S(1)}, f32[24,16,128]{2,1,0:T(8,128)S(1)}, u32[]{:S(2)}, u32[]{:S(2)}) collective-permute-start(f32[24,16,128]{2,1,0:T(8,128)S(1)} %merge.2), channel_id=1, source_target_pairs={{0,24},{24,0},{2,26},{26,2},{4,28},{28,4},{6,30},{30,6},{1,25},{25... | collective-permute-start | bytes 589832 | tf_op jit(solution)/shard_map/ppermute | solution.py:442
  26.0 1.7 %stage_fields.1 = (f32[1,24,32,256]{3,2,1,0:T(8,128)S(1)}, f32[1,32,256]{2,1,0:T(8,128)S(1)}, f32[1,32,256]{2,1,0:T(8,128)S(1)}, f32[1,32,256]{2,1,0:T(8,128)S(1...) custom-call(f32[8,128]{1,0:T(8,128)S(1)} %copy-done.7, ...), custom_call_target="tpu_custom_call" | custom-call | tf_op jit(solution)/shard_map/stage_fields/pallas_call | solution.py:500
  27.7 6.2 %collective-permute-done.4.rest_4_ = f32[24,16,128]{2,1,0:T(8,128)S(1)} collective-permute-done((f32[24,16,128]{2,1,0:T(8,128)}, f32[24,16,128]{2,1,0:T(8,128)S(1)}, u32[]{:S(2)}, u32[]{:S(2)}) %collective-permute-start.4) | collective-permute-done | bytes 196640 | tf_op jit(solution)/shard_map/ppermute | solution.py:442
  33.9 0.0 collective-permute-done.7.rest_6_
  33.9 0.0 collective-permute-done.6.rest_5_
  33.9 1.7 %update.2 = (f32[24,32,256]{2,1,0:T(8,128)S(1)}, f32[24,32,256]{2,1,0:T(8,128)S(1)}, f32[24,256]{1,0:T(8,128)S(1)}, f32[24,256]{1,0:T(8,128)S(1)}, f32[32,128]{1,0:T(8,128)S(1)}) custom-call(s32[19]{0:T(128)S(1)} %get-tuple-element.48.plan.rest_0_, f32[3,1,256]{2,1,0:T(1,128)S(1)} %get-tuple-element.49.rates, f32[24,32,256]{2,1,0:T(8,128)S(1)} %bitcast.4, ...), custom_call_target="tpu_custom_call" | custom-call | tf_op jit(solution)/shard_map/update/pallas_call | solution.py:518
  35.6 1.4 %collective-permute-start.8 = (f32[24,256]{1,0:T(8,128)S(1)}, f32[24,256]{1,0:T(8,128)S(1)}, u32[]{:S(2)}, u32[]{:S(2)}) collective-permute-start(f32[24,256]{1,0:T(8,128)S(1)} %get-tuple-element.69), channel_id=1, source_target_pairs={{2,4},{4,2},{6,0},{0,6},{3,5},{5,3},{7,1},{1,7},{10,12},{12,10},{1... | collective-permute-start | bytes 73736 | tf_op jit(solution)/shard_map/ppermute | solution.py:532
  37.1 2.0 %collective-permute-start.9 = (f32[24,256]{1,0:T(8,128)S(1)}, f32[24,256]{1,0:T(8,128)S(1)}, u32[]{:S(2)}, u32[]{:S(2)}) collective-permute-start(f32[24,256]{1,0:T(8,128)S(1)} %get-tuple-element.70), channel_id=1, source_target_pairs={{0,2},{2,0},{4,6},{6,4},{1,3},{3,1},{5,7},{7,5},{8,10},{10,8},{12,... | collective-permute-start | bytes 73736 | tf_op jit(solution)/shard_map/ppermute | solution.py:532
  39.1 1.2 %spread.1 = (f32[24,32,256]{2,1,0:T(8,128)S(1)}, f32[24,16,128]{2,1,0:T(8,128)S(1)}) custom-call(f32[24,32,256]{2,1,0:T(8,128)S(1)} %get-tuple-element.65.wets, f32[24,32,256]{2,1,0:T(8,128)S(1)} %get-tuple-element.66.flux, f32[1,32,256]{2,1,0:T(8,128)S(1)} %get-tuple-element.51.sponge.rest_0_.rest_2_), custom_call_target="tpu_custom_call" | custom-call | tf_op jit(solution)/shard_map/spread/pallas_call | solution.py:535
  40.3 0.0 collective-permute-done.10.rest_6_
  40.3 0.1 collective-permute-done.8.rest_4_
  40.4 0.7 collective-permute-done.9.rest_5_
  41.1 1.0 %halo.1 = (f32[24,32,256]{2,1,0:T(8,128)S(1)}, f32[24,16,128]{2,1,0:T(8,128)S(1)}, f32[24,16,128]{2,1,0:T(8,128)S(1)}, f32[8,128]{1,0:T(8,128)S(1)}, f32[80,128]{1,0:T(8,128)S(1)}) custom-call(s32[19]{0:T(128)S(1)} %get-tuple-element.48.plan.rest_0_, f32[24,32,256]{2,1,0:T(8,128)S(1)} %get-tuple-element.67.rest_1_, ...), custom_call_target="tpu_custom_call" | custom-call | tf_op jit(solution)/shard_map/halo/pallas_call | solution.py:546
  42.1 1.9 %collective-permute-start.11 = (f32[24,16,128]{2,1,0:T(8,128)S(1)}, f32[24,16,128]{2,1,0:T(8,128)S(1)}, u32[]{:S(2)}, u32[]{:S(2)}) collective-permute-start(f32[24,16,128]{2,1,0:T(8,128)S(1)} %get-tuple-element.73), channel_id=1, source_target_pairs={{0,8},{8,0},{2,10},{10,2},{4,12},{12,4},{6,14},{14,6},{1,9},{9,1},... | collective-permute-start | bytes 589832 | tf_op jit(solution)/shard_map/ppermute | solution.py:442
  44.1 1.2 %late_payload.1 = (f32[24,16,128]{2,1,0:T(8,128)S(1)}, f32[24,16,128]{2,1,0:T(8,128)S(1)}, f32[24,16,128]{2,1,0:T(8,128)S(1)}, f32[24,16,128]{2,1,0:T(8,128)S(1)}, f32[24,16,128]{2,1,0:T(8,128)S(1)}) custom-call(s32[19]{0:T(128)S(1)} %get-tuple-element.48.plan.rest_0_, f32[24,32,256]{2,1,0:T(8,128)S(1)} %get-tuple-element.72.state, ...), custom_call_target="tpu_custom_call" | custom-call | tf_op jit(solution)/shard_map/late_payload/pallas_call | solution.py:557
  45.3 1.9 %collective-permute-start.14 = (f32[24,16,128]{2,1,0:T(8,128)S(1)}, f32[24,16,128]{2,1,0:T(8,128)S(1)}, u32[]{:S(2)}, u32[]{:S(2)}) collective-permute-start(f32[24,16,128]{2,1,0:T(8,128)S(1)} %get-tuple-element.77), channel_id=1, source_target_pairs={{0,16},{16,0},{2,18},{18,2},{4,20},{20,4},{6,22},{22,6},{1,17},{17... | collective-permute-start | bytes 589832 | tf_op jit(solution)/shard_map/ppermute | solution.py:442
  47.2 3.2 %collective-permute-start.16 = (f32[24,16,128]{2,1,0:T(8,128)S(1)}, f32[24,16,128]{2,1,0:T(8,128)S(1)}, u32[]{:S(2)}, u32[]{:S(2)}) collective-permute-start(f32[24,16,128]{2,1,0:T(8,128)S(1)} %get-tuple-element.82), channel_id=1, source_target_pairs={{0,2},{2,0},{4,6},{6,4},{1,3},{3,1},{5,7},{7,5}} | collective-permute-start | bytes 589832 | tf_op jit(solution)/shard_map/ppermute | solution.py:433
  50.5 1.3 %collective-permute-start.12 = (f32[24,16,128]{2,1,0:T(8,128)S(1)}, f32[24,16,128]{2,1,0:T(8,128)S(1)}, u32[]{:S(2)}, u32[]{:S(2)}) collective-permute-start(f32[24,16,128]{2,1,0:T(8,128)S(1)} %get-tuple-element.75), channel_id=1, source_target_pairs={{0,10},{2,8},{4,14},{6,12},{1,11},{3,9},{5,15},{7,13}} | collective-permute-start | bytes 589832 | tf_op jit(solution)/shard_map/ppermute | solution.py:442
  51.8 1.3 %collective-permute-start.13 = (f32[24,16,128]{2,1,0:T(8,128)S(1)}, f32[24,16,128]{2,1,0:T(8,128)S(1)}, u32[]{:S(2)}, u32[]{:S(2)}) collective-permute-start(f32[24,16,128]{2,1,0:T(8,128)S(1)} %get-tuple-element.76), channel_id=1, source_target_pairs={{26,0},{24,2},{30,4},{28,6},{27,1},{25,3},{31,5},{29,7}} | collective-permute-start | bytes 589832 | tf_op jit(solution)/shard_map/ppermute | solution.py:442
  53.1 1.7 %collective-permute-done.11.rest_0_ = f32[24,16,128]{2,1,0:T(8,128)S(1)} collective-permute-done((f32[24,16,128]{2,1,0:T(8,128)S(1)}, f32[24,16,128]{2,1,0:T(8,128)S(1)}, u32[]{:S(2)}, u32[]{:S(2)}) %collective-permute-start.11) | collective-permute-done | bytes 196640 | tf_op jit(solution)/shard_map/ppermute | solution.py:442
  54.8 1.9 %collective-permute-start.15 = (f32[24,16,128]{2,1,0:T(8,128)S(1)}, f32[24,16,128]{2,1,0:T(8,128)S(1)}, u32[]{:S(2)}, u32[]{:S(2)}) collective-permute-start(f32[24,16,128]{2,1,0:T(8,128)S(1)} %get-tuple-element.79), channel_id=1, source_target_pairs={{0,18},{18,0},{2,16},{16,2},{4,22},{22,4},{6,20},{20,6},{1,19},{19... | collective-permute-start | bytes 589832 | tf_op jit(solution)/shard_map/ppermute | solution.py:442
  56.7 2.6 %collective-permute-start.18 = (f32[24,16,128]{2,1,0:T(8,128)S(1)}, f32[24,16,128]{2,1,0:T(8,128)S(1)}, u32[]{:S(2)}, u32[]{:S(2)}) collective-permute-start(f32[24,16,128]{2,1,0:T(8,128)S(1)} %collective-permute-done.11.rest_0_), channel_id=1, source_target_pairs={{0,2},{2,0},{4,6},{6,4},{1,3},{3,1},{5,7},{7,5}} | collective-permute-start | bytes 589832 | tf_op jit(solution)/shard_map/ppermute | solution.py:433
  59.4 1.9 %collective-permute-start.17 = (f32[24,16,128]{2,1,0:T(8,128)S(1)}, f32[24,16,128]{2,1,0:T(8,128)S(1)}, u32[]{:S(2)}, u32[]{:S(2)}) collective-permute-start(f32[24,16,128]{2,1,0:T(8,128)S(1)} %merge.3), channel_id=1, source_target_pairs={{0,24},{24,0},{2,26},{26,2},{4,28},{28,4},{6,30},{30,6},{1,25},{25... | collective-permute-start | bytes 589832 | tf_op jit(solution)/shard_map/ppermute | solution.py:442
  61.3 1.0 %collective-permute-done.13.rest_2_ = f32[24,16,128]{2,1,0:T(8,128)S(1)} collective-permute-done((f32[24,16,128]{2,1,0:T(8,128)S(1)}, f32[24,16,128]{2,1,0:T(8,128)S(1)}, u32[]{:S(2)}, u32[]{:S(2)}) %collective-permute-start.13) | collective-permute-done | bytes 196640 | tf_op jit(solution)/shard_map/ppermute | solution.py:442
  62.3 7.7 %collective-permute-done.15.rest_4_ = f32[24,16,128]{2,1,0:T(8,128)S(1)} collective-permute-done((f32[24,16,128]{2,1,0:T(8,128)S(1)}, f32[24,16,128]{2,1,0:T(8,128)S(1)}, u32[]{:S(2)}, u32[]{:S(2)}) %collective-permute-start.15) | collective-permute-done | bytes 196640 | tf_op jit(solution)/shard_map/ppermute | solution.py:442
  69.9 0.0 collective-permute-done.17.rest_5_
  69.9 1.7 %update.3 = (f32[24,32,256]{2,1,0:T(8,128)S(1)}, f32[24,32,256]{2,1,0:T(8,128)S(1)}, f32[24,256]{1,0:T(8,128)S(1)}, f32[24,256]{1,0:T(8,128)S(1)}, f32[32,128]{1,0:T(8,128)S(1)}) custom-call(s32[19]{0:T(128)S(1)} %get-tuple-element.48.plan.rest_0_, f32[3,1,256]{2,1,0:T(1,128)S(1)} %get-tuple-element.49.rates, f32[24,32,256]{2,1,0:T(8,128)S(1)} %get-tuple-element.72.state, ...), custom_call_target="tpu_custom_call" | custom-call | tf_op jit(solution)/shard_map/update/pallas_call | solution.py:518
  71.6 0.6 collective-permute-start.19
  72.3 1.7 %collective-permute-start.20 = (f32[24,256]{1,0:T(8,128)S(1)}, f32[24,256]{1,0:T(8,128)S(1)}, u32[]{:S(2)}, u32[]{:S(2)}) collective-permute-start(f32[24,256]{1,0:T(8,128)S(1)} %get-tuple-element.87), channel_id=1, source_target_pairs={{0,2},{2,0},{4,6},{6,4},{1,3},{3,1},{5,7},{7,5},{8,10},{10,8},{12,... | collective-permute-start | bytes 73736 | tf_op jit(solution)/shard_map/ppermute | solution.py:532
  74.0 1.2 %spread_last.1.rest_0_ = f32[1,24,32,256]{3,2,1,0:T(8,128)S(1)} custom-call(f32[24,32,256]{2,1,0:T(8,128)S(1)} %get-tuple-element.84.wets, f32[24,32,256]{2,1,0:T(8,128)S(1)} %get-tuple-element.85.flux), custom_call_target="tpu_custom_call" | custom-call | tf_op jit(solution)/shard_map/spread_last/pallas_call | solution.py:535
  75.2 1.2 %collective-permute-done.19.rest_1_ = f32[24,256]{1,0:T(8,128)S(1)} collective-permute-done((f32[24,256]{1,0:T(8,128)S(1)}, f32[24,256]{1,0:T(8,128)S(1)}, u32[]{:S(2)}, u32[]{:S(2)}) %collective-permute-start.19) | collective-permute-done | bytes 24608 | tf_op jit(solution)/shard_map/ppermute | solution.py:532
  76.4 1.1 %halo_last.1 = f32[1,24,32,256]{3,2,1,0:T(8,128)} custom-call(f32[1,24,32,256]{3,2,1,0:T(8,128)S(1)} %spread_last.1.rest_0_, f32[24,256]{1,0:T(8,128)S(1)} %collective-permute-done.19.rest_1_, f32[24,256]{1,0:T(8,128)S(1)} %collective-permute-done.20.rest_2_, f32[32,128]{1,0:T(8,128)S(1)} %collective-permute-done.21.rest_3_), custom_call_target="tpu_custom_call" | custom-call | tf_op jit(solution)/shard_map/halo_last/pallas_call | solution.py:546
  (31 shorter events, 0.1 us)
Async XLA Ops:
  0.0 25.9 %copy-start = (f32[1,24,32,256]{3,2,1,0:T(8,128)S(1)}, f32[1,24,32,256]{3,2,1,0:T(8,128)}, u32[]{:S(2)}) copy-start(f32[1,24,32,256]{3,2,1,0:T(8,128)} %refs_0_.1) | copy-start | bytes 2359300
  3.3 12.6 %collective-permute-start = (f32[24,16,128]{2,1,0:T(8,128)}, f32[24,16,128]{2,1,0:T(8,128)S(1)}, u32[]{:S(2)}, u32[]{:S(2)}) collective-permute-start(f32[24,16,128]{2,1,0:T(8,128)} %get-tuple-element.56), channel_id=1, source_target_pairs={{0,8},{8,0},{2,10},{10,2},{4,12},{12,4},{6,14},{14,6},{1,9},{9,1},... | collective-permute-start | bytes 589832 | tf_op jit(solution)/shard_map/ppermute | solution.py:442
  7.9 9.9 %collective-permute-start.3 = (f32[24,16,128]{2,1,0:T(8,128)}, f32[24,16,128]{2,1,0:T(8,128)S(1)}, u32[]{:S(2)}, u32[]{:S(2)}) collective-permute-start(f32[24,16,128]{2,1,0:T(8,128)} %get-tuple-element.59), channel_id=1, source_target_pairs={{0,16},{16,0},{2,18},{18,2},{4,20},{20,4},{6,22},{22,6},{1,17},{17... | collective-permute-start | bytes 589832 | tf_op jit(solution)/shard_map/ppermute | solution.py:442
  9.9 12.9 %collective-permute-start.5 = (f32[24,16,128]{2,1,0:T(8,128)}, f32[24,16,128]{2,1,0:T(8,128)S(1)}, u32[]{:S(2)}, u32[]{:S(2)}) collective-permute-start(f32[24,16,128]{2,1,0:T(8,128)} %get-tuple-element.63), channel_id=1, source_target_pairs={{0,2},{2,0},{4,6},{6,4},{1,3},{3,1},{5,7},{7,5}} | collective-permute-start | bytes 589832 | tf_op jit(solution)/shard_map/ppermute | solution.py:433
  13.3 9.5 %copy-start.7 = (f32[8,128]{1,0:T(8,128)S(1)}, f32[8,128]{1,0:T(8,128)}, u32[]{:S(2)}) copy-start(f32[8,128]{1,0:T(8,128)} %get-tuple-element.47.token.mask) | copy-start | bytes 12292
  13.3 14.4 %collective-permute-start.1 = (f32[24,16,128]{2,1,0:T(8,128)}, f32[24,16,128]{2,1,0:T(8,128)S(1)}, u32[]{:S(2)}, u32[]{:S(2)}) collective-permute-start(f32[24,16,128]{2,1,0:T(8,128)} %get-tuple-element.57), channel_id=1, source_target_pairs={{0,10},{2,8},{4,14},{6,12},{1,11},{3,9},{5,15},{7,13}} | collective-permute-start | bytes 589832 | tf_op jit(solution)/shard_map/ppermute | solution.py:442
  14.6 13.1 %collective-permute-start.2 = (f32[24,16,128]{2,1,0:T(8,128)}, f32[24,16,128]{2,1,0:T(8,128)S(1)}, u32[]{:S(2)}, u32[]{:S(2)}) collective-permute-start(f32[24,16,128]{2,1,0:T(8,128)} %get-tuple-element.58), channel_id=1, source_target_pairs={{26,0},{24,2},{30,4},{28,6},{27,1},{25,3},{31,5},{29,7}} | collective-permute-start | bytes 589832 | tf_op jit(solution)/shard_map/ppermute | solution.py:442
  15.9 18.0 %collective-permute-start.4 = (f32[24,16,128]{2,1,0:T(8,128)}, f32[24,16,128]{2,1,0:T(8,128)S(1)}, u32[]{:S(2)}, u32[]{:S(2)}) collective-permute-start(f32[24,16,128]{2,1,0:T(8,128)} %get-tuple-element.61), channel_id=1, source_target_pairs={{0,18},{18,0},{2,16},{16,2},{4,22},{22,4},{6,20},{20,6},{1,19},{19... | collective-permute-start | bytes 589832 | tf_op jit(solution)/shard_map/ppermute | solution.py:442
  17.8 16.1 %collective-permute-start.7 = (f32[24,16,128]{2,1,0:T(8,128)S(1)}, f32[24,16,128]{2,1,0:T(8,128)S(1)}, u32[]{:S(2)}, u32[]{:S(2)}) collective-permute-start(f32[24,16,128]{2,1,0:T(8,128)S(1)} %collective-permute-done.rest_0_), channel_id=1, source_target_pairs={{0,2},{2,0},{4,6},{6,4},{1,3},{3,1},{5,7},{7,5}} | collective-permute-start | bytes 589832 | tf_op jit(solution)/shard_map/ppermute | solution.py:433
  22.8 0.9 %copy-start.1 = (f32[24,16,128]{2,1,0:T(8,128)S(1)}, f32[24,16,128]{2,1,0:T(8,128)}, u32[]{:S(2)}) copy-start(f32[24,16,128]{2,1,0:T(8,128)} %get-tuple-element.62.own) | copy-start | bytes 589828
  23.7 2.2 %copy-start.2 = (f32[1,32,256]{2,1,0:T(8,128)S(1)}, f32[1,32,256]{2,1,0:T(8,128)}, u32[]{:S(2)}) copy-start(f32[1,32,256]{2,1,0:T(8,128)} %refs_1_.1) | copy-start | bytes 98308
  23.7 2.2 %copy-start.3 = (f32[1,32,256]{2,1,0:T(8,128)S(1)}, f32[1,32,256]{2,1,0:T(8,128)}, u32[]{:S(2)}) copy-start(f32[1,32,256]{2,1,0:T(8,128)} %refs_2_.1) | copy-start | bytes 98308
  23.7 2.2 %copy-start.4 = (f32[1,32,256]{2,1,0:T(8,128)S(1)}, f32[1,32,256]{2,1,0:T(8,128)}, u32[]{:S(2)}) copy-start(f32[1,32,256]{2,1,0:T(8,128)} %refs_3_.3) | copy-start | bytes 98308
  23.7 2.2 %copy-start.5 = (s32[1,32,256]{2,1,0:T(8,128)S(1)}, s32[1,32,256]{2,1,0:T(8,128)}, u32[]{:S(2)}) copy-start(s32[1,32,256]{2,1,0:T(8,128)} %refs_4_.3) | copy-start | bytes 98308
  23.7 2.2 %copy-start.6 = (f32[1,32,256]{2,1,0:T(8,128)S(1)}, f32[1,32,256]{2,1,0:T(8,128)}, u32[]{:S(2)}) copy-start(f32[1,32,256]{2,1,0:T(8,128)} %refs_5_.1) | copy-start | bytes 98308
  23.8 2.2 %copy-start.8 = (s32[3,4,2]{1,2,0:T(2,128)S(1)}, s32[3,4,2]{1,2,0:T(2,128)}, u32[]{:S(2)}) copy-start(s32[3,4,2]{1,2,0:T(2,128)} %param.17) | copy-start | bytes 292
  23.8 2.2 %copy-start.9 = (s32[3,4,2]{1,2,0:T(2,128)S(1)}, s32[3,4,2]{1,2,0:T(2,128)}, u32[]{:S(2)}) copy-start(s32[3,4,2]{1,2,0:T(2,128)} %param.18) | copy-start | bytes 292
  23.8 2.2 %copy-start.10 = (s32[3,4,2]{1,2,0:T(2,128)S(1)}, s32[3,4,2]{1,2,0:T(2,128)}, u32[]{:S(2)}) copy-start(s32[3,4,2]{1,2,0:T(2,128)} %param.19) | copy-start | bytes 292
  23.8 2.2 %copy-start.11 = (f32[4,3]{1,0:T(4,128)S(1)}, f32[4,3]{1,0:T(4,128)}, u32[]{:S(2)}) copy-start(f32[4,3]{1,0:T(4,128)} %refs_6_.1) | copy-start | bytes 148
  23.8 10.1 %collective-permute-start.6 = (f32[24,16,128]{2,1,0:T(8,128)S(1)}, f32[24,16,128]{2,1,0:T(8,128)S(1)}, u32[]{:S(2)}, u32[]{:S(2)}) collective-permute-start(f32[24,16,128]{2,1,0:T(8,128)S(1)} %merge.2), channel_id=1, source_target_pairs={{0,24},{24,0},{2,26},{26,2},{4,28},{28,4},{6,30},{30,6},{1,25},{25... | collective-permute-start | bytes 589832 | tf_op jit(solution)/shard_map/ppermute | solution.py:442
  35.6 4.8 %collective-permute-start.8 = (f32[24,256]{1,0:T(8,128)S(1)}, f32[24,256]{1,0:T(8,128)S(1)}, u32[]{:S(2)}, u32[]{:S(2)}) collective-permute-start(f32[24,256]{1,0:T(8,128)S(1)} %get-tuple-element.69), channel_id=1, source_target_pairs={{2,4},{4,2},{6,0},{0,6},{3,5},{5,3},{7,1},{1,7},{10,12},{12,10},{1... | collective-permute-start | bytes 73736 | tf_op jit(solution)/shard_map/ppermute | solution.py:532
  37.1 4.1 %collective-permute-start.9 = (f32[24,256]{1,0:T(8,128)S(1)}, f32[24,256]{1,0:T(8,128)S(1)}, u32[]{:S(2)}, u32[]{:S(2)}) collective-permute-start(f32[24,256]{1,0:T(8,128)S(1)} %get-tuple-element.70), channel_id=1, source_target_pairs={{0,2},{2,0},{4,6},{6,4},{1,3},{3,1},{5,7},{7,5},{8,10},{10,8},{12,... | collective-permute-start | bytes 73736 | tf_op jit(solution)/shard_map/ppermute | solution.py:532
  39.1 1.3 %collective-permute-start.10 = (f32[32,128]{1,0:T(8,128)S(1)}, f32[32,128]{1,0:T(8,128)S(1)}, u32[]{:S(2)}, u32[]{:S(2)}) collective-permute-start(f32[32,128]{1,0:T(8,128)S(1)} %get-tuple-element.71), channel_id=1, source_target_pairs={{0,1},{1,0},{2,3},{3,2},{4,5},{5,4},{6,7},{7,6},{8,9},{9,8},{10,11... | collective-permute-start | bytes 49160 | tf_op jit(solution)/shard_map/ppermute | solution.py:533
  42.1 12.7 %collective-permute-start.11 = (f32[24,16,128]{2,1,0:T(8,128)S(1)}, f32[24,16,128]{2,1,0:T(8,128)S(1)}, u32[]{:S(2)}, u32[]{:S(2)}) collective-permute-start(f32[24,16,128]{2,1,0:T(8,128)S(1)} %get-tuple-element.73), channel_id=1, source_target_pairs={{0,8},{8,0},{2,10},{10,2},{4,12},{12,4},{6,14},{14,6},{1,9},{9,1},... | collective-permute-start | bytes 589832 | tf_op jit(solution)/shard_map/ppermute | solution.py:442
  45.3 11.4 %collective-permute-start.14 = (f32[24,16,128]{2,1,0:T(8,128)S(1)}, f32[24,16,128]{2,1,0:T(8,128)S(1)}, u32[]{:S(2)}, u32[]{:S(2)}) collective-permute-start(f32[24,16,128]{2,1,0:T(8,128)S(1)} %get-tuple-element.77), channel_id=1, source_target_pairs={{0,16},{16,0},{2,18},{18,2},{4,20},{20,4},{6,22},{22,6},{1,17},{17... | collective-permute-start | bytes 589832 | tf_op jit(solution)/shard_map/ppermute | solution.py:442
  47.2 12.1 %collective-permute-start.16 = (f32[24,16,128]{2,1,0:T(8,128)S(1)}, f32[24,16,128]{2,1,0:T(8,128)S(1)}, u32[]{:S(2)}, u32[]{:S(2)}) collective-permute-start(f32[24,16,128]{2,1,0:T(8,128)S(1)} %get-tuple-element.82), channel_id=1, source_target_pairs={{0,2},{2,0},{4,6},{6,4},{1,3},{3,1},{5,7},{7,5}} | collective-permute-start | bytes 589832 | tf_op jit(solution)/shard_map/ppermute | solution.py:433
  50.5 10.8 %collective-permute-start.12 = (f32[24,16,128]{2,1,0:T(8,128)S(1)}, f32[24,16,128]{2,1,0:T(8,128)S(1)}, u32[]{:S(2)}, u32[]{:S(2)}) collective-permute-start(f32[24,16,128]{2,1,0:T(8,128)S(1)} %get-tuple-element.75), channel_id=1, source_target_pairs={{0,10},{2,8},{4,14},{6,12},{1,11},{3,9},{5,15},{7,13}} | collective-permute-start | bytes 589832 | tf_op jit(solution)/shard_map/ppermute | solution.py:442
  51.8 10.5 %collective-permute-start.13 = (f32[24,16,128]{2,1,0:T(8,128)S(1)}, f32[24,16,128]{2,1,0:T(8,128)S(1)}, u32[]{:S(2)}, u32[]{:S(2)}) collective-permute-start(f32[24,16,128]{2,1,0:T(8,128)S(1)} %get-tuple-element.76), channel_id=1, source_target_pairs={{26,0},{24,2},{30,4},{28,6},{27,1},{25,3},{31,5},{29,7}} | collective-permute-start | bytes 589832 | tf_op jit(solution)/shard_map/ppermute | solution.py:442
  54.8 15.1 %collective-permute-start.15 = (f32[24,16,128]{2,1,0:T(8,128)S(1)}, f32[24,16,128]{2,1,0:T(8,128)S(1)}, u32[]{:S(2)}, u32[]{:S(2)}) collective-permute-start(f32[24,16,128]{2,1,0:T(8,128)S(1)} %get-tuple-element.79), channel_id=1, source_target_pairs={{0,18},{18,0},{2,16},{16,2},{4,22},{22,4},{6,20},{20,6},{1,19},{19... | collective-permute-start | bytes 589832 | tf_op jit(solution)/shard_map/ppermute | solution.py:442
  56.7 13.2 %collective-permute-start.18 = (f32[24,16,128]{2,1,0:T(8,128)S(1)}, f32[24,16,128]{2,1,0:T(8,128)S(1)}, u32[]{:S(2)}, u32[]{:S(2)}) collective-permute-start(f32[24,16,128]{2,1,0:T(8,128)S(1)} %collective-permute-done.11.rest_0_), channel_id=1, source_target_pairs={{0,2},{2,0},{4,6},{6,4},{1,3},{3,1},{5,7},{7,5}} | collective-permute-start | bytes 589832 | tf_op jit(solution)/shard_map/ppermute | solution.py:433
  59.4 10.6 %collective-permute-start.17 = (f32[24,16,128]{2,1,0:T(8,128)S(1)}, f32[24,16,128]{2,1,0:T(8,128)S(1)}, u32[]{:S(2)}, u32[]{:S(2)}) collective-permute-start(f32[24,16,128]{2,1,0:T(8,128)S(1)} %merge.3), channel_id=1, source_target_pairs={{0,24},{24,0},{2,26},{26,2},{4,28},{28,4},{6,30},{30,6},{1,25},{25... | collective-permute-start | bytes 589832 | tf_op jit(solution)/shard_map/ppermute | solution.py:442
  71.6 4.8 %collective-permute-start.19 = (f32[24,256]{1,0:T(8,128)S(1)}, f32[24,256]{1,0:T(8,128)S(1)}, u32[]{:S(2)}, u32[]{:S(2)}) collective-permute-start(f32[24,256]{1,0:T(8,128)S(1)} %get-tuple-element.86), channel_id=1, source_target_pairs={{2,4},{4,2},{6,0},{0,6},{3,5},{5,3},{7,1},{1,7},{10,12},{12,10},{1... | collective-permute-start | bytes 73736 | tf_op jit(solution)/shard_map/ppermute | solution.py:532
  72.3 4.2 %collective-permute-start.20 = (f32[24,256]{1,0:T(8,128)S(1)}, f32[24,256]{1,0:T(8,128)S(1)}, u32[]{:S(2)}, u32[]{:S(2)}) collective-permute-start(f32[24,256]{1,0:T(8,128)S(1)} %get-tuple-element.87), channel_id=1, source_target_pairs={{0,2},{2,0},{4,6},{6,4},{1,3},{3,1},{5,7},{7,5},{8,10},{10,8},{12,... | collective-permute-start | bytes 73736 | tf_op jit(solution)/shard_map/ppermute | solution.py:532
  74.0 1.3 %collective-permute-start.21 = (f32[32,128]{1,0:T(8,128)S(1)}, f32[32,128]{1,0:T(8,128)S(1)}, u32[]{:S(2)}, u32[]{:S(2)}) collective-permute-start(f32[32,128]{1,0:T(8,128)S(1)} %get-tuple-element.88), channel_id=1, source_target_pairs={{0,1},{1,0},{2,3},{3,2},{4,5},{5,4},{6,7},{7,6},{8,9},{9,8},{10,11... | collective-permute-start | bytes 49160 | tf_op jit(solution)/shard_map/ppermute | solution.py:533

commit v7 on v6

--- a/solution.py
+++ b/solution.py
@@ -28,7 +28,7 @@
 TURNED = 2
 FORWARDED = 0
 EARLY = ((FORWARDED, 0), (TURNED, 1))
-LATE = ((0, 1), (2, 1), (1, 0), (1, 1), (2, 0))
+LATE = ((1, 0), (2, 1), (0, 1), (1, 1), (2, 0))
 GOT = (EARLY[0],) + LATE
 
 
@@ -459,7 +459,7 @@
         with_children(blocks[slot, kind], slot, kind, up=(slot, kind) != (FORWARDED, 1), down=(slot, kind) != (TURNED, 1))
         for slot, kind in GOT
     ]
-    forward, got[3] = lax.optimization_barrier((got[0], got[3]))
+    forward, got[1] = lax.optimization_barrier((got[0], got[1]))
     return got + [between_parents(forward)]
 
 

time: 78.3 us -> 76.6 us (0.978)
  starting transfers between devices: 43.3 us -> 40 us
  waiting for transfers between devices: 18.6 us -> 20 us
  Pallas kernels: 14.2 us -> 15 us
    ppermute x12, waiting for transfers between devices: 16.6 us -> 11.6 us  [with_children(): return lax.ppermute(block, ('grid', 'gx'), pairs)]
    ppermute x4, waiting for transfers between devices: 0.01 us -> 3.92 us  [between_parents(): lax.ppermute(block, ('grid', 'gx'), [(i, i ^ 1) for i in range(lax.axis_s...]
    ppermute x4, waiting for transfers between devices: 2 us -> 4.46 us  [local(): lax.ppermute(sides[k], 'gx', swap_pairs(n_x, 1 - k))]
    ppermute x4, starting transfers between devices: 5.76 us -> 3.95 us  [local(): lax.ppermute(sides[k], 'gx', swap_pairs(n_x, 1 - k))]
    ppermute x4, starting transfers between devices: 14.1 us -> 12.9 us  [between_parents(): lax.ppermute(block, ('grid', 'gx'), [(i, i ^ 1) for i in range(lax.axis_s...]
  transfers between devices with their start and end apart: 22 -> 22, of which waited for: 7 -> 10; matrix products, arithmetic and copies ran while one was open for 0% -> 0% of each run, Pallas kernels for 7% -> 7%
where the time goes in v7:
time: 76.6 us; the launch traced here: 76.4 us
  starting transfers between devices  40 us (52%)
  waiting for transfers between devices  20 us (26%)
  Pallas kernels  15 us (20%)
  local copies, waits for them, and re-layouts  0.97 us (1%)
    ppermute x12, starting transfers between devices, with_children(): return lax.ppermute(block, ('grid', 'gx'), pairs)  23.2 us
    ppermute x4, starting transfers between devices, between_parents(): lax.ppermute(block, ('grid', 'gx'), [(i, i ^ 1) for i in range(lax.axis_s...  12.9 us
    ppermute x12, waiting for transfers between devices, with_children(): return lax.ppermute(block, ('grid', 'gx'), pairs)  11.6 us
    ppermute x4, waiting for transfers between devices, local(): lax.ppermute(sides[k], 'gx', swap_pairs(n_x, 1 - k))  4.46 us
    ppermute x4, starting transfers between devices, local(): lax.ppermute(sides[k], 'gx', swap_pairs(n_x, 1 - k))  3.95 us
    ppermute x4, waiting for transfers between devices, between_parents(): lax.ppermute(block, ('grid', 'gx'), [(i, i ^ 1) for i in range(lax.axis_s...  3.92 us
    pallas_call x2, Pallas kernels, local(): pl.pallas_call(functools.partial(update_kernel, n_cols), out_shape=[tile]...  3.67 us
    pallas_call x1, Pallas kernels, local(): pl.pallas_call(first_kernel, out_shape=[block] * 2 + [flag] + [block] * 5...  3.47 us
  transfers between devices with their start and end apart: 22, of which 10 were waited for; matrix products, arithmetic and copies ran while one was open for 0% of the time, Pallas kernels for 7%

profile of v7, /device:TPU:0, one launch (start us, length us, event | category | flops | bytes accessed | tf_op | source)
XLA Modules:
  0.0 76.4 jit_solution(15942695627263279043)
XLA Ops:
  0.0 3.5 %first_payload.1 = (f32[24,16,128]{2,1,0:T(8,128)}, f32[24,16,128]{2,1,0:T(8,128)}, f32[8,128]{1,0:T(8,128)}, f32[24,16,128]{2,1,0:T(8,128)}, f32[24,16,128]{2,1...) custom-call(s32[3,2,4]{2,1,0:T(2,128)} %bitcast.5, s32[3,2,4]{2,1,0:T(2,128)} %bitcast.7, ...), custom_call_target="tpu_custom_call" | custom-call | tf_op jit(solution)/shard_map/first_payload/pallas_call | solution.py:487
  3.5 4.4 %collective-permute-start = (f32[24,16,128]{2,1,0:T(8,128)}, f32[24,16,128]{2,1,0:T(8,128)S(1)}, u32[]{:S(2)}, u32[]{:S(2)}) collective-permute-start(f32[24,16,128]{2,1,0:T(8,128)} %get-tuple-element.56), channel_id=1, source_target_pairs={{0,8},{8,0},{2,10},{10,2},{4,12},{12,4},{6,14},{14,6},{1,9},{9,1},... | collective-permute-start | bytes 589832 | tf_op jit(solution)/shard_map/ppermute | solution.py:442
  7.9 1.9 %collective-permute-start.1 = (f32[24,16,128]{2,1,0:T(8,128)}, f32[24,16,128]{2,1,0:T(8,128)S(1)}, u32[]{:S(2)}, u32[]{:S(2)}) collective-permute-start(f32[24,16,128]{2,1,0:T(8,128)} %get-tuple-element.57), channel_id=1, source_target_pairs={{0,16},{16,0},{2,18},{18,2},{4,20},{20,4},{6,22},{22,6},{1,17},{17... | collective-permute-start | bytes 589832 | tf_op jit(solution)/shard_map/ppermute | solution.py:442
  9.9 3.4 %collective-permute-start.5 = (f32[24,16,128]{2,1,0:T(8,128)}, f32[24,16,128]{2,1,0:T(8,128)S(1)}, u32[]{:S(2)}, u32[]{:S(2)}) collective-permute-start(f32[24,16,128]{2,1,0:T(8,128)} %get-tuple-element.63), channel_id=1, source_target_pairs={{0,2},{2,0},{4,6},{6,4},{1,3},{3,1},{5,7},{7,5}} | collective-permute-start | bytes 589832 | tf_op jit(solution)/shard_map/ppermute | solution.py:433
  13.3 1.3 %collective-permute-start.2 = (f32[24,16,128]{2,1,0:T(8,128)}, f32[24,16,128]{2,1,0:T(8,128)S(1)}, u32[]{:S(2)}, u32[]{:S(2)}) collective-permute-start(f32[24,16,128]{2,1,0:T(8,128)} %get-tuple-element.59), channel_id=1, source_target_pairs={{26,0},{24,2},{30,4},{28,6},{27,1},{25,3},{31,5},{29,7}} | collective-permute-start | bytes 589832 | tf_op jit(solution)/shard_map/ppermute | solution.py:442
  14.6 1.3 %collective-permute-start.3 = (f32[24,16,128]{2,1,0:T(8,128)}, f32[24,16,128]{2,1,0:T(8,128)S(1)}, u32[]{:S(2)}, u32[]{:S(2)}) collective-permute-start(f32[24,16,128]{2,1,0:T(8,128)} %get-tuple-element.60), channel_id=1, source_target_pairs={{0,10},{2,8},{4,14},{6,12},{1,11},{3,9},{5,15},{7,13}} | collective-permute-start | bytes 589832 | tf_op jit(solution)/shard_map/ppermute | solution.py:442
  15.9 1.9 %collective-permute-start.4 = (f32[24,16,128]{2,1,0:T(8,128)}, f32[24,16,128]{2,1,0:T(8,128)S(1)}, u32[]{:S(2)}, u32[]{:S(2)}) collective-permute-start(f32[24,16,128]{2,1,0:T(8,128)} %get-tuple-element.61), channel_id=1, source_target_pairs={{0,18},{18,0},{2,16},{16,2},{4,22},{22,4},{6,20},{20,6},{1,19},{19... | collective-permute-start | bytes 589832 | tf_op jit(solution)/shard_map/ppermute | solution.py:442
  17.8 0.0 collective-permute-done.1.rest_1_
  17.8 4.9 %collective-permute-start.7 = (f32[24,16,128]{2,1,0:T(8,128)S(1)}, f32[24,16,128]{2,1,0:T(8,128)S(1)}, u32[]{:S(2)}, u32[]{:S(2)}) collective-permute-start(f32[24,16,128]{2,1,0:T(8,128)S(1)} %collective-permute-done.rest_0_), channel_id=1, source_target_pairs={{0,2},{2,0},{4,6},{6,4},{1,3},{3,1},{5,7},{7,5}} | collective-permute-start | bytes 589832 | tf_op jit(solution)/shard_map/ppermute | solution.py:433
  22.8 0.9 %copy-done.1 = f32[24,16,128]{2,1,0:T(8,128)S(1)} copy-done((f32[24,16,128]{2,1,0:T(8,128)S(1)}, f32[24,16,128]{2,1,0:T(8,128)}, u32[]{:S(2)}) %copy-start.1) | copy-done | bytes 196632
  23.7 0.0 copy-start.6
  23.7 0.0 copy-start.8
  23.7 0.0 copy-start.9
  23.8 0.0 copy-start.10
  23.8 0.0 copy-start.11
  23.8 2.1 %collective-permute-start.6 = (f32[24,16,128]{2,1,0:T(8,128)S(1)}, f32[24,16,128]{2,1,0:T(8,128)S(1)}, u32[]{:S(2)}, u32[]{:S(2)}) collective-permute-start(f32[24,16,128]{2,1,0:T(8,128)S(1)} %merge.2), channel_id=1, source_target_pairs={{0,24},{24,0},{2,26},{26,2},{4,28},{28,4},{6,30},{30,6},{1,25},{25... | collective-permute-start | bytes 589832 | tf_op jit(solution)/shard_map/ppermute | solution.py:442
  26.0 1.7 %stage_fields.1 = (f32[1,24,32,256]{3,2,1,0:T(8,128)S(1)}, f32[1,32,256]{2,1,0:T(8,128)S(1)}, f32[1,32,256]{2,1,0:T(8,128)S(1)}, f32[1,32,256]{2,1,0:T(8,128)S(1...) custom-call(f32[8,128]{1,0:T(8,128)S(1)} %copy-done.7, ...), custom_call_target="tpu_custom_call" | custom-call | tf_op jit(solution)/shard_map/stage_fields/pallas_call | solution.py:500
  27.7 0.0 collective-permute-done.3.rest_3_
  27.7 2.9 %collective-permute-done.4.rest_4_ = f32[24,16,128]{2,1,0:T(8,128)S(1)} collective-permute-done((f32[24,16,128]{2,1,0:T(8,128)}, f32[24,16,128]{2,1,0:T(8,128)S(1)}, u32[]{:S(2)}, u32[]{:S(2)}) %collective-permute-start.4) | collective-permute-done | bytes 196640 | tf_op jit(solution)/shard_map/ppermute | solution.py:442
  30.6 2.0 %collective-permute-done.7.rest_6_ = f32[24,16,128]{2,1,0:T(8,128)S(1)} collective-permute-done((f32[24,16,128]{2,1,0:T(8,128)S(1)}, f32[24,16,128]{2,1,0:T(8,128)S(1)}, u32[]{:S(2)}, u32[]{:S(2)}) %collective-permute-start.7) | collective-permute-done | bytes 196640 | tf_op jit(solution)/shard_map/ppermute | solution.py:433
  32.6 0.7 collective-permute-done.6.rest_5_
  33.3 1.8 %update.2 = (f32[24,32,256]{2,1,0:T(8,128)S(1)}, f32[24,32,256]{2,1,0:T(8,128)S(1)}, f32[24,256]{1,0:T(8,128)S(1)}, f32[24,256]{1,0:T(8,128)S(1)}, f32[32,128]{1,0:T(8,128)S(1)}) custom-call(s32[19]{0:T(128)S(1)} %get-tuple-element.48.plan.rest_0_, f32[3,1,256]{2,1,0:T(1,128)S(1)} %get-tuple-element.49.rates, f32[24,32,256]{2,1,0:T(8,128)S(1)} %bitcast.4, ...), custom_call_target="tpu_custom_call" | custom-call | tf_op jit(solution)/shard_map/update/pallas_call | solution.py:518
  35.1 1.7 %collective-permute-start.8 = (f32[24,256]{1,0:T(8,128)S(1)}, f32[24,256]{1,0:T(8,128)S(1)}, u32[]{:S(2)}, u32[]{:S(2)}) collective-permute-start(f32[24,256]{1,0:T(8,128)S(1)} %get-tuple-element.69), channel_id=1, source_target_pairs={{2,4},{4,2},{6,0},{0,6},{3,5},{5,3},{7,1},{1,7},{10,12},{12,10},{1... | collective-permute-start | bytes 73736 | tf_op jit(solution)/shard_map/ppermute | solution.py:532
  36.9 0.3 collective-permute-start.9
  37.2 1.2 %spread.1 = (f32[24,32,256]{2,1,0:T(8,128)S(1)}, f32[24,16,128]{2,1,0:T(8,128)S(1)}) custom-call(f32[24,32,256]{2,1,0:T(8,128)S(1)} %get-tuple-element.65.wets, f32[24,32,256]{2,1,0:T(8,128)S(1)} %get-tuple-element.66.flux, f32[1,32,256]{2,1,0:T(8,128)S(1)} %get-tuple-element.51.sponge.rest_0_.rest_2_), custom_call_target="tpu_custom_call" | custom-call | tf_op jit(solution)/shard_map/spread/pallas_call | solution.py:535
  38.4 0.0 collective-permute-done.10.rest_6_
  38.5 1.5 %collective-permute-done.8.rest_4_ = f32[24,256]{1,0:T(8,128)S(1)} collective-permute-done((f32[24,256]{1,0:T(8,128)S(1)}, f32[24,256]{1,0:T(8,128)S(1)}, u32[]{:S(2)}, u32[]{:S(2)}) %collective-permute-start.8) | collective-permute-done | bytes 24608 | tf_op jit(solution)/shard_map/ppermute | solution.py:532
  39.9 0.8 collective-permute-done.9.rest_5_
  40.7 1.2 %halo.1 = (f32[24,32,256]{2,1,0:T(8,128)S(1)}, f32[24,16,128]{2,1,0:T(8,128)S(1)}, f32[24,16,128]{2,1,0:T(8,128)S(1)}, f32[8,128]{1,0:T(8,128)S(1)}, f32[80,128]{1,0:T(8,128)S(1)}) custom-call(s32[19]{0:T(128)S(1)} %get-tuple-element.48.plan.rest_0_, f32[24,32,256]{2,1,0:T(8,128)S(1)} %get-tuple-element.67.rest_1_, ...), custom_call_target="tpu_custom_call" | custom-call | tf_op jit(solution)/shard_map/halo/pallas_call | solution.py:546
  41.9 1.9 %collective-permute-start.11 = (f32[24,16,128]{2,1,0:T(8,128)S(1)}, f32[24,16,128]{2,1,0:T(8,128)S(1)}, u32[]{:S(2)}, u32[]{:S(2)}) collective-permute-start(f32[24,16,128]{2,1,0:T(8,128)S(1)} %get-tuple-element.73), channel_id=1, source_target_pairs={{0,8},{8,0},{2,10},{10,2},{4,12},{12,4},{6,14},{14,6},{1,9},{9,1},... | collective-permute-start | bytes 589832 | tf_op jit(solution)/shard_map/ppermute | solution.py:442
  43.8 1.2 %late_payload.1 = (f32[24,16,128]{2,1,0:T(8,128)S(1)}, f32[24,16,128]{2,1,0:T(8,128)S(1)}, f32[24,16,128]{2,1,0:T(8,128)S(1)}, f32[24,16,128]{2,1,0:T(8,128)S(1)}, f32[24,16,128]{2,1,0:T(8,128)S(1)}) custom-call(s32[19]{0:T(128)S(1)} %get-tuple-element.48.plan.rest_0_, f32[24,32,256]{2,1,0:T(8,128)S(1)} %get-tuple-element.72.state, ...), custom_call_target="tpu_custom_call" | custom-call | tf_op jit(solution)/shard_map/late_payload/pallas_call | solution.py:557
  45.1 1.9 %collective-permute-start.12 = (f32[24,16,128]{2,1,0:T(8,128)S(1)}, f32[24,16,128]{2,1,0:T(8,128)S(1)}, u32[]{:S(2)}, u32[]{:S(2)}) collective-permute-start(f32[24,16,128]{2,1,0:T(8,128)S(1)} %get-tuple-element.75), channel_id=1, source_target_pairs={{0,16},{16,0},{2,18},{18,2},{4,20},{20,4},{6,22},{22,6},{1,17},{17... | collective-permute-start | bytes 589832 | tf_op jit(solution)/shard_map/ppermute | solution.py:442
  47.0 1.9 %collective-permute-start.16 = (f32[24,16,128]{2,1,0:T(8,128)S(1)}, f32[24,16,128]{2,1,0:T(8,128)S(1)}, u32[]{:S(2)}, u32[]{:S(2)}) collective-permute-start(f32[24,16,128]{2,1,0:T(8,128)S(1)} %get-tuple-element.82), channel_id=1, source_target_pairs={{0,2},{2,0},{4,6},{6,4},{1,3},{3,1},{5,7},{7,5}} | collective-permute-start | bytes 589832 | tf_op jit(solution)/shard_map/ppermute | solution.py:433
  48.9 1.3 %collective-permute-start.13 = (f32[24,16,128]{2,1,0:T(8,128)S(1)}, f32[24,16,128]{2,1,0:T(8,128)S(1)}, u32[]{:S(2)}, u32[]{:S(2)}) collective-permute-start(f32[24,16,128]{2,1,0:T(8,128)S(1)} %get-tuple-element.77), channel_id=1, source_target_pairs={{26,0},{24,2},{30,4},{28,6},{27,1},{25,3},{31,5},{29,7}} | collective-permute-start | bytes 589832 | tf_op jit(solution)/shard_map/ppermute | solution.py:442
  50.2 1.3 %collective-permute-start.14 = (f32[24,16,128]{2,1,0:T(8,128)S(1)}, f32[24,16,128]{2,1,0:T(8,128)S(1)}, u32[]{:S(2)}, u32[]{:S(2)}) collective-permute-start(f32[24,16,128]{2,1,0:T(8,128)S(1)} %get-tuple-element.78), channel_id=1, source_target_pairs={{0,10},{2,8},{4,14},{6,12},{1,11},{3,9},{5,15},{7,13}} | collective-permute-start | bytes 589832 | tf_op jit(solution)/shard_map/ppermute | solution.py:442
  51.6 2.1 %collective-permute-done.11.rest_0_ = f32[24,16,128]{2,1,0:T(8,128)S(1)} collective-permute-done((f32[24,16,128]{2,1,0:T(8,128)S(1)}, f32[24,16,128]{2,1,0:T(8,128)S(1)}, u32[]{:S(2)}, u32[]{:S(2)}) %collective-permute-start.11) | collective-permute-done | bytes 196640 | tf_op jit(solution)/shard_map/ppermute | solution.py:442
  53.7 1.9 %collective-permute-start.15 = (f32[24,16,128]{2,1,0:T(8,128)S(1)}, f32[24,16,128]{2,1,0:T(8,128)S(1)}, u32[]{:S(2)}, u32[]{:S(2)}) collective-permute-start(f32[24,16,128]{2,1,0:T(8,128)S(1)} %get-tuple-element.79), channel_id=1, source_target_pairs={{0,18},{18,0},{2,16},{16,2},{4,22},{22,4},{6,20},{20,6},{1,19},{19... | collective-permute-start | bytes 589832 | tf_op jit(solution)/shard_map/ppermute | solution.py:442
  55.6 2.6 %collective-permute-start.18 = (f32[24,16,128]{2,1,0:T(8,128)S(1)}, f32[24,16,128]{2,1,0:T(8,128)S(1)}, u32[]{:S(2)}, u32[]{:S(2)}) collective-permute-start(f32[24,16,128]{2,1,0:T(8,128)S(1)} %collective-permute-done.11.rest_0_), channel_id=1, source_target_pairs={{0,2},{2,0},{4,6},{6,4},{1,3},{3,1},{5,7},{7,5}} | collective-permute-start | bytes 589832 | tf_op jit(solution)/shard_map/ppermute | solution.py:433
  58.3 1.9 %collective-permute-start.17 = (f32[24,16,128]{2,1,0:T(8,128)S(1)}, f32[24,16,128]{2,1,0:T(8,128)S(1)}, u32[]{:S(2)}, u32[]{:S(2)}) collective-permute-start(f32[24,16,128]{2,1,0:T(8,128)S(1)} %merge.3), channel_id=1, source_target_pairs={{0,24},{24,0},{2,26},{26,2},{4,28},{28,4},{6,30},{30,6},{1,25},{25... | collective-permute-start | bytes 589832 | tf_op jit(solution)/shard_map/ppermute | solution.py:442
  60.2 5.9 %collective-permute-done.15.rest_4_ = f32[24,16,128]{2,1,0:T(8,128)S(1)} collective-permute-done((f32[24,16,128]{2,1,0:T(8,128)S(1)}, f32[24,16,128]{2,1,0:T(8,128)S(1)}, u32[]{:S(2)}, u32[]{:S(2)}) %collective-permute-start.15) | collective-permute-done | bytes 196640 | tf_op jit(solution)/shard_map/ppermute | solution.py:442
  66.1 2.0 %collective-permute-done.18.rest_6_ = f32[24,16,128]{2,1,0:T(8,128)S(1)} collective-permute-done((f32[24,16,128]{2,1,0:T(8,128)S(1)}, f32[24,16,128]{2,1,0:T(8,128)S(1)}, u32[]{:S(2)}, u32[]{:S(2)}) %collective-permute-start.18) | collective-permute-done | bytes 196640 | tf_op jit(solution)/shard_map/ppermute | solution.py:433
  68.1 1.8 %update.3 = (f32[24,32,256]{2,1,0:T(8,128)S(1)}, f32[24,32,256]{2,1,0:T(8,128)S(1)}, f32[24,256]{1,0:T(8,128)S(1)}, f32[24,256]{1,0:T(8,128)S(1)}, f32[32,128]{1,0:T(8,128)S(1)}) custom-call(s32[19]{0:T(128)S(1)} %get-tuple-element.48.plan.rest_0_, f32[3,1,256]{2,1,0:T(1,128)S(1)} %get-tuple-element.49.rates, f32[24,32,256]{2,1,0:T(8,128)S(1)} %get-tuple-element.72.state, ...), custom_call_target="tpu_custom_call" | custom-call | tf_op jit(solution)/shard_map/update/pallas_call | solution.py:518
  69.9 1.6 %collective-permute-start.19 = (f32[24,256]{1,0:T(8,128)S(1)}, f32[24,256]{1,0:T(8,128)S(1)}, u32[]{:S(2)}, u32[]{:S(2)}) collective-permute-start(f32[24,256]{1,0:T(8,128)S(1)} %get-tuple-element.86), channel_id=1, source_target_pairs={{2,4},{4,2},{6,0},{0,6},{3,5},{5,3},{7,1},{1,7},{10,12},{12,10},{1... | collective-permute-start | bytes 73736 | tf_op jit(solution)/shard_map/ppermute | solution.py:532
  71.5 0.3 collective-permute-start.20
  71.8 1.2 %spread_last.1.rest_0_ = f32[1,24,32,256]{3,2,1,0:T(8,128)S(1)} custom-call(f32[24,32,256]{2,1,0:T(8,128)S(1)} %get-tuple-element.84.wets, f32[24,32,256]{2,1,0:T(8,128)S(1)} %get-tuple-element.85.flux), custom_call_target="tpu_custom_call" | custom-call | tf_op jit(solution)/shard_map/spread_last/pallas_call | solution.py:535
  73.1 1.6 %collective-permute-done.19.rest_1_ = f32[24,256]{1,0:T(8,128)S(1)} collective-permute-done((f32[24,256]{1,0:T(8,128)S(1)}, f32[24,256]{1,0:T(8,128)S(1)}, u32[]{:S(2)}, u32[]{:S(2)}) %collective-permute-start.19) | collective-permute-done | bytes 24608 | tf_op jit(solution)/shard_map/ppermute | solution.py:532
  74.7 0.6 collective-permute-done.20.rest_2_
  75.3 1.1 %halo_last.1 = f32[1,24,32,256]{3,2,1,0:T(8,128)} custom-call(f32[1,24,32,256]{3,2,1,0:T(8,128)S(1)} %spread_last.1.rest_0_, f32[24,256]{1,0:T(8,128)S(1)} %collective-permute-done.19.rest_1_, f32[24,256]{1,0:T(8,128)S(1)} %collective-permute-done.20.rest_2_, f32[32,128]{1,0:T(8,128)S(1)} %collective-permute-done.21.rest_3_), custom_call_target="tpu_custom_call" | custom-call | tf_op jit(solution)/shard_map/halo_last/pallas_call | solution.py:546
  (31 shorter events, 0.1 us)
Async XLA Ops:
  0.0 25.9 %copy-start = (f32[1,24,32,256]{3,2,1,0:T(8,128)S(1)}, f32[1,24,32,256]{3,2,1,0:T(8,128)}, u32[]{:S(2)}) copy-start(f32[1,24,32,256]{3,2,1,0:T(8,128)} %refs_0_.1) | copy-start | bytes 2359300
  3.5 12.4 %collective-permute-start = (f32[24,16,128]{2,1,0:T(8,128)}, f32[24,16,128]{2,1,0:T(8,128)S(1)}, u32[]{:S(2)}, u32[]{:S(2)}) collective-permute-start(f32[24,16,128]{2,1,0:T(8,128)} %get-tuple-element.56), channel_id=1, source_target_pairs={{0,8},{8,0},{2,10},{10,2},{4,12},{12,4},{6,14},{14,6},{1,9},{9,1},... | collective-permute-start | bytes 589832 | tf_op jit(solution)/shard_map/ppermute | solution.py:442
  7.9 9.9 %collective-permute-start.1 = (f32[24,16,128]{2,1,0:T(8,128)}, f32[24,16,128]{2,1,0:T(8,128)S(1)}, u32[]{:S(2)}, u32[]{:S(2)}) collective-permute-start(f32[24,16,128]{2,1,0:T(8,128)} %get-tuple-element.57), channel_id=1, source_target_pairs={{0,16},{16,0},{2,18},{18,2},{4,20},{20,4},{6,22},{22,6},{1,17},{17... | collective-permute-start | bytes 589832 | tf_op jit(solution)/shard_map/ppermute | solution.py:442
  9.9 12.9 %collective-permute-start.5 = (f32[24,16,128]{2,1,0:T(8,128)}, f32[24,16,128]{2,1,0:T(8,128)S(1)}, u32[]{:S(2)}, u32[]{:S(2)}) collective-permute-start(f32[24,16,128]{2,1,0:T(8,128)} %get-tuple-element.63), channel_id=1, source_target_pairs={{0,2},{2,0},{4,6},{6,4},{1,3},{3,1},{5,7},{7,5}} | collective-permute-start | bytes 589832 | tf_op jit(solution)/shard_map/ppermute | solution.py:433
  13.3 9.5 %copy-start.7 = (f32[8,128]{1,0:T(8,128)S(1)}, f32[8,128]{1,0:T(8,128)}, u32[]{:S(2)}) copy-start(f32[8,128]{1,0:T(8,128)} %get-tuple-element.47.token.mask) | copy-start | bytes 12292
  13.3 14.4 %collective-permute-start.2 = (f32[24,16,128]{2,1,0:T(8,128)}, f32[24,16,128]{2,1,0:T(8,128)S(1)}, u32[]{:S(2)}, u32[]{:S(2)}) collective-permute-start(f32[24,16,128]{2,1,0:T(8,128)} %get-tuple-element.59), channel_id=1, source_target_pairs={{26,0},{24,2},{30,4},{28,6},{27,1},{25,3},{31,5},{29,7}} | collective-permute-start | bytes 589832 | tf_op jit(solution)/shard_map/ppermute | solution.py:442
  14.6 13.1 %collective-permute-start.3 = (f32[24,16,128]{2,1,0:T(8,128)}, f32[24,16,128]{2,1,0:T(8,128)S(1)}, u32[]{:S(2)}, u32[]{:S(2)}) collective-permute-start(f32[24,16,128]{2,1,0:T(8,128)} %get-tuple-element.60), channel_id=1, source_target_pairs={{0,10},{2,8},{4,14},{6,12},{1,11},{3,9},{5,15},{7,13}} | collective-permute-start | bytes 589832 | tf_op jit(solution)/shard_map/ppermute | solution.py:442
  15.9 14.7 %collective-permute-start.4 = (f32[24,16,128]{2,1,0:T(8,128)}, f32[24,16,128]{2,1,0:T(8,128)S(1)}, u32[]{:S(2)}, u32[]{:S(2)}) collective-permute-start(f32[24,16,128]{2,1,0:T(8,128)} %get-tuple-element.61), channel_id=1, source_target_pairs={{0,18},{18,0},{2,16},{16,2},{4,22},{22,4},{6,20},{20,6},{1,19},{19... | collective-permute-start | bytes 589832 | tf_op jit(solution)/shard_map/ppermute | solution.py:442
  17.8 14.7 %collective-permute-start.7 = (f32[24,16,128]{2,1,0:T(8,128)S(1)}, f32[24,16,128]{2,1,0:T(8,128)S(1)}, u32[]{:S(2)}, u32[]{:S(2)}) collective-permute-start(f32[24,16,128]{2,1,0:T(8,128)S(1)} %collective-permute-done.rest_0_), channel_id=1, source_target_pairs={{0,2},{2,0},{4,6},{6,4},{1,3},{3,1},{5,7},{7,5}} | collective-permute-start | bytes 589832 | tf_op jit(solution)/shard_map/ppermute | solution.py:433
  22.8 0.9 %copy-start.1 = (f32[24,16,128]{2,1,0:T(8,128)S(1)}, f32[24,16,128]{2,1,0:T(8,128)}, u32[]{:S(2)}) copy-start(f32[24,16,128]{2,1,0:T(8,128)} %get-tuple-element.62.own) | copy-start | bytes 589828
  23.7 2.2 %copy-start.2 = (f32[1,32,256]{2,1,0:T(8,128)S(1)}, f32[1,32,256]{2,1,0:T(8,128)}, u32[]{:S(2)}) copy-start(f32[1,32,256]{2,1,0:T(8,128)} %refs_1_.1) | copy-start | bytes 98308
  23.7 2.2 %copy-start.3 = (f32[1,32,256]{2,1,0:T(8,128)S(1)}, f32[1,32,256]{2,1,0:T(8,128)}, u32[]{:S(2)}) copy-start(f32[1,32,256]{2,1,0:T(8,128)} %refs_2_.1) | copy-start | bytes 98308
  23.7 2.2 %copy-start.4 = (f32[1,32,256]{2,1,0:T(8,128)S(1)}, f32[1,32,256]{2,1,0:T(8,128)}, u32[]{:S(2)}) copy-start(f32[1,32,256]{2,1,0:T(8,128)} %refs_3_.3) | copy-start | bytes 98308
  23.7 2.2 %copy-start.5 = (s32[1,32,256]{2,1,0:T(8,128)S(1)}, s32[1,32,256]{2,1,0:T(8,128)}, u32[]{:S(2)}) copy-start(s32[1,32,256]{2,1,0:T(8,128)} %refs_4_.3) | copy-start | bytes 98308
  23.7 2.2 %copy-start.6 = (f32[1,32,256]{2,1,0:T(8,128)S(1)}, f32[1,32,256]{2,1,0:T(8,128)}, u32[]{:S(2)}) copy-start(f32[1,32,256]{2,1,0:T(8,128)} %refs_5_.1) | copy-start | bytes 98308
  23.7 2.2 %copy-start.8 = (s32[3,4,2]{1,2,0:T(2,128)S(1)}, s32[3,4,2]{1,2,0:T(2,128)}, u32[]{:S(2)}) copy-start(s32[3,4,2]{1,2,0:T(2,128)} %param.17) | copy-start | bytes 292
  23.7 2.2 %copy-start.9 = (s32[3,4,2]{1,2,0:T(2,128)S(1)}, s32[3,4,2]{1,2,0:T(2,128)}, u32[]{:S(2)}) copy-start(s32[3,4,2]{1,2,0:T(2,128)} %param.18) | copy-start | bytes 292
  23.8 2.2 %copy-start.10 = (s32[3,4,2]{1,2,0:T(2,128)S(1)}, s32[3,4,2]{1,2,0:T(2,128)}, u32[]{:S(2)}) copy-start(s32[3,4,2]{1,2,0:T(2,128)} %param.19) | copy-start | bytes 292
  23.8 2.2 %copy-start.11 = (f32[4,3]{1,0:T(4,128)S(1)}, f32[4,3]{1,0:T(4,128)}, u32[]{:S(2)}) copy-start(f32[4,3]{1,0:T(4,128)} %refs_6_.1) | copy-start | bytes 148
  23.8 9.5 %collective-permute-start.6 = (f32[24,16,128]{2,1,0:T(8,128)S(1)}, f32[24,16,128]{2,1,0:T(8,128)S(1)}, u32[]{:S(2)}, u32[]{:S(2)}) collective-permute-start(f32[24,16,128]{2,1,0:T(8,128)S(1)} %merge.2), channel_id=1, source_target_pairs={{0,24},{24,0},{2,26},{26,2},{4,28},{28,4},{6,30},{30,6},{1,25},{25... | collective-permute-start | bytes 589832 | tf_op jit(solution)/shard_map/ppermute | solution.py:442
  35.1 4.8 %collective-permute-start.8 = (f32[24,256]{1,0:T(8,128)S(1)}, f32[24,256]{1,0:T(8,128)S(1)}, u32[]{:S(2)}, u32[]{:S(2)}) collective-permute-start(f32[24,256]{1,0:T(8,128)S(1)} %get-tuple-element.69), channel_id=1, source_target_pairs={{2,4},{4,2},{6,0},{0,6},{3,5},{5,3},{7,1},{1,7},{10,12},{12,10},{1... | collective-permute-start | bytes 73736 | tf_op jit(solution)/shard_map/ppermute | solution.py:532
  36.9 3.8 %collective-permute-start.9 = (f32[24,256]{1,0:T(8,128)S(1)}, f32[24,256]{1,0:T(8,128)S(1)}, u32[]{:S(2)}, u32[]{:S(2)}) collective-permute-start(f32[24,256]{1,0:T(8,128)S(1)} %get-tuple-element.70), channel_id=1, source_target_pairs={{0,2},{2,0},{4,6},{6,4},{1,3},{3,1},{5,7},{7,5},{8,10},{10,8},{12,... | collective-permute-start | bytes 73736 | tf_op jit(solution)/shard_map/ppermute | solution.py:532
  37.2 1.3 %collective-permute-start.10 = (f32[32,128]{1,0:T(8,128)S(1)}, f32[32,128]{1,0:T(8,128)S(1)}, u32[]{:S(2)}, u32[]{:S(2)}) collective-permute-start(f32[32,128]{1,0:T(8,128)S(1)} %get-tuple-element.71), channel_id=1, source_target_pairs={{0,1},{1,0},{2,3},{3,2},{4,5},{5,4},{6,7},{7,6},{8,9},{9,8},{10,11... | collective-permute-start | bytes 49160 | tf_op jit(solution)/shard_map/ppermute | solution.py:533
  41.9 11.8 %collective-permute-start.11 = (f32[24,16,128]{2,1,0:T(8,128)S(1)}, f32[24,16,128]{2,1,0:T(8,128)S(1)}, u32[]{:S(2)}, u32[]{:S(2)}) collective-permute-start(f32[24,16,128]{2,1,0:T(8,128)S(1)} %get-tuple-element.73), channel_id=1, source_target_pairs={{0,8},{8,0},{2,10},{10,2},{4,12},{12,4},{6,14},{14,6},{1,9},{9,1},... | collective-permute-start | bytes 589832 | tf_op jit(solution)/shard_map/ppermute | solution.py:442
  45.1 10.5 %collective-permute-start.12 = (f32[24,16,128]{2,1,0:T(8,128)S(1)}, f32[24,16,128]{2,1,0:T(8,128)S(1)}, u32[]{:S(2)}, u32[]{:S(2)}) collective-permute-start(f32[24,16,128]{2,1,0:T(8,128)S(1)} %get-tuple-element.75), channel_id=1, source_target_pairs={{0,16},{16,0},{2,18},{18,2},{4,20},{20,4},{6,22},{22,6},{1,17},{17... | collective-permute-start | bytes 589832 | tf_op jit(solution)/shard_map/ppermute | solution.py:442
  47.0 11.2 %collective-permute-start.16 = (f32[24,16,128]{2,1,0:T(8,128)S(1)}, f32[24,16,128]{2,1,0:T(8,128)S(1)}, u32[]{:S(2)}, u32[]{:S(2)}) collective-permute-start(f32[24,16,128]{2,1,0:T(8,128)S(1)} %get-tuple-element.82), channel_id=1, source_target_pairs={{0,2},{2,0},{4,6},{6,4},{1,3},{3,1},{5,7},{7,5}} | collective-permute-start | bytes 589832 | tf_op jit(solution)/shard_map/ppermute | solution.py:433
  48.9 11.3 %collective-permute-start.13 = (f32[24,16,128]{2,1,0:T(8,128)S(1)}, f32[24,16,128]{2,1,0:T(8,128)S(1)}, u32[]{:S(2)}, u32[]{:S(2)}) collective-permute-start(f32[24,16,128]{2,1,0:T(8,128)S(1)} %get-tuple-element.77), channel_id=1, source_target_pairs={{26,0},{24,2},{30,4},{28,6},{27,1},{25,3},{31,5},{29,7}} | collective-permute-start | bytes 589832 | tf_op jit(solution)/shard_map/ppermute | solution.py:442
  50.2 10.0 %collective-permute-start.14 = (f32[24,16,128]{2,1,0:T(8,128)S(1)}, f32[24,16,128]{2,1,0:T(8,128)S(1)}, u32[]{:S(2)}, u32[]{:S(2)}) collective-permute-start(f32[24,16,128]{2,1,0:T(8,128)S(1)} %get-tuple-element.78), channel_id=1, source_target_pairs={{0,10},{2,8},{4,14},{6,12},{1,11},{3,9},{5,15},{7,13}} | collective-permute-start | bytes 589832 | tf_op jit(solution)/shard_map/ppermute | solution.py:442
  53.7 12.4 %collective-permute-start.15 = (f32[24,16,128]{2,1,0:T(8,128)S(1)}, f32[24,16,128]{2,1,0:T(8,128)S(1)}, u32[]{:S(2)}, u32[]{:S(2)}) collective-permute-start(f32[24,16,128]{2,1,0:T(8,128)S(1)} %get-tuple-element.79), channel_id=1, source_target_pairs={{0,18},{18,0},{2,16},{16,2},{4,22},{22,4},{6,20},{20,6},{1,19},{19... | collective-permute-start | bytes 589832 | tf_op jit(solution)/shard_map/ppermute | solution.py:442
  55.6 12.4 %collective-permute-start.18 = (f32[24,16,128]{2,1,0:T(8,128)S(1)}, f32[24,16,128]{2,1,0:T(8,128)S(1)}, u32[]{:S(2)}, u32[]{:S(2)}) collective-permute-start(f32[24,16,128]{2,1,0:T(8,128)S(1)} %collective-permute-done.11.rest_0_), channel_id=1, source_target_pairs={{0,2},{2,0},{4,6},{6,4},{1,3},{3,1},{5,7},{7,5}} | collective-permute-start | bytes 589832 | tf_op jit(solution)/shard_map/ppermute | solution.py:433
  58.3 9.8 %collective-permute-start.17 = (f32[24,16,128]{2,1,0:T(8,128)S(1)}, f32[24,16,128]{2,1,0:T(8,128)S(1)}, u32[]{:S(2)}, u32[]{:S(2)}) collective-permute-start(f32[24,16,128]{2,1,0:T(8,128)S(1)} %merge.3), channel_id=1, source_target_pairs={{0,24},{24,0},{2,26},{26,2},{4,28},{28,4},{6,30},{30,6},{1,25},{25... | collective-permute-start | bytes 589832 | tf_op jit(solution)/shard_map/ppermute | solution.py:442
  69.9 4.8 %collective-permute-start.19 = (f32[24,256]{1,0:T(8,128)S(1)}, f32[24,256]{1,0:T(8,128)S(1)}, u32[]{:S(2)}, u32[]{:S(2)}) collective-permute-start(f32[24,256]{1,0:T(8,128)S(1)} %get-tuple-element.86), channel_id=1, source_target_pairs={{2,4},{4,2},{6,0},{0,6},{3,5},{5,3},{7,1},{1,7},{10,12},{12,10},{1... | collective-permute-start | bytes 73736 | tf_op jit(solution)/shard_map/ppermute | solution.py:532
  71.5 3.8 %collective-permute-start.20 = (f32[24,256]{1,0:T(8,128)S(1)}, f32[24,256]{1,0:T(8,128)S(1)}, u32[]{:S(2)}, u32[]{:S(2)}) collective-permute-start(f32[24,256]{1,0:T(8,128)S(1)} %get-tuple-element.87), channel_id=1, source_target_pairs={{0,2},{2,0},{4,6},{6,4},{1,3},{3,1},{5,7},{7,5},{8,10},{10,8},{12,... | collective-permute-start | bytes 73736 | tf_op jit(solution)/shard_map/ppermute | solution.py:532
  71.8 1.3 %collective-permute-start.21 = (f32[32,128]{1,0:T(8,128)S(1)}, f32[32,128]{1,0:T(8,128)S(1)}, u32[]{:S(2)}, u32[]{:S(2)}) collective-permute-start(f32[32,128]{1,0:T(8,128)S(1)} %get-tuple-element.88), channel_id=1, source_target_pairs={{0,1},{1,0},{2,3},{3,2},{4,5},{5,4},{6,7},{7,6},{8,9},{9,8},{10,11... | collective-permute-start | bytes 49160 | tf_op jit(solution)/shard_map/ppermute | solution.py:533

commit v8 on v7

--- a/solution.py
+++ b/solution.py
@@ -28,7 +28,8 @@
 TURNED = 2
 FORWARDED = 0
 EARLY = ((FORWARDED, 0), (TURNED, 1))
-LATE = ((1, 0), (2, 1), (0, 1), (1, 1), (2, 0))
+MIXED = (FORWARDED, 1)
+LATE = ((1, 0), MIXED, (1, 1), (2, 0))
 GOT = (EARLY[0],) + LATE
 
 
@@ -158,7 +159,7 @@
 
 
 def first_kernel(*refs):
-    given, early, mask, late, refs = refs[:5], refs[5:7], refs[7], refs[8:13], refs[13:]
+    given, early, mask, late, refs = refs[:5], refs[5:7], refs[7], refs[8:12], refs[12:]
     rows, fine, *held, done = refs
     copies = [pltpu.make_async_copy(source, to, done.at[k]) for k, (source, to) in enumerate(zip(given, held))]
     for copy in copies:
@@ -214,8 +215,12 @@
     return even, jnp.logical_not(even)
 
 
+def arrived(slot, kind):
+    return -1 if (slot, kind) == MIXED else GOT.index(MIXED if (slot, kind) == (TURNED, 1) else (slot, kind))
+
+
 def update_kernel(n_cols, plan, rates, state, sponge, agg, brk, mask, diff, *rest):
-    got, rest = rest[: 2 * SLOTS + 1], rest[2 * SLOTS + 1 :]
+    got, rest = rest[: 2 * SLOTS], rest[2 * SLOTS :]
     wets, flux, sides = rest[0], rest[1], rest[2 : 4 + n_cols]
     nested, wide, coarse, fine = rest[4 + n_cols :]
     comps, cells_r, cells_c = wets.shape
@@ -242,7 +247,7 @@
 
             @pl.when(serves)
             def _():
-                add_at(nested, got[-1 if (slot, kind) == (FORWARDED, 1) else GOT.index((slot, kind))], first, begin)
+                add_at(nested, got[arrived(slot, kind)], first, begin)
 
     @pl.when(grid > 0)
     def _():
@@ -407,7 +412,7 @@
 def child_outs(slot, early, late):
     if slot == FORWARDED:
         return [early[0]]
-    return [late[LATE.index((slot, kind))] for kind in range(2)]
+    return [late[LATE.index(MIXED if (slot, kind) == (TURNED, 1) else (slot, kind))] for kind in range(2)]
 
 
 def late_kernel(plan, state, folded, packed, *outs):
@@ -433,12 +438,13 @@
     return lax.ppermute(block, ("grid", "gx"), [(i, i ^ 1) for i in range(lax.axis_size("gx"))])
 
 
-def with_children(block, slot, kind, down=True, up=True):
+def with_children(block, slot, kind):
     n_x = lax.axis_size("gx")
     pairs = []
     for i in range(n_x):
         parent, child = i, (slot + 1) * n_x + (i ^ kind)
-        pairs += [(parent, child)] * down + [(child, parent)] * up
+        source = (TURNED + 1) * n_x + (i ^ kind) if (slot, kind) == MIXED else child
+        pairs += [(parent, child), (source, parent)]
     return lax.ppermute(block, ("grid", "gx"), pairs)
 
 
@@ -456,7 +462,7 @@
         name="merge",
     )(mask, own, other)
     got = [
-        with_children(blocks[slot, kind], slot, kind, up=(slot, kind) != (FORWARDED, 1), down=(slot, kind) != (TURNED, 1))
+        with_children(blocks[slot, kind], slot, kind)
         for slot, kind in GOT
     ]
     forward, got[1] = lax.optimization_barrier((got[0], got[1]))
@@ -486,9 +492,9 @@
     flag = jax.ShapeDtypeStruct((8, half_c), f32)
     blocks = pl.pallas_call(
         first_kernel,
-        out_shape=[block] * 2 + [flag] + [block] * 5,
+        out_shape=[block] * 2 + [flag] + [block] * 4,
         in_specs=[pl.BlockSpec(memory_space=pltpu.HBM)] * 5,
-        out_specs=[VM] * 8,
+        out_specs=[VM] * 7,
         scratch_shapes=fold_scratch
         + [pltpu.SMEM(table.shape, table.dtype) for table in tables]
         + [pltpu.VMEM(adjoint.shape, f32), pltpu.VMEM(sponge.shape, f32), pltpu.SemaphoreType.DMA((5,))],
@@ -518,7 +524,7 @@
         wets, flux, *sides = pl.pallas_call(
             functools.partial(update_kernel, n_cols),
             out_shape=[tile] * 2 + side,
-            in_specs=[SM] + [VM] * (8 + 2 * SLOTS),
+            in_specs=[SM] + [VM] * (7 + 2 * SLOTS),
             out_specs=[VM] * (2 + len(side)),
             scratch_shapes=[
                 pltpu.VMEM(tile.shape, f32),
@@ -556,9 +562,9 @@
             early, mask, packed = out[:2], out[2], out[3]
             late = pl.pallas_call(
                 late_kernel,
-                out_shape=[block] * 5,
+                out_shape=[block] * 4,
                 in_specs=[SM] + [VM] * 3,
-                out_specs=[VM] * 5,
+                out_specs=[VM] * 4,
                 compiler_params=PARAMS,
                 name="late_payload",
             )(plan, state, *folded, packed)

time: 76.6 us -> 75.6 us (0.987)
  Pallas kernels: 15 us -> 12.7 us
  starting transfers between devices: 40 us -> 41.6 us
    ppermute x12 -> x10, waiting for transfers between devices: 11.6 us -> 16.5 us  [with_children(): return lax.ppermute(block, ('grid', 'gx'), pairs)]
    ppermute x4, waiting for transfers between devices: 3.92 us -> 0.01 us  [between_parents(): lax.ppermute(block, ('grid', 'gx'), [(i, i ^ 1) for i in range(lax.axis_s...]
    ppermute x4, waiting for transfers between devices: 4.46 us -> 2.88 us  [local(): lax.ppermute(sides[k], 'gx', swap_pairs(n_x, 1 - k))]
    pallas_call x2, Pallas kernels: 4.71 us -> 3.32 us  [the longest x1 2.74 us: local(): pl.pallas_call(first_kernel, out_shape=[block] * 2 + [flag] + [block] * 4...]
    ppermute x4, starting transfers between devices: 12.9 us -> 14.3 us  [between_parents(): lax.ppermute(block, ('grid', 'gx'), [(i, i ^ 1) for i in range(lax.axis_s...]
    pallas_call x2, Pallas kernels: 3.67 us -> 2.81 us  [local(): pl.pallas_call(functools.partial(update_kernel, n_cols), out_shape=[tile]...]
    ppermute x4, starting transfers between devices: 3.95 us -> 4.78 us  [local(): lax.ppermute(sides[k], 'gx', swap_pairs(n_x, 1 - k))]
    ppermute x12 -> x10, starting transfers between devices: 23.2 us -> 22.5 us  [with_children(): return lax.ppermute(block, ('grid', 'gx'), pairs)]
  transfers between devices with their start and end apart: 22 -> 20, of which waited for: 10 -> 7; matrix products, arithmetic and copies ran while one was open for 0% -> 0% of each run, Pallas kernels for 7% -> 6%
where the time goes in v8:
time: 75.6 us; the launch traced here: 75.1 us
  starting transfers between devices  41.6 us (55%)
  waiting for transfers between devices  19.4 us (26%)
  Pallas kernels  12.7 us (17%)
  local copies, waits for them, and re-layouts  0.97 us (1%)
    ppermute x10, starting transfers between devices, with_children(): return lax.ppermute(block, ('grid', 'gx'), pairs)  22.5 us
    ppermute x10, waiting for transfers between devices, with_children(): return lax.ppermute(block, ('grid', 'gx'), pairs)  16.5 us
    ppermute x4, starting transfers between devices, between_parents(): lax.ppermute(block, ('grid', 'gx'), [(i, i ^ 1) for i in range(lax.axis_s...  14.3 us
    ppermute x4, starting transfers between devices, local(): lax.ppermute(sides[k], 'gx', swap_pairs(n_x, 1 - k))  4.78 us
    ppermute x4, waiting for transfers between devices, local(): lax.ppermute(sides[k], 'gx', swap_pairs(n_x, 1 - k))  2.88 us
    pallas_call x2, Pallas kernels, local(): pl.pallas_call(functools.partial(update_kernel, n_cols), out_shape=[tile]...  2.81 us
    pallas_call x1, Pallas kernels, local(): pl.pallas_call(first_kernel, out_shape=[block] * 2 + [flag] + [block] * 4...  2.74 us
    pallas_call x2, Pallas kernels, local(): pl.pallas_call(functools.partial(spread_kernel, last), out_shape=[new] +...  2.49 us
  transfers between devices with their start and end apart: 20, of which 7 were waited for; matrix products, arithmetic and copies ran while one was open for 0% of the time, Pallas kernels for 6%

profile of v8, /device:TPU:0, one launch (start us, length us, event | category | flops | bytes accessed | tf_op | source)
XLA Modules:
  0.0 75.1 jit_solution(15227543439539145967)
XLA Ops:
  0.0 2.7 %first_payload.1 = (f32[24,16,128]{2,1,0:T(8,128)}, f32[24,16,128]{2,1,0:T(8,128)}, f32[8,128]{1,0:T(8,128)}, f32[24,16,128]{2,1,0:T(8,128)}, f32[24,16,128]{2,1...) custom-call(s32[3,2,4]{2,1,0:T(2,128)} %bitcast.5, s32[3,2,4]{2,1,0:T(2,128)} %bitcast.7, ...), custom_call_target="tpu_custom_call" | custom-call | tf_op jit(solution)/shard_map/first_payload/pallas_call | solution.py:493
  2.7 5.1 %collective-permute-start = (f32[24,16,128]{2,1,0:T(8,128)}, f32[24,16,128]{2,1,0:T(8,128)S(1)}, u32[]{:S(2)}, u32[]{:S(2)}) collective-permute-start(f32[24,16,128]{2,1,0:T(8,128)} %get-tuple-element.54), channel_id=1, source_target_pairs={{0,8},{8,0},{2,10},{10,2},{4,12},{12,4},{6,14},{14,6},{1,9},{9,1},... | collective-permute-start | bytes 589832 | tf_op jit(solution)/shard_map/ppermute | solution.py:448
  7.9 1.9 %collective-permute-start.1 = (f32[24,16,128]{2,1,0:T(8,128)}, f32[24,16,128]{2,1,0:T(8,128)S(1)}, u32[]{:S(2)}, u32[]{:S(2)}) collective-permute-start(f32[24,16,128]{2,1,0:T(8,128)} %get-tuple-element.55), channel_id=1, source_target_pairs={{0,16},{16,0},{2,18},{18,2},{4,20},{20,4},{6,22},{22,6},{1,17},{17... | collective-permute-start | bytes 589832 | tf_op jit(solution)/shard_map/ppermute | solution.py:448
  9.8 3.4 %collective-permute-start.4 = (f32[24,16,128]{2,1,0:T(8,128)}, f32[24,16,128]{2,1,0:T(8,128)S(1)}, u32[]{:S(2)}, u32[]{:S(2)}) collective-permute-start(f32[24,16,128]{2,1,0:T(8,128)} %get-tuple-element.60), channel_id=1, source_target_pairs={{0,2},{2,0},{4,6},{6,4},{1,3},{3,1},{5,7},{7,5}} | collective-permute-start | bytes 589832 | tf_op jit(solution)/shard_map/ppermute | solution.py:438
  13.2 1.9 %collective-permute-start.2 = (f32[24,16,128]{2,1,0:T(8,128)}, f32[24,16,128]{2,1,0:T(8,128)S(1)}, u32[]{:S(2)}, u32[]{:S(2)}) collective-permute-start(f32[24,16,128]{2,1,0:T(8,128)} %get-tuple-element.57), channel_id=1, source_target_pairs={{0,10},{26,0},{2,8},{24,2},{4,14},{30,4},{6,12},{28,6},{1,11},{27,... | collective-permute-start | bytes 589832 | tf_op jit(solution)/shard_map/ppermute | solution.py:448
  15.1 1.9 %collective-permute-start.3 = (f32[24,16,128]{2,1,0:T(8,128)}, f32[24,16,128]{2,1,0:T(8,128)S(1)}, u32[]{:S(2)}, u32[]{:S(2)}) collective-permute-start(f32[24,16,128]{2,1,0:T(8,128)} %get-tuple-element.58), channel_id=1, source_target_pairs={{0,18},{18,0},{2,16},{16,2},{4,22},{22,4},{6,20},{20,6},{1,19},{19... | collective-permute-start | bytes 589832 | tf_op jit(solution)/shard_map/ppermute | solution.py:448
  17.1 0.0 collective-permute-done.rest_0_
  17.1 0.6 collective-permute-done.1.rest_1_
  17.7 3.7 %collective-permute-start.6 = (f32[24,16,128]{2,1,0:T(8,128)S(1)}, f32[24,16,128]{2,1,0:T(8,128)S(1)}, u32[]{:S(2)}, u32[]{:S(2)}) collective-permute-start(f32[24,16,128]{2,1,0:T(8,128)S(1)} %collective-permute-done.rest_0_), channel_id=1, source_target_pairs={{0,2},{2,0},{4,6},{6,4},{1,3},{3,1},{5,7},{7,5}} | collective-permute-start | bytes 589832 | tf_op jit(solution)/shard_map/ppermute | solution.py:438
  21.4 0.0 collective-permute-done.4.other
  21.5 0.9 %copy-done.1 = f32[24,16,128]{2,1,0:T(8,128)S(1)} copy-done((f32[24,16,128]{2,1,0:T(8,128)S(1)}, f32[24,16,128]{2,1,0:T(8,128)}, u32[]{:S(2)}) %copy-start.1) | copy-done | bytes 196632
  22.4 0.0 copy-start.6
  22.4 0.0 copy-start.8
  22.4 0.0 copy-start.9
  22.4 0.0 copy-start.10
  22.4 0.0 copy-start.11
  22.5 2.1 %collective-permute-start.5 = (f32[24,16,128]{2,1,0:T(8,128)S(1)}, f32[24,16,128]{2,1,0:T(8,128)S(1)}, u32[]{:S(2)}, u32[]{:S(2)}) collective-permute-start(f32[24,16,128]{2,1,0:T(8,128)S(1)} %merge.2), channel_id=1, source_target_pairs={{0,24},{24,0},{2,26},{26,2},{4,28},{28,4},{6,30},{30,6},{1,25},{25... | collective-permute-start | bytes 589832 | tf_op jit(solution)/shard_map/ppermute | solution.py:448
  24.6 1.7 %stage_fields.1 = (f32[1,24,32,256]{3,2,1,0:T(8,128)S(1)}, f32[1,32,256]{2,1,0:T(8,128)S(1)}, f32[1,32,256]{2,1,0:T(8,128)S(1)}, f32[1,32,256]{2,1,0:T(8,128)S(1...) custom-call(f32[8,128]{1,0:T(8,128)S(1)} %copy-done.7, ...), custom_call_target="tpu_custom_call" | custom-call | tf_op jit(solution)/shard_map/stage_fields/pallas_call | solution.py:506
  26.4 0.0 collective-permute-done.2.rest_2_
  26.4 6.2 %collective-permute-done.3.rest_3_ = f32[24,16,128]{2,1,0:T(8,128)S(1)} collective-permute-done((f32[24,16,128]{2,1,0:T(8,128)}, f32[24,16,128]{2,1,0:T(8,128)S(1)}, u32[]{:S(2)}, u32[]{:S(2)}) %collective-permute-start.3) | collective-permute-done | bytes 196640 | tf_op jit(solution)/shard_map/ppermute | solution.py:448
  32.6 0.0 collective-permute-done.6.rest_5_
  32.6 1.4 %update.2 = (f32[24,32,256]{2,1,0:T(8,128)S(1)}, f32[24,32,256]{2,1,0:T(8,128)S(1)}, f32[24,256]{1,0:T(8,128)S(1)}, f32[24,256]{1,0:T(8,128)S(1)}, f32[32,128]{1,0:T(8,128)S(1)}) custom-call(s32[19]{0:T(128)S(1)} %get-tuple-element.46.plan.rest_0_, f32[3,1,256]{2,1,0:T(1,128)S(1)} %get-tuple-element.47.rates, f32[24,32,256]{2,1,0:T(8,128)S(1)} %bitcast.4, ...), custom_call_target="tpu_custom_call" | custom-call | tf_op jit(solution)/shard_map/update/pallas_call | solution.py:524
  34.0 1.5 %collective-permute-start.7 = (f32[24,256]{1,0:T(8,128)S(1)}, f32[24,256]{1,0:T(8,128)S(1)}, u32[]{:S(2)}, u32[]{:S(2)}) collective-permute-start(f32[24,256]{1,0:T(8,128)S(1)} %get-tuple-element.66), channel_id=1, source_target_pairs={{2,4},{4,2},{6,0},{0,6},{3,5},{5,3},{7,1},{1,7},{10,12},{12,10},{1... | collective-permute-start | bytes 73736 | tf_op jit(solution)/shard_map/ppermute | solution.py:538
  35.5 1.8 %collective-permute-start.8 = (f32[24,256]{1,0:T(8,128)S(1)}, f32[24,256]{1,0:T(8,128)S(1)}, u32[]{:S(2)}, u32[]{:S(2)}) collective-permute-start(f32[24,256]{1,0:T(8,128)S(1)} %get-tuple-element.67), channel_id=1, source_target_pairs={{0,2},{2,0},{4,6},{6,4},{1,3},{3,1},{5,7},{7,5},{8,10},{10,8},{12,... | collective-permute-start | bytes 73736 | tf_op jit(solution)/shard_map/ppermute | solution.py:538
  37.3 1.2 %spread.1 = (f32[24,32,256]{2,1,0:T(8,128)S(1)}, f32[24,16,128]{2,1,0:T(8,128)S(1)}) custom-call(f32[24,32,256]{2,1,0:T(8,128)S(1)} %get-tuple-element.62.wets, f32[24,32,256]{2,1,0:T(8,128)S(1)} %get-tuple-element.63.flux, f32[1,32,256]{2,1,0:T(8,128)S(1)} %get-tuple-element.49.sponge.rest_0_.rest_2_), custom_call_target="tpu_custom_call" | custom-call | tf_op jit(solution)/shard_map/spread/pallas_call | solution.py:541
  38.6 0.3 collective-permute-done.7.rest_4_
  38.9 0.5 collective-permute-done.8.rest_5_
  39.4 1.2 %halo.1 = (f32[24,32,256]{2,1,0:T(8,128)S(1)}, f32[24,16,128]{2,1,0:T(8,128)S(1)}, f32[24,16,128]{2,1,0:T(8,128)S(1)}, f32[8,128]{1,0:T(8,128)S(1)}, f32[80,128]{1,0:T(8,128)S(1)}) custom-call(s32[19]{0:T(128)S(1)} %get-tuple-element.46.plan.rest_0_, f32[24,32,256]{2,1,0:T(8,128)S(1)} %get-tuple-element.64.rest_1_, ...), custom_call_target="tpu_custom_call" | custom-call | tf_op jit(solution)/shard_map/halo/pallas_call | solution.py:552
  40.6 1.9 %collective-permute-start.10 = (f32[24,16,128]{2,1,0:T(8,128)S(1)}, f32[24,16,128]{2,1,0:T(8,128)S(1)}, u32[]{:S(2)}, u32[]{:S(2)}) collective-permute-start(f32[24,16,128]{2,1,0:T(8,128)S(1)} %get-tuple-element.70), channel_id=1, source_target_pairs={{0,8},{8,0},{2,10},{10,2},{4,12},{12,4},{6,14},{14,6},{1,9},{9,1},... | collective-permute-start | bytes 589832 | tf_op jit(solution)/shard_map/ppermute | solution.py:448
  42.5 0.6 late_payload.1
  43.1 1.9 %collective-permute-start.11 = (f32[24,16,128]{2,1,0:T(8,128)S(1)}, f32[24,16,128]{2,1,0:T(8,128)S(1)}, u32[]{:S(2)}, u32[]{:S(2)}) collective-permute-start(f32[24,16,128]{2,1,0:T(8,128)S(1)} %get-tuple-element.72), channel_id=1, source_target_pairs={{0,16},{16,0},{2,18},{18,2},{4,20},{20,4},{6,22},{22,6},{1,17},{17... | collective-permute-start | bytes 589832 | tf_op jit(solution)/shard_map/ppermute | solution.py:448
  45.1 4.1 %collective-permute-start.14 = (f32[24,16,128]{2,1,0:T(8,128)S(1)}, f32[24,16,128]{2,1,0:T(8,128)S(1)}, u32[]{:S(2)}, u32[]{:S(2)}) collective-permute-start(f32[24,16,128]{2,1,0:T(8,128)S(1)} %get-tuple-element.78), channel_id=1, source_target_pairs={{0,2},{2,0},{4,6},{6,4},{1,3},{3,1},{5,7},{7,5}} | collective-permute-start | bytes 589832 | tf_op jit(solution)/shard_map/ppermute | solution.py:438
  49.2 1.9 %collective-permute-start.12 = (f32[24,16,128]{2,1,0:T(8,128)S(1)}, f32[24,16,128]{2,1,0:T(8,128)S(1)}, u32[]{:S(2)}, u32[]{:S(2)}) collective-permute-start(f32[24,16,128]{2,1,0:T(8,128)S(1)} %get-tuple-element.74), channel_id=1, source_target_pairs={{0,10},{26,0},{2,8},{24,2},{4,14},{30,4},{6,12},{28,6},{1,11},{27,... | collective-permute-start | bytes 589832 | tf_op jit(solution)/shard_map/ppermute | solution.py:448
  51.1 1.9 %collective-permute-start.13 = (f32[24,16,128]{2,1,0:T(8,128)S(1)}, f32[24,16,128]{2,1,0:T(8,128)S(1)}, u32[]{:S(2)}, u32[]{:S(2)}) collective-permute-start(f32[24,16,128]{2,1,0:T(8,128)S(1)} %get-tuple-element.75), channel_id=1, source_target_pairs={{0,18},{18,0},{2,16},{16,2},{4,22},{22,4},{6,20},{20,6},{1,19},{19... | collective-permute-start | bytes 589832 | tf_op jit(solution)/shard_map/ppermute | solution.py:448
  53.0 0.0 collective-permute-done.11.rest_1_
  53.0 3.0 %collective-permute-start.16 = (f32[24,16,128]{2,1,0:T(8,128)S(1)}, f32[24,16,128]{2,1,0:T(8,128)S(1)}, u32[]{:S(2)}, u32[]{:S(2)}) collective-permute-start(f32[24,16,128]{2,1,0:T(8,128)S(1)} %collective-permute-done.10.rest_0_), channel_id=1, source_target_pairs={{0,2},{2,0},{4,6},{6,4},{1,3},{3,1},{5,7},{7,5}} | collective-permute-start | bytes 589832 | tf_op jit(solution)/shard_map/ppermute | solution.py:438
  56.1 1.9 %collective-permute-start.15 = (f32[24,16,128]{2,1,0:T(8,128)S(1)}, f32[24,16,128]{2,1,0:T(8,128)S(1)}, u32[]{:S(2)}, u32[]{:S(2)}) collective-permute-start(f32[24,16,128]{2,1,0:T(8,128)S(1)} %merge.3), channel_id=1, source_target_pairs={{0,24},{24,0},{2,26},{26,2},{4,28},{28,4},{6,30},{30,6},{1,25},{25... | collective-permute-start | bytes 589832 | tf_op jit(solution)/shard_map/ppermute | solution.py:448
  58.0 1.5 %collective-permute-done.12.rest_2_ = f32[24,16,128]{2,1,0:T(8,128)S(1)} collective-permute-done((f32[24,16,128]{2,1,0:T(8,128)S(1)}, f32[24,16,128]{2,1,0:T(8,128)S(1)}, u32[]{:S(2)}, u32[]{:S(2)}) %collective-permute-start.12) | collective-permute-done | bytes 196640 | tf_op jit(solution)/shard_map/ppermute | solution.py:448
  59.5 8.2 %collective-permute-done.13.rest_3_ = f32[24,16,128]{2,1,0:T(8,128)S(1)} collective-permute-done((f32[24,16,128]{2,1,0:T(8,128)S(1)}, f32[24,16,128]{2,1,0:T(8,128)S(1)}, u32[]{:S(2)}, u32[]{:S(2)}) %collective-permute-start.13) | collective-permute-done | bytes 196640 | tf_op jit(solution)/shard_map/ppermute | solution.py:448
  67.8 1.4 %update.3 = (f32[24,32,256]{2,1,0:T(8,128)S(1)}, f32[24,32,256]{2,1,0:T(8,128)S(1)}, f32[24,256]{1,0:T(8,128)S(1)}, f32[24,256]{1,0:T(8,128)S(1)}, f32[32,128]{1,0:T(8,128)S(1)}) custom-call(s32[19]{0:T(128)S(1)} %get-tuple-element.46.plan.rest_0_, f32[3,1,256]{2,1,0:T(1,128)S(1)} %get-tuple-element.47.rates, f32[24,32,256]{2,1,0:T(8,128)S(1)} %get-tuple-element.69.state, ...), custom_call_target="tpu_custom_call" | custom-call | tf_op jit(solution)/shard_map/update/pallas_call | solution.py:524
  69.2 0.8 %collective-permute-start.17 = (f32[24,256]{1,0:T(8,128)S(1)}, f32[24,256]{1,0:T(8,128)S(1)}, u32[]{:S(2)}, u32[]{:S(2)}) collective-permute-start(f32[24,256]{1,0:T(8,128)S(1)} %get-tuple-element.82), channel_id=1, source_target_pairs={{2,4},{4,2},{6,0},{0,6},{3,5},{5,3},{7,1},{1,7},{10,12},{12,10},{1... | collective-permute-start | bytes 73736 | tf_op jit(solution)/shard_map/ppermute | solution.py:538
  70.0 0.6 collective-permute-start.18
  70.6 0.0 collective-permute-start.19
  70.6 1.2 %spread_last.1.rest_0_ = f32[1,24,32,256]{3,2,1,0:T(8,128)S(1)} custom-call(f32[24,32,256]{2,1,0:T(8,128)S(1)} %get-tuple-element.80.wets, f32[24,32,256]{2,1,0:T(8,128)S(1)} %get-tuple-element.81.flux), custom_call_target="tpu_custom_call" | custom-call | tf_op jit(solution)/shard_map/spread_last/pallas_call | solution.py:541
  71.9 0.0 collective-permute-done.19.rest_3_
  71.9 2.1 %collective-permute-done.17.rest_1_ = f32[24,256]{1,0:T(8,128)S(1)} collective-permute-done((f32[24,256]{1,0:T(8,128)S(1)}, f32[24,256]{1,0:T(8,128)S(1)}, u32[]{:S(2)}, u32[]{:S(2)}) %collective-permute-start.17) | collective-permute-done | bytes 24608 | tf_op jit(solution)/shard_map/ppermute | solution.py:538
  74.0 0.0 collective-permute-done.18.rest_2_
  74.0 1.1 %halo_last.1 = f32[1,24,32,256]{3,2,1,0:T(8,128)} custom-call(f32[1,24,32,256]{3,2,1,0:T(8,128)S(1)} %spread_last.1.rest_0_, f32[24,256]{1,0:T(8,128)S(1)} %collective-permute-done.17.rest_1_, f32[24,256]{1,0:T(8,128)S(1)} %collective-permute-done.18.rest_2_, f32[32,128]{1,0:T(8,128)S(1)} %collective-permute-done.19.rest_3_), custom_call_target="tpu_custom_call" | custom-call | tf_op jit(solution)/shard_map/halo_last/pallas_call | solution.py:552
  (27 shorter events, 0.1 us)
Async XLA Ops:
  0.0 24.5 %copy-start = (f32[1,24,32,256]{3,2,1,0:T(8,128)S(1)}, f32[1,24,32,256]{3,2,1,0:T(8,128)}, u32[]{:S(2)}) copy-start(f32[1,24,32,256]{3,2,1,0:T(8,128)} %refs_0_.1) | copy-start | bytes 2359300
  2.7 14.3 %collective-permute-start = (f32[24,16,128]{2,1,0:T(8,128)}, f32[24,16,128]{2,1,0:T(8,128)S(1)}, u32[]{:S(2)}, u32[]{:S(2)}) collective-permute-start(f32[24,16,128]{2,1,0:T(8,128)} %get-tuple-element.54), channel_id=1, source_target_pairs={{0,8},{8,0},{2,10},{10,2},{4,12},{12,4},{6,14},{14,6},{1,9},{9,1},... | collective-permute-start | bytes 589832 | tf_op jit(solution)/shard_map/ppermute | solution.py:448
  7.9 9.8 %collective-permute-start.1 = (f32[24,16,128]{2,1,0:T(8,128)}, f32[24,16,128]{2,1,0:T(8,128)S(1)}, u32[]{:S(2)}, u32[]{:S(2)}) collective-permute-start(f32[24,16,128]{2,1,0:T(8,128)} %get-tuple-element.55), channel_id=1, source_target_pairs={{0,16},{16,0},{2,18},{18,2},{4,20},{20,4},{6,22},{22,6},{1,17},{17... | collective-permute-start | bytes 589832 | tf_op jit(solution)/shard_map/ppermute | solution.py:448
  9.8 11.7 %copy-start.7 = (f32[8,128]{1,0:T(8,128)S(1)}, f32[8,128]{1,0:T(8,128)}, u32[]{:S(2)}) copy-start(f32[8,128]{1,0:T(8,128)} %get-tuple-element.45.token.mask) | copy-start | bytes 12292
  9.8 11.6 %collective-permute-start.4 = (f32[24,16,128]{2,1,0:T(8,128)}, f32[24,16,128]{2,1,0:T(8,128)S(1)}, u32[]{:S(2)}, u32[]{:S(2)}) collective-permute-start(f32[24,16,128]{2,1,0:T(8,128)} %get-tuple-element.60), channel_id=1, source_target_pairs={{0,2},{2,0},{4,6},{6,4},{1,3},{3,1},{5,7},{7,5}} | collective-permute-start | bytes 589832 | tf_op jit(solution)/shard_map/ppermute | solution.py:438
  13.2 13.2 %collective-permute-start.2 = (f32[24,16,128]{2,1,0:T(8,128)}, f32[24,16,128]{2,1,0:T(8,128)S(1)}, u32[]{:S(2)}, u32[]{:S(2)}) collective-permute-start(f32[24,16,128]{2,1,0:T(8,128)} %get-tuple-element.57), channel_id=1, source_target_pairs={{0,10},{26,0},{2,8},{24,2},{4,14},{30,4},{6,12},{28,6},{1,11},{27,... | collective-permute-start | bytes 589832 | tf_op jit(solution)/shard_map/ppermute | solution.py:448
  15.1 17.4 %collective-permute-start.3 = (f32[24,16,128]{2,1,0:T(8,128)}, f32[24,16,128]{2,1,0:T(8,128)S(1)}, u32[]{:S(2)}, u32[]{:S(2)}) collective-permute-start(f32[24,16,128]{2,1,0:T(8,128)} %get-tuple-element.58), channel_id=1, source_target_pairs={{0,18},{18,0},{2,16},{16,2},{4,22},{22,4},{6,20},{20,6},{1,19},{19... | collective-permute-start | bytes 589832 | tf_op jit(solution)/shard_map/ppermute | solution.py:448
  17.7 14.9 %collective-permute-start.6 = (f32[24,16,128]{2,1,0:T(8,128)S(1)}, f32[24,16,128]{2,1,0:T(8,128)S(1)}, u32[]{:S(2)}, u32[]{:S(2)}) collective-permute-start(f32[24,16,128]{2,1,0:T(8,128)S(1)} %collective-permute-done.rest_0_), channel_id=1, source_target_pairs={{0,2},{2,0},{4,6},{6,4},{1,3},{3,1},{5,7},{7,5}} | collective-permute-start | bytes 589832 | tf_op jit(solution)/shard_map/ppermute | solution.py:438
  21.4 0.9 %copy-start.1 = (f32[24,16,128]{2,1,0:T(8,128)S(1)}, f32[24,16,128]{2,1,0:T(8,128)}, u32[]{:S(2)}) copy-start(f32[24,16,128]{2,1,0:T(8,128)} %get-tuple-element.59.own) | copy-start | bytes 589828
  22.4 2.2 %copy-start.2 = (f32[1,32,256]{2,1,0:T(8,128)S(1)}, f32[1,32,256]{2,1,0:T(8,128)}, u32[]{:S(2)}) copy-start(f32[1,32,256]{2,1,0:T(8,128)} %refs_1_.1) | copy-start | bytes 98308
  22.4 2.2 %copy-start.3 = (f32[1,32,256]{2,1,0:T(8,128)S(1)}, f32[1,32,256]{2,1,0:T(8,128)}, u32[]{:S(2)}) copy-start(f32[1,32,256]{2,1,0:T(8,128)} %refs_2_.1) | copy-start | bytes 98308
  22.4 2.2 %copy-start.4 = (f32[1,32,256]{2,1,0:T(8,128)S(1)}, f32[1,32,256]{2,1,0:T(8,128)}, u32[]{:S(2)}) copy-start(f32[1,32,256]{2,1,0:T(8,128)} %refs_3_.3) | copy-start | bytes 98308
  22.4 2.2 %copy-start.5 = (s32[1,32,256]{2,1,0:T(8,128)S(1)}, s32[1,32,256]{2,1,0:T(8,128)}, u32[]{:S(2)}) copy-start(s32[1,32,256]{2,1,0:T(8,128)} %refs_4_.3) | copy-start | bytes 98308
  22.4 2.2 %copy-start.6 = (f32[1,32,256]{2,1,0:T(8,128)S(1)}, f32[1,32,256]{2,1,0:T(8,128)}, u32[]{:S(2)}) copy-start(f32[1,32,256]{2,1,0:T(8,128)} %refs_5_.1) | copy-start | bytes 98308
  22.4 2.2 %copy-start.8 = (s32[3,4,2]{1,2,0:T(2,128)S(1)}, s32[3,4,2]{1,2,0:T(2,128)}, u32[]{:S(2)}) copy-start(s32[3,4,2]{1,2,0:T(2,128)} %param.17) | copy-start | bytes 292
  22.4 2.2 %copy-start.9 = (s32[3,4,2]{1,2,0:T(2,128)S(1)}, s32[3,4,2]{1,2,0:T(2,128)}, u32[]{:S(2)}) copy-start(s32[3,4,2]{1,2,0:T(2,128)} %param.18) | copy-start | bytes 292
  22.4 2.2 %copy-start.10 = (s32[3,4,2]{1,2,0:T(2,128)S(1)}, s32[3,4,2]{1,2,0:T(2,128)}, u32[]{:S(2)}) copy-start(s32[3,4,2]{1,2,0:T(2,128)} %param.19) | copy-start | bytes 292
  22.4 2.2 %copy-start.11 = (f32[4,3]{1,0:T(4,128)S(1)}, f32[4,3]{1,0:T(4,128)}, u32[]{:S(2)}) copy-start(f32[4,3]{1,0:T(4,128)} %refs_6_.1) | copy-start | bytes 148
  22.5 10.1 %collective-permute-start.5 = (f32[24,16,128]{2,1,0:T(8,128)S(1)}, f32[24,16,128]{2,1,0:T(8,128)S(1)}, u32[]{:S(2)}, u32[]{:S(2)}) collective-permute-start(f32[24,16,128]{2,1,0:T(8,128)S(1)} %merge.2), channel_id=1, source_target_pairs={{0,24},{24,0},{2,26},{26,2},{4,28},{28,4},{6,30},{30,6},{1,25},{25... | collective-permute-start | bytes 589832 | tf_op jit(solution)/shard_map/ppermute | solution.py:448
  34.0 4.9 %collective-permute-start.7 = (f32[24,256]{1,0:T(8,128)S(1)}, f32[24,256]{1,0:T(8,128)S(1)}, u32[]{:S(2)}, u32[]{:S(2)}) collective-permute-start(f32[24,256]{1,0:T(8,128)S(1)} %get-tuple-element.66), channel_id=1, source_target_pairs={{2,4},{4,2},{6,0},{0,6},{3,5},{5,3},{7,1},{1,7},{10,12},{12,10},{1... | collective-permute-start | bytes 73736 | tf_op jit(solution)/shard_map/ppermute | solution.py:538
  35.5 3.9 %collective-permute-start.8 = (f32[24,256]{1,0:T(8,128)S(1)}, f32[24,256]{1,0:T(8,128)S(1)}, u32[]{:S(2)}, u32[]{:S(2)}) collective-permute-start(f32[24,256]{1,0:T(8,128)S(1)} %get-tuple-element.67), channel_id=1, source_target_pairs={{0,2},{2,0},{4,6},{6,4},{1,3},{3,1},{5,7},{7,5},{8,10},{10,8},{12,... | collective-permute-start | bytes 73736 | tf_op jit(solution)/shard_map/ppermute | solution.py:538
  37.3 1.3 %collective-permute-start.9 = (f32[32,128]{1,0:T(8,128)S(1)}, f32[32,128]{1,0:T(8,128)S(1)}, u32[]{:S(2)}, u32[]{:S(2)}) collective-permute-start(f32[32,128]{1,0:T(8,128)S(1)} %get-tuple-element.68), channel_id=1, source_target_pairs={{0,1},{1,0},{2,3},{3,2},{4,5},{5,4},{6,7},{7,6},{8,9},{9,8},{10,11... | collective-permute-start | bytes 49160 | tf_op jit(solution)/shard_map/ppermute | solution.py:539
  40.6 12.4 %collective-permute-start.10 = (f32[24,16,128]{2,1,0:T(8,128)S(1)}, f32[24,16,128]{2,1,0:T(8,128)S(1)}, u32[]{:S(2)}, u32[]{:S(2)}) collective-permute-start(f32[24,16,128]{2,1,0:T(8,128)S(1)} %get-tuple-element.70), channel_id=1, source_target_pairs={{0,8},{8,0},{2,10},{10,2},{4,12},{12,4},{6,14},{14,6},{1,9},{9,1},... | collective-permute-start | bytes 589832 | tf_op jit(solution)/shard_map/ppermute | solution.py:448
  43.1 9.9 %collective-permute-start.11 = (f32[24,16,128]{2,1,0:T(8,128)S(1)}, f32[24,16,128]{2,1,0:T(8,128)S(1)}, u32[]{:S(2)}, u32[]{:S(2)}) collective-permute-start(f32[24,16,128]{2,1,0:T(8,128)S(1)} %get-tuple-element.72), channel_id=1, source_target_pairs={{0,16},{16,0},{2,18},{18,2},{4,20},{20,4},{6,22},{22,6},{1,17},{17... | collective-permute-start | bytes 589832 | tf_op jit(solution)/shard_map/ppermute | solution.py:448
  45.1 11.0 %collective-permute-start.14 = (f32[24,16,128]{2,1,0:T(8,128)S(1)}, f32[24,16,128]{2,1,0:T(8,128)S(1)}, u32[]{:S(2)}, u32[]{:S(2)}) collective-permute-start(f32[24,16,128]{2,1,0:T(8,128)S(1)} %get-tuple-element.78), channel_id=1, source_target_pairs={{0,2},{2,0},{4,6},{6,4},{1,3},{3,1},{5,7},{7,5}} | collective-permute-start | bytes 589832 | tf_op jit(solution)/shard_map/ppermute | solution.py:438
  49.2 10.4 %collective-permute-start.12 = (f32[24,16,128]{2,1,0:T(8,128)S(1)}, f32[24,16,128]{2,1,0:T(8,128)S(1)}, u32[]{:S(2)}, u32[]{:S(2)}) collective-permute-start(f32[24,16,128]{2,1,0:T(8,128)S(1)} %get-tuple-element.74), channel_id=1, source_target_pairs={{0,10},{26,0},{2,8},{24,2},{4,14},{30,4},{6,12},{28,6},{1,11},{27,... | collective-permute-start | bytes 589832 | tf_op jit(solution)/shard_map/ppermute | solution.py:448
  51.1 16.7 %collective-permute-start.13 = (f32[24,16,128]{2,1,0:T(8,128)S(1)}, f32[24,16,128]{2,1,0:T(8,128)S(1)}, u32[]{:S(2)}, u32[]{:S(2)}) collective-permute-start(f32[24,16,128]{2,1,0:T(8,128)S(1)} %get-tuple-element.75), channel_id=1, source_target_pairs={{0,18},{18,0},{2,16},{16,2},{4,22},{22,4},{6,20},{20,6},{1,19},{19... | collective-permute-start | bytes 589832 | tf_op jit(solution)/shard_map/ppermute | solution.py:448
  53.0 14.7 %collective-permute-start.16 = (f32[24,16,128]{2,1,0:T(8,128)S(1)}, f32[24,16,128]{2,1,0:T(8,128)S(1)}, u32[]{:S(2)}, u32[]{:S(2)}) collective-permute-start(f32[24,16,128]{2,1,0:T(8,128)S(1)} %collective-permute-done.10.rest_0_), channel_id=1, source_target_pairs={{0,2},{2,0},{4,6},{6,4},{1,3},{3,1},{5,7},{7,5}} | collective-permute-start | bytes 589832 | tf_op jit(solution)/shard_map/ppermute | solution.py:438
  56.1 11.7 %collective-permute-start.15 = (f32[24,16,128]{2,1,0:T(8,128)S(1)}, f32[24,16,128]{2,1,0:T(8,128)S(1)}, u32[]{:S(2)}, u32[]{:S(2)}) collective-permute-start(f32[24,16,128]{2,1,0:T(8,128)S(1)} %merge.3), channel_id=1, source_target_pairs={{0,24},{24,0},{2,26},{26,2},{4,28},{28,4},{6,30},{30,6},{1,25},{25... | collective-permute-start | bytes 589832 | tf_op jit(solution)/shard_map/ppermute | solution.py:448
  69.2 4.8 %collective-permute-start.17 = (f32[24,256]{1,0:T(8,128)S(1)}, f32[24,256]{1,0:T(8,128)S(1)}, u32[]{:S(2)}, u32[]{:S(2)}) collective-permute-start(f32[24,256]{1,0:T(8,128)S(1)} %get-tuple-element.82), channel_id=1, source_target_pairs={{2,4},{4,2},{6,0},{0,6},{3,5},{5,3},{7,1},{1,7},{10,12},{12,10},{1... | collective-permute-start | bytes 73736 | tf_op jit(solution)/shard_map/ppermute | solution.py:538
  70.0 4.0 %collective-permute-start.18 = (f32[24,256]{1,0:T(8,128)S(1)}, f32[24,256]{1,0:T(8,128)S(1)}, u32[]{:S(2)}, u32[]{:S(2)}) collective-permute-start(f32[24,256]{1,0:T(8,128)S(1)} %get-tuple-element.83), channel_id=1, source_target_pairs={{0,2},{2,0},{4,6},{6,4},{1,3},{3,1},{5,7},{7,5},{8,10},{10,8},{12,... | collective-permute-start | bytes 73736 | tf_op jit(solution)/shard_map/ppermute | solution.py:538
  70.6 1.3 %collective-permute-start.19 = (f32[32,128]{1,0:T(8,128)S(1)}, f32[32,128]{1,0:T(8,128)S(1)}, u32[]{:S(2)}, u32[]{:S(2)}) collective-permute-start(f32[32,128]{1,0:T(8,128)S(1)} %get-tuple-element.84), channel_id=1, source_target_pairs={{0,1},{1,0},{2,3},{3,2},{4,5},{5,4},{6,7},{7,6},{8,9},{9,8},{10,11... | collective-permute-start | bytes 49160 | tf_op jit(solution)/shard_map/ppermute | solution.py:539

commit v9 on v8

--- a/solution.py
+++ b/solution.py
@@ -330,7 +330,7 @@
         bulk[c] = total
         return carry
 
-    lax.fori_loop(0, comps, one, 0, unroll=2)
+    lax.fori_loop(0, comps, one, 0, unroll=6)
     if not last:
         sponge, _, folded, rows, fine = rest
 

time: 75.6 us -> 75.3 us (level)
  starting transfers between devices: 41.6 us -> 39.2 us
  waiting for transfers between devices: 19.4 us -> 21.3 us
    ppermute x4, starting transfers between devices: 14.3 us -> 12.7 us  [between_parents(): lax.ppermute(block, ('grid', 'gx'), [(i, i ^ 1) for i in range(lax.axis_s...]
    pallas_call x2, Pallas kernels: 2.49 us -> 1.42 us  [local(): pl.pallas_call(functools.partial(spread_kernel, last), out_shape=[new] +...]
    ppermute x2, waiting for transfers between devices: 0.01 us -> 0.93 us  [local(): lax.ppermute(sides[2 + k], 'gy', swap_pairs(n_y, k))]
    ppermute x4, waiting for transfers between devices: 2.88 us -> 3.73 us  [local(): lax.ppermute(sides[k], 'gx', swap_pairs(n_x, 1 - k))]
  transfers between devices with their start and end apart: 20 -> 20, of which waited for: 7 -> 10; matrix products, arithmetic and copies ran while one was open for 0% -> 0% of each run, Pallas kernels for 6% -> 6%
where the time goes in v9:
time: 75.3 us; the launch traced here: 74.9 us
  starting transfers between devices  39.2 us (52%)
  waiting for transfers between devices  21.3 us (28%)
  Pallas kernels  13.1 us (17%)
  local copies, waits for them, and re-layouts  0.97 us (1%)
    ppermute x10, starting transfers between devices, with_children(): return lax.ppermute(block, ('grid', 'gx'), pairs)  22.5 us
    ppermute x10, waiting for transfers between devices, with_children(): return lax.ppermute(block, ('grid', 'gx'), pairs)  16.6 us
    ppermute x4, starting transfers between devices, between_parents(): lax.ppermute(block, ('grid', 'gx'), [(i, i ^ 1) for i in range(lax.axis_s...  12.7 us
    ppermute x4, starting transfers between devices, local(): lax.ppermute(sides[k], 'gx', swap_pairs(n_x, 1 - k))  4.03 us
    ppermute x4, waiting for transfers between devices, local(): lax.ppermute(sides[k], 'gx', swap_pairs(n_x, 1 - k))  3.73 us
    pallas_call x2, Pallas kernels, local(): pl.pallas_call(functools.partial(update_kernel, n_cols), out_shape=[tile]...  3.4 us
    pallas_call x1, Pallas kernels, local(): pl.pallas_call(first_kernel, out_shape=[block] * 2 + [flag] + [block] * 4...  3.17 us
    pallas_call x2, Pallas kernels, local(): pl.pallas_call(functools.partial(halo_kernel, n_cols, (n_x, n_y), last),...  2.33 us
  transfers between devices with their start and end apart: 20, of which 10 were waited for; matrix products, arithmetic and copies ran while one was open for 0% of the time, Pallas kernels for 6%

profile of v9, /device:TPU:0, one launch (start us, length us, event | category | flops | bytes accessed | tf_op | source)
XLA Modules:
  0.0 74.9 jit_solution(3498777692487991601)
XLA Ops:
  0.0 3.2 %first_payload.1 = (f32[24,16,128]{2,1,0:T(8,128)}, f32[24,16,128]{2,1,0:T(8,128)}, f32[8,128]{1,0:T(8,128)}, f32[24,16,128]{2,1,0:T(8,128)}, f32[24,16,128]{2,1...) custom-call(s32[3,2,4]{2,1,0:T(2,128)} %bitcast.5, s32[3,2,4]{2,1,0:T(2,128)} %bitcast.7, ...), custom_call_target="tpu_custom_call" | custom-call | tf_op jit(solution)/shard_map/first_payload/pallas_call | solution.py:493
  3.2 4.7 %collective-permute-start = (f32[24,16,128]{2,1,0:T(8,128)}, f32[24,16,128]{2,1,0:T(8,128)S(1)}, u32[]{:S(2)}, u32[]{:S(2)}) collective-permute-start(f32[24,16,128]{2,1,0:T(8,128)} %get-tuple-element.54), channel_id=1, source_target_pairs={{0,8},{8,0},{2,10},{10,2},{4,12},{12,4},{6,14},{14,6},{1,9},{9,1},... | collective-permute-start | bytes 589832 | tf_op jit(solution)/shard_map/ppermute | solution.py:448
  7.9 1.9 %collective-permute-start.1 = (f32[24,16,128]{2,1,0:T(8,128)}, f32[24,16,128]{2,1,0:T(8,128)S(1)}, u32[]{:S(2)}, u32[]{:S(2)}) collective-permute-start(f32[24,16,128]{2,1,0:T(8,128)} %get-tuple-element.55), channel_id=1, source_target_pairs={{0,16},{16,0},{2,18},{18,2},{4,20},{20,4},{6,22},{22,6},{1,17},{17... | collective-permute-start | bytes 589832 | tf_op jit(solution)/shard_map/ppermute | solution.py:448
  9.8 3.4 %collective-permute-start.4 = (f32[24,16,128]{2,1,0:T(8,128)}, f32[24,16,128]{2,1,0:T(8,128)S(1)}, u32[]{:S(2)}, u32[]{:S(2)}) collective-permute-start(f32[24,16,128]{2,1,0:T(8,128)} %get-tuple-element.60), channel_id=1, source_target_pairs={{0,2},{2,0},{4,6},{6,4},{1,3},{3,1},{5,7},{7,5}} | collective-permute-start | bytes 589832 | tf_op jit(solution)/shard_map/ppermute | solution.py:438
  13.2 1.9 %collective-permute-start.2 = (f32[24,16,128]{2,1,0:T(8,128)}, f32[24,16,128]{2,1,0:T(8,128)S(1)}, u32[]{:S(2)}, u32[]{:S(2)}) collective-permute-start(f32[24,16,128]{2,1,0:T(8,128)} %get-tuple-element.57), channel_id=1, source_target_pairs={{0,10},{26,0},{2,8},{24,2},{4,14},{30,4},{6,12},{28,6},{1,11},{27,... | collective-permute-start | bytes 589832 | tf_op jit(solution)/shard_map/ppermute | solution.py:448
  15.1 1.9 %collective-permute-start.3 = (f32[24,16,128]{2,1,0:T(8,128)}, f32[24,16,128]{2,1,0:T(8,128)S(1)}, u32[]{:S(2)}, u32[]{:S(2)}) collective-permute-start(f32[24,16,128]{2,1,0:T(8,128)} %get-tuple-element.58), channel_id=1, source_target_pairs={{0,18},{18,0},{2,16},{16,2},{4,22},{22,4},{6,20},{20,6},{1,19},{19... | collective-permute-start | bytes 589832 | tf_op jit(solution)/shard_map/ppermute | solution.py:448
  17.1 0.0 collective-permute-done.rest_0_
  17.1 0.6 collective-permute-done.1.rest_1_
  17.7 3.4 %collective-permute-start.6 = (f32[24,16,128]{2,1,0:T(8,128)S(1)}, f32[24,16,128]{2,1,0:T(8,128)S(1)}, u32[]{:S(2)}, u32[]{:S(2)}) collective-permute-start(f32[24,16,128]{2,1,0:T(8,128)S(1)} %collective-permute-done.rest_0_), channel_id=1, source_target_pairs={{0,2},{2,0},{4,6},{6,4},{1,3},{3,1},{5,7},{7,5}} | collective-permute-start | bytes 589832 | tf_op jit(solution)/shard_map/ppermute | solution.py:438
  21.1 0.0 collective-permute-done.4.other
  21.1 0.9 %copy-done.1 = f32[24,16,128]{2,1,0:T(8,128)S(1)} copy-done((f32[24,16,128]{2,1,0:T(8,128)S(1)}, f32[24,16,128]{2,1,0:T(8,128)}, u32[]{:S(2)}) %copy-start.1) | copy-done | bytes 196632
  22.0 0.0 copy-start.6
  22.0 0.0 copy-start.8
  22.1 0.0 copy-start.9
  22.1 0.0 copy-start.10
  22.1 0.0 copy-start.11
  22.1 2.1 %collective-permute-start.5 = (f32[24,16,128]{2,1,0:T(8,128)S(1)}, f32[24,16,128]{2,1,0:T(8,128)S(1)}, u32[]{:S(2)}, u32[]{:S(2)}) collective-permute-start(f32[24,16,128]{2,1,0:T(8,128)S(1)} %merge.2), channel_id=1, source_target_pairs={{0,24},{24,0},{2,26},{26,2},{4,28},{28,4},{6,30},{30,6},{1,25},{25... | collective-permute-start | bytes 589832 | tf_op jit(solution)/shard_map/ppermute | solution.py:448
  24.3 1.7 %stage_fields.1 = (f32[1,24,32,256]{3,2,1,0:T(8,128)S(1)}, f32[1,32,256]{2,1,0:T(8,128)S(1)}, f32[1,32,256]{2,1,0:T(8,128)S(1)}, f32[1,32,256]{2,1,0:T(8,128)S(1...) custom-call(f32[8,128]{1,0:T(8,128)S(1)} %copy-done.7, ...), custom_call_target="tpu_custom_call" | custom-call | tf_op jit(solution)/shard_map/stage_fields/pallas_call | solution.py:506
  26.0 0.0 collective-permute-done.2.rest_2_
  26.0 6.5 %collective-permute-done.3.rest_3_ = f32[24,16,128]{2,1,0:T(8,128)S(1)} collective-permute-done((f32[24,16,128]{2,1,0:T(8,128)}, f32[24,16,128]{2,1,0:T(8,128)S(1)}, u32[]{:S(2)}, u32[]{:S(2)}) %collective-permute-start.3) | collective-permute-done | bytes 196640 | tf_op jit(solution)/shard_map/ppermute | solution.py:448
  32.6 1.7 %update.2 = (f32[24,32,256]{2,1,0:T(8,128)S(1)}, f32[24,32,256]{2,1,0:T(8,128)S(1)}, f32[24,256]{1,0:T(8,128)S(1)}, f32[24,256]{1,0:T(8,128)S(1)}, f32[32,128]{1,0:T(8,128)S(1)}) custom-call(s32[19]{0:T(128)S(1)} %get-tuple-element.46.plan.rest_0_, f32[3,1,256]{2,1,0:T(1,128)S(1)} %get-tuple-element.47.rates, f32[24,32,256]{2,1,0:T(8,128)S(1)} %bitcast.4, ...), custom_call_target="tpu_custom_call" | custom-call | tf_op jit(solution)/shard_map/update/pallas_call | solution.py:524
  34.3 1.5 %collective-permute-start.7 = (f32[24,256]{1,0:T(8,128)S(1)}, f32[24,256]{1,0:T(8,128)S(1)}, u32[]{:S(2)}, u32[]{:S(2)}) collective-permute-start(f32[24,256]{1,0:T(8,128)S(1)} %get-tuple-element.66), channel_id=1, source_target_pairs={{2,4},{4,2},{6,0},{0,6},{3,5},{5,3},{7,1},{1,7},{10,12},{12,10},{1... | collective-permute-start | bytes 73736 | tf_op jit(solution)/shard_map/ppermute | solution.py:538
  35.8 1.2 %collective-permute-start.8 = (f32[24,256]{1,0:T(8,128)S(1)}, f32[24,256]{1,0:T(8,128)S(1)}, u32[]{:S(2)}, u32[]{:S(2)}) collective-permute-start(f32[24,256]{1,0:T(8,128)S(1)} %get-tuple-element.67), channel_id=1, source_target_pairs={{0,2},{2,0},{4,6},{6,4},{1,3},{3,1},{5,7},{7,5},{8,10},{10,8},{12,... | collective-permute-start | bytes 73736 | tf_op jit(solution)/shard_map/ppermute | solution.py:538
  37.0 0.0 collective-permute-start.9
  37.0 0.7 spread.1
  37.7 0.5 collective-permute-done.9.rest_6_
  38.2 0.8 %collective-permute-done.7.rest_4_ = f32[24,256]{1,0:T(8,128)S(1)} collective-permute-done((f32[24,256]{1,0:T(8,128)S(1)}, f32[24,256]{1,0:T(8,128)S(1)}, u32[]{:S(2)}, u32[]{:S(2)}) %collective-permute-start.7) | collective-permute-done | bytes 24608 | tf_op jit(solution)/shard_map/ppermute | solution.py:538
  39.1 0.5 collective-permute-done.8.rest_5_
  39.6 1.2 %halo.1 = (f32[24,32,256]{2,1,0:T(8,128)S(1)}, f32[24,16,128]{2,1,0:T(8,128)S(1)}, f32[24,16,128]{2,1,0:T(8,128)S(1)}, f32[8,128]{1,0:T(8,128)S(1)}, f32[80,128]{1,0:T(8,128)S(1)}) custom-call(s32[19]{0:T(128)S(1)} %get-tuple-element.46.plan.rest_0_, f32[24,32,256]{2,1,0:T(8,128)S(1)} %get-tuple-element.64.rest_1_, ...), custom_call_target="tpu_custom_call" | custom-call | tf_op jit(solution)/shard_map/halo/pallas_call | solution.py:552
  40.8 1.9 %collective-permute-start.10 = (f32[24,16,128]{2,1,0:T(8,128)S(1)}, f32[24,16,128]{2,1,0:T(8,128)S(1)}, u32[]{:S(2)}, u32[]{:S(2)}) collective-permute-start(f32[24,16,128]{2,1,0:T(8,128)S(1)} %get-tuple-element.70), channel_id=1, source_target_pairs={{0,8},{8,0},{2,10},{10,2},{4,12},{12,4},{6,14},{14,6},{1,9},{9,1},... | collective-permute-start | bytes 589832 | tf_op jit(solution)/shard_map/ppermute | solution.py:448
  42.8 1.0 %late_payload.1 = (f32[24,16,128]{2,1,0:T(8,128)S(1)}, f32[24,16,128]{2,1,0:T(8,128)S(1)}, f32[24,16,128]{2,1,0:T(8,128)S(1)}, f32[24,16,128]{2,1,0:T(8,128)S(1)}) custom-call(s32[19]{0:T(128)S(1)} %get-tuple-element.46.plan.rest_0_, f32[24,32,256]{2,1,0:T(8,128)S(1)} %get-tuple-element.69.state, f32[24,16,128]{2,1,0:T(8,128)S(1)} %get-tuple-element.65.rest_3_.folded, ...), custom_call_target="tpu_custom_call" | custom-call | tf_op jit(solution)/shard_map/late_payload/pallas_call | solution.py:563
  43.8 1.9 %collective-permute-start.11 = (f32[24,16,128]{2,1,0:T(8,128)S(1)}, f32[24,16,128]{2,1,0:T(8,128)S(1)}, u32[]{:S(2)}, u32[]{:S(2)}) collective-permute-start(f32[24,16,128]{2,1,0:T(8,128)S(1)} %get-tuple-element.72), channel_id=1, source_target_pairs={{0,16},{16,0},{2,18},{18,2},{4,20},{20,4},{6,22},{22,6},{1,17},{17... | collective-permute-start | bytes 589832 | tf_op jit(solution)/shard_map/ppermute | solution.py:448
  45.7 2.7 %collective-permute-start.14 = (f32[24,16,128]{2,1,0:T(8,128)S(1)}, f32[24,16,128]{2,1,0:T(8,128)S(1)}, u32[]{:S(2)}, u32[]{:S(2)}) collective-permute-start(f32[24,16,128]{2,1,0:T(8,128)S(1)} %get-tuple-element.78), channel_id=1, source_target_pairs={{0,2},{2,0},{4,6},{6,4},{1,3},{3,1},{5,7},{7,5}} | collective-permute-start | bytes 589832 | tf_op jit(solution)/shard_map/ppermute | solution.py:438
  48.4 1.9 %collective-permute-start.12 = (f32[24,16,128]{2,1,0:T(8,128)S(1)}, f32[24,16,128]{2,1,0:T(8,128)S(1)}, u32[]{:S(2)}, u32[]{:S(2)}) collective-permute-start(f32[24,16,128]{2,1,0:T(8,128)S(1)} %get-tuple-element.74), channel_id=1, source_target_pairs={{0,10},{26,0},{2,8},{24,2},{4,14},{30,4},{6,12},{28,6},{1,11},{27,... | collective-permute-start | bytes 589832 | tf_op jit(solution)/shard_map/ppermute | solution.py:448
  50.4 1.9 %collective-permute-start.13 = (f32[24,16,128]{2,1,0:T(8,128)S(1)}, f32[24,16,128]{2,1,0:T(8,128)S(1)}, u32[]{:S(2)}, u32[]{:S(2)}) collective-permute-start(f32[24,16,128]{2,1,0:T(8,128)S(1)} %get-tuple-element.75), channel_id=1, source_target_pairs={{0,18},{18,0},{2,16},{16,2},{4,22},{22,4},{6,20},{20,6},{1,19},{19... | collective-permute-start | bytes 589832 | tf_op jit(solution)/shard_map/ppermute | solution.py:448
  52.3 0.3 collective-permute-done.10.rest_0_
  52.6 3.1 %collective-permute-start.16 = (f32[24,16,128]{2,1,0:T(8,128)S(1)}, f32[24,16,128]{2,1,0:T(8,128)S(1)}, u32[]{:S(2)}, u32[]{:S(2)}) collective-permute-start(f32[24,16,128]{2,1,0:T(8,128)S(1)} %collective-permute-done.10.rest_0_), channel_id=1, source_target_pairs={{0,2},{2,0},{4,6},{6,4},{1,3},{3,1},{5,7},{7,5}} | collective-permute-start | bytes 589832 | tf_op jit(solution)/shard_map/ppermute | solution.py:438
  55.8 2.4 %collective-permute-start.15 = (f32[24,16,128]{2,1,0:T(8,128)S(1)}, f32[24,16,128]{2,1,0:T(8,128)S(1)}, u32[]{:S(2)}, u32[]{:S(2)}) collective-permute-start(f32[24,16,128]{2,1,0:T(8,128)S(1)} %merge.3), channel_id=1, source_target_pairs={{0,24},{24,0},{2,26},{26,2},{4,28},{28,4},{6,30},{30,6},{1,25},{25... | collective-permute-start | bytes 589832 | tf_op jit(solution)/shard_map/ppermute | solution.py:448
  58.2 0.9 %collective-permute-done.12.rest_2_ = f32[24,16,128]{2,1,0:T(8,128)S(1)} collective-permute-done((f32[24,16,128]{2,1,0:T(8,128)S(1)}, f32[24,16,128]{2,1,0:T(8,128)S(1)}, u32[]{:S(2)}, u32[]{:S(2)}) %collective-permute-start.12) | collective-permute-done | bytes 196640 | tf_op jit(solution)/shard_map/ppermute | solution.py:448
  59.0 8.3 %collective-permute-done.13.rest_3_ = f32[24,16,128]{2,1,0:T(8,128)S(1)} collective-permute-done((f32[24,16,128]{2,1,0:T(8,128)S(1)}, f32[24,16,128]{2,1,0:T(8,128)S(1)}, u32[]{:S(2)}, u32[]{:S(2)}) %collective-permute-start.13) | collective-permute-done | bytes 196640 | tf_op jit(solution)/shard_map/ppermute | solution.py:448
  67.3 1.7 %update.3 = (f32[24,32,256]{2,1,0:T(8,128)S(1)}, f32[24,32,256]{2,1,0:T(8,128)S(1)}, f32[24,256]{1,0:T(8,128)S(1)}, f32[24,256]{1,0:T(8,128)S(1)}, f32[32,128]{1,0:T(8,128)S(1)}) custom-call(s32[19]{0:T(128)S(1)} %get-tuple-element.46.plan.rest_0_, f32[3,1,256]{2,1,0:T(1,128)S(1)} %get-tuple-element.47.rates, f32[24,32,256]{2,1,0:T(8,128)S(1)} %get-tuple-element.69.state, ...), custom_call_target="tpu_custom_call" | custom-call | tf_op jit(solution)/shard_map/update/pallas_call | solution.py:524
  69.0 0.9 %collective-permute-start.17 = (f32[24,256]{1,0:T(8,128)S(1)}, f32[24,256]{1,0:T(8,128)S(1)}, u32[]{:S(2)}, u32[]{:S(2)}) collective-permute-start(f32[24,256]{1,0:T(8,128)S(1)} %get-tuple-element.82), channel_id=1, source_target_pairs={{2,4},{4,2},{6,0},{0,6},{3,5},{5,3},{7,1},{1,7},{10,12},{12,10},{1... | collective-permute-start | bytes 73736 | tf_op jit(solution)/shard_map/ppermute | solution.py:538
  70.0 0.3 collective-permute-start.18
  70.3 0.0 collective-permute-start.19
  70.3 0.7 spread_last.1.rest_0_
  71.0 0.5 collective-permute-done.19.rest_3_
  71.5 2.3 %collective-permute-done.17.rest_1_ = f32[24,256]{1,0:T(8,128)S(1)} collective-permute-done((f32[24,256]{1,0:T(8,128)S(1)}, f32[24,256]{1,0:T(8,128)S(1)}, u32[]{:S(2)}, u32[]{:S(2)}) %collective-permute-start.17) | collective-permute-done | bytes 24608 | tf_op jit(solution)/shard_map/ppermute | solution.py:538
  73.8 1.1 %halo_last.1 = f32[1,24,32,256]{3,2,1,0:T(8,128)} custom-call(f32[1,24,32,256]{3,2,1,0:T(8,128)S(1)} %spread_last.1.rest_0_, f32[24,256]{1,0:T(8,128)S(1)} %collective-permute-done.17.rest_1_, f32[24,256]{1,0:T(8,128)S(1)} %collective-permute-done.18.rest_2_, f32[32,128]{1,0:T(8,128)S(1)} %collective-permute-done.19.rest_3_), custom_call_target="tpu_custom_call" | custom-call | tf_op jit(solution)/shard_map/halo_last/pallas_call | solution.py:552
  (27 shorter events, 0.1 us)
Async XLA Ops:
  0.0 24.2 %copy-start = (f32[1,24,32,256]{3,2,1,0:T(8,128)S(1)}, f32[1,24,32,256]{3,2,1,0:T(8,128)}, u32[]{:S(2)}) copy-start(f32[1,24,32,256]{3,2,1,0:T(8,128)} %refs_0_.1) | copy-start | bytes 2359300
  3.2 13.9 %collective-permute-start = (f32[24,16,128]{2,1,0:T(8,128)}, f32[24,16,128]{2,1,0:T(8,128)S(1)}, u32[]{:S(2)}, u32[]{:S(2)}) collective-permute-start(f32[24,16,128]{2,1,0:T(8,128)} %get-tuple-element.54), channel_id=1, source_target_pairs={{0,8},{8,0},{2,10},{10,2},{4,12},{12,4},{6,14},{14,6},{1,9},{9,1},... | collective-permute-start | bytes 589832 | tf_op jit(solution)/shard_map/ppermute | solution.py:448
  7.9 9.8 %collective-permute-start.1 = (f32[24,16,128]{2,1,0:T(8,128)}, f32[24,16,128]{2,1,0:T(8,128)S(1)}, u32[]{:S(2)}, u32[]{:S(2)}) collective-permute-start(f32[24,16,128]{2,1,0:T(8,128)} %get-tuple-element.55), channel_id=1, source_target_pairs={{0,16},{16,0},{2,18},{18,2},{4,20},{20,4},{6,22},{22,6},{1,17},{17... | collective-permute-start | bytes 589832 | tf_op jit(solution)/shard_map/ppermute | solution.py:448
  9.8 11.3 %copy-start.7 = (f32[8,128]{1,0:T(8,128)S(1)}, f32[8,128]{1,0:T(8,128)}, u32[]{:S(2)}) copy-start(f32[8,128]{1,0:T(8,128)} %get-tuple-element.45.token.mask) | copy-start | bytes 12292
  9.8 11.3 %collective-permute-start.4 = (f32[24,16,128]{2,1,0:T(8,128)}, f32[24,16,128]{2,1,0:T(8,128)S(1)}, u32[]{:S(2)}, u32[]{:S(2)}) collective-permute-start(f32[24,16,128]{2,1,0:T(8,128)} %get-tuple-element.60), channel_id=1, source_target_pairs={{0,2},{2,0},{4,6},{6,4},{1,3},{3,1},{5,7},{7,5}} | collective-permute-start | bytes 589832 | tf_op jit(solution)/shard_map/ppermute | solution.py:438
  13.2 12.8 %collective-permute-start.2 = (f32[24,16,128]{2,1,0:T(8,128)}, f32[24,16,128]{2,1,0:T(8,128)S(1)}, u32[]{:S(2)}, u32[]{:S(2)}) collective-permute-start(f32[24,16,128]{2,1,0:T(8,128)} %get-tuple-element.57), channel_id=1, source_target_pairs={{0,10},{26,0},{2,8},{24,2},{4,14},{30,4},{6,12},{28,6},{1,11},{27,... | collective-permute-start | bytes 589832 | tf_op jit(solution)/shard_map/ppermute | solution.py:448
  15.1 17.4 %collective-permute-start.3 = (f32[24,16,128]{2,1,0:T(8,128)}, f32[24,16,128]{2,1,0:T(8,128)S(1)}, u32[]{:S(2)}, u32[]{:S(2)}) collective-permute-start(f32[24,16,128]{2,1,0:T(8,128)} %get-tuple-element.58), channel_id=1, source_target_pairs={{0,18},{18,0},{2,16},{16,2},{4,22},{22,4},{6,20},{20,6},{1,19},{19... | collective-permute-start | bytes 589832 | tf_op jit(solution)/shard_map/ppermute | solution.py:448
  17.7 14.9 %collective-permute-start.6 = (f32[24,16,128]{2,1,0:T(8,128)S(1)}, f32[24,16,128]{2,1,0:T(8,128)S(1)}, u32[]{:S(2)}, u32[]{:S(2)}) collective-permute-start(f32[24,16,128]{2,1,0:T(8,128)S(1)} %collective-permute-done.rest_0_), channel_id=1, source_target_pairs={{0,2},{2,0},{4,6},{6,4},{1,3},{3,1},{5,7},{7,5}} | collective-permute-start | bytes 589832 | tf_op jit(solution)/shard_map/ppermute | solution.py:438
  21.1 0.9 %copy-start.1 = (f32[24,16,128]{2,1,0:T(8,128)S(1)}, f32[24,16,128]{2,1,0:T(8,128)}, u32[]{:S(2)}) copy-start(f32[24,16,128]{2,1,0:T(8,128)} %get-tuple-element.59.own) | copy-start | bytes 589828
  22.0 2.2 %copy-start.2 = (f32[1,32,256]{2,1,0:T(8,128)S(1)}, f32[1,32,256]{2,1,0:T(8,128)}, u32[]{:S(2)}) copy-start(f32[1,32,256]{2,1,0:T(8,128)} %refs_1_.1) | copy-start | bytes 98308
  22.0 2.2 %copy-start.3 = (f32[1,32,256]{2,1,0:T(8,128)S(1)}, f32[1,32,256]{2,1,0:T(8,128)}, u32[]{:S(2)}) copy-start(f32[1,32,256]{2,1,0:T(8,128)} %refs_2_.1) | copy-start | bytes 98308
  22.0 2.2 %copy-start.4 = (f32[1,32,256]{2,1,0:T(8,128)S(1)}, f32[1,32,256]{2,1,0:T(8,128)}, u32[]{:S(2)}) copy-start(f32[1,32,256]{2,1,0:T(8,128)} %refs_3_.3) | copy-start | bytes 98308
  22.0 2.2 %copy-start.5 = (s32[1,32,256]{2,1,0:T(8,128)S(1)}, s32[1,32,256]{2,1,0:T(8,128)}, u32[]{:S(2)}) copy-start(s32[1,32,256]{2,1,0:T(8,128)} %refs_4_.3) | copy-start | bytes 98308
  22.0 2.2 %copy-start.6 = (f32[1,32,256]{2,1,0:T(8,128)S(1)}, f32[1,32,256]{2,1,0:T(8,128)}, u32[]{:S(2)}) copy-start(f32[1,32,256]{2,1,0:T(8,128)} %refs_5_.1) | copy-start | bytes 98308
  22.0 2.2 %copy-start.8 = (s32[3,4,2]{1,2,0:T(2,128)S(1)}, s32[3,4,2]{1,2,0:T(2,128)}, u32[]{:S(2)}) copy-start(s32[3,4,2]{1,2,0:T(2,128)} %param.17) | copy-start | bytes 292
  22.1 2.2 %copy-start.9 = (s32[3,4,2]{1,2,0:T(2,128)S(1)}, s32[3,4,2]{1,2,0:T(2,128)}, u32[]{:S(2)}) copy-start(s32[3,4,2]{1,2,0:T(2,128)} %param.18) | copy-start | bytes 292
  22.1 2.2 %copy-start.10 = (s32[3,4,2]{1,2,0:T(2,128)S(1)}, s32[3,4,2]{1,2,0:T(2,128)}, u32[]{:S(2)}) copy-start(s32[3,4,2]{1,2,0:T(2,128)} %param.19) | copy-start | bytes 292
  22.1 2.2 %copy-start.11 = (f32[4,3]{1,0:T(4,128)S(1)}, f32[4,3]{1,0:T(4,128)}, u32[]{:S(2)}) copy-start(f32[4,3]{1,0:T(4,128)} %refs_6_.1) | copy-start | bytes 148
  22.1 10.4 %collective-permute-start.5 = (f32[24,16,128]{2,1,0:T(8,128)S(1)}, f32[24,16,128]{2,1,0:T(8,128)S(1)}, u32[]{:S(2)}, u32[]{:S(2)}) collective-permute-start(f32[24,16,128]{2,1,0:T(8,128)S(1)} %merge.2), channel_id=1, source_target_pairs={{0,24},{24,0},{2,26},{26,2},{4,28},{28,4},{6,30},{30,6},{1,25},{25... | collective-permute-start | bytes 589832 | tf_op jit(solution)/shard_map/ppermute | solution.py:448
  34.3 4.8 %collective-permute-start.7 = (f32[24,256]{1,0:T(8,128)S(1)}, f32[24,256]{1,0:T(8,128)S(1)}, u32[]{:S(2)}, u32[]{:S(2)}) collective-permute-start(f32[24,256]{1,0:T(8,128)S(1)} %get-tuple-element.66), channel_id=1, source_target_pairs={{2,4},{4,2},{6,0},{0,6},{3,5},{5,3},{7,1},{1,7},{10,12},{12,10},{1... | collective-permute-start | bytes 73736 | tf_op jit(solution)/shard_map/ppermute | solution.py:538
  35.8 3.8 %collective-permute-start.8 = (f32[24,256]{1,0:T(8,128)S(1)}, f32[24,256]{1,0:T(8,128)S(1)}, u32[]{:S(2)}, u32[]{:S(2)}) collective-permute-start(f32[24,256]{1,0:T(8,128)S(1)} %get-tuple-element.67), channel_id=1, source_target_pairs={{0,2},{2,0},{4,6},{6,4},{1,3},{3,1},{5,7},{7,5},{8,10},{10,8},{12,... | collective-permute-start | bytes 73736 | tf_op jit(solution)/shard_map/ppermute | solution.py:538
  37.0 1.2 %collective-permute-start.9 = (f32[32,128]{1,0:T(8,128)S(1)}, f32[32,128]{1,0:T(8,128)S(1)}, u32[]{:S(2)}, u32[]{:S(2)}) collective-permute-start(f32[32,128]{1,0:T(8,128)S(1)} %get-tuple-element.68), channel_id=1, source_target_pairs={{0,1},{1,0},{2,3},{3,2},{4,5},{5,4},{6,7},{7,6},{8,9},{9,8},{10,11... | collective-permute-start | bytes 49160 | tf_op jit(solution)/shard_map/ppermute | solution.py:539
  40.8 11.8 %collective-permute-start.10 = (f32[24,16,128]{2,1,0:T(8,128)S(1)}, f32[24,16,128]{2,1,0:T(8,128)S(1)}, u32[]{:S(2)}, u32[]{:S(2)}) collective-permute-start(f32[24,16,128]{2,1,0:T(8,128)S(1)} %get-tuple-element.70), channel_id=1, source_target_pairs={{0,8},{8,0},{2,10},{10,2},{4,12},{12,4},{6,14},{14,6},{1,9},{9,1},... | collective-permute-start | bytes 589832 | tf_op jit(solution)/shard_map/ppermute | solution.py:448
  43.8 8.8 %collective-permute-start.11 = (f32[24,16,128]{2,1,0:T(8,128)S(1)}, f32[24,16,128]{2,1,0:T(8,128)S(1)}, u32[]{:S(2)}, u32[]{:S(2)}) collective-permute-start(f32[24,16,128]{2,1,0:T(8,128)S(1)} %get-tuple-element.72), channel_id=1, source_target_pairs={{0,16},{16,0},{2,18},{18,2},{4,20},{20,4},{6,22},{22,6},{1,17},{17... | collective-permute-start | bytes 589832 | tf_op jit(solution)/shard_map/ppermute | solution.py:448
  45.7 10.1 %collective-permute-start.14 = (f32[24,16,128]{2,1,0:T(8,128)S(1)}, f32[24,16,128]{2,1,0:T(8,128)S(1)}, u32[]{:S(2)}, u32[]{:S(2)}) collective-permute-start(f32[24,16,128]{2,1,0:T(8,128)S(1)} %get-tuple-element.78), channel_id=1, source_target_pairs={{0,2},{2,0},{4,6},{6,4},{1,3},{3,1},{5,7},{7,5}} | collective-permute-start | bytes 589832 | tf_op jit(solution)/shard_map/ppermute | solution.py:438
  48.4 10.6 %collective-permute-start.12 = (f32[24,16,128]{2,1,0:T(8,128)S(1)}, f32[24,16,128]{2,1,0:T(8,128)S(1)}, u32[]{:S(2)}, u32[]{:S(2)}) collective-permute-start(f32[24,16,128]{2,1,0:T(8,128)S(1)} %get-tuple-element.74), channel_id=1, source_target_pairs={{0,10},{26,0},{2,8},{24,2},{4,14},{30,4},{6,12},{28,6},{1,11},{27,... | collective-permute-start | bytes 589832 | tf_op jit(solution)/shard_map/ppermute | solution.py:448
  50.4 17.0 %collective-permute-start.13 = (f32[24,16,128]{2,1,0:T(8,128)S(1)}, f32[24,16,128]{2,1,0:T(8,128)S(1)}, u32[]{:S(2)}, u32[]{:S(2)}) collective-permute-start(f32[24,16,128]{2,1,0:T(8,128)S(1)} %get-tuple-element.75), channel_id=1, source_target_pairs={{0,18},{18,0},{2,16},{16,2},{4,22},{22,4},{6,20},{20,6},{1,19},{19... | collective-permute-start | bytes 589832 | tf_op jit(solution)/shard_map/ppermute | solution.py:448
  52.6 14.7 %collective-permute-start.16 = (f32[24,16,128]{2,1,0:T(8,128)S(1)}, f32[24,16,128]{2,1,0:T(8,128)S(1)}, u32[]{:S(2)}, u32[]{:S(2)}) collective-permute-start(f32[24,16,128]{2,1,0:T(8,128)S(1)} %collective-permute-done.10.rest_0_), channel_id=1, source_target_pairs={{0,2},{2,0},{4,6},{6,4},{1,3},{3,1},{5,7},{7,5}} | collective-permute-start | bytes 589832 | tf_op jit(solution)/shard_map/ppermute | solution.py:438
  55.8 11.5 %collective-permute-start.15 = (f32[24,16,128]{2,1,0:T(8,128)S(1)}, f32[24,16,128]{2,1,0:T(8,128)S(1)}, u32[]{:S(2)}, u32[]{:S(2)}) collective-permute-start(f32[24,16,128]{2,1,0:T(8,128)S(1)} %merge.3), channel_id=1, source_target_pairs={{0,24},{24,0},{2,26},{26,2},{4,28},{28,4},{6,30},{30,6},{1,25},{25... | collective-permute-start | bytes 589832 | tf_op jit(solution)/shard_map/ppermute | solution.py:448
  69.0 4.8 %collective-permute-start.17 = (f32[24,256]{1,0:T(8,128)S(1)}, f32[24,256]{1,0:T(8,128)S(1)}, u32[]{:S(2)}, u32[]{:S(2)}) collective-permute-start(f32[24,256]{1,0:T(8,128)S(1)} %get-tuple-element.82), channel_id=1, source_target_pairs={{2,4},{4,2},{6,0},{0,6},{3,5},{5,3},{7,1},{1,7},{10,12},{12,10},{1... | collective-permute-start | bytes 73736 | tf_op jit(solution)/shard_map/ppermute | solution.py:538
  70.0 3.9 %collective-permute-start.18 = (f32[24,256]{1,0:T(8,128)S(1)}, f32[24,256]{1,0:T(8,128)S(1)}, u32[]{:S(2)}, u32[]{:S(2)}) collective-permute-start(f32[24,256]{1,0:T(8,128)S(1)} %get-tuple-element.83), channel_id=1, source_target_pairs={{0,2},{2,0},{4,6},{6,4},{1,3},{3,1},{5,7},{7,5},{8,10},{10,8},{12,... | collective-permute-start | bytes 73736 | tf_op jit(solution)/shard_map/ppermute | solution.py:538
  70.3 1.2 %collective-permute-start.19 = (f32[32,128]{1,0:T(8,128)S(1)}, f32[32,128]{1,0:T(8,128)S(1)}, u32[]{:S(2)}, u32[]{:S(2)}) collective-permute-start(f32[32,128]{1,0:T(8,128)S(1)} %get-tuple-element.84), channel_id=1, source_target_pairs={{0,1},{1,0},{2,3},{3,2},{4,5},{5,4},{6,7},{7,6},{8,9},{9,8},{10,11... | collective-permute-start | bytes 49160 | tf_op jit(solution)/shard_map/ppermute | solution.py:539
